TPU v7x, 32 devices: a whole 2x2x4 slice. The times are simulated.
32 devices in a mesh: dp: 4 (over y, core), group: 8 (over z, x).
Axes of the slice: x: 2, y: 2, z: 4, core: 2. Of those that a mesh axis runs over, the one named last changes fastest.
Arguments:
- tile_maps: bfloat16 [256, 16, 16, 384], P(('dp', 'group')), may hold values from -45 to 45
- positions: int32 [2, 256], P(None, ('dp', 'group')), may hold values from 0 to 511
- counts: int32 [4], P('dp'), may hold values from 1 to 64, as said below
- routing: int32 [4, 8, 8], P(None, 'group'), may hold values from -1 to 15, as said below
- depth_kernel: float32 [49, 384], replicated, may hold values from -0.875 to 0.875
- depth_bias: float32 [384], replicated, may hold values from -3 to 3
- norm_gain: float32 [384], replicated, may hold values from 0.25 to 1.75
- norm_shift: float32 [384], replicated, may hold values from -2 to 2
- expand_weight: bfloat16 [384, 1536], replicated, may hold values from -0.3125 to 0.3125
- expand_bias: float32 [1536], replicated, may hold values from -1.15 to -0.75
- reduce_weight: bfloat16 [1536, 384], replicated, may hold values from -0.15625 to 0.15625
- reduce_bias: float32 [384], replicated, may hold values from -2 to 2
- layer_scale: float32 [384], replicated, may hold values from 0.3 to 1.5
- head_weight: bfloat16 [384, 768], replicated, may hold values from -0.3125 to 0.3125
- slide_taps: float32 [7, 768], replicated, may hold values from -2.5 to 2.5
- slide_weight: bfloat16 [768, 768], replicated, may hold values from -0.21875 to 0.21875
- slide_bias: float32 [768], replicated, may hold values from -2 to 2
- cotangent: float32 [4, 768], P('dp'), may hold values from -180 to 180
Outputs:
- tile_out: bfloat16 [128, 16, 16, 384], P(('dp', 'group'))
- slide_feature: float32 [4, 768], P('dp')
- grad_expand: float32 [589824], P(('dp', 'group'))
- grad_reduce: float32 [589824], P(('dp', 'group'))
- grad_depth: float32 [18816], P(('dp', 'group'))
Inputs may be any that keep to these rules, and one draw needn't show every extreme that they name: counts[d] is the number of tiles of slide d. At each group index the present tiles of all slides number at most 16, at group index 0 exactly that. routing[d, g, s] is -1 where the slot holds no tile, else e * 4 + p: the tile is processed at slot p of the device with dp index e and group index g. Each processing slot receives at most one tile; at group index 0 every one receives a tile. A device sends at most 2 tiles to each dp index, and some device sends exactly 2 to each.
All inputs are finite; a program needn't handle non-finite values.
Results may differ from a plain program's by a relative error of at most 0.013.
Values may be sent and summed in bfloat16 or wider, within the bound.
No kernel may reach another device: no remote copies, remote signals or barrier semaphores. Data moves between devices by JAX's collectives and lax.ppermute only.
A program may use at most 128 MiB of HBM per device.

v0:
```python
import functools
import math

import jax
import jax.numpy as jnp
import numpy as np
from jax import lax
from jax.experimental import pallas as pl
from jax.experimental.pallas import tpu as pltpu
from jax.sharding import Mesh, PartitionSpec as P

E = 768
KS = 7
KERNEL_TAPS = 7
TILE_DILATION = 3
PROC = 4
DP = ("y", "core")
GROUP = ("g1", "g2")
ALL = DP + GROUP

EPSILON = 1e-06
HALF_ROOT = 0.7071067811865476
INV_ROOT_TAU = 0.3989422804014327
LANES = 128
ROW_UNIT = 16
DEPTH_ROWS = 4
VMEM_BYTES = 56 * 1024 * 1024
ERFC_P = 0.3275911
ERFC_A = (0.254829592, -0.284496736, 1.421413741, -1.453152027, 1.061405429)

HBM = pl.BlockSpec(memory_space=pl.ANY)


def whole(shape):
    return pl.BlockSpec(shape, lambda *_: (0,) * len(shape))


def gelu_and_slope(values):
    size = jnp.abs(values)
    divisor = 1.0 + (ERFC_P * HALF_ROOT) * size
    guess = pl.reciprocal(divisor, approx=True)
    t = guess * (2.0 - divisor * guess)
    bell = jnp.exp(-0.5 * values * values)
    poly = 0.5 * ERFC_A[4]
    for coefficient in ERFC_A[3::-1]:
        poly = poly * t + 0.5 * coefficient
    tail = poly * t * bell
    phi = jnp.where(values >= 0.0, 1.0 - tail, tail)
    return values * phi, phi + values * (INV_ROOT_TAU * bell)


def mix_cols(left_side, right_side):
    return lax.dot_general(
        left_side, right_side, (((1,), (1,)), ((), ())), preferred_element_type=jnp.float32
    )


def mix(left_side, right_side):
    return jnp.dot(left_side, right_side, preferred_element_type=jnp.float32)


def pack_kernel(slides, slots, places, my_ref, route_ref, tiles_ref, packed_ref, table_ref, count_ref, sems):
    my_slide = my_ref[0]

    def copy_of(slot, target):
        return pltpu.make_async_copy(tiles_ref.at[slot], packed_ref.at[target], sems.at[slot])

    for dest in range(slides):
        count_ref[dest] = 0
    for slot in range(slots):
        entry = route_ref[my_slide * slots + slot]

        @pl.when(entry >= 0)
        def _send():
            dest = lax.div(entry, PROC)
            rank = count_ref[dest]
            count_ref[dest] = rank + 1
            copy_of(slot, dest * places + rank).start()

    for field in range(4 * PROC):
        table_ref[field] = 0
    for source in range(slides):
        count_ref[0] = 0
        for slot in range(slots):
            entry = route_ref[source * slots + slot]
            inside = (entry >= my_slide * PROC) & (entry < my_slide * PROC + PROC)

            @pl.when(inside)
            def _take():
                proc = entry - my_slide * PROC
                rank = count_ref[0]
                count_ref[0] = rank + 1
                table_ref[proc] = source * places + rank
                table_ref[PROC + proc] = 1
                table_ref[2 * PROC + proc] = source
                table_ref[3 * PROC + proc] = slot

    for slot in range(slots):
        entry = route_ref[my_slide * slots + slot]

        @pl.when(entry >= 0)
        def _wait():
            copy_of(slot, 0).wait()


def pack_tiles(my_slide, route, tile_maps, slides, places):
    slots = tile_maps.shape[0]
    smem = pl.BlockSpec(memory_space=pltpu.SMEM)
    return pl.pallas_call(
        functools.partial(pack_kernel, slides, slots, places),
        out_shape=(
            jax.ShapeDtypeStruct((slides * places,) + tile_maps.shape[1:], tile_maps.dtype),
            jax.ShapeDtypeStruct((4 * PROC,), jnp.int32),
        ),
        in_specs=[smem, smem, HBM],
        out_specs=(HBM, smem),
        scratch_shapes=[pltpu.SMEM((slides,), jnp.int32), pltpu.SemaphoreType.DMA((slots,))],
        name="pack_tiles",
    )(my_slide, route, tile_maps)


def forward_kernel(
    table_ref,
    tile_ref,
    taps_ref,
    depth_bias_ref,
    gain_ref,
    shift_ref,
    expand_ref,
    expand_bias_ref,
    reduce_ref,
    reduce_bias_ref,
    scale_ref,
    head_ref,
    out_ref,
    embed_ref,
    unit_ref,
    inv_ref,
    hidden_ref,
    slope_ref,
    head_slope_ref,
    source_ref,
    padded,
    depth_out,
    normed,
):
    filled = table_ref[PROC + pl.program_id(0)]
    side = tile_ref.shape[1]
    channels = tile_ref.shape[3]
    cells = side * side
    bands = channels // LANES
    low = ROW_UNIT // 2
    reach = KS // 2

    @pl.when(filled == 0)
    def _empty():
        for ref in (out_ref, embed_ref, unit_ref, inv_ref, hidden_ref, slope_ref, head_slope_ref, source_ref):
            ref[...] = jnp.zeros(ref.shape, ref.dtype)

    @pl.when(filled != 0)
    def _work():
        source_ref[...] = tile_ref[...]
        edge = jnp.zeros((side, low, LANES), jnp.float32)
        for band in range(bands):
            padded[band, :, 0:low, :] = edge
            padded[band, :, low + side :, :] = edge
            padded[band, :, low : low + side, :] = tile_ref[
                0, :, :, band * LANES : (band + 1) * LANES
            ].astype(jnp.float32)

        def convolve(band, carry):
            totals = [
                jnp.broadcast_to(depth_bias_ref[band], (side, LANES)) for _ in range(side)
            ]
            for col in range(KS):
                start = low - reach + col
                weights = [taps_ref[band, pl.ds(row * KS + col, 1), :] for row in range(KS)]
                for at in range(side):
                    line = padded[band, at, start : start + side, :]
                    for row in range(KS):
                        place = at - row + reach
                        if 0 <= place < side:
                            totals[place] = totals[place] + weights[row] * line
            for place in range(side):
                depth_out[band, place * side : (place + 1) * side, :] = totals[place]
            return carry

        lax.fori_loop(0, bands, convolve, 0)

        part = 64
        for start in range(0, cells, part):
            rows = slice(start, start + part)
            pieces = [depth_out[band, rows, :] for band in range(bands)]
            mean = jnp.sum(sum(pieces), axis=1, keepdims=True) * (1.0 / channels)
            pieces = [piece - mean for piece in pieces]
            var = jnp.sum(sum(p * p for p in pieces), axis=1, keepdims=True) * (1.0 / channels)
            inv = lax.rsqrt(var + EPSILON)
            inv_ref[0, rows, :] = jnp.broadcast_to(inv, (part, LANES))
            for band in range(bands):
                lanes = slice(band * LANES, (band + 1) * LANES)
                unit = pieces[band] * inv
                unit_ref[0, rows, lanes] = unit
                normed[rows, lanes] = (unit * gain_ref[:, lanes] + shift_ref[:, lanes]).astype(
                    jnp.bfloat16
                )

        width = 256
        for start in range(0, expand_ref.shape[1], width):
            cols = slice(start, start + width)
            pre = mix(normed[...], expand_ref[:, cols]) + expand_bias_ref[:, cols]
            act, slope = gelu_and_slope(pre)
            hidden_ref[0, :, cols] = act.astype(jnp.bfloat16)
            slope_ref[0, :, cols] = slope.astype(jnp.bfloat16)
        branch = scale_ref[...] * (mix(hidden_ref[0], reduce_ref[...]) + reduce_bias_ref[...])
        section = (tile_ref[0].reshape(cells, channels).astype(jnp.float32) + branch).astype(
            jnp.bfloat16
        )
        out_ref[0] = section.reshape(side, side, channels)
        for start in range(0, head_ref.shape[1], width):
            cols = slice(start, start + width)
            act, slope = gelu_and_slope(mix(section, head_ref[:, cols]))
            head_slope_ref[0, :, cols] = slope.astype(jnp.bfloat16)
            embed_ref[0, :, cols] = jnp.sum(act, axis=0, keepdims=True) * (1.0 / cells)


def forward_block(table, arrived, taps, depth_bias, gain, shift, expand, expand_bias, reduce, reduce_bias, scale, head):
    side, channels = arrived.shape[1], arrived.shape[3]
    cells, hid, embed = side * side, expand.shape[1], head.shape[1]
    bands = channels // LANES

    def per_slot(*shape):
        return pl.BlockSpec((1,) + shape, lambda i, table: (i,) + (0,) * len(shape))

    outs = (
        ((side, side, channels), jnp.bfloat16),
        ((1, embed), jnp.float32),
        ((cells, channels), jnp.float32),
        ((cells, LANES), jnp.float32),
        ((cells, hid), jnp.bfloat16),
        ((cells, hid), jnp.bfloat16),
        ((cells, embed), jnp.bfloat16),
        ((side, side, channels), jnp.bfloat16),
    )
    consts = (taps, depth_bias, gain, shift, expand, expand_bias, reduce, reduce_bias, scale, head)
    return pl.pallas_call(
        forward_kernel,
        out_shape=tuple(jax.ShapeDtypeStruct((PROC,) + shape, kind) for shape, kind in outs),
        grid_spec=pltpu.PrefetchScalarGridSpec(
            num_scalar_prefetch=1,
            grid=(PROC,),
            in_specs=[
                pl.BlockSpec((1, side, side, channels), lambda i, table: (table[i], 0, 0, 0))
            ]
            + [whole(const.shape) for const in consts],
            out_specs=[per_slot(*shape) for shape, _ in outs],
            scratch_shapes=[
                pltpu.VMEM((bands, side, side + ROW_UNIT, LANES), jnp.float32),
                pltpu.VMEM((bands, cells, LANES), jnp.float32),
                pltpu.VMEM((cells, channels), jnp.bfloat16),
            ],
        ),
        compiler_params=pltpu.CompilerParams(vmem_limit_bytes=VMEM_BYTES),
        cost_estimate=pl.CostEstimate(
            flops=2 * PROC * cells * channels * (2 * hid + embed + KS * KS),
            bytes_accessed=24 * 1024 * 1024,
            transcendentals=2 * PROC * cells * (hid + embed),
        ),
        name="forward_block",
    )(table, arrived, *consts)


def slide_kernel(
    length,
    slides,
    info_ref,
    embeds_ref,
    pick_ref,
    codes_ref,
    weight_ref,
    cot_ref,
    taps_ref,
    matrix_ref,
    bias_ref,
    feature_ref,
    grad_ref,
    rows,
    back,
    features,
):
    border = ROW_UNIT
    edge = jnp.zeros((border, rows.shape[2]), jnp.float32)
    reach = KERNEL_TAPS // 2

    def dilate(ref, slide, direction):
        total = ref[slide, border : border + length, :]
        for tap in range(KERNEL_TAPS):
            start = border + direction * (tap - reach) * TILE_DILATION
            total = total + taps_ref[tap : tap + 1, :] * ref[slide, start : start + length, :]
        return total

    def one_slide(slide, carry):
        share = weight_ref[slide]
        here = share > 0.0
        own = mix(pick_ref[slide], embeds_ref[...]) + codes_ref[slide]
        for ref in (rows, back):
            ref[slide, 0:border, :] = edge
            ref[slide, border + length :, :] = edge
        rows[slide, border : border + length, :] = (
            jnp.where(here, own, 0.0).astype(jnp.bfloat16).astype(jnp.float32)
        )
        mixed = dilate(rows, slide, 1).astype(jnp.bfloat16)
        act, slope = gelu_and_slope(mix(mixed, matrix_ref[...]) + bias_ref[...])
        features[pl.ds(slide, 1), :] = jnp.sum(act * share, axis=0, keepdims=True)
        grad_agg = (cot_ref[slide] * share * slope).astype(jnp.bfloat16)
        back[slide, border : border + length, :] = mix_cols(grad_agg, matrix_ref[...])
        total = jnp.where(here, dilate(back, slide, -1), 0.0)
        rows[slide, border : border + length, :] = total.astype(jnp.bfloat16).astype(jnp.float32)
        return carry

    lax.fori_loop(0, slides, one_slide, 0)
    feature_ref[...] = features[pl.ds(info_ref[4 * PROC], 1), :]
    for proc in range(PROC):
        filled = info_ref[PROC + proc]
        at = border + info_ref[3 * PROC + proc]
        row = rows[info_ref[2 * PROC + proc], pl.ds(at, 1), :]
        grad_ref[proc] = jnp.where(filled != 0, row, 0.0)


def slide_grads(info, embeds, pick, codes, weight, cot, taps, matrix, bias):
    slides, length, embed = codes.shape
    smem = pl.BlockSpec(memory_space=pltpu.SMEM)
    vmem = pl.BlockSpec(memory_space=pltpu.VMEM)
    padded = (slides, length + 2 * ROW_UNIT, embed)
    return pl.pallas_call(
        functools.partial(slide_kernel, length, slides),
        out_shape=(
            jax.ShapeDtypeStruct((1, embed), jnp.float32),
            jax.ShapeDtypeStruct((PROC, 1, embed), jnp.float32),
        ),
        in_specs=[smem] + [vmem] * 8,
        out_specs=(vmem, vmem),
        scratch_shapes=[
            pltpu.VMEM(padded, jnp.float32),
            pltpu.VMEM(padded, jnp.float32),
            pltpu.VMEM((max(slides, 8), embed), jnp.float32),
        ],
        compiler_params=pltpu.CompilerParams(vmem_limit_bytes=VMEM_BYTES),
        name="slide_grads",
    )(info, embeds, pick, codes, weight, cot, taps, matrix, bias)


def backward_kernel(
    plan,
    table_ref,
    grad_ref,
    source_ref,
    unit_ref,
    inv_ref,
    hidden_ref,
    slope_ref,
    head_slope_ref,
    gain_ref,
    shift_ref,
    scale_ref,
    expand_ref,
    reduce_ref,
    head_ref,
    expand_order_ref,
    reduce_order_ref,
    eye_ref,
    out_ref,
    grad_pre_all,
    hidden_all,
    normed_all,
    grad_mlp_all,
    padded,
    depth_back,
    tap_sums,
    tap_rows,
):
    step = pl.program_id(0)
    filled = table_ref[PROC + step]
    side = source_ref.shape[1]
    channels = source_ref.shape[3]
    cells = side * side
    bands = channels // LANES
    low = ROW_UNIT // 2
    reach = KS // 2
    rows = pl.ds(pl.multiple_of(step * cells, cells), cells)

    @pl.when(step == 0)
    def _start():
        tap_sums[...] = jnp.zeros(tap_sums.shape, jnp.float32)

    @pl.when(filled == 0)
    def _empty():
        grad_pre_all[rows, :] = jnp.zeros((cells, grad_pre_all.shape[1]), jnp.bfloat16)
        hidden_all[rows, :] = jnp.zeros((cells, hidden_all.shape[1]), jnp.bfloat16)
        normed_all[step] = jnp.zeros(normed_all.shape[1:], jnp.bfloat16)
        grad_mlp_all[step] = jnp.zeros(grad_mlp_all.shape[1:], jnp.bfloat16)

    @pl.when(filled != 0)
    def _work():
        grad_head = (grad_ref[0] * (1.0 / cells) * head_slope_ref[0].astype(jnp.float32)).astype(
            jnp.bfloat16
        )
        grad_mlp = (scale_ref[...] * mix_cols(grad_head, head_ref[...])).astype(jnp.bfloat16)
        grad_mlp_all[step] = mix_cols(eye_ref[...], grad_mlp).astype(jnp.bfloat16)
        hidden_all[rows, :] = hidden_ref[0]
        width = 256
        for start in range(0, expand_ref.shape[1], width):
            cols = slice(start, start + width)
            grad_hidden = mix_cols(grad_mlp, reduce_ref[cols, :])
            grad_pre_all[rows, cols] = (
                grad_hidden * slope_ref[0, :, cols].astype(jnp.float32)
            ).astype(jnp.bfloat16)
        grad_norm = mix_cols(grad_pre_all[rows, :], expand_ref[...])
        normed = (unit_ref[0] * gain_ref[...] + shift_ref[...]).astype(jnp.bfloat16)
        normed_all[step] = mix_cols(expand_order_ref[...], normed).astype(jnp.bfloat16)

        scaled = grad_norm * gain_ref[...]
        unit = unit_ref[0]
        mean = jnp.sum(scaled, axis=1, keepdims=True) * (1.0 / channels)
        mean_unit = jnp.sum(scaled * unit, axis=1, keepdims=True) * (1.0 / channels)
        depth_grad = inv_ref[0, :, 0:1] * (scaled - mean - unit * mean_unit)
        edge = jnp.zeros((side, low, LANES), jnp.float32)
        for band in range(bands):
            lanes = slice(band * LANES, (band + 1) * LANES)
            depth_back[band] = depth_grad[:, lanes]
            padded[band, :, 0:low, :] = edge
            padded[band, :, low + side :, :] = edge
            padded[band, :, low : low + side, :] = source_ref[0, :, :, lanes].astype(jnp.float32)

        def taps_of(band, carry):
            for col in range(KS):
                start = low - reach + col
                sums = [None] * KS
                for at in range(side):
                    line = padded[band, at, start : start + side, :]
                    for row in range(KS):
                        place = at - row + reach
                        if 0 <= place < side:
                            term = line * depth_back[band, place * side : (place + 1) * side, :]
                            sums[row] = term if sums[row] is None else sums[row] + term
                for row in range(KS):
                    total = sums[row]
                    folded = total[0:8, :]
                    for piece in range(8, side, 8):
                        folded = folded + total[piece : piece + 8, :]
                    tap_sums[band, row * KS + col] = tap_sums[band, row * KS + col] + folded
            return carry

        lax.fori_loop(0, bands, taps_of, 0)

    @pl.when(step == pl.num_programs(0) - 1)
    def _finish():
        for band in range(bands):
            lanes = slice(band * LANES, (band + 1) * LANES)
            tap_rows[0 : KS * KS, lanes] = jnp.sum(tap_sums[band], axis=1)
            tap_rows[KS * KS :, lanes] = jnp.zeros((tap_rows.shape[0] - KS * KS, LANES), jnp.float32)
        pieces = expand_ref.shape[1] // channels
        parts = 2 * plan.cross
        for quarter in range(pieces):
            cols = slice(quarter * channels, (quarter + 1) * channels)
            total = mix(normed_all[0], grad_pre_all[0:cells, cols])
            for slot in range(1, PROC):
                total = total + mix(
                    normed_all[slot], grad_pre_all[slot * cells : (slot + 1) * cells, cols]
                )
            out_ref[:, quarter * plan.expand_pad : (quarter + 1) * plan.expand_pad, :] = (
                total.astype(jnp.bfloat16).reshape(parts, plan.expand_pad, channels)
            )
        base = pieces * plan.expand_pad
        block = plan.reduce_block
        span = plan.depth_span * plan.reduce_rows
        for index in range(expand_ref.shape[1] // block):
            cols = slice(index * block, (index + 1) * block)
            total = mix(grad_mlp_all[0], hidden_all[0:cells, cols])
            for slot in range(1, PROC):
                total = total + mix(
                    grad_mlp_all[slot], hidden_all[slot * cells : (slot + 1) * cells, cols]
                )
            turned = mix_cols(reduce_order_ref[...], total.astype(jnp.bfloat16)).astype(jnp.bfloat16)
            y, core = divmod(index, 2)
            for x in range(plan.g2):
                out_ref[core * plan.cross + y * plan.g2 + x, base : base + span, :] = turned[
                    x * span : (x + 1) * span, :
                ]
        base = base + span
        for part in range(parts):
            starts = [plan.tap_start(part, z) for z in range(plan.g1)]
            out_ref[part, base : base + plan.g1 * DEPTH_ROWS, :] = jnp.concatenate(
                [tap_rows[start : start + DEPTH_ROWS, :] for start in starts], axis=0
            ).astype(jnp.bfloat16)


class Plan:

    def __init__(self, slides, members, channels, hid):
        self.devices = slides * members
        self.ys, self.g1, self.g2 = slides // 2, 4, members // 4
        self.cross = self.ys * self.g2
        self.depth_span = self.g1
        self.expand_rows = channels // self.devices
        self.expand_pad = -(-self.g1 * self.expand_rows // ROW_UNIT) * ROW_UNIT
        self.reduce_rows = hid // self.devices
        self.reduce_block = hid // slides
        self.share = KS * KS * channels // self.devices
        self.channels = channels
        self.pieces = hid // channels
        self.rows = self.pieces * self.expand_pad + self.g1 * (self.reduce_rows + DEPTH_ROWS)

    def device(self, part, z):
        core, cross = divmod(part, self.cross)
        y, x = divmod(cross, self.g2)
        return ((y * 2 + core) * self.g1 + z) * self.g2 + x

    def tap_start(self, part, z):
        return self.device(part, z) * self.share // self.channels

    def expand_order(self):
        order = np.zeros((2 * self.cross * self.expand_pad, self.channels), np.float32)
        for part in range(2 * self.cross):
            for z in range(self.g1):
                for row in range(self.expand_rows):
                    target = part * self.expand_pad + z * self.expand_rows + row
                    order[target, self.device(part, z) * self.expand_rows + row] = 1.0
        return order

    def reduce_order(self):
        order = np.zeros((self.reduce_block, self.reduce_block), np.float32)
        for x in range(self.g2):
            for z in range(self.g1):
                for row in range(self.reduce_rows):
                    target = (x * self.g1 + z) * self.reduce_rows + row
                    order[target, (z * self.g2 + x) * self.reduce_rows + row] = 1.0
        return order


def backward_block(plan, table, embed_grad, saved, gain, shift, scale, expand, reduce, head):
    source, unit, inv, hidden, slope, head_slope = saved
    side, channels = source.shape[1], source.shape[3]
    cells, hid = side * side, expand.shape[1]
    bands = channels // LANES
    orders = tuple(
        jnp.asarray(order, jnp.bfloat16)
        for order in (plan.expand_order(), plan.reduce_order(), np.eye(channels, dtype=np.float32))
    )

    def per_slot(array):
        shape = array.shape[1:]
        return pl.BlockSpec((1,) + shape, lambda i, table: (i,) + (0,) * len(shape))

    streams = (embed_grad, source, unit, inv, hidden, slope, head_slope)
    consts = (gain, shift, scale, expand, reduce, head) + orders
    out = (2 * plan.cross, plan.rows, channels)
    return pl.pallas_call(
        functools.partial(backward_kernel, plan),
        out_shape=jax.ShapeDtypeStruct(out, jnp.bfloat16),
        grid_spec=pltpu.PrefetchScalarGridSpec(
            num_scalar_prefetch=1,
            grid=(PROC,),
            in_specs=[per_slot(stream) for stream in streams]
            + [whole(const.shape) for const in consts],
            out_specs=whole(out),
            scratch_shapes=[
                pltpu.VMEM((PROC * cells, hid), jnp.bfloat16),
                pltpu.VMEM((PROC * cells, hid), jnp.bfloat16),
                pltpu.VMEM((PROC, orders[0].shape[0], cells), jnp.bfloat16),
                pltpu.VMEM((PROC, channels, cells), jnp.bfloat16),
                pltpu.VMEM((bands, side, side + ROW_UNIT, LANES), jnp.float32),
                pltpu.VMEM((bands, cells, LANES), jnp.float32),
                pltpu.VMEM((bands, KS * KS, 8, LANES), jnp.float32),
                pltpu.VMEM((KS * KS + 7, channels), jnp.float32),
            ],
        ),
        compiler_params=pltpu.CompilerParams(vmem_limit_bytes=VMEM_BYTES),
        name="backward_block",
    )(table, *streams, *consts)


def exchange(values, names):
    return lax.all_to_all(values, names, split_axis=0, concat_axis=0, tiled=True)


def scatter_sum(plan, payload, my_device):
    channels = plan.channels
    grid = payload.reshape(2, plan.cross, plan.rows, channels)
    grid = jnp.sum(exchange(grid, ("core",)).astype(jnp.float32), axis=0).astype(jnp.bfloat16)
    total = jnp.sum(exchange(grid, ("y", "g2")).astype(jnp.float32), axis=0).astype(jnp.bfloat16)
    cut = plan.pieces * plan.expand_pad
    later = cut + plan.g1 * plan.reduce_rows
    expand = total[:cut].reshape(plan.pieces, plan.expand_pad, channels)
    expand = expand[:, : plan.g1 * plan.expand_rows].reshape(
        plan.pieces, plan.g1, plan.expand_rows, channels
    )
    expand = expand.transpose(1, 0, 2, 3).reshape(plan.g1, -1, channels)
    reduce = total[cut:later].reshape(plan.g1, plan.reduce_rows, channels)
    depth = total[later:].reshape(plan.g1, DEPTH_ROWS, channels)
    last = jnp.concatenate([expand, reduce, depth], axis=1)
    last = jnp.sum(exchange(last, ("g1",)).astype(jnp.float32), axis=0)
    cut = plan.pieces * plan.expand_rows
    later = cut + plan.reduce_rows
    expand = last[:cut].reshape(plan.pieces, plan.expand_rows, channels).transpose(1, 0, 2)
    first = my_device * plan.share
    depth = lax.dynamic_slice(
        last[later:].reshape(-1), (first - first // channels * channels,), (plan.share,)
    )
    return expand.reshape(-1), last[cut:later].reshape(-1), depth


def position_code(positions):
    half_width = E // 2
    channel_ids = jnp.arange(E, dtype=jnp.int32) % half_width
    frequency = jnp.exp(
        (2 * (channel_ids // 2)).astype(jnp.float32) * (-math.log(10000.0) / half_width)
    )
    phase = jnp.where(channel_ids % 2 == 0, 0.0, 0.5 * math.pi)
    rows = jnp.where(
        jnp.arange(E, dtype=jnp.int32) < half_width, positions[0][..., None], positions[1][..., None]
    )
    return jnp.sin(rows.astype(jnp.float32) * frequency + phase)


def on_device(
    tile_maps,
    positions,
    counts,
    routing,
    depth_kernel,
    depth_bias,
    norm_gain,
    norm_shift,
    expand_weight,
    expand_bias,
    reduce_weight,
    reduce_bias,
    layer_scale,
    head_weight,
    slide_taps,
    slide_weight,
    slide_bias,
    cotangent,
):
    slides = lax.axis_size(DP)
    members = lax.axis_size(GROUP)
    my_slide = lax.axis_index(DP)
    my_member = lax.axis_index(GROUP)
    my_device = my_slide * members + my_member
    slots, channels = tile_maps.shape[0], tile_maps.shape[3]
    devices, length, places = slides * members, slots * members, slots // slides
    plan = Plan(slides, members, channels, expand_weight.shape[1])
    route = routing.reshape(-1)
    bands = channels // LANES

    packed, table = pack_tiles(my_slide.reshape(1), route, tile_maps, slides, places)
    arrived = exchange(packed, DP)

    extras = jnp.concatenate(
        [
            cotangent[0],
            route.astype(jnp.float32),
            jnp.zeros((960 - E - slides * slots,), jnp.float32),
            positions.reshape(-1).astype(jnp.float32),
            jnp.zeros((1023 - 960 - 2 * slots,), jnp.float32),
            counts.astype(jnp.float32),
        ]
    )
    extras = exchange(jnp.broadcast_to(extras, (devices, 1024)), ALL)
    route_all = extras[:, E : E + slides * slots].astype(jnp.int32)
    route_all = route_all.reshape(slides, members, slides, slots)[0]
    pos_all = extras[:, 960 : 960 + 2 * slots].reshape(slides, members, 2, slots)
    pos_all = pos_all.transpose(2, 0, 3, 1).reshape(2, slides, length)
    counts_all = extras[:, 1023].reshape(slides, members)[:, 0]
    cot_all = extras[:, :E].reshape(slides, members, 1, E)[:, 0]
    codes = position_code(pos_all)
    member_ids = jnp.arange(members, dtype=jnp.int32)[:, None, None]
    target = jnp.where(
        route_all >= 0, (route_all // PROC * members + member_ids) * PROC + route_all % PROC, -1
    )
    target = target.transpose(1, 2, 0).reshape(slides, length, 1)
    pick = (target == jnp.arange(devices * PROC, dtype=jnp.int32)).astype(jnp.bfloat16)
    steps = jnp.arange(length, dtype=jnp.int32)[None, :, None].astype(jnp.float32)
    weight = jnp.where(steps < counts_all[:, None, None], 1.0 / counts_all[:, None, None], 0.0)

    def row(vector):
        return vector.reshape(1, -1)

    outs = forward_block(
        table,
        arrived,
        depth_kernel.reshape(KS * KS, bands, LANES).transpose(1, 0, 2),
        depth_bias.reshape(bands, 1, LANES),
        row(norm_gain),
        row(norm_shift),
        expand_weight,
        row(expand_bias),
        reduce_weight,
        row(reduce_bias),
        row(layer_scale),
        head_weight,
    )
    tile_out, tile_embed, unit, inv, hidden, slope, head_slope, source = outs
    embeds = exchange(
        jnp.broadcast_to(tile_embed.reshape(PROC, E).astype(jnp.bfloat16), (devices, PROC, E)), ALL
    )
    info = jnp.concatenate(
        [
            table[: 3 * PROC],
            table[3 * PROC :] * members + my_member,
            my_slide.reshape(1),
            jnp.zeros((3,), jnp.int32),
        ]
    )
    feature, embed_grad = slide_grads(
        info,
        embeds.reshape(devices * PROC, E),
        pick,
        codes,
        weight,
        cot_all,
        slide_taps,
        slide_weight,
        row(slide_bias),
    )
    payload = backward_block(
        plan,
        table,
        embed_grad,
        (source, unit, inv, hidden, slope, head_slope),
        row(norm_gain),
        row(norm_shift),
        row(layer_scale),
        expand_weight,
        reduce_weight,
        head_weight,
    )
    shares = scatter_sum(plan, payload, my_device)
    return (tile_out, feature, shares[0], shares[1], shares[2])


def solution(mesh):
    slides, members = mesh.shape["dp"], mesh.shape["group"]
    fine = Mesh(mesh.devices.reshape(slides // 2, 2, 4, members // 4), ALL)
    return jax.shard_map(
        on_device,
        mesh=fine,
        in_specs=(
            P(ALL, None, None, None),
            P(None, ALL),
            P(DP),
            P(None, GROUP, None),
        )
        + (P(),) * 13
        + (P(DP, None),),
        out_specs=(
            P(ALL, None, None, None),
            P(DP, None),
            P(ALL),
            P(ALL),
            P(ALL),
        ),
        check_vma=False,
    )
```

profile of v0, /device:TPU:0, one launch (start us, length us, event | category | flops | bytes accessed | tf_op | source)
XLA Modules:
  0.0 207.2 jit_solution(5821867953281520706)
XLA Ops:
  0.7 0.5 broadcast.209
  1.2 1.3 reduce.10
  2.6 0.1 reshape.232.route_ref
  2.7 0.7 convert_element_type.49
  4.1 0.7 reduce.3
  4.8 0.1 concatenate.10
  4.9 0.7 broadcast_in_dim.66
  5.6 7.3 %all-to-all-start.2 = ((f32[32,1,1024]{2,1,0:T(1,128)}), f32[32,1,1024]{2,1,0:T(1,128)S(1)}, u32[]{:S(2)}, u32[]{:S(2)}) async-start(f32[32,1,1024]{2,1,0:T(1,128)} %broadcast_in_dim.66), calls=%async_computation.2 | async-start | bytes 262144 | tf_op jit(solution)/shard_map/all_to_all | solution.py:583
  13.0 50.0 %pack_tiles.1 = (bf16[8,16,16,384]{3,2,1,0:T(8,128)(2,1)}, s32[16]{0:T(128)}) custom-call(s32[1]{0:T(128)} %bitcast.my_ref, s32[32]{0:T(128)} %copy-done.4, bf16[8,16,16,384]{3,2,1,0:T(8,128)(2,1)} %tiles_ref.1), custom_call_target="tpu_custom_call" | custom-call | tf_op jit(solution)/shard_map/pack_tiles/pallas_call | solution.py:109
  63.0 0.7 multiply_add_fusion
  63.7 1.3 pad_add_fusion.info_ref
  65.0 0.6 copy.87
  65.7 0.6 reshape.234.depth_bias_ref
  66.3 0.5 reshape.235.gain_ref
  66.8 0.6 reshape.236.shift_ref
  67.4 0.6 reshape.237.expand_bias_ref
  68.0 0.5 reshape.238.reduce_bias_ref
  68.5 0.6 reshape.239.scale_ref
  69.1 0.6 reshape.243.bias_ref
  69.7 3.6 %all-to-all-start = ((bf16[8,16,16,384]{3,2,1,0:T(8,128)(2,1)}), bf16[8,16,16,384]{3,2,1,0:T(8,128)(2,1)S(1)}, u32[]{:S(2)}, u32[]{:S(2)}) async-start(bf16[8,16,16,384]{3,2,1,0:T(8,128)(2,1)} %get-tuple-element.18), calls=%async_computation | async-start | bytes 3145728 | tf_op jit(solution)/shard_map/all_to_all | solution.py:583
  73.6 0.1 reshape.241
  74.1 0.2 slice_reduce_fusion
  74.3 0.1 slice_reduce_fusion.1
  74.5 0.6 slice_bitcast_fusion.1.cot_ref
  75.1 0.7 compare_select_fusion.weight_ref
  75.8 17.5 %all-to-all-done.tile_ref = bf16[8,16,16,384]{3,2,1,0:T(8,128)(2,1)S(1)} async-done(((bf16[8,16,16,384]{3,2,1,0:T(8,128)(2,1)}), bf16[8,16,16,384]{3,2,1,0:T(8,128)(2,1)S(1)}, u32[]{:S(2)}, u32[]{:S(2)}) %all-to-all-start) | async-done | bytes 1572896 | tf_op jit(solution)/shard_map/all_to_all | solution.py:583
  93.4 1.1 copy-done
  94.5 23.7 %forward_block.1 = (bf16[4,16,16,384]{3,2,1,0:T(8,128)(2,1)}, f32[4,1,768]{2,1,0:T(1,128)}, f32[4,256,384]{2,1,0:T(8,128)}, f32[4,256,128]{2,1,0:T(8,128)}, bf16...) custom-call(s32[16]{0:T(128)} %get-tuple-element.17.table_ref, ...), custom_call_target="tpu_custom_call" | custom-call | flops 3058434048 | bytes 25165824 | tf_op jit(solution)/shard_map/forward_block/pallas_call | solution.py:245
  118.2 0.7 convert_element_type.46
  118.9 0.7 broadcast_in_dim.63
  119.7 4.3 %all-to-all-start.1 = ((bf16[32,4,768]{2,1,0:T(4,128)(2,1)}), bf16[32,4,768]{2,1,0:T(4,128)(2,1)S(1)}, u32[]{:S(2)}, u32[]{:S(2)}) async-start(bf16[32,4,768]{2,1,0:T(4,128)(2,1)} %broadcast_in_dim.63), calls=%async_computation.1 | async-start | bytes 393216 | tf_op jit(solution)/shard_map/all_to_all | solution.py:583
  124.0 0.7 fusion.pick_ref
  124.7 3.5 %add_sine_fusion.codes_ref = f32[4,64,768]{2,1,0:T(8,128)} fusion(f32[768]{0:T(1024)S(1)} %get-tuple-element.36, f32[768]{0:T(1024)S(1)} %get-tuple-element.35, f32[4,64]{1,0:T(4,128)S(1)} %broadcast_in_dim.70, f32[4,64]{1,0:T(4,128)S(1)} %broadcast_in_dim.68, pred[768]{0:T(1024)(128)(4,1)S(1)} %iota_compare_fusion.1), kind=kLoop, calls=%fused_computation | loop fusion | flops 589824 | bytes 795392 | tf_op jit(solution)/shard_map/sin | solution.py:622
  128.2 4.1 %all-to-all-done.1 = bf16[32,4,768]{2,1,0:T(4,128)(2,1)S(1)} async-done(((bf16[32,4,768]{2,1,0:T(4,128)(2,1)}), bf16[32,4,768]{2,1,0:T(4,128)(2,1)S(1)}, u32[]{:S(2)}, u32[]{:S(2)}) %all-to-all-start.1) | async-done | bytes 196640 | tf_op jit(solution)/shard_map/all_to_all | solution.py:583
  132.4 0.7 reshape.240.embeds_ref
  133.1 6.6 %slide_grads.1 = (f32[1,768]{1,0:T(1,128)}, f32[4,1,768]{2,1,0:T(1,128)}) custom-call(s32[20]{0:T(128)} %pad_add_fusion.info_ref, bf16[128,768]{1,0:T(8,128)(2,1)} %reshape.240.embeds_ref, bf16[4,64,128]{2,1,0:T(8,128)(2,1)} %fusion.pick_ref, f32[4,64,768]{2,1,0:T(8,128)} %add_sine_fusion.codes_ref, f32[4,64,1]{2,1,0:T(8,128)} %compare_select_fusion.weight_ref, ...), custom_call_target="tpu_custom_call" | custom-call | tf_op jit(solution)/shard_map/slide_grads/pallas_call | solution.py:334
  139.7 21.5 %backward_block.1 = bf16[8,400,384]{2,1,0:T(8,128)(2,1)} custom-call(s32[16]{0:T(128)} %get-tuple-element.17.table_ref, f32[4,1,768]{2,1,0:T(1,128)} %get-tuple-element.22.grad_ref, bf16[4,16,16,384]{3,2,1,0:T(8,128)(2,1)} %get-tuple-element.23.source_ref, f32[4,256,384]{2,1,0:T(8,128)} %get-tuple-element.24.unit_ref, ...), custom_call_target="tpu_custom_call" | custom-call | tf_op jit(solution)/shard_map/backward_block/pallas_call | solution.py:557
  161.2 6.9 %all_to_all.34 = bf16[2,4,400,384]{3,2,1,0:T(8,128)(2,1)S(1)} all-to-all(bf16[2,4,400,384]{3,2,1,0:T(8,128)(2,1)} %bitcast.29), channel_id=1, replica_groups=mesh['y'=2,'core'=2,'g1'=4,'g2'=2] {'core'}, dimensions={0} | all-to-all | bytes 4915200 | tf_op jit(solution)/shard_map/all_to_all | solution.py:583
  168.2 1.8 reduce_sum.33
  170.0 20.4 %all_to_all.35 = bf16[4,400,384]{2,1,0:T(8,128)(2,1)S(1)} all-to-all(bf16[4,400,384]{2,1,0:T(8,128)(2,1)} %reduce_sum.33), channel_id=1, replica_groups=mesh['y'=2,'core'=2,'g1'=4,'g2'=2] {'y','g2'}, dimensions={0} | all-to-all | bytes 2457600 | tf_op jit(solution)/shard_map/all_to_all | solution.py:583
  190.4 0.3 reduce_sum.34
  190.9 0.2 pad_maximum_fusion
  191.2 0.8 copy.79
  191.9 3.5 %all-to-all-start.5 = ((bf16[4,100,384]{2,1,0:T(8,128)(2,1)}), bf16[4,100,384]{2,1,0:T(8,128)(2,1)S(1)}, u32[]{:S(2)}, u32[]{:S(2)}) async-start(bf16[4,100,384]{2,1,0:T(8,128)(2,1)} %copy.79), calls=%async_computation.5 | async-start | bytes 638976 | tf_op jit(solution)/shard_map/all_to_all | solution.py:583
  195.4 9.7 %all-to-all-done.5 = bf16[4,100,384]{2,1,0:T(8,128)(2,1)S(1)} async-done(((bf16[4,100,384]{2,1,0:T(8,128)(2,1)}), bf16[4,100,384]{2,1,0:T(8,128)(2,1)S(1)}, u32[]{:S(2)}, u32[]{:S(2)}) %all-to-all-start.5) | async-done | bytes 307232 | tf_op jit(solution)/shard_map/all_to_all | solution.py:583
  205.2 0.7 reshape.249
  205.9 0.6 reshape.250
  206.5 0.7 dynamic_slice.3
  (60 shorter events, 1.2 us)
Async XLA Ops:
  0.6 64.4 %copy-start.1 = (f32[49,384]{1,0:T(8,128)S(1)}, f32[49,384]{1,0:T(8,128)}, u32[]{:S(2)}) copy-start(f32[49,384]{1,0:T(8,128)} %param.25) | copy-start | bytes 225796
  0.6 65.0 %copy-start.5 = (f32[384]{0:T(512)S(1)}, f32[384]{0:T(512)}, u32[]{:S(2)}) copy-start(f32[384]{0:T(512)} %param.26) | copy-start | bytes 4612
  0.7 65.6 %copy-start.6 = (f32[384]{0:T(512)S(1)}, f32[384]{0:T(512)}, u32[]{:S(2)}) copy-start(f32[384]{0:T(512)} %param.27) | copy-start | bytes 4612
  0.7 66.1 %copy-start.7 = (f32[384]{0:T(512)S(1)}, f32[384]{0:T(512)}, u32[]{:S(2)}) copy-start(f32[384]{0:T(512)} %param.28) | copy-start | bytes 4612
  0.7 66.7 %copy-start.2 = (f32[1536]{0:T(1024)S(1)}, f32[1536]{0:T(1024)}, u32[]{:S(2)}) copy-start(f32[1536]{0:T(1024)} %param.30) | copy-start | bytes 18436
  0.7 67.3 %copy-start.8 = (f32[384]{0:T(512)S(1)}, f32[384]{0:T(512)}, u32[]{:S(2)}) copy-start(f32[384]{0:T(512)} %param.32) | copy-start | bytes 4612
  0.7 67.8 %copy-start.9 = (f32[384]{0:T(512)S(1)}, f32[384]{0:T(512)}, u32[]{:S(2)}) copy-start(f32[384]{0:T(512)} %param.33) | copy-start | bytes 4612
  0.7 68.4 %copy-start.3 = (f32[768]{0:T(1024)S(1)}, f32[768]{0:T(1024)}, u32[]{:S(2)}) copy-start(f32[768]{0:T(1024)} %param.37) | copy-start | bytes 9220
  2.7 10.3 %copy-start.4 = (s32[32]{0:T(128)}, s32[32]{0:T(128)S(1)}, u32[]{:S(2)}) copy-start(s32[32]{0:T(128)S(1)} %reshape.232.route_ref) | copy-start | bytes 388
  5.6 64.1 %all-to-all-start.2 = ((f32[32,1,1024]{2,1,0:T(1,128)}), f32[32,1,1024]{2,1,0:T(1,128)S(1)}, u32[]{:S(2)}, u32[]{:S(2)}) async-start(f32[32,1,1024]{2,1,0:T(1,128)} %broadcast_in_dim.66), calls=%async_computation.2 | async-start | bytes 262144 | tf_op jit(solution)/shard_map/all_to_all | solution.py:583
  69.7 23.6 %all-to-all-start = ((bf16[8,16,16,384]{3,2,1,0:T(8,128)(2,1)}), bf16[8,16,16,384]{3,2,1,0:T(8,128)(2,1)S(1)}, u32[]{:S(2)}, u32[]{:S(2)}) async-start(bf16[8,16,16,384]{3,2,1,0:T(8,128)(2,1)} %get-tuple-element.18), calls=%async_computation | async-start | bytes 3145728 | tf_op jit(solution)/shard_map/all_to_all | solution.py:583
  93.4 1.1 copy-start
  119.7 12.7 %all-to-all-start.1 = ((bf16[32,4,768]{2,1,0:T(4,128)(2,1)}), bf16[32,4,768]{2,1,0:T(4,128)(2,1)S(1)}, u32[]{:S(2)}, u32[]{:S(2)}) async-start(bf16[32,4,768]{2,1,0:T(4,128)(2,1)} %broadcast_in_dim.63), calls=%async_computation.1 | async-start | bytes 393216 | tf_op jit(solution)/shard_map/all_to_all | solution.py:583
  191.9 13.1 %all-to-all-start.5 = ((bf16[4,100,384]{2,1,0:T(8,128)(2,1)}), bf16[4,100,384]{2,1,0:T(8,128)(2,1)S(1)}, u32[]{:S(2)}, u32[]{:S(2)}) async-start(bf16[4,100,384]{2,1,0:T(8,128)(2,1)} %copy.79), calls=%async_computation.5 | async-start | bytes 638976 | tf_op jit(solution)/shard_map/all_to_all | solution.py:583
where the time goes:
time: 208 us; the launch traced here: 207 us
  Pallas kernels  102 us (49%)
  waiting for transfers between devices  31.3 us (15%)
  blocking collectives  27.3 us (13%)
  starting transfers between devices  18.6 us (9%)
  local copies, waits for them, and re-layouts  13.5 us (6%)
  other arithmetic  12.9 us (6%)
    pallas_call x1, Pallas kernels, pack_tiles(): pl.pallas_call(functools.partial(pack_kernel, slides, slots, places), out...  50 us
    all_to_all x4, waiting for transfers between devices, exchange(): lax.all_to_all(values, names, split_axis=0, concat_axis=0, tiled=True)  31.3 us
    all_to_all x2, blocking collectives, exchange(): lax.all_to_all(values, names, split_axis=0, concat_axis=0, tiled=True)  27.3 us
    pallas_call x1, Pallas kernels, forward_block(): pl.pallas_call(forward_kernel, out_shape=tuple((jax.ShapeDtypeStruct((PRO...  23.7 us
    pallas_call x1, Pallas kernels, backward_block(): pl.pallas_call(functools.partial(backward_kernel, plan), out_shape=jax.Sh...  21.5 us
    all_to_all x4, starting transfers between devices, exchange(): lax.all_to_all(values, names, split_axis=0, concat_axis=0, tiled=True)  18.6 us
    pallas_call x1, Pallas kernels, slide_grads(): pl.pallas_call(functools.partial(slide_kernel, length, slides), out_shape...  6.61 us
  transfers between devices with their start and end apart: 4, of which 3 were waited for; matrix products, arithmetic and copies ran while one was open for 6% of the time, Pallas kernels for 24%

commit v1 on v0

--- a/solution.py
+++ b/solution.py
@@ -25,6 +25,9 @@
 ROW_UNIT = 16
 DEPTH_ROWS = 4
 VMEM_BYTES = 56 * 1024 * 1024
+PART = 32
+WIDTH = 256
+GAIN, SHIFT, SCALE, REDUCE_BIAS, DEPTH_BIAS, EXPAND_BIAS, SLIDE_BIAS = range(7)
 ERFC_P = 0.3275911
 ERFC_A = (0.254829592, -0.284496736, 1.421413741, -1.453152027, 1.061405429)
 
@@ -113,7 +116,7 @@
             jax.ShapeDtypeStruct((4 * PROC,), jnp.int32),
         ),
         in_specs=[smem, smem, HBM],
-        out_specs=(HBM, smem),
+        out_specs=(pl.BlockSpec(memory_space=pltpu.VMEM), smem),
         scratch_shapes=[pltpu.SMEM((slides,), jnp.int32), pltpu.SemaphoreType.DMA((slots,))],
         name="pack_tiles",
     )(my_slide, route, tile_maps)
@@ -123,14 +126,9 @@
     table_ref,
     tile_ref,
     taps_ref,
-    depth_bias_ref,
-    gain_ref,
-    shift_ref,
+    vectors_ref,
     expand_ref,
-    expand_bias_ref,
     reduce_ref,
-    reduce_bias_ref,
-    scale_ref,
     head_ref,
     out_ref,
     embed_ref,
@@ -143,6 +141,8 @@
     padded,
     depth_out,
     normed,
+    pre,
+    section,
 ):
     filled = table_ref[PROC + pl.program_id(0)]
     side = tile_ref.shape[1]
@@ -164,17 +164,20 @@
         for band in range(bands):
             padded[band, :, 0:low, :] = edge
             padded[band, :, low + side :, :] = edge
-            padded[band, :, low : low + side, :] = tile_ref[
-                0, :, :, band * LANES : (band + 1) * LANES
-            ].astype(jnp.float32)
+            for at in range(side):
+                padded[band, at, low : low + side, :] = tile_ref[
+                    0, at, :, band * LANES : (band + 1) * LANES
+                ].astype(jnp.float32)
 
         def convolve(band, carry):
-            totals = [
-                jnp.broadcast_to(depth_bias_ref[band], (side, LANES)) for _ in range(side)
-            ]
+            lanes = pl.ds(pl.multiple_of(band * LANES, LANES), LANES)
+            bias = jnp.broadcast_to(vectors_ref[DEPTH_BIAS : DEPTH_BIAS + 1, lanes], (side, LANES))
+            totals = [bias for _ in range(side)]
             for col in range(KS):
                 start = low - reach + col
-                weights = [taps_ref[band, pl.ds(row * KS + col, 1), :] for row in range(KS)]
+                weights = [
+                    taps_ref[row * KS + col : row * KS + col + 1, lanes] for row in range(KS)
+                ]
                 for at in range(side):
                     line = padded[band, at, start : start + side, :]
                     for row in range(KS):
@@ -187,43 +190,59 @@
 
         lax.fori_loop(0, bands, convolve, 0)
 
-        part = 64
-        for start in range(0, cells, part):
-            rows = slice(start, start + part)
+        def vector(index, lanes):
+            return vectors_ref[index : index + 1, lanes]
+
+        for start in range(0, cells, PART):
+            rows = slice(start, start + PART)
             pieces = [depth_out[band, rows, :] for band in range(bands)]
             mean = jnp.sum(sum(pieces), axis=1, keepdims=True) * (1.0 / channels)
             pieces = [piece - mean for piece in pieces]
             var = jnp.sum(sum(p * p for p in pieces), axis=1, keepdims=True) * (1.0 / channels)
             inv = lax.rsqrt(var + EPSILON)
-            inv_ref[0, rows, :] = jnp.broadcast_to(inv, (part, LANES))
+            inv_ref[0, rows, :] = jnp.broadcast_to(inv, (PART, LANES))
             for band in range(bands):
                 lanes = slice(band * LANES, (band + 1) * LANES)
                 unit = pieces[band] * inv
                 unit_ref[0, rows, lanes] = unit
-                normed[rows, lanes] = (unit * gain_ref[:, lanes] + shift_ref[:, lanes]).astype(
+                normed[rows, lanes] = (unit * vector(GAIN, lanes) + vector(SHIFT, lanes)).astype(
                     jnp.bfloat16
                 )
 
-        width = 256
-        for start in range(0, expand_ref.shape[1], width):
-            cols = slice(start, start + width)
-            pre = mix(normed[...], expand_ref[:, cols]) + expand_bias_ref[:, cols]
-            act, slope = gelu_and_slope(pre)
-            hidden_ref[0, :, cols] = act.astype(jnp.bfloat16)
-            slope_ref[0, :, cols] = slope.astype(jnp.bfloat16)
-        branch = scale_ref[...] * (mix(hidden_ref[0], reduce_ref[...]) + reduce_bias_ref[...])
-        section = (tile_ref[0].reshape(cells, channels).astype(jnp.float32) + branch).astype(
-            jnp.bfloat16
-        )
-        out_ref[0] = section.reshape(side, side, channels)
-        for start in range(0, head_ref.shape[1], width):
-            cols = slice(start, start + width)
-            act, slope = gelu_and_slope(mix(section, head_ref[:, cols]))
-            head_slope_ref[0, :, cols] = slope.astype(jnp.bfloat16)
-            embed_ref[0, :, cols] = jnp.sum(act, axis=0, keepdims=True) * (1.0 / cells)
-
-
-def forward_block(table, arrived, taps, depth_bias, gain, shift, expand, expand_bias, reduce, reduce_bias, scale, head):
+        for index, begin in enumerate(range(0, expand_ref.shape[1], WIDTH)):
+            cols = slice(begin, begin + WIDTH)
+            buffer = index % pre.shape[0]
+            pre[buffer] = mix(normed[...], expand_ref[:, cols])
+            for start in range(0, cells, PART):
+                rows = slice(start, start + PART)
+                act, slope = gelu_and_slope(pre[buffer, rows, :] + vector(EXPAND_BIAS, cols))
+                hidden_ref[0, rows, cols] = act.astype(jnp.bfloat16)
+                slope_ref[0, rows, cols] = slope.astype(jnp.bfloat16)
+        lanes = slice(0, channels)
+        depth_rows = mix(hidden_ref[0], reduce_ref[...])
+        for at in range(side):
+            rows = slice(at * side, (at + 1) * side)
+            branch = vector(SCALE, lanes) * (depth_rows[rows] + vector(REDUCE_BIAS, lanes))
+            line = (tile_ref[0, at].astype(jnp.float32) + branch).astype(jnp.bfloat16)
+            section[rows, :] = line
+            out_ref[0, at] = line
+        for index, begin in enumerate(range(0, head_ref.shape[1], WIDTH)):
+            cols = slice(begin, begin + WIDTH)
+            buffer = index % pre.shape[0]
+            pre[buffer] = mix(section[...], head_ref[:, cols])
+            total = None
+            for start in range(0, cells, PART):
+                rows = slice(start, start + PART)
+                act, slope = gelu_and_slope(pre[buffer, rows, :])
+                head_slope_ref[0, rows, cols] = slope.astype(jnp.bfloat16)
+                folded = act[0:8]
+                for piece in range(8, PART, 8):
+                    folded = folded + act[piece : piece + 8]
+                total = folded if total is None else total + folded
+            embed_ref[0, :, cols] = jnp.sum(total, axis=0, keepdims=True) * (1.0 / cells)
+
+
+def forward_block(table, arrived, taps, vectors, expand, reduce, head):
     side, channels = arrived.shape[1], arrived.shape[3]
     cells, hid, embed = side * side, expand.shape[1], head.shape[1]
     bands = channels // LANES
@@ -241,7 +260,7 @@
         ((cells, embed), jnp.bfloat16),
         ((side, side, channels), jnp.bfloat16),
     )
-    consts = (taps, depth_bias, gain, shift, expand, expand_bias, reduce, reduce_bias, scale, head)
+    consts = (taps, vectors, expand, reduce, head)
     return pl.pallas_call(
         forward_kernel,
         out_shape=tuple(jax.ShapeDtypeStruct((PROC,) + shape, kind) for shape, kind in outs),
@@ -257,6 +276,8 @@
                 pltpu.VMEM((bands, side, side + ROW_UNIT, LANES), jnp.float32),
                 pltpu.VMEM((bands, cells, LANES), jnp.float32),
                 pltpu.VMEM((cells, channels), jnp.bfloat16),
+                pltpu.VMEM((3, cells, WIDTH), jnp.float32),
+                pltpu.VMEM((cells, channels), jnp.bfloat16),
             ],
         ),
         compiler_params=pltpu.CompilerParams(vmem_limit_bytes=VMEM_BYTES),
@@ -280,41 +301,60 @@
     cot_ref,
     taps_ref,
     matrix_ref,
-    bias_ref,
+    vectors_ref,
     feature_ref,
     grad_ref,
     rows,
     back,
     features,
+    mixed,
+    pre,
+    grad_agg,
 ):
     border = ROW_UNIT
     edge = jnp.zeros((border, rows.shape[2]), jnp.float32)
     reach = KERNEL_TAPS // 2
-
-    def dilate(ref, slide, direction):
-        total = ref[slide, border : border + length, :]
+    blocks = [slice(start, start + WIDTH) for start in range(0, rows.shape[2], WIDTH)]
+
+    def dilate(ref, slide, direction, cols):
+        total = ref[slide, border : border + length, cols]
         for tap in range(KERNEL_TAPS):
             start = border + direction * (tap - reach) * TILE_DILATION
-            total = total + taps_ref[tap : tap + 1, :] * ref[slide, start : start + length, :]
+            total = total + taps_ref[tap : tap + 1, cols] * ref[slide, start : start + length, cols]
         return total
 
     def one_slide(slide, carry):
-        share = weight_ref[slide]
-        here = share > 0.0
-        own = mix(pick_ref[slide], embeds_ref[...]) + codes_ref[slide]
+        here = weight_ref[slide] > 0.0
         for ref in (rows, back):
             ref[slide, 0:border, :] = edge
             ref[slide, border + length :, :] = edge
-        rows[slide, border : border + length, :] = (
-            jnp.where(here, own, 0.0).astype(jnp.bfloat16).astype(jnp.float32)
-        )
-        mixed = dilate(rows, slide, 1).astype(jnp.bfloat16)
-        act, slope = gelu_and_slope(mix(mixed, matrix_ref[...]) + bias_ref[...])
-        features[pl.ds(slide, 1), :] = jnp.sum(act * share, axis=0, keepdims=True)
-        grad_agg = (cot_ref[slide] * share * slope).astype(jnp.bfloat16)
-        back[slide, border : border + length, :] = mix_cols(grad_agg, matrix_ref[...])
-        total = jnp.where(here, dilate(back, slide, -1), 0.0)
-        rows[slide, border : border + length, :] = total.astype(jnp.bfloat16).astype(jnp.float32)
+        for cols in blocks:
+            own = mix(pick_ref[slide], embeds_ref[:, cols]) + codes_ref[slide, :, cols]
+            rows[slide, border : border + length, cols] = (
+                jnp.where(here, own, 0.0).astype(jnp.bfloat16).astype(jnp.float32)
+            )
+            mixed[:, cols] = dilate(rows, slide, 1, cols).astype(jnp.bfloat16)
+        for cols in blocks:
+            pre[:, cols] = mix(mixed[...], matrix_ref[:, cols])
+            total = None
+            for start in range(0, length, PART):
+                part = slice(start, start + PART)
+                share = weight_ref[slide, part, :]
+                act, slope = gelu_and_slope(
+                    pre[part, cols] + vectors_ref[SLIDE_BIAS : SLIDE_BIAS + 1, cols]
+                )
+                grad_agg[part, cols] = (cot_ref[slide, :, cols] * share * slope).astype(jnp.bfloat16)
+                piece = jnp.sum(act * share, axis=0, keepdims=True)
+                total = piece if total is None else total + piece
+            features[pl.ds(slide, 1), cols] = total
+        for cols in blocks:
+            back[slide, border : border + length, cols] = mix_cols(
+                grad_agg[...], matrix_ref[cols, :]
+            )
+            total = jnp.where(here, dilate(back, slide, -1, cols), 0.0)
+            rows[slide, border : border + length, cols] = total.astype(jnp.bfloat16).astype(
+                jnp.float32
+            )
         return carry
 
     lax.fori_loop(0, slides, one_slide, 0)
@@ -326,7 +366,7 @@
         grad_ref[proc] = jnp.where(filled != 0, row, 0.0)
 
 
-def slide_grads(info, embeds, pick, codes, weight, cot, taps, matrix, bias):
+def slide_grads(info, embeds, pick, codes, weight, cot, taps, matrix, vectors):
     slides, length, embed = codes.shape
     smem = pl.BlockSpec(memory_space=pltpu.SMEM)
     vmem = pl.BlockSpec(memory_space=pltpu.VMEM)
@@ -343,10 +383,13 @@
             pltpu.VMEM(padded, jnp.float32),
             pltpu.VMEM(padded, jnp.float32),
             pltpu.VMEM((max(slides, 8), embed), jnp.float32),
+            pltpu.VMEM((length, embed), jnp.bfloat16),
+            pltpu.VMEM((length, embed), jnp.float32),
+            pltpu.VMEM((length, embed), jnp.bfloat16),
         ],
         compiler_params=pltpu.CompilerParams(vmem_limit_bytes=VMEM_BYTES),
         name="slide_grads",
-    )(info, embeds, pick, codes, weight, cot, taps, matrix, bias)
+    )(info, embeds, pick, codes, weight, cot, taps, matrix, vectors)
 
 
 def backward_kernel(
@@ -359,24 +402,27 @@
     hidden_ref,
     slope_ref,
     head_slope_ref,
-    gain_ref,
-    shift_ref,
-    scale_ref,
+    vectors_ref,
     expand_ref,
     reduce_ref,
     head_ref,
     expand_order_ref,
     reduce_order_ref,
     eye_ref,
-    out_ref,
+    keep_ref,
+    send_ref,
     grad_pre_all,
     hidden_all,
     normed_all,
     grad_mlp_all,
+    grad_head,
+    grad_norm,
     padded,
     depth_back,
     tap_sums,
     tap_rows,
+    staged,
+    sems,
 ):
     step = pl.program_id(0)
     filled = table_ref[PROC + step]
@@ -386,7 +432,10 @@
     bands = channels // LANES
     low = ROW_UNIT // 2
     reach = KS // 2
-    rows = pl.ds(pl.multiple_of(step * cells, cells), cells)
+    rows_all = pl.ds(pl.multiple_of(step * cells, cells), cells)
+
+    def vector(index, lanes):
+        return vectors_ref[index : index + 1, lanes]
 
     @pl.when(step == 0)
     def _start():
@@ -394,53 +443,71 @@
 
     @pl.when(filled == 0)
     def _empty():
-        grad_pre_all[rows, :] = jnp.zeros((cells, grad_pre_all.shape[1]), jnp.bfloat16)
-        hidden_all[rows, :] = jnp.zeros((cells, hidden_all.shape[1]), jnp.bfloat16)
-        normed_all[step] = jnp.zeros(normed_all.shape[1:], jnp.bfloat16)
-        grad_mlp_all[step] = jnp.zeros(grad_mlp_all.shape[1:], jnp.bfloat16)
+        for ref in (grad_pre_all, hidden_all):
+            ref[rows_all, :] = jnp.zeros((cells, ref.shape[1]), jnp.bfloat16)
+        for ref in (normed_all, grad_mlp_all):
+            ref[:, rows_all] = jnp.zeros((ref.shape[0], cells), jnp.bfloat16)
 
     @pl.when(filled != 0)
     def _work():
-        grad_head = (grad_ref[0] * (1.0 / cells) * head_slope_ref[0].astype(jnp.float32)).astype(
+        every = slice(0, channels)
+        for start in range(0, cells, PART):
+            rows = slice(start, start + PART)
+            grad_head[rows, :] = (
+                (grad_ref[0] * (1.0 / cells)) * head_slope_ref[0, rows, :].astype(jnp.float32)
+            ).astype(jnp.bfloat16)
+        grad_mlp = (vector(SCALE, every) * mix_cols(grad_head[...], head_ref[...])).astype(
             jnp.bfloat16
         )
-        grad_mlp = (scale_ref[...] * mix_cols(grad_head, head_ref[...])).astype(jnp.bfloat16)
-        grad_mlp_all[step] = mix_cols(eye_ref[...], grad_mlp).astype(jnp.bfloat16)
-        hidden_all[rows, :] = hidden_ref[0]
-        width = 256
-        for start in range(0, expand_ref.shape[1], width):
-            cols = slice(start, start + width)
+        grad_mlp_all[:, rows_all] = mix_cols(eye_ref[...], grad_mlp).astype(jnp.bfloat16)
+        hidden_all[rows_all, :] = hidden_ref[0]
+        for begin in range(0, expand_ref.shape[1], WIDTH):
+            cols = slice(begin, begin + WIDTH)
             grad_hidden = mix_cols(grad_mlp, reduce_ref[cols, :])
-            grad_pre_all[rows, cols] = (
+            grad_pre_all[rows_all, cols] = (
                 grad_hidden * slope_ref[0, :, cols].astype(jnp.float32)
             ).astype(jnp.bfloat16)
-        grad_norm = mix_cols(grad_pre_all[rows, :], expand_ref[...])
-        normed = (unit_ref[0] * gain_ref[...] + shift_ref[...]).astype(jnp.bfloat16)
-        normed_all[step] = mix_cols(expand_order_ref[...], normed).astype(jnp.bfloat16)
-
-        scaled = grad_norm * gain_ref[...]
-        unit = unit_ref[0]
-        mean = jnp.sum(scaled, axis=1, keepdims=True) * (1.0 / channels)
-        mean_unit = jnp.sum(scaled * unit, axis=1, keepdims=True) * (1.0 / channels)
-        depth_grad = inv_ref[0, :, 0:1] * (scaled - mean - unit * mean_unit)
+        grad_norm[...] = mix_cols(grad_pre_all[rows_all, :], expand_ref[...])
+        normed = (unit_ref[0] * vector(GAIN, every) + vector(SHIFT, every)).astype(jnp.bfloat16)
+        normed_all[:, rows_all] = mix_cols(expand_order_ref[...], normed).astype(jnp.bfloat16)
+
+        for start in range(0, cells, PART):
+            rows = slice(start, start + PART)
+            scaled = grad_norm[rows, :] * vector(GAIN, every)
+            unit = unit_ref[0, rows, :]
+            mean = jnp.sum(scaled, axis=1, keepdims=True) * (1.0 / channels)
+            mean_unit = jnp.sum(scaled * unit, axis=1, keepdims=True) * (1.0 / channels)
+            inv = inv_ref[0, rows, 0:1]
+            for band in range(bands):
+                lanes = slice(band * LANES, (band + 1) * LANES)
+                depth_back[band, rows, :] = inv * (
+                    scaled[:, lanes] - mean - unit[:, lanes] * mean_unit
+                )
         edge = jnp.zeros((side, low, LANES), jnp.float32)
         for band in range(bands):
             lanes = slice(band * LANES, (band + 1) * LANES)
-            depth_back[band] = depth_grad[:, lanes]
             padded[band, :, 0:low, :] = edge
             padded[band, :, low + side :, :] = edge
-            padded[band, :, low : low + side, :] = source_ref[0, :, :, lanes].astype(jnp.float32)
+            for at in range(side):
+                padded[band, at, low : low + side, :] = source_ref[0, at, :, lanes].astype(
+                    jnp.float32
+                )
 
         def taps_of(band, carry):
             for col in range(KS):
                 start = low - reach + col
                 sums = [None] * KS
+                grads = {}
                 for at in range(side):
                     line = padded[band, at, start : start + side, :]
                     for row in range(KS):
                         place = at - row + reach
                         if 0 <= place < side:
-                            term = line * depth_back[band, place * side : (place + 1) * side, :]
+                            if place not in grads:
+                                grads[place] = depth_back[
+                                    band, place * side : (place + 1) * side, :
+                                ]
+                            term = line * grads[place]
                             sums[row] = term if sums[row] is None else sums[row] + term
                 for row in range(KS):
                     total = sums[row]
@@ -454,44 +521,51 @@
 
     @pl.when(step == pl.num_programs(0) - 1)
     def _finish():
+        my_core = table_ref[4 * PROC]
         for band in range(bands):
             lanes = slice(band * LANES, (band + 1) * LANES)
             tap_rows[0 : KS * KS, lanes] = jnp.sum(tap_sums[band], axis=1)
             tap_rows[KS * KS :, lanes] = jnp.zeros((tap_rows.shape[0] - KS * KS, LANES), jnp.float32)
         pieces = expand_ref.shape[1] // channels
-        parts = 2 * plan.cross
+        pad = plan.expand_pad
         for quarter in range(pieces):
             cols = slice(quarter * channels, (quarter + 1) * channels)
-            total = mix(normed_all[0], grad_pre_all[0:cells, cols])
-            for slot in range(1, PROC):
-                total = total + mix(
-                    normed_all[slot], grad_pre_all[slot * cells : (slot + 1) * cells, cols]
-                )
-            out_ref[:, quarter * plan.expand_pad : (quarter + 1) * plan.expand_pad, :] = (
-                total.astype(jnp.bfloat16).reshape(parts, plan.expand_pad, channels)
-            )
-        base = pieces * plan.expand_pad
+            total = mix(normed_all[...], grad_pre_all[:, cols]).astype(jnp.bfloat16)
+            for core in range(2):
+                for cross in range(plan.cross):
+                    part = core * plan.cross + cross
+                    staged[core ^ my_core, cross, quarter * pad : (quarter + 1) * pad, :] = total[
+                        part * pad : (part + 1) * pad, :
+                    ]
+        base = pieces * pad
         block = plan.reduce_block
-        span = plan.depth_span * plan.reduce_rows
+        span = plan.g1 * plan.reduce_rows
         for index in range(expand_ref.shape[1] // block):
             cols = slice(index * block, (index + 1) * block)
-            total = mix(grad_mlp_all[0], hidden_all[0:cells, cols])
-            for slot in range(1, PROC):
-                total = total + mix(
-                    grad_mlp_all[slot], hidden_all[slot * cells : (slot + 1) * cells, cols]
-                )
-            turned = mix_cols(reduce_order_ref[...], total.astype(jnp.bfloat16)).astype(jnp.bfloat16)
+            total = mix(grad_mlp_all[...], hidden_all[:, cols]).astype(jnp.bfloat16)
+            turned = mix_cols(reduce_order_ref[...], total).astype(jnp.bfloat16)
             y, core = divmod(index, 2)
             for x in range(plan.g2):
-                out_ref[core * plan.cross + y * plan.g2 + x, base : base + span, :] = turned[
+                staged[core ^ my_core, y * plan.g2 + x, base : base + span, :] = turned[
                     x * span : (x + 1) * span, :
                 ]
         base = base + span
-        for part in range(parts):
-            starts = [plan.tap_start(part, z) for z in range(plan.g1)]
-            out_ref[part, base : base + plan.g1 * DEPTH_ROWS, :] = jnp.concatenate(
-                [tap_rows[start : start + DEPTH_ROWS, :] for start in starts], axis=0
-            ).astype(jnp.bfloat16)
+        for core in range(2):
+            for cross in range(plan.cross):
+                starts = [plan.tap_start(core * plan.cross + cross, z) for z in range(plan.g1)]
+                staged[core ^ my_core, cross, base : base + plan.g1 * DEPTH_ROWS, :] = (
+                    jnp.concatenate(
+                        [tap_rows[start : start + DEPTH_ROWS, :] for start in starts], axis=0
+                    ).astype(jnp.bfloat16)
+                )
+        copies = [
+            pltpu.make_async_copy(staged.at[index], ref, sems.at[index])
+            for index, ref in enumerate((keep_ref, send_ref))
+        ]
+        for copy in copies:
+            copy.start()
+        for copy in copies:
+            copy.wait()
 
 
 class Plan:
@@ -500,7 +574,6 @@
         self.devices = slides * members
         self.ys, self.g1, self.g2 = slides // 2, 4, members // 4
         self.cross = self.ys * self.g2
-        self.depth_span = self.g1
         self.expand_rows = channels // self.devices
         self.expand_pad = -(-self.g1 * self.expand_rows // ROW_UNIT) * ROW_UNIT
         self.reduce_rows = hid // self.devices
@@ -537,7 +610,7 @@
         return order
 
 
-def backward_block(plan, table, embed_grad, saved, gain, shift, scale, expand, reduce, head):
+def backward_block(plan, table, embed_grad, saved, vectors, expand, reduce, head):
     source, unit, inv, hidden, slope, head_slope = saved
     side, channels = source.shape[1], source.shape[3]
     cells, hid = side * side, expand.shape[1]
@@ -552,26 +625,30 @@
         return pl.BlockSpec((1,) + shape, lambda i, table: (i,) + (0,) * len(shape))
 
     streams = (embed_grad, source, unit, inv, hidden, slope, head_slope)
-    consts = (gain, shift, scale, expand, reduce, head) + orders
-    out = (2 * plan.cross, plan.rows, channels)
+    consts = (vectors, expand, reduce, head) + orders
+    out = (plan.cross, plan.rows, channels)
     return pl.pallas_call(
         functools.partial(backward_kernel, plan),
-        out_shape=jax.ShapeDtypeStruct(out, jnp.bfloat16),
+        out_shape=(jax.ShapeDtypeStruct(out, jnp.bfloat16),) * 2,
         grid_spec=pltpu.PrefetchScalarGridSpec(
             num_scalar_prefetch=1,
             grid=(PROC,),
             in_specs=[per_slot(stream) for stream in streams]
             + [whole(const.shape) for const in consts],
-            out_specs=whole(out),
+            out_specs=(HBM, HBM),
             scratch_shapes=[
                 pltpu.VMEM((PROC * cells, hid), jnp.bfloat16),
                 pltpu.VMEM((PROC * cells, hid), jnp.bfloat16),
-                pltpu.VMEM((PROC, orders[0].shape[0], cells), jnp.bfloat16),
-                pltpu.VMEM((PROC, channels, cells), jnp.bfloat16),
+                pltpu.VMEM((orders[0].shape[0], PROC * cells), jnp.bfloat16),
+                pltpu.VMEM((channels, PROC * cells), jnp.bfloat16),
+                pltpu.VMEM((cells, head.shape[1]), jnp.bfloat16),
+                pltpu.VMEM((cells, channels), jnp.float32),
                 pltpu.VMEM((bands, side, side + ROW_UNIT, LANES), jnp.float32),
                 pltpu.VMEM((bands, cells, LANES), jnp.float32),
                 pltpu.VMEM((bands, KS * KS, 8, LANES), jnp.float32),
                 pltpu.VMEM((KS * KS + 7, channels), jnp.float32),
+                pltpu.VMEM((2,) + out, jnp.bfloat16),
+                pltpu.SemaphoreType.DMA((2,)),
             ],
         ),
         compiler_params=pltpu.CompilerParams(vmem_limit_bytes=VMEM_BYTES),
@@ -583,10 +660,10 @@
     return lax.all_to_all(values, names, split_axis=0, concat_axis=0, tiled=True)
 
 
-def scatter_sum(plan, payload, my_device):
+def scatter_sum(plan, kept, sent, my_device):
     channels = plan.channels
-    grid = payload.reshape(2, plan.cross, plan.rows, channels)
-    grid = jnp.sum(exchange(grid, ("core",)).astype(jnp.float32), axis=0).astype(jnp.bfloat16)
+    other = lax.ppermute(sent, "core", [(0, 1), (1, 0)])
+    grid = (kept.astype(jnp.float32) + other.astype(jnp.float32)).astype(jnp.bfloat16)
     total = jnp.sum(exchange(grid, ("y", "g2")).astype(jnp.float32), axis=0).astype(jnp.bfloat16)
     cut = plan.pieces * plan.expand_pad
     later = cut + plan.g1 * plan.reduce_rows
@@ -651,9 +728,26 @@
     devices, length, places = slides * members, slots * members, slots // slides
     plan = Plan(slides, members, channels, expand_weight.shape[1])
     route = routing.reshape(-1)
-    bands = channels // LANES
 
     packed, table = pack_tiles(my_slide.reshape(1), route, tile_maps, slides, places)
+    vectors = jnp.stack(
+        [
+            jnp.pad(vector, (0, expand_bias.shape[0] - vector.shape[0]))
+            for vector in (
+                norm_gain,
+                norm_shift,
+                layer_scale,
+                reduce_bias,
+                depth_bias,
+                expand_bias,
+                slide_bias,
+                slide_bias,
+            )
+        ]
+    )
+    packed, route, cotangent, positions, counts = lax.optimization_barrier(
+        (packed, route, cotangent, positions, counts)
+    )
     arrived = exchange(packed, DP)
 
     extras = jnp.concatenate(
@@ -683,22 +777,8 @@
     steps = jnp.arange(length, dtype=jnp.int32)[None, :, None].astype(jnp.float32)
     weight = jnp.where(steps < counts_all[:, None, None], 1.0 / counts_all[:, None, None], 0.0)
 
-    def row(vector):
-        return vector.reshape(1, -1)
-
     outs = forward_block(
-        table,
-        arrived,
-        depth_kernel.reshape(KS * KS, bands, LANES).transpose(1, 0, 2),
-        depth_bias.reshape(bands, 1, LANES),
-        row(norm_gain),
-        row(norm_shift),
-        expand_weight,
-        row(expand_bias),
-        reduce_weight,
-        row(reduce_bias),
-        row(layer_scale),
-        head_weight,
+        table, arrived, depth_kernel, vectors, expand_weight, reduce_weight, head_weight
     )
     tile_out, tile_embed, unit, inv, hidden, slope, head_slope, source = outs
     embeds = exchange(
@@ -709,7 +789,6 @@
             table[: 3 * PROC],
             table[3 * PROC :] * members + my_member,
             my_slide.reshape(1),
-            jnp.zeros((3,), jnp.int32),
         ]
     )
     feature, embed_grad = slide_grads(
@@ -721,21 +800,19 @@
         cot_all,
         slide_taps,
         slide_weight,
-        row(slide_bias),
-    )
-    payload = backward_block(
+        vectors,
+    )
+    kept, sent = backward_block(
         plan,
-        table,
+        jnp.concatenate([table, lax.axis_index("core").reshape(1)]),
         embed_grad,
         (source, unit, inv, hidden, slope, head_slope),
-        row(norm_gain),
-        row(norm_shift),
-        row(layer_scale),
+        vectors,
         expand_weight,
         reduce_weight,
         head_weight,
     )
-    shares = scatter_sum(plan, payload, my_device)
+    shares = scatter_sum(plan, kept, sent, my_device)
     return (tile_out, feature, shares[0], shares[1], shares[2])
 
 

time: 208 us -> 154 us (0.74)
  Pallas kernels: 102 us -> 55 us
  blocking collectives: 27.3 us -> 19.4 us
  waiting for transfers between devices: 31.3 us -> 37.5 us
  local copies, waits for them, and re-layouts: 13.5 us -> 10.1 us
    pallas_call x1, Pallas kernels: 50 us -> 3.38 us  [pack_tiles(): pl.pallas_call(functools.partial(pack_kernel, slides, slots, places), out...]
    all_to_all x2 -> x1, blocking collectives: 27.3 us -> 19.4 us  [exchange(): lax.all_to_all(values, names, split_axis=0, concat_axis=0, tiled=True)]
    reshape x9 -> x0, local copies, waits for them, and re-layouts: 4.68 us -> none  [the longest x6 3.42 us: row(): return vector.reshape(1, -1)]
    all_to_all x4, waiting for transfers between devices: 31.3 us -> 34.5 us  [exchange(): lax.all_to_all(values, names, split_axis=0, concat_axis=0, tiled=True)]
    ppermute x0 -> x1, waiting for transfers between devices: none -> 2.99 us  [scatter_sum(): other = lax.ppermute(sent, 'core', [(0, 1), (1, 0)])]
  transfers between devices with their start and end apart: 4 -> 5, of which waited for: 3 -> 5; matrix products, arithmetic and copies ran while one was open for 6% -> 7% of each run, Pallas kernels for 24% -> 0%
where the time goes in v1:
time: 154 us; the launch traced here: 153 us
  Pallas kernels  55 us (36%)
  waiting for transfers between devices  37.5 us (24%)
  blocking collectives  19.4 us (13%)
  starting transfers between devices  16.8 us (11%)
  other arithmetic  12.5 us (8%)
  local copies, waits for them, and re-layouts  10.1 us (7%)
  between operations  1.86 us (1%)
    all_to_all x4, waiting for transfers between devices, exchange(): lax.all_to_all(values, names, split_axis=0, concat_axis=0, tiled=True)  34.5 us
    pallas_call x1, Pallas kernels, forward_block(): pl.pallas_call(forward_kernel, out_shape=tuple((jax.ShapeDtypeStruct((PRO...  23.5 us
    pallas_call x1, Pallas kernels, backward_block(): pl.pallas_call(functools.partial(backward_kernel, plan), out_shape=(jax.S...  21.5 us
    all_to_all x1, blocking collectives, exchange(): lax.all_to_all(values, names, split_axis=0, concat_axis=0, tiled=True)  19.4 us
    all_to_all x4, starting transfers between devices, exchange(): lax.all_to_all(values, names, split_axis=0, concat_axis=0, tiled=True)  16.6 us
    pallas_call x1, Pallas kernels, slide_grads(): pl.pallas_call(functools.partial(slide_kernel, length, slides), out_shape...  6.62 us
    sin x1, other arithmetic, position_code(): return jnp.sin(rows.astype(jnp.float32) * frequency + phase)  3.51 us
    pallas_call x1, Pallas kernels, pack_tiles(): pl.pallas_call(functools.partial(pack_kernel, slides, slots, places), out...  3.38 us
  transfers between devices with their start and end apart: 5, of which 5 were waited for; matrix products, arithmetic and copies ran while one was open for 7% of the time, Pallas kernels for 0%

profile of v1, /device:TPU:0, one launch (start us, length us, event | category | flops | bytes accessed | tf_op | source)
XLA Modules:
  0.0 153.2 jit_solution(16824545656010021245)
XLA Ops:
  0.7 0.5 broadcast.217
  1.2 1.3 reduce.9
  2.6 0.6 reshape.205.route_ref
  3.9 3.4 %pack_tiles.1 = (bf16[8,16,16,384]{3,2,1,0:T(8,128)(2,1)}, s32[16]{0:T(128)}) custom-call(s32[1]{0:T(128)} %bitcast.my_ref, s32[32]{0:T(128)} %reshape.205.route_ref, bf16[8,16,16,384]{3,2,1,0:T(8,128)(2,1)} %tiles_ref.1), custom_call_target="tpu_custom_call" | custom-call | tf_op jit(solution)/shard_map/pack_tiles/pallas_call | solution.py:112
  7.3 0.1 convert_element_type.66
  7.4 0.1 concatenate.13
  7.5 0.7 broadcast_in_dim.66
  8.2 6.9 %all-to-all-start.2 = ((f32[32,1,1024]{2,1,0:T(1,128)}), f32[32,1,1024]{2,1,0:T(1,128)S(1)}, u32[]{:S(2)}, u32[]{:S(2)}) async-start(f32[32,1,1024]{2,1,0:T(1,128)} %broadcast_in_dim.66), calls=%async_computation.2 | async-start | bytes 262144 | tf_op jit(solution)/shard_map/all_to_all | solution.py:660
  15.1 0.7 multiply_add_fusion
  15.8 1.2 pad_add_fusion.1.table_ref
  17.0 1.2 pad_add_fusion.info_ref
  18.5 0.7 stack.32.vectors_ref
  19.2 3.6 %all-to-all-done.2 = f32[32,1,1024]{2,1,0:T(1,128)S(1)} async-done(((f32[32,1,1024]{2,1,0:T(1,128)}), f32[32,1,1024]{2,1,0:T(1,128)S(1)}, u32[]{:S(2)}, u32[]{:S(2)}) %all-to-all-start.2) | async-done | bytes 131104 | tf_op jit(solution)/shard_map/all_to_all | solution.py:660
  22.8 3.6 %all-to-all-start = ((bf16[8,16,16,384]{3,2,1,0:T(8,128)(2,1)}), bf16[8,16,16,384]{3,2,1,0:T(8,128)(2,1)S(1)}, u32[]{:S(2)}, u32[]{:S(2)}) async-start(bf16[8,16,16,384]{3,2,1,0:T(8,128)(2,1)} %get-tuple-element.26), calls=%async_computation | async-start | bytes 3145728 | tf_op jit(solution)/shard_map/all_to_all | solution.py:660
  26.5 0.1 squeeze.10
  26.7 0.1 reshape.207
  26.9 0.1 eq.28
  27.0 0.1 broadcast_in_dim.70
  27.1 0.1 broadcast_in_dim.68
  27.2 0.2 slice_reduce_fusion
  27.3 0.1 reshape_squeeze.3
  27.4 0.1 slice_reduce_fusion.1
  27.6 0.6 slice_bitcast_fusion.1.cot_ref
  28.2 0.7 compare_select_fusion.weight_ref
  28.9 17.5 %all-to-all-done.tile_ref = bf16[8,16,16,384]{3,2,1,0:T(8,128)(2,1)S(1)} async-done(((bf16[8,16,16,384]{3,2,1,0:T(8,128)(2,1)}), bf16[8,16,16,384]{3,2,1,0:T(8,128)(2,1)S(1)}, u32[]{:S(2)}, u32[]{:S(2)}) %all-to-all-start) | async-done | bytes 1572896 | tf_op jit(solution)/shard_map/all_to_all | solution.py:660
  46.5 1.1 copy-done
  47.6 23.5 %forward_block.1 = (bf16[4,16,16,384]{3,2,1,0:T(8,128)(2,1)}, f32[4,1,768]{2,1,0:T(1,128)}, f32[4,256,384]{2,1,0:T(8,128)}, f32[4,256,128]{2,1,0:T(8,128)}, bf16...) custom-call(s32[16]{0:T(128)} %get-tuple-element.24.table_ref, ...), custom_call_target="tpu_custom_call" | custom-call | flops 3058434048 | bytes 25165824 | tf_op jit(solution)/shard_map/forward_block/pallas_call | solution.py:264
  71.1 0.7 convert_element_type.62
  71.9 0.7 broadcast_in_dim.63
  72.6 2.8 %all-to-all-start.1 = ((bf16[32,4,768]{2,1,0:T(4,128)(2,1)}), bf16[32,4,768]{2,1,0:T(4,128)(2,1)S(1)}, u32[]{:S(2)}, u32[]{:S(2)}) async-start(bf16[32,4,768]{2,1,0:T(4,128)(2,1)} %broadcast_in_dim.63), calls=%async_computation.1 | async-start | bytes 393216 | tf_op jit(solution)/shard_map/all_to_all | solution.py:660
  75.4 0.7 fusion.pick_ref
  76.1 3.5 %add_sine_fusion.codes_ref = f32[4,64,768]{2,1,0:T(8,128)} fusion(f32[768]{0:T(1024)S(1)} %get-tuple-element.50, f32[768]{0:T(1024)S(1)} %get-tuple-element.49, f32[4,64]{1,0:T(4,128)S(1)} %broadcast_in_dim.70, f32[4,64]{1,0:T(4,128)S(1)} %broadcast_in_dim.68, pred[768]{0:T(1024)(128)(4,1)S(1)} %iota_compare_fusion.1), kind=kLoop, calls=%fused_computation.1 | loop fusion | flops 589824 | bytes 795392 | tf_op jit(solution)/shard_map/sin | solution.py:699
  79.6 4.1 %all-to-all-done.1 = bf16[32,4,768]{2,1,0:T(4,128)(2,1)S(1)} async-done(((bf16[32,4,768]{2,1,0:T(4,128)(2,1)}), bf16[32,4,768]{2,1,0:T(4,128)(2,1)S(1)}, u32[]{:S(2)}, u32[]{:S(2)}) %all-to-all-start.1) | async-done | bytes 196640 | tf_op jit(solution)/shard_map/all_to_all | solution.py:660
  83.8 0.7 reshape.206.embeds_ref
  84.5 6.6 %slide_grads.1 = (f32[1,768]{1,0:T(1,128)}, f32[4,1,768]{2,1,0:T(1,128)}) custom-call(s32[17]{0:T(128)} %pad_add_fusion.info_ref, bf16[128,768]{1,0:T(8,128)(2,1)} %reshape.206.embeds_ref, bf16[4,64,128]{2,1,0:T(8,128)(2,1)} %fusion.pick_ref, f32[4,64,768]{2,1,0:T(8,128)} %add_sine_fusion.codes_ref, f32[4,64,1]{2,1,0:T(8,128)} %compare_select_fusion.weight_ref, ...), custom_call_target="tpu_custom_call" | custom-call | tf_op jit(solution)/shard_map/slide_grads/pallas_call | solution.py:374
  91.1 21.5 %backward_block.1 = (bf16[4,400,384]{2,1,0:T(8,128)(2,1)}, bf16[4,400,384]{2,1,0:T(8,128)(2,1)}) custom-call(s32[17]{0:T(128)} %pad_add_fusion.1.table_ref, f32[4,1,768]{2,1,0:T(1,128)} %get-tuple-element.34.grad_ref, bf16[4,16,16,384]{3,2,1,0:T(8,128)(2,1)} %get-tuple-element.35.source_ref, f32[4,256,384]{2,1,0:T(8,128)} %get-tuple-element.36.unit_ref, ...), custom_call_target="tpu_custom_call" | custom-call | tf_op jit(solution)/shard_map/backward_block/pallas_call | solution.py:630
  112.6 0.2 collective-permute-start
  112.8 3.0 %collective-permute-done = bf16[4,400,384]{2,1,0:T(8,128)(2,1)S(1)} collective-permute-done((bf16[4,400,384]{2,1,0:T(8,128)(2,1)}, bf16[4,400,384]{2,1,0:T(8,128)(2,1)S(1)}, u32[]{:S(2)}, u32[]{:S(2)}) %collective-permute-start) | collective-permute-done | bytes 1228832 | tf_op jit(solution)/shard_map/ppermute | solution.py:665
  115.8 1.6 %add_convert_fusion = bf16[4,400,384]{2,1,0:T(8,128)(2,1)S(1)} fusion(bf16[4,400,384]{2,1,0:T(8,128)(2,1)S(1)} %collective-permute-done, bf16[4,400,384]{2,1,0:T(8,128)(2,1)} %get-tuple-element.41), kind=kLoop, calls=%fused_computation | loop fusion | flops 2457600 | bytes 3686400 | tf_op jit(solution)/shard_map/convert_element_type | solution.py:666
  117.4 19.4 %all_to_all.29 = bf16[4,400,384]{2,1,0:T(8,128)(2,1)S(1)} all-to-all(bf16[4,400,384]{2,1,0:T(8,128)(2,1)S(1)} %add_convert_fusion), channel_id=1, replica_groups=mesh['y'=2,'core'=2,'g1'=4,'g2'=2] {'y','g2'}, dimensions={0} | all-to-all | bytes 2457600 | tf_op jit(solution)/shard_map/all_to_all | solution.py:660
  136.8 0.3 reduce_sum.21
  137.4 0.2 pad_maximum_fusion
  137.6 0.8 copy.64
  138.4 3.5 %all-to-all-start.4 = ((bf16[4,100,384]{2,1,0:T(8,128)(2,1)}), bf16[4,100,384]{2,1,0:T(8,128)(2,1)S(1)}, u32[]{:S(2)}, u32[]{:S(2)}) async-start(bf16[4,100,384]{2,1,0:T(8,128)(2,1)} %copy.64), calls=%async_computation.4 | async-start | bytes 638976 | tf_op jit(solution)/shard_map/all_to_all | solution.py:660
  141.9 9.2 %all-to-all-done.4 = bf16[4,100,384]{2,1,0:T(8,128)(2,1)S(1)} async-done(((bf16[4,100,384]{2,1,0:T(8,128)(2,1)}), bf16[4,100,384]{2,1,0:T(8,128)(2,1)S(1)}, u32[]{:S(2)}, u32[]{:S(2)}) %all-to-all-start.4) | async-done | bytes 307232 | tf_op jit(solution)/shard_map/all_to_all | solution.py:660
  151.2 0.7 reshape.214
  151.9 0.6 reshape.215
  152.6 0.7 dynamic_slice.3
  (68 shorter events, 0.8 us)
Async XLA Ops:
  0.6 6.7 %copy-start.3 = (f32[1,768]{1,0:T(1,128)S(1)}, f32[1,768]{1,0:T(1,128)}, u32[]{:S(2)}) copy-start(f32[1,768]{1,0:T(1,128)} %param.38) | copy-start | bytes 9220
  0.6 6.6 %copy-start.10 = (s32[2,8]{1,0:T(2,128)S(1)}, s32[2,8]{1,0:T(2,128)}, u32[]{:S(2)}) copy-start(s32[2,8]{1,0:T(2,128)} %param.22) | copy-start | bytes 196
  0.7 17.6 %copy-start.5 = (f32[384]{0:T(512)S(1)}, f32[384]{0:T(512)}, u32[]{:S(2)}) copy-start(f32[384]{0:T(512)} %param.27) | copy-start | bytes 4612
  0.7 17.6 %copy-start.6 = (f32[384]{0:T(512)S(1)}, f32[384]{0:T(512)}, u32[]{:S(2)}) copy-start(f32[384]{0:T(512)} %param.28) | copy-start | bytes 4612
  0.7 17.6 %copy-start.7 = (f32[384]{0:T(512)S(1)}, f32[384]{0:T(512)}, u32[]{:S(2)}) copy-start(f32[384]{0:T(512)} %param.33) | copy-start | bytes 4612
  0.7 17.7 %copy-start.8 = (f32[384]{0:T(512)S(1)}, f32[384]{0:T(512)}, u32[]{:S(2)}) copy-start(f32[384]{0:T(512)} %param.32) | copy-start | bytes 4612
  0.7 17.7 %copy-start.9 = (f32[384]{0:T(512)S(1)}, f32[384]{0:T(512)}, u32[]{:S(2)}) copy-start(f32[384]{0:T(512)} %param.26) | copy-start | bytes 4612
  0.7 17.7 %copy-start.1 = (f32[1536]{0:T(1024)S(1)}, f32[1536]{0:T(1024)}, u32[]{:S(2)}) copy-start(f32[1536]{0:T(1024)} %param.30) | copy-start | bytes 18436
  0.7 17.7 %copy-start.2 = (f32[768]{0:T(1024)S(1)}, f32[768]{0:T(1024)}, u32[]{:S(2)}) copy-start(f32[768]{0:T(1024)} %param.37) | copy-start | bytes 9220
  3.2 4.1 %copy-start.4 = (s32[32]{0:T(128)S(1)}, s32[32]{0:T(128)}, u32[]{:S(2)}) copy-start(s32[32]{0:T(128)} %reshape.205.route_ref) | copy-start | bytes 388
  8.2 14.6 %all-to-all-start.2 = ((f32[32,1,1024]{2,1,0:T(1,128)}), f32[32,1,1024]{2,1,0:T(1,128)S(1)}, u32[]{:S(2)}, u32[]{:S(2)}) async-start(f32[32,1,1024]{2,1,0:T(1,128)} %broadcast_in_dim.66), calls=%async_computation.2 | async-start | bytes 262144 | tf_op jit(solution)/shard_map/all_to_all | solution.py:660
  22.8 23.6 %all-to-all-start = ((bf16[8,16,16,384]{3,2,1,0:T(8,128)(2,1)}), bf16[8,16,16,384]{3,2,1,0:T(8,128)(2,1)S(1)}, u32[]{:S(2)}, u32[]{:S(2)}) async-start(bf16[8,16,16,384]{3,2,1,0:T(8,128)(2,1)} %get-tuple-element.26), calls=%async_computation | async-start | bytes 3145728 | tf_op jit(solution)/shard_map/all_to_all | solution.py:660
  46.4 1.2 copy-start
  72.6 11.1 %all-to-all-start.1 = ((bf16[32,4,768]{2,1,0:T(4,128)(2,1)}), bf16[32,4,768]{2,1,0:T(4,128)(2,1)S(1)}, u32[]{:S(2)}, u32[]{:S(2)}) async-start(bf16[32,4,768]{2,1,0:T(4,128)(2,1)} %broadcast_in_dim.63), calls=%async_computation.1 | async-start | bytes 393216 | tf_op jit(solution)/shard_map/all_to_all | solution.py:660
  112.6 3.2 %collective-permute-start = (bf16[4,400,384]{2,1,0:T(8,128)(2,1)}, bf16[4,400,384]{2,1,0:T(8,128)(2,1)S(1)}, u32[]{:S(2)}, u32[]{:S(2)}) collective-permute-start(bf16[4,400,384]{2,1,0:T(8,128)(2,1)} %get-tuple-element.42), channel_id=1, source_target_pairs={{0,8},{8,0},{1,9},{9,1},{2,10},{10,2},{3,11},{11,3},{4,12},{12,4},... | collective-permute-start | bytes 3686408 | tf_op jit(solution)/shard_map/ppermute | solution.py:665
  138.4 12.7 %all-to-all-start.4 = ((bf16[4,100,384]{2,1,0:T(8,128)(2,1)}), bf16[4,100,384]{2,1,0:T(8,128)(2,1)S(1)}, u32[]{:S(2)}, u32[]{:S(2)}) async-start(bf16[4,100,384]{2,1,0:T(8,128)(2,1)} %copy.64), calls=%async_computation.4 | async-start | bytes 638976 | tf_op jit(solution)/shard_map/all_to_all | solution.py:660

commit v2 on v1

v2 whole, which is shorter than its diff:
```python
import functools
import math

import jax
import jax.numpy as jnp
import numpy as np
from jax import lax
from jax.experimental import pallas as pl
from jax.experimental.pallas import tpu as pltpu
from jax.sharding import Mesh, PartitionSpec as P

E = 768
KS = 7
KERNEL_TAPS = 7
TILE_DILATION = 3
PROC = 4
DP = ("y", "core")
GROUP = ("g1", "g2")
ALL = DP + GROUP

EPSILON = 1e-06
HALF_ROOT = 0.7071067811865476
INV_ROOT_TAU = 0.3989422804014327
LANES = 128
ROW_UNIT = 16
DEPTH_ROWS = 4
VMEM_BYTES = 56 * 1024 * 1024
PART = 32
WIDTH = 256
GAIN, SHIFT, SCALE, REDUCE_BIAS, DEPTH_BIAS, EXPAND_BIAS, SLIDE_BIAS = range(7)
ERFC_P = 0.3275911
ERFC_A = (0.254829592, -0.284496736, 1.421413741, -1.453152027, 1.061405429)

HBM = pl.BlockSpec(memory_space=pl.ANY)


def whole(shape):
    return pl.BlockSpec(shape, lambda *_: (0,) * len(shape))


def gelu_and_slope(values):
    size = jnp.abs(values)
    divisor = 1.0 + (ERFC_P * HALF_ROOT) * size
    guess = pl.reciprocal(divisor, approx=True)
    t = guess * (2.0 - divisor * guess)
    bell = jnp.exp(-0.5 * values * values)
    poly = 0.5 * ERFC_A[4]
    for coefficient in ERFC_A[3::-1]:
        poly = poly * t + 0.5 * coefficient
    tail = poly * t * bell
    phi = jnp.where(values >= 0.0, 1.0 - tail, tail)
    return values * phi, phi + values * (INV_ROOT_TAU * bell)


def mix_cols(left_side, right_side):
    return lax.dot_general(
        left_side, right_side, (((1,), (1,)), ((), ())), preferred_element_type=jnp.float32
    )


def mix(left_side, right_side):
    return jnp.dot(left_side, right_side, preferred_element_type=jnp.float32)


FILLED, SLIDE, PLACE, CLASSES = 0, PROC, 2 * PROC, 3 * PROC
CLASS_SIZE = 1 + 3 * PROC


def class_field(kind, field, item=0):
    return CLASSES + kind * CLASS_SIZE + (1 + field * PROC + item if field >= 0 else 0)


SLOT, FROM, OWN = range(3)


def pack_kernel(slides, slots, places, route_ref, tiles_ref, *refs):
    send_refs, (table_ref, count_ref, slot_ref, sems) = refs[:-4], refs[-4:]
    my_slide = lax.axis_index(DP)
    members = lax.axis_size(GROUP)
    my_member = lax.axis_index(GROUP)

    targets = [(0, rank, rank) for rank in range(places)]
    for rank in range(places):
        for other in range(2, slides):
            targets.append((1 + rank * (slides - 2) + other - 2, 0, other * places + rank))
    targets[:places] = [(0, rank, places + rank) for rank in range(places)]

    def copy_of(index, slot):
        buffer, row, _ = targets[index]
        return pltpu.make_async_copy(tiles_ref.at[slot], send_refs[buffer].at[row], sems.at[index])

    for index in range(slides):
        count_ref[index] = 0
    for index in range(slides * places):
        slot_ref[index] = -1

    def place_slot(slot, carry):
        entry = route_ref[my_slide, 0, slot]

        @pl.when(entry >= 0)
        def _send():
            other = lax.div(entry, PROC) ^ my_slide
            rank = count_ref[other]
            count_ref[other] = rank + 1
            slot_ref[other * places + rank] = slot

        return carry

    lax.fori_loop(0, slots, place_slot, 0)
    for index, (_, _, key) in enumerate(targets):
        slot = slot_ref[key]

        @pl.when(slot >= 0)
        def _start():
            copy_of(index, slot).start()

    kinds = 1 + places
    for field in range(CLASSES + kinds * CLASS_SIZE):
        table_ref[field] = 0
    for kind in range(kinds):
        for item in range(PROC):
            table_ref[class_field(kind, SLOT, item)] = PROC
    for other in range(slides):
        source = my_slide ^ other
        count_ref[0] = 0

        def take(slot, carry):
            entry = route_ref[source, 0, slot]
            proc = entry - my_slide * PROC

            @pl.when((proc >= 0) & (proc < PROC))
            def _take():
                rank = count_ref[0]
                count_ref[0] = rank + 1
                table_ref[FILLED + proc] = 1
                table_ref[SLIDE + proc] = source
                table_ref[PLACE + proc] = slot * members + my_member
                kind = 0 if other < 2 else 1 + rank
                base = CLASSES + kind * CLASS_SIZE
                item = table_ref[base]
                table_ref[base] = item + 1
                table_ref[base + 1 + SLOT * PROC + item] = proc
                if other == 0:
                    table_ref[base + 1 + FROM * PROC + item] = 0
                    table_ref[base + 1 + OWN * PROC + item] = slot
                else:
                    table_ref[base + 1 + FROM * PROC + item] = 1 + rank if other == 1 else other - 2

            return carry

        lax.fori_loop(0, slots, take, 0)
        if other == 0:
            own = table_ref[class_field(0, -1)]
            for item in range(1, PROC):

                @pl.when(item >= own)
                def _hold():
                    table_ref[class_field(0, OWN, item)] = table_ref[class_field(0, OWN, item - 1)]

    for kind in range(kinds):
        items = table_ref[class_field(kind, -1)]
        for item in range(1, PROC):

            @pl.when(item >= items)
            def _hold_slot():
                table_ref[class_field(kind, SLOT, item)] = table_ref[class_field(kind, SLOT, item - 1)]

    for index, (_, _, key) in enumerate(targets):

        @pl.when(slot_ref[key] >= 0)
        def _wait():
            copy_of(index, 0).wait()


def pack_tiles(routing, tile_maps, slides, places):
    slots = tile_maps.shape[0]
    smem = pl.BlockSpec(memory_space=pltpu.SMEM)
    vmem = pl.BlockSpec(memory_space=pltpu.VMEM)
    buffers = 1 + places * (slides - 2)
    shapes = [places] + [1] * (buffers - 1)
    outs = pl.pallas_call(
        functools.partial(pack_kernel, slides, slots, places),
        out_shape=tuple(
            jax.ShapeDtypeStruct((size,) + tile_maps.shape[1:], tile_maps.dtype) for size in shapes
        )
        + (jax.ShapeDtypeStruct((CLASSES + (1 + places) * CLASS_SIZE,), jnp.int32),),
        in_specs=[smem, HBM],
        out_specs=(vmem,) * buffers + (smem,),
        scratch_shapes=[
            pltpu.SMEM((slides,), jnp.int32),
            pltpu.SMEM((slides * places,), jnp.int32),
            pltpu.SemaphoreType.DMA((slides * places,)),
        ],
        compiler_params=pltpu.CompilerParams(vmem_limit_bytes=16 * 1024 * 1024),
        name="pack_tiles",
    )(routing, tile_maps)
    return outs[:-1], outs[-1]


def forward_kernel(kind, inputs, aliased, table_ref, *refs):
    forward_items(kind, table_ref, refs[:inputs], *refs[inputs : inputs + 5], *refs[inputs + 5 + aliased :])


def forward_items(
    kind,
    table_ref,
    tile_refs,
    taps_ref,
    vectors_ref,
    expand_ref,
    reduce_ref,
    head_ref,
    out_ref,
    embed_ref,
    unit_ref,
    inv_ref,
    hidden_ref,
    slope_ref,
    head_slope_ref,
    source_ref,
    padded,
    depth_out,
    normed,
    pre,
    section,
):
    item = pl.program_id(0)
    side = out_ref.shape[1]
    channels = out_ref.shape[3]
    cells = side * side
    bands = channels // LANES
    low = ROW_UNIT // 2
    reach = KS // 2

    @pl.when(item < table_ref[class_field(kind, -1)])
    def _work():
        origin = table_ref[class_field(kind, FROM) + item]
        edge = jnp.zeros((side, low, LANES), jnp.float32)
        for band in range(bands):
            padded[band, :, 0:low, :] = edge
            padded[band, :, low + side :, :] = edge
        place = 0
        for ref in tile_refs:
            for row in range(ref.shape[0]):

                @pl.when(origin == place)
                def _load():
                    source_ref[0] = ref[row]

                place += 1
        for band in range(bands):
            for at in range(side):
                padded[band, at, low : low + side, :] = source_ref[
                    0, at, :, band * LANES : (band + 1) * LANES
                ].astype(jnp.float32)

        def convolve(band, carry):
            lanes = pl.ds(pl.multiple_of(band * LANES, LANES), LANES)
            bias = jnp.broadcast_to(vectors_ref[DEPTH_BIAS : DEPTH_BIAS + 1, lanes], (side, LANES))
            totals = [bias for _ in range(side)]
            for col in range(KS):
                start = low - reach + col
                weights = [
                    taps_ref[row * KS + col : row * KS + col + 1, lanes] for row in range(KS)
                ]
                for at in range(side):
                    line = padded[band, at, start : start + side, :]
                    for row in range(KS):
                        place = at - row + reach
                        if 0 <= place < side:
                            totals[place] = totals[place] + weights[row] * line
            for place in range(side):
                depth_out[band, place * side : (place + 1) * side, :] = totals[place]
            return carry

        lax.fori_loop(0, bands, convolve, 0)

        def vector(index, lanes):
            return vectors_ref[index : index + 1, lanes]

        for start in range(0, cells, PART):
            rows = slice(start, start + PART)
            pieces = [depth_out[band, rows, :] for band in range(bands)]
            mean = jnp.sum(sum(pieces), axis=1, keepdims=True) * (1.0 / channels)
            pieces = [piece - mean for piece in pieces]
            var = jnp.sum(sum(p * p for p in pieces), axis=1, keepdims=True) * (1.0 / channels)
            inv = lax.rsqrt(var + EPSILON)
            inv_ref[0, rows, :] = jnp.broadcast_to(inv, (PART, LANES))
            for band in range(bands):
                lanes = slice(band * LANES, (band + 1) * LANES)
                unit = pieces[band] * inv
                unit_ref[0, rows, lanes] = unit
                normed[rows, lanes] = (unit * vector(GAIN, lanes) + vector(SHIFT, lanes)).astype(
                    jnp.bfloat16
                )

        for index, begin in enumerate(range(0, expand_ref.shape[1], WIDTH)):
            cols = slice(begin, begin + WIDTH)
            buffer = index % pre.shape[0]
            pre[buffer] = mix(normed[...], expand_ref[:, cols])
            for start in range(0, cells, PART):
                rows = slice(start, start + PART)
                act, slope = gelu_and_slope(pre[buffer, rows, :] + vector(EXPAND_BIAS, cols))
                hidden_ref[0, rows, cols] = act.astype(jnp.bfloat16)
                slope_ref[0, rows, cols] = slope.astype(jnp.bfloat16)
        lanes = slice(0, channels)
        depth_rows = mix(hidden_ref[0], reduce_ref[...])
        for at in range(side):
            rows = slice(at * side, (at + 1) * side)
            branch = vector(SCALE, lanes) * (depth_rows[rows] + vector(REDUCE_BIAS, lanes))
            line = (source_ref[0, at].astype(jnp.float32) + branch).astype(jnp.bfloat16)
            section[rows, :] = line
            out_ref[0, at] = line
        for index, begin in enumerate(range(0, head_ref.shape[1], WIDTH)):
            cols = slice(begin, begin + WIDTH)
            buffer = index % pre.shape[0]
            pre[buffer] = mix(section[...], head_ref[:, cols])
            total = None
            for start in range(0, cells, PART):
                rows = slice(start, start + PART)
                act, slope = gelu_and_slope(pre[buffer, rows, :])
                head_slope_ref[0, rows, cols] = slope.astype(jnp.bfloat16)
                folded = act[0:8]
                for piece in range(8, PART, 8):
                    folded = folded + act[piece : piece + 8]
                total = folded if total is None else total + folded
            embed_ref[0, :, cols] = jnp.sum(total, axis=0, keepdims=True) * (1.0 / cells)


def forward_block(kind, items, table, tiles, consts, before):
    side, channels = tiles[0].shape[1], tiles[0].shape[3]
    taps, vectors, expand, reduce, head = consts
    cells, hid, embed = side * side, expand.shape[1], head.shape[1]
    bands = channels // LANES

    def per_slot(*shape):
        return pl.BlockSpec(
            (1,) + shape,
            lambda i, table: (table[class_field(kind, SLOT) + i],) + (0,) * len(shape),
        )

    outs = (
        ((side, side, channels), jnp.bfloat16),
        ((1, embed), jnp.float32),
        ((cells, channels), jnp.float32),
        ((cells, LANES), jnp.float32),
        ((cells, hid), jnp.bfloat16),
        ((cells, hid), jnp.bfloat16),
        ((cells, embed), jnp.bfloat16),
        ((side, side, channels), jnp.bfloat16),
    )
    tile_specs = [whole(tile.shape) for tile in tiles]
    if kind == 0:
        tile_specs[0] = pl.BlockSpec(
            (1, side, side, channels),
            lambda i, table: (table[class_field(kind, OWN) + i], 0, 0, 0),
        )
    first = 1 + len(tiles) + len(consts)
    return pl.pallas_call(
        functools.partial(forward_kernel, kind, len(tiles), len(before)),
        out_shape=tuple(jax.ShapeDtypeStruct((PROC + 1,) + shape, dtype) for shape, dtype in outs),
        grid_spec=pltpu.PrefetchScalarGridSpec(
            num_scalar_prefetch=1,
            grid=(items,),
            in_specs=tile_specs + [whole(const.shape) for const in consts] + [HBM] * len(before),
            out_specs=[per_slot(*shape) for shape, _ in outs],
            scratch_shapes=[
                pltpu.VMEM((bands, side, side + ROW_UNIT, LANES), jnp.float32),
                pltpu.VMEM((bands, cells, LANES), jnp.float32),
                pltpu.VMEM((cells, channels), jnp.bfloat16),
                pltpu.VMEM((3, cells, WIDTH), jnp.float32),
                pltpu.VMEM((cells, channels), jnp.bfloat16),
            ],
        ),
        input_output_aliases={first + index: index for index in range(len(before))},
        compiler_params=pltpu.CompilerParams(vmem_limit_bytes=VMEM_BYTES),
        cost_estimate=cost(6.0 * min(items, 2)),
        name="forward_block_" + str(kind),
    )(table, *tiles, *consts, *before)


def cost(micros):
    return pl.CostEstimate(flops=int(micros * 1e9), bytes_accessed=1024, transcendentals=0)


def slide_kernel(
    length,
    slides,
    pieces,
    table_ref,
    *refs,
):
    slide_items(length, slides, table_ref, refs[:pieces], *refs[pieces:])


def slide_items(
    length,
    slides,
    table_ref,
    piece_refs,
    pick_ref,
    codes_ref,
    weight_ref,
    cot_ref,
    taps_ref,
    matrix_ref,
    vectors_ref,
    feature_ref,
    grad_ref,
    rows,
    back,
    features,
    mixed,
    pre,
    grad_agg,
    embeds_ref,
):
    for index, ref in enumerate(piece_refs):
        size = ref.shape[0]
        embeds_ref[index * size : (index + 1) * size, :] = ref[...]
    border = ROW_UNIT
    edge = jnp.zeros((border, rows.shape[2]), jnp.float32)
    reach = KERNEL_TAPS // 2
    blocks = [slice(start, start + WIDTH) for start in range(0, rows.shape[2], WIDTH)]

    def dilate(ref, slide, direction, cols):
        total = ref[slide, border : border + length, cols]
        for tap in range(KERNEL_TAPS):
            start = border + direction * (tap - reach) * TILE_DILATION
            total = total + taps_ref[tap : tap + 1, cols] * ref[slide, start : start + length, cols]
        return total

    def one_slide(slide, carry):
        here = weight_ref[slide] > 0.0
        for ref in (rows, back):
            ref[slide, 0:border, :] = edge
            ref[slide, border + length :, :] = edge
        for cols in blocks:
            own = mix(pick_ref[slide], embeds_ref[:, cols]) + codes_ref[slide, :, cols]
            rows[slide, border : border + length, cols] = (
                jnp.where(here, own, 0.0).astype(jnp.bfloat16).astype(jnp.float32)
            )
            mixed[:, cols] = dilate(rows, slide, 1, cols).astype(jnp.bfloat16)
        for cols in blocks:
            pre[:, cols] = mix(mixed[...], matrix_ref[:, cols])
            total = None
            for start in range(0, length, PART):
                part = slice(start, start + PART)
                share = weight_ref[slide, part, :]
                act, slope = gelu_and_slope(
                    pre[part, cols] + vectors_ref[SLIDE_BIAS : SLIDE_BIAS + 1, cols]
                )
                grad_agg[part, cols] = (cot_ref[slide, :, cols] * share * slope).astype(jnp.bfloat16)
                piece = jnp.sum(act * share, axis=0, keepdims=True)
                total = piece if total is None else total + piece
            features[pl.ds(slide, 1), cols] = total
        for cols in blocks:
            back[slide, border : border + length, cols] = mix_cols(
                grad_agg[...], matrix_ref[cols, :]
            )
            total = jnp.where(here, dilate(back, slide, -1, cols), 0.0)
            rows[slide, border : border + length, cols] = total.astype(jnp.bfloat16).astype(
                jnp.float32
            )
        return carry

    lax.fori_loop(0, slides, one_slide, 0)
    feature_ref[...] = features[pl.ds(lax.axis_index(DP), 1), :]
    for proc in range(PROC):
        filled = table_ref[FILLED + proc]
        at = border + table_ref[PLACE + proc]
        row = rows[table_ref[SLIDE + proc], pl.ds(at, 1), :]
        grad_ref[proc] = jnp.where(filled != 0, row, 0.0)


def slide_grads(table, pieces, pick, codes, weight, cot, taps, matrix, vectors):
    slides, length, embed = codes.shape
    smem = pl.BlockSpec(memory_space=pltpu.SMEM)
    vmem = pl.BlockSpec(memory_space=pltpu.VMEM)
    padded = (slides, length + 2 * ROW_UNIT, embed)
    return pl.pallas_call(
        functools.partial(slide_kernel, length, slides, len(pieces)),
        out_shape=(
            jax.ShapeDtypeStruct((1, embed), jnp.float32),
            jax.ShapeDtypeStruct((PROC, 1, embed), jnp.float32),
        ),
        in_specs=[smem] + [vmem] * (7 + len(pieces)),
        out_specs=(vmem, vmem),
        scratch_shapes=[
            pltpu.VMEM(padded, jnp.float32),
            pltpu.VMEM(padded, jnp.float32),
            pltpu.VMEM((max(slides, 8), embed), jnp.float32),
            pltpu.VMEM((length, embed), jnp.bfloat16),
            pltpu.VMEM((length, embed), jnp.float32),
            pltpu.VMEM((length, embed), jnp.bfloat16),
            pltpu.VMEM((sum(piece.shape[0] for piece in pieces), embed), jnp.bfloat16),
        ],
        compiler_params=pltpu.CompilerParams(vmem_limit_bytes=VMEM_BYTES),
        cost_estimate=cost(6.0),
        name="slide_grads",
    )(table, *pieces, pick, codes, weight, cot, taps, matrix, vectors)


class Plan:
    def __init__(self, slides, members, channels, hid):
        self.devices = slides * members
        self.ys, self.g1, self.g2 = slides // 2, 4, members // 4
        self.cross = self.ys * self.g2
        self.channels = channels
        self.pieces = hid // channels
        self.expand_rows = channels // self.devices
        self.reduce_rows = hid // self.devices
        self.block_rows = -(-self.reduce_rows // ROW_UNIT) * ROW_UNIT
        self.share = KS * KS * channels // self.devices

    def blocks(self, rows):
        return (self.cross, self.g1, rows, self.channels)

    def spots(self):
        my_core, my_y = lax.axis_index("core"), lax.axis_index("y")
        my_z, my_x = lax.axis_index("g1"), lax.axis_index("g2")
        for device in range(self.devices):
            slide, member = divmod(device, self.g1 * self.g2)
            (y, core), (z, x) = divmod(slide, 2), divmod(member, self.g2)
            cross = lax.rem(y - my_y + self.ys, self.ys) * self.g2
            cross = cross + lax.rem(x - my_x + self.g2, self.g2)
            yield device, (my_core ^ core, cross, lax.rem(z - my_z + self.g1, self.g1))


def send_out(staged, sems, refs):
    copies = [
        pltpu.make_async_copy(staged.at[index], ref, sems.at[index]) for index, ref in enumerate(refs)
    ]
    for copy in copies:
        copy.start()
    for copy in copies:
        copy.wait()


def padded_block(block, rows):
    extra = rows - block.shape[0]
    if extra:
        block = jnp.concatenate([block, jnp.zeros((extra, block.shape[1]), block.dtype)], axis=0)
    return block.astype(jnp.bfloat16)


def reduce_kernel(
    plan,
    table_ref,
    grad_ref,
    hidden_ref,
    head_slope_ref,
    vectors_ref,
    head_ref,
    eye_ref,
    grad_mlp_ref,
    keep_ref,
    send_ref,
    hidden_all,
    grad_mlp_all,
    grad_head,
    staged,
    sems,
):
    step = pl.program_id(0)
    filled = table_ref[FILLED + step]
    cells, channels = grad_mlp_ref.shape[1:]
    rows_all = pl.ds(pl.multiple_of(step * cells, cells), cells)

    @pl.when(filled == 0)
    def _empty():
        hidden_all[rows_all, :] = jnp.zeros((cells, hidden_all.shape[1]), jnp.bfloat16)
        grad_mlp_all[:, rows_all] = jnp.zeros((channels, cells), jnp.bfloat16)
        grad_mlp_ref[...] = jnp.zeros(grad_mlp_ref.shape, jnp.bfloat16)

    @pl.when(filled != 0)
    def _work():
        for start in range(0, cells, PART):
            rows = slice(start, start + PART)
            grad_head[rows, :] = (
                (grad_ref[0] * (1.0 / cells)) * head_slope_ref[0, rows, :].astype(jnp.float32)
            ).astype(jnp.bfloat16)
        scale = vectors_ref[SCALE : SCALE + 1, 0:channels]
        grad_mlp = (scale * mix_cols(grad_head[...], head_ref[...])).astype(jnp.bfloat16)
        grad_mlp_ref[0] = grad_mlp
        grad_mlp_all[:, rows_all] = mix_cols(eye_ref[...], grad_mlp).astype(jnp.bfloat16)
        hidden_all[rows_all, :] = hidden_ref[0]

    @pl.when(step == pl.num_programs(0) - 1)
    def _finish():
        spots = dict(plan.spots())
        per_block = channels // plan.reduce_rows
        for index in range(plan.pieces):
            cols = slice(index * channels, (index + 1) * channels)
            total = mix(grad_mlp_all[...], hidden_all[:, cols]).astype(jnp.bfloat16)
            turned = mix_cols(eye_ref[...], total)
            for part in range(per_block):
                block = turned[part * plan.reduce_rows : (part + 1) * plan.reduce_rows]
                staged[spots[index * per_block + part]] = padded_block(block, plan.block_rows)
        send_out(staged, sems, (keep_ref, send_ref))


def expand_kernel(
    plan,
    table_ref,
    grad_mlp_ref,
    slope_ref,
    unit_ref,
    inv_ref,
    vectors_ref,
    expand_ref,
    reduce_ref,
    eye_ref,
    depth_back_ref,
    keep_ref,
    send_ref,
    grad_pre_all,
    normed_all,
    grad_norm,
    staged,
    sems,
):
    step = pl.program_id(0)
    filled = table_ref[FILLED + step]
    cells, channels = unit_ref.shape[1:]
    bands = channels // LANES
    rows_all = pl.ds(pl.multiple_of(step * cells, cells), cells)
    every = slice(0, channels)

    def vector(index, lanes):
        return vectors_ref[index : index + 1, lanes]

    @pl.when(filled == 0)
    def _empty():
        grad_pre_all[rows_all, :] = jnp.zeros((cells, grad_pre_all.shape[1]), jnp.bfloat16)
        normed_all[:, rows_all] = jnp.zeros((channels, cells), jnp.bfloat16)

    @pl.when(filled != 0)
    def _work():
        for begin in range(0, expand_ref.shape[1], WIDTH):
            cols = slice(begin, begin + WIDTH)
            grad_hidden = mix_cols(grad_mlp_ref[0], reduce_ref[cols, :])
            grad_pre_all[rows_all, cols] = (
                grad_hidden * slope_ref[0, :, cols].astype(jnp.float32)
            ).astype(jnp.bfloat16)
        grad_norm[...] = mix_cols(grad_pre_all[rows_all, :], expand_ref[...])
        normed = (unit_ref[0] * vector(GAIN, every) + vector(SHIFT, every)).astype(jnp.bfloat16)
        normed_all[:, rows_all] = mix_cols(eye_ref[...], normed).astype(jnp.bfloat16)
        for start in range(0, cells, PART):
            rows = slice(start, start + PART)
            scaled = grad_norm[rows, :] * vector(GAIN, every)
            unit = unit_ref[0, rows, :]
            mean = jnp.sum(scaled, axis=1, keepdims=True) * (1.0 / channels)
            mean_unit = jnp.sum(scaled * unit, axis=1, keepdims=True) * (1.0 / channels)
            inv = inv_ref[0, rows, 0:1]
            for band in range(bands):
                lanes = slice(band * LANES, (band + 1) * LANES)
                depth_back_ref[0, band, rows, :] = inv * (
                    scaled[:, lanes] - mean - unit[:, lanes] * mean_unit
                )

    @pl.when(step == pl.num_programs(0) - 1)
    def _finish():
        spots = dict(plan.spots())
        totals = []
        for quarter in range(plan.pieces):
            cols = slice(quarter * channels, (quarter + 1) * channels)
            totals.append(mix(normed_all[...], grad_pre_all[:, cols]))
        size = plan.expand_rows
        for device in range(plan.devices):
            rows = slice(device * size, (device + 1) * size)
            block = jnp.concatenate([total[rows] for total in totals], axis=0)
            staged[spots[device]] = padded_block(block, plan.block_rows)
        send_out(staged, sems, (keep_ref, send_ref))


def taps_kernel(
    plan,
    table_ref,
    source_ref,
    depth_back,
    keep_ref,
    send_ref,
    padded,
    tap_sums,
    tap_rows,
    staged,
    sems,
):
    step = pl.program_id(0)
    filled = table_ref[FILLED + step]
    side, channels = source_ref.shape[1], source_ref.shape[3]
    bands = channels // LANES
    low = ROW_UNIT // 2
    reach = KS // 2

    @pl.when(step == 0)
    def _start():
        tap_sums[...] = jnp.zeros(tap_sums.shape, jnp.float32)

    @pl.when(filled != 0)
    def _work():
        edge = jnp.zeros((side, low, LANES), jnp.float32)
        for band in range(bands):
            lanes = slice(band * LANES, (band + 1) * LANES)
            padded[band, :, 0:low, :] = edge
            padded[band, :, low + side :, :] = edge
            for at in range(side):
                padded[band, at, low : low + side, :] = source_ref[0, at, :, lanes].astype(
                    jnp.float32
                )

        def taps_of(band, carry):
            for col in range(KS):
                start = low - reach + col
                sums = [None] * KS
                grads = {}
                for at in range(side):
                    line = padded[band, at, start : start + side, :]
                    for row in range(KS):
                        place = at - row + reach
                        if 0 <= place < side:
                            if place not in grads:
                                grads[place] = depth_back[
                                    0, band, place * side : (place + 1) * side, :
                                ]
                            term = line * grads[place]
                            sums[row] = term if sums[row] is None else sums[row] + term
                for row in range(KS):
                    total = sums[row]
                    folded = total[0:8, :]
                    for piece in range(8, side, 8):
                        folded = folded + total[piece : piece + 8, :]
                    tap_sums[band, row * KS + col] = tap_sums[band, row * KS + col] + folded
            return carry

        lax.fori_loop(0, bands, taps_of, 0)

    @pl.when(step == pl.num_programs(0) - 1)
    def _finish():
        for band in range(bands):
            lanes = slice(band * LANES, (band + 1) * LANES)
            tap_rows[0 : KS * KS, lanes] = jnp.sum(tap_sums[band], axis=1)
            tap_rows[KS * KS :, lanes] = jnp.zeros((tap_rows.shape[0] - KS * KS, LANES), jnp.float32)
        for device, spot in plan.spots():
            start = device * plan.share // channels
            staged[spot] = padded_block(tap_rows[start : start + DEPTH_ROWS, :], ROW_UNIT)
        send_out(staged, sems, (keep_ref, send_ref))


def backward_call(plan, kernel, name, micros, rows, table, streams, consts, outs, scratch):
    def per_slot(shape):
        return pl.BlockSpec((1,) + tuple(shape), lambda i, table: (i,) + (0,) * len(shape))

    blocks = jax.ShapeDtypeStruct(plan.blocks(rows), jnp.bfloat16)
    return pl.pallas_call(
        functools.partial(kernel, plan),
        out_shape=tuple(jax.ShapeDtypeStruct((PROC,) + shape, kind) for shape, kind in outs)
        + (blocks, blocks),
        grid_spec=pltpu.PrefetchScalarGridSpec(
            num_scalar_prefetch=1,
            grid=(PROC,),
            in_specs=[per_slot(stream.shape[1:]) for stream in streams]
            + [whole(const.shape) for const in consts],
            out_specs=[per_slot(shape) for shape, _ in outs] + [HBM, HBM],
            scratch_shapes=scratch
            + [pltpu.VMEM((2,) + blocks.shape, jnp.bfloat16), pltpu.SemaphoreType.DMA((2,))],
        ),
        compiler_params=pltpu.CompilerParams(vmem_limit_bytes=VMEM_BYTES),
        cost_estimate=cost(micros),
        name=name,
    )(table, *streams, *consts)


def shifted(values, names, sizes, shift):
    count = math.prod(sizes)
    pairs = []
    for index in range(count):
        spot = []
        rest = index
        for size in reversed(sizes):
            spot.append(rest % size)
            rest //= size
        spot = spot[::-1]
        target = 0
        for at, step, size in zip(spot, shift, sizes):
            target = target * size + (at + step) % size
        pairs.append((index, target))
    return lax.ppermute(values, names, pairs)


def shifts(sizes):
    steps = [()]
    for size in sizes:
        steps = [step + (more,) for step in steps for more in range(size)]
    return steps


def gather_all(plan, values):
    pair = jnp.concatenate([values, shifted(values, ("core",), (2,), (1,))], axis=0)
    sizes = (plan.ys, plan.g2)
    column = jnp.concatenate(
        [pair] + [shifted(pair, ("y", "g2"), sizes, step) for step in shifts(sizes)[1:]], axis=0
    )
    return [column] + [shifted(column, ("g1",), (plan.g1,), (step,)) for step in range(1, plan.g1)]


def distance(plan, slide, member):
    my_core, my_y = lax.axis_index("core"), lax.axis_index("y")
    my_z, my_x = lax.axis_index("g1"), lax.axis_index("g2")
    y, core, z, x = slide // 2, slide % 2, member // plan.g2, member % plan.g2
    cross = (my_y - y) % plan.ys * plan.g2 + (my_x - x) % plan.g2
    return ((my_z - z) % plan.g1 * plan.cross + cross) * 2 + (core ^ my_core)


def add_all(parts, kind=jnp.bfloat16):
    total = parts[0].astype(jnp.float32)
    for part in parts[1:]:
        total = total + part.astype(jnp.float32)
    return total.astype(kind)


def other_core(values):
    return shifted(values, ("core",), (2,), (1,))


def sum_axis(kept, sent, name, size, kind=jnp.bfloat16):
    return [kept] + [shifted(part, (name,), (size,), (step + 1,)) for step, part in enumerate(sent)]


def position_code(positions):
    half_width = E // 2
    channel_ids = jnp.arange(E, dtype=jnp.int32) % half_width
    frequency = jnp.exp(
        (2 * (channel_ids // 2)).astype(jnp.float32) * (-math.log(10000.0) / half_width)
    )
    phase = jnp.where(channel_ids % 2 == 0, 0.0, 0.5 * math.pi)
    rows = jnp.where(
        jnp.arange(E, dtype=jnp.int32) < half_width, positions[0][..., None], positions[1][..., None]
    )
    return jnp.sin(rows.astype(jnp.float32) * frequency + phase)


def on_device(
    tile_maps,
    positions,
    counts,
    routing,
    depth_kernel,
    depth_bias,
    norm_gain,
    norm_shift,
    expand_weight,
    expand_bias,
    reduce_weight,
    reduce_bias,
    layer_scale,
    head_weight,
    slide_taps,
    slide_weight,
    slide_bias,
    cotangent,
):
    slides = lax.axis_size(DP)
    members = lax.axis_size(GROUP)
    my_device = lax.axis_index(ALL)
    slots, channels = tile_maps.shape[0], tile_maps.shape[3]
    devices, length, places = slides * members, slots * members, slots // slides
    plan = Plan(slides, members, channels, expand_weight.shape[1])

    packed, table = pack_tiles(routing, tile_maps, slides, places)
    from_core = other_core(packed[0])

    def from_other(buffers):
        return [
            lax.ppermute(buffer, DP, [(index, index ^ (other + 2)) for index in range(slides)])
            for other, buffer in enumerate(buffers)
        ]

    arrived = []
    for rank in range(places):
        buffers = packed[1 + rank * (slides - 2) : 1 + (rank + 1) * (slides - 2)]
        if arrived:
            held = lax.optimization_barrier((tuple(buffers), tuple(arrived[-1])))
            buffers, arrived[-1] = held[0], list(held[1])
        arrived.append(from_other(buffers))

    vectors = jnp.stack(
        [
            jnp.pad(vector, (0, expand_bias.shape[0] - vector.shape[0]))
            for vector in (
                norm_gain,
                norm_shift,
                layer_scale,
                reduce_bias,
                depth_bias,
                expand_bias,
                slide_bias,
                slide_bias,
            )
        ]
    )
    consts = (depth_kernel, vectors, expand_weight, reduce_weight, head_weight)
    saved = forward_block(0, PROC, table, (tile_maps, from_core), consts, ())
    for rank in range(places):
        items = min(PROC, slides - 2)
        saved = forward_block(1 + rank, items, table, arrived[rank], consts, saved)
    section, tile_embed, unit, inv, hidden, slope, head_slope, source = saved
    filled = table[FILLED : FILLED + PROC] != 0
    tile_embed = jnp.where(filled[:, None], tile_embed[:PROC, 0], 0.0).astype(jnp.bfloat16)
    embeds = gather_all(plan, tile_embed)
    tile_out = jnp.where(filled[:, None, None, None], section[:PROC], jnp.zeros((), jnp.bfloat16))

    packed_last, routing, cotangent, positions, counts = lax.optimization_barrier(
        (table, routing, cotangent, positions, counts)
    )
    extras = jnp.concatenate(
        [
            cotangent[0],
            routing.reshape(-1).astype(jnp.float32),
            jnp.zeros((960 - E - slides * slots,), jnp.float32),
            positions.reshape(-1).astype(jnp.float32),
            jnp.zeros((1023 - 960 - 2 * slots,), jnp.float32),
            counts.astype(jnp.float32),
        ]
    )
    extras = jnp.concatenate(gather_all(plan, extras[None, :]), axis=0)
    ids = jnp.arange(devices, dtype=jnp.int32)
    spots = distance(plan, ids // members, ids % members)
    extras = jnp.take(extras, spots, axis=0)
    route_all = extras[:, E : E + slides * slots].astype(jnp.int32)
    route_all = route_all.reshape(slides, members, slides, slots)[0]
    pos_all = extras[:, 960 : 960 + 2 * slots].reshape(slides, members, 2, slots)
    pos_all = pos_all.transpose(2, 0, 3, 1).reshape(2, slides, length)
    counts_all = extras[:, 1023].reshape(slides, members)[:, 0]
    cot_all = extras[:, :E].reshape(slides, members, 1, E)[:, 0]
    codes = position_code(pos_all)
    member_ids = jnp.arange(members, dtype=jnp.int32)[:, None, None]
    target = jnp.where(
        route_all >= 0,
        distance(plan, route_all // PROC, member_ids) * PROC + route_all % PROC,
        -1,
    )
    target = target.transpose(1, 2, 0).reshape(slides, length, 1)
    pick = (target == jnp.arange(devices * PROC, dtype=jnp.int32)).astype(jnp.bfloat16)
    steps = jnp.arange(length, dtype=jnp.int32)[None, :, None].astype(jnp.float32)
    weight = jnp.where(steps < counts_all[:, None, None], 1.0 / counts_all[:, None, None], 0.0)

    feature, embed_grad = slide_grads(
        table, embeds, pick, codes, weight, cot_all, slide_taps, slide_weight, vectors
    )

    side, hid = tile_maps.shape[1], expand_weight.shape[1]
    cells, bands = side * side, channels // LANES
    eye = jnp.asarray(np.eye(channels, dtype=np.float32), jnp.bfloat16)
    grad_mlp, reduce_kept, reduce_sent = backward_call(
        plan,
        reduce_kernel,
        "reduce_grads",
        5.0,
        plan.block_rows,
        table,
        (embed_grad, hidden, head_slope),
        (vectors, head_weight, eye),
        (((cells, channels), jnp.bfloat16),),
        [
            pltpu.VMEM((PROC * cells, hid), jnp.bfloat16),
            pltpu.VMEM((channels, PROC * cells), jnp.bfloat16),
            pltpu.VMEM((cells, E), jnp.bfloat16),
        ],
    )
    reduce_came = other_core(reduce_sent)
    depth_back, expand_kept, expand_sent = backward_call(
        plan,
        expand_kernel,
        "expand_grads",
        8.0,
        plan.block_rows,
        table,
        (grad_mlp, slope, unit, inv),
        (vectors, expand_weight, reduce_weight, eye),
        (((bands, cells, LANES), jnp.float32),),
        [
            pltpu.VMEM((PROC * cells, hid), jnp.bfloat16),
            pltpu.VMEM((channels, PROC * cells), jnp.bfloat16),
            pltpu.VMEM((cells, channels), jnp.float32),
        ],
    )
    expand_came = other_core(expand_sent)

    def column(kept, came, wanted):
        grid = [
            part.reshape((plan.ys, plan.g2) + part.shape[1:]) for part in (kept, came)
        ]
        return add_all([wanted(part) for part in grid])

    reduce_out = [
        column(reduce_kept, reduce_came, lambda part: part[:, step]) for step in range(1, plan.g2)
    ]
    reduce_stay = column(reduce_kept, reduce_came, lambda part: part[:, 0])
    depth_back, reduce_out = lax.optimization_barrier((depth_back, reduce_out))
    reduce_parts = sum_axis(reduce_stay, reduce_out, "g2", plan.g2)
    depth_kept, depth_sent = backward_call(
        plan,
        taps_kernel,
        "tap_grads",
        8.0,
        ROW_UNIT,
        table,
        (source, depth_back),
        (),
        (),
        [
            pltpu.VMEM((bands, side, side + ROW_UNIT, LANES), jnp.float32),
            pltpu.VMEM((bands, KS * KS, 8, LANES), jnp.float32),
            pltpu.VMEM((KS * KS + 7, channels), jnp.float32),
        ],
    )
    depth_came = other_core(depth_sent)
    expand_out = [
        column(expand_kept, expand_came, lambda part: part[step]) for step in range(1, plan.ys)
    ]
    expand_stay = column(expand_kept, expand_came, lambda part: part[0])
    expand_parts = sum_axis(expand_stay, expand_out, "y", plan.ys)

    def finish(parts, name, size):
        out = [add_all([part[step] for part in parts]) for step in range(1, size)]
        stay = add_all([part[0] for part in parts])
        parts = sum_axis(stay, out, name, size)
        out = [add_all([part[step] for part in parts]) for step in range(1, plan.g1)]
        stay = add_all([part[0] for part in parts])
        return add_all(sum_axis(stay, out, "g1", plan.g1), jnp.float32)

    reduce_total = finish(reduce_parts, "y", plan.ys)
    expand_total = finish(expand_parts, "g2", plan.g2)
    sizes = (plan.ys, plan.g2)
    depth_all = add_all([depth_kept, depth_came])
    depth_parts = [depth_all[0]] + [
        shifted(depth_all[index], ("y", "g2"), sizes, step)
        for index, step in enumerate(shifts(sizes))
        if index
    ]
    depth_all = add_all(depth_parts)
    depth_total = add_all(
        sum_axis(depth_all[0], [depth_all[step] for step in range(1, plan.g1)], "g1", plan.g1),
        jnp.float32,
    )

    expand_share = expand_total[: plan.pieces * plan.expand_rows]
    expand_share = expand_share.reshape(plan.pieces, plan.expand_rows, channels).transpose(1, 0, 2)
    reduce_share = reduce_total[: plan.reduce_rows]
    depth_share = lax.dynamic_slice(
        depth_total[:DEPTH_ROWS].reshape(-1), (my_device * plan.share % channels,), (plan.share,)
    )
    return (tile_out, feature, expand_share.reshape(-1), reduce_share.reshape(-1), depth_share)


def solution(mesh):
    slides, members = mesh.shape["dp"], mesh.shape["group"]
    fine = Mesh(mesh.devices.reshape(slides // 2, 2, 4, members // 4), ALL)
    return jax.shard_map(
        on_device,
        mesh=fine,
        in_specs=(
            P(ALL, None, None, None),
            P(None, ALL),
            P(DP),
            P(None, GROUP, None),
        )
        + (P(),) * 13
        + (P(DP, None),),
        out_specs=(
            P(ALL, None, None, None),
            P(DP, None),
            P(ALL),
            P(ALL),
            P(ALL),
        ),
        check_vma=False,
    )
```

time: 154 us -> 168 us (1.091)
  starting transfers between devices: 16.8 us -> 42.9 us
  blocking collectives: 19.4 us -> 0 us
  Pallas kernels: 55 us -> 73.1 us
  waiting for transfers between devices: 37.5 us -> 24.3 us
  local copies, waits for them, and re-layouts: 10.1 us -> 15.7 us
  other arithmetic: 12.5 us -> 9.36 us
    ppermute x1 -> x38, starting transfers between devices: 0.2 us -> 42.9 us  [the longest x34 37.5 us: shifted(): return lax.ppermute(values, names, pairs)]
    all_to_all x4 -> x0, waiting for transfers between devices: 34.5 us -> none  [exchange(): lax.all_to_all(values, names, split_axis=0, concat_axis=0, tiled=True)]
    ppermute x1 -> x38, waiting for transfers between devices: 2.99 us -> 24.3 us  [the longest x34 24.3 us: shifted(): return lax.ppermute(values, names, pairs)]
    all_to_all x1 -> x0, blocking collectives: 19.4 us -> none  [exchange(): lax.all_to_all(values, names, split_axis=0, concat_axis=0, tiled=True)]
    pallas_call x3 -> x7, Pallas kernels: 51.7 us -> 70.5 us  [the longest x3 33.5 us: forward_block(): pl.pallas_call(functools.partial(forward_kernel, kind, len(tiles), len(be...]
    all_to_all x4 -> x0, starting transfers between devices: 16.6 us -> none  [exchange(): lax.all_to_all(values, names, split_axis=0, concat_axis=0, tiled=True)]
    pad x6, local copies, waits for them, and re-layouts: 0.02 us -> 4.11 us  [on_device(): jnp.pad(vector, (0, expand_bias.shape[0] - vector.shape[0]))]
    unnamed x25 -> x32, local copies, waits for them, and re-layouts: 1.74 us -> 4.81 us
  transfers between devices with their start and end apart: 5 -> 38, of which waited for: 5 -> 19; matrix products, arithmetic and copies ran while one was open for 7% -> 11% of each run, Pallas kernels for 0% -> 21%
where the time goes in v2:
time: 168 us; the launch traced here: 167 us
  Pallas kernels  73.1 us (44%)
  starting transfers between devices  42.9 us (26%)
  waiting for transfers between devices  24.3 us (14%)
  local copies, waits for them, and re-layouts  15.7 us (9%)
  other arithmetic  9.36 us (6%)
  between operations  1.71 us (1%)
    ppermute x34, starting transfers between devices, shifted(): return lax.ppermute(values, names, pairs)  37.5 us
    pallas_call x3, Pallas kernels, forward_block(): pl.pallas_call(functools.partial(forward_kernel, kind, len(tiles), len(be...  33.5 us
    pallas_call x3, Pallas kernels, backward_call(): pl.pallas_call(functools.partial(kernel, plan), out_shape=tuple((jax.Shap...  30.5 us
    ppermute x34, waiting for transfers between devices, shifted(): return lax.ppermute(values, names, pairs)  24.3 us
    pallas_call x1, Pallas kernels, slide_grads(): pl.pallas_call(functools.partial(slide_kernel, length, slides, len(pieces...  6.51 us
    ppermute x4, starting transfers between devices, from_other(): lax.ppermute(buffer, DP, [(index, index ^ other + 2) for index in range(s...  5.46 us
    unnamed x32, local copies, waits for them, and re-layouts  4.81 us
    pad x6, local copies, waits for them, and re-layouts, on_device(): jnp.pad(vector, (0, expand_bias.shape[0] - vector.shape[0]))  4.11 us
  transfers between devices with their start and end apart: 38, of which 19 were waited for; matrix products, arithmetic and copies ran while one was open for 11% of the time, Pallas kernels for 21%

profile of v2, /device:TPU:0, one launch (start us, length us, event | category | flops | bytes accessed | tf_op | source)
XLA Modules:
  0.0 167.2 jit_solution(5050275835883689010)
XLA Ops:
  0.6 1.4 copy-done
  2.7 2.6 %pack_tiles.1 = (bf16[2,16,16,384]{3,2,1,0:T(8,128)(2,1)S(1)}, bf16[1,16,16,384]{3,2,1,0:T(8,128)(2,1)S(1)}, bf16[1,16,16,384]{3,2,1,0:T(8,128)(2,1)S(1)}, bf16[...) custom-call(s32[4,1,8]{2,1,0:T(1,128)S(1)} %copy-done.1, ...), custom_call_target="tpu_custom_call" | custom-call | tf_op jit(solution)/shard_map/pack_tiles/pallas_call | solution.py:181
  5.3 3.0 %collective-permute-start = (bf16[1,16,16,384]{3,2,1,0:T(8,128)(2,1)S(1)}, bf16[1,16,16,384]{3,2,1,0:T(8,128)(2,1)S(1)}, u32[]{:S(2)}, u32[]{:S(2)}) collective-permute-start(bf16[1,16,16,384]{3,2,1,0:T(8,128)(2,1)S(1)} %get-tuple-element.58), channel_id=1, source_target_pairs={{0,16},{8,24},{16,0},{24,8},{1,17},{9,25},{17,1},{25,9},{2,18},{10... | collective-permute-start | bytes 589832 | tf_op jit(solution)/shard_map/ppermute | solution.py:876
  11.4 1.0 collective-permute-done.12
  12.4 1.6 collective-permute-start.13
  14.0 1.7 collective-permute-start.14
  16.1 2.2 %collective-permute-done.14 = f32[2,1024]{1,0:T(2,128)S(1)} collective-permute-done((f32[2,1024]{1,0:T(2,128)S(1)}, f32[2,1024]{1,0:T(2,128)S(1)}, u32[]{:S(2)}, u32[]{:S(2)}) %collective-permute-start.14) | collective-permute-done | bytes 8224 | tf_op jit(solution)/shard_map/ppermute | solution.py:789
  18.4 1.8 %collective-permute-done.15 = f32[2,1024]{1,0:T(2,128)S(1)} collective-permute-done((f32[2,1024]{1,0:T(2,128)S(1)}, f32[2,1024]{1,0:T(2,128)S(1)}, u32[]{:S(2)}, u32[]{:S(2)}) %collective-permute-start.15) | collective-permute-done | bytes 8224 | tf_op jit(solution)/shard_map/ppermute | solution.py:789
  20.2 1.6 collective-permute-start.16
  21.8 2.6 %collective-permute-start.17 = (f32[8,1024]{1,0:T(8,128)S(1)}, f32[8,1024]{1,0:T(8,128)S(1)}, u32[]{:S(2)}, u32[]{:S(2)}) collective-permute-start(f32[8,1024]{1,0:T(8,128)S(1)} %concatenate.25), channel_id=1, source_target_pairs={{0,4},{2,6},{4,0},{6,2},{1,5},{3,7},{5,1},{7,3},{8,12},{10,14},{12... | collective-permute-start | bytes 98312 | tf_op jit(solution)/shard_map/ppermute | solution.py:789
  24.4 1.3 collective-permute-start.18
  33.0 3.5 %add_sine_fusion.refs_5_ = f32[4,64,768]{2,1,0:T(8,128)} fusion(f32[768]{0:T(1024)S(1)} %get-tuple-element.131, f32[768]{0:T(1024)S(1)} %get-tuple-element.130, f32[4,64]{1,0:T(4,128)S(1)} %broadcast_in_dim.108, f32[4,64]{1,0:T(4,128)S(1)} %broadcast_in_dim.106, pred[768]{0:T(1024)(128)(4,1)S(1)} %iota_compare_fusion.1), kind=kLoop, calls=%fused_computation.1 | loop fusion | flops 589824 | bytes 795392 | tf_op jit(solution)/shard_map/sin | solution.py:841
  38.3 1.5 collective-permute-start.3
  39.8 0.7 copy-done.8
  40.5 14.5 %forward_block_0.1 = (bf16[5,16,16,384]{3,2,1,0:T(8,128)(2,1)}, f32[5,1,768]{2,1,0:T(1,128)}, f32[5,256,384]{2,1,0:T(8,128)}, f32[5,256,128]{2,1,0:T(8,128)}, bf...) custom-call(s32[51]{0:T(128)} %copy-done.2, ...), custom_call_target="tpu_custom_call" | custom-call | flops 12000000000 | bytes 1024 | tf_op jit(solution)/shard_map/forward_block_0/pallas_call | solution.py:359
  55.0 9.3 %forward_block_1.1 = (bf16[5,16,16,384]{3,2,1,0:T(8,128)(2,1)}, f32[5,1,768]{2,1,0:T(1,128)}, f32[5,256,384]{2,1,0:T(8,128)}, f32[5,256,128]{2,1,0:T(8,128)}, bf...) custom-call(s32[51]{0:T(128)} %copy-done.2, ...), custom_call_target="tpu_custom_call", output_to_operand_aliasing={{0}: (8, {}), {1}: (9, {}), {2}: (10, {}), {3}: (11, {}), {... | custom-call | flops 12000000000 | bytes 1024 | tf_op jit(solution)/shard_map/forward_block_1/pallas_call | solution.py:359
  65.1 9.6 %forward_block_2.1 = (bf16[5,16,16,384]{3,2,1,0:T(8,128)(2,1)}, f32[5,1,768]{2,1,0:T(1,128)}, f32[5,256,384]{2,1,0:T(8,128)}, f32[5,256,128]{2,1,0:T(8,128)}, bf...) custom-call(s32[51]{0:T(128)} %copy-done.2, ...), custom_call_target="tpu_custom_call", output_to_operand_aliasing={{0}: (8, {}), {1}: (9, {}), {2}: (10, {}), {3}: (11, {}), {... | custom-call | flops 12000000000 | bytes 1024 | tf_op jit(solution)/shard_map/forward_block_2/pallas_call | solution.py:359
  75.9 0.8 collective-permute-done.5
  77.3 0.9 collective-permute-start.7
  78.3 2.0 %collective-permute-start.8 = (bf16[8,768]{1,0:T(8,128)(2,1)S(1)}, bf16[8,768]{1,0:T(8,128)(2,1)S(1)}, u32[]{:S(2)}, u32[]{:S(2)}) collective-permute-start(bf16[8,768]{1,0:T(8,128)(2,1)S(1)} %pad_maximum_fusion), channel_id=1, source_target_pairs={{0,17},{1,16},{16,1},{17,0},{2,19},{3,18},{18,3},{19,2},{4,21},{5,... | collective-permute-start | bytes 36872 | tf_op jit(solution)/shard_map/ppermute | solution.py:789
  81.0 1.8 %collective-permute-done.8 = bf16[8,768]{1,0:T(8,128)(2,1)S(1)} collective-permute-done((bf16[8,768]{1,0:T(8,128)(2,1)S(1)}, bf16[8,768]{1,0:T(8,128)(2,1)S(1)}, u32[]{:S(2)}, u32[]{:S(2)}) %collective-permute-start.8) | collective-permute-done | bytes 12320 | tf_op jit(solution)/shard_map/ppermute | solution.py:789
  82.9 0.7 collective-permute-start.9
  84.0 2.8 %collective-permute-start.11 = (bf16[32,768]{1,0:T(8,128)(2,1)S(1)}, bf16[32,768]{1,0:T(8,128)(2,1)S(1)}, u32[]{:S(2)}, u32[]{:S(2)}) collective-permute-start(bf16[32,768]{1,0:T(8,128)(2,1)S(1)} %concatenate.22.refs_0_), channel_id=1, source_target_pairs={{0,6},{2,0},{4,2},{6,4},{1,7},{3,1},{5,3},{7,5},{8,14},{10,8},{12,... | collective-permute-start | bytes 147464 | tf_op jit(solution)/shard_map/ppermute | solution.py:789
  87.5 1.4 collective-permute-done.9.refs_1_
  88.9 0.7 collective-permute-done.10.refs_2_
  90.9 6.5 %slide_grads.1 = (f32[1,768]{1,0:T(1,128)}, f32[4,1,768]{2,1,0:T(1,128)}) custom-call(s32[51]{0:T(128)} %copy-done.2, bf16[32,768]{1,0:T(8,128)(2,1)} %copy-done.7, bf16[32,768]{1,0:T(8,128)(2,1)} %copy-done.13, bf16[32,768]{1,0:T(8,128)(2,1)} %copy-done.14, bf16[32,768]{1,0:T(8,128)(2,1)} %copy-done.15, bf16[4,64,128]{2,1,0:T(8,128)(2,1)} %fusion.5.refs_4_, ...), custom_call_target="tpu_custom_call" | custom-call | flops 6000000000 | bytes 1024 | tf_op jit(solution)/shard_map/slide_grads/pallas_call | solution.py:481
  97.4 10.4 %reduce_grads.1 = (bf16[4,256,384]{2,1,0:T(8,128)(2,1)}, bf16[4,4,48,384]{3,2,1,0:T(8,128)(2,1)}, bf16[4,4,48,384]{3,2,1,0:T(8,128)(2,1)}) custom-call(s32[51]{0:T(128)} %copy-done.2, f32[4,1,768]{2,1,0:T(1,128)} %get-tuple-element.88.grad_ref, bf16[5,256,1536]{2,1,0:T(8,128)(2,1)} %get-tuple-element.89.hidden_ref, ...), custom_call_target="tpu_custom_call" | custom-call | flops 5000000000 | bytes 1024 | tf_op jit(solution)/shard_map/reduce_grads/pallas_call | solution.py:756
  108.0 12.0 %expand_grads.1 = (f32[4,3,256,128]{3,2,1,0:T(8,128)}, bf16[4,4,48,384]{3,2,1,0:T(8,128)(2,1)}, bf16[4,4,48,384]{3,2,1,0:T(8,128)(2,1)}) custom-call(s32[51]{0:T(128)} %copy-done.2, bf16[4,256,384]{2,1,0:T(8,128)(2,1)} %get-tuple-element.91.grad_mlp_ref, bf16[5,256,1536]{2,1,0:T(8,128)(2,1)} %get-tuple-element.92.slope_ref, ...), custom_call_target="tpu_custom_call" | custom-call | flops 8000000000 | bytes 1024 | tf_op jit(solution)/shard_map/expand_grads/pallas_call | solution.py:756
  120.2 8.1 %tap_grads.1 = (bf16[4,4,16,384]{3,2,1,0:T(8,128)(2,1)}, bf16[4,4,16,384]{3,2,1,0:T(8,128)(2,1)}) custom-call(s32[51]{0:T(128)} %copy-done.2, bf16[5,16,16,384]{3,2,1,0:T(8,128)(2,1)} %get-tuple-element.101.source_ref, f32[4,3,256,128]{3,2,1,0:T(8,128)} %get-tuple-element.102.depth_back), custom_call_target="tpu_custom_call" | custom-call | flops 8000000000 | bytes 1024 | tf_op jit(solution)/shard_map/tap_grads/pallas_call | solution.py:756
  128.9 1.2 collective-permute-done.31
  130.1 1.0 add_convert_fusion.4
  131.1 2.0 %collective-permute-start.34 = (bf16[4,16,384]{2,1,0:T(8,128)(2,1)S(1)}, bf16[4,16,384]{2,1,0:T(8,128)(2,1)S(1)}, u32[]{:S(2)}, u32[]{:S(2)}) collective-permute-start(bf16[4,16,384]{2,1,0:T(8,128)(2,1)S(1)} %get-tuple-element.120), channel_id=1, source_target_pairs={{0,17},{1,16},{16,1},{17,0},{2,19},{3,18},{18,3},{19,2},{4,21},{5,... | collective-permute-start | bytes 147464 | tf_op jit(solution)/shard_map/ppermute | solution.py:789
  133.4 1.3 collective-permute-start.32
  134.8 1.1 collective-permute-start.20
  136.2 1.2 collective-permute-done.33
  137.6 2.3 %collective-permute-start.37 = (bf16[16,384]{1,0:T(8,128)(2,1)S(1)}, bf16[16,384]{1,0:T(8,128)(2,1)S(1)}, u32[]{:S(2)}, u32[]{:S(2)}) collective-permute-start(bf16[16,384]{1,0:T(8,128)(2,1)S(1)} %get-tuple-element.123), channel_id=1, source_target_pairs={{0,6},{2,0},{4,2},{6,4},{1,7},{3,1},{5,3},{7,5},{8,14},{10,8},{12,... | collective-permute-start | bytes 36872 | tf_op jit(solution)/shard_map/ppermute | solution.py:789
  140.5 1.0 slice_select_fusion
  141.6 1.3 collective-permute-start.26
  142.9 1.5 collective-permute-done.36
  144.4 1.6 collective-permute-done.35
  146.8 0.8 collective-permute-start.21
  147.6 2.9 %collective-permute-done.26 = bf16[2,4,48,384]{3,2,1,0:T(8,128)(2,1)S(1)} collective-permute-done((bf16[2,4,48,384]{3,2,1,0:T(8,128)(2,1)S(1)}, bf16[2,4,48,384]{3,2,1,0:T(8,128)(2,1)S(1)}, u32[]{:S(2)}, u32[]{:S(2)}) %collective-permute-start.26) | collective-permute-done | bytes 294944 | tf_op jit(solution)/shard_map/ppermute | solution.py:789
  150.6 1.5 collective-permute-start.27
  152.1 3.6 %collective-permute-start.24 = (bf16[48,384]{1,0:T(8,128)(2,1)S(1)}, bf16[48,384]{1,0:T(8,128)(2,1)S(1)}, u32[]{:S(2)}, u32[]{:S(2)}) collective-permute-start(bf16[48,384]{1,0:T(8,128)(2,1)S(1)} %get-tuple-element.117), channel_id=1, source_target_pairs={{0,6},{2,0},{4,2},{6,4},{1,7},{3,1},{5,3},{7,5},{8,14},{10,8},{12,... | collective-permute-start | bytes 110600 | tf_op jit(solution)/shard_map/ppermute | solution.py:789
  156.5 3.6 %collective-permute-start.30 = (bf16[48,384]{1,0:T(8,128)(2,1)S(1)}, bf16[48,384]{1,0:T(8,128)(2,1)S(1)}, u32[]{:S(2)}, u32[]{:S(2)}) collective-permute-start(bf16[48,384]{1,0:T(8,128)(2,1)S(1)} %get-tuple-element.114), channel_id=1, source_target_pairs={{0,6},{2,0},{4,2},{6,4},{1,7},{3,1},{5,3},{7,5},{8,14},{10,8},{12,... | collective-permute-start | bytes 110600 | tf_op jit(solution)/shard_map/ppermute | solution.py:789
  160.8 1.2 collective-permute-done.22
  162.7 2.3 %collective-permute-done.29 = bf16[48,384]{1,0:T(8,128)(2,1)S(1)} collective-permute-done((bf16[48,384]{1,0:T(8,128)(2,1)S(1)}, bf16[48,384]{1,0:T(8,128)(2,1)S(1)}, u32[]{:S(2)}, u32[]{:S(2)}) %collective-permute-start.29) | collective-permute-done | bytes 36896 | tf_op jit(solution)/shard_map/ppermute | solution.py:789
  165.0 1.5 collective-permute-done.28
  (151 shorter events, 24.0 us)
Async XLA Ops:
  0.6 1.4 copy-start
  5.3 34.4 %copy-start.2 = (s32[51]{0:T(128)}, s32[51]{0:T(128)S(1)}, u32[]{:S(2)}) copy-start(s32[51]{0:T(128)S(1)} %get-tuple-element.55.table_ref) | copy-start | bytes 616
  5.3 32.5 %collective-permute-start = (bf16[1,16,16,384]{3,2,1,0:T(8,128)(2,1)S(1)}, bf16[1,16,16,384]{3,2,1,0:T(8,128)(2,1)S(1)}, u32[]{:S(2)}, u32[]{:S(2)}) collective-permute-start(bf16[1,16,16,384]{3,2,1,0:T(8,128)(2,1)S(1)} %get-tuple-element.58), channel_id=1, source_target_pairs={{0,16},{8,24},{16,0},{24,8},{1,17},{9,25},{17,1},{25,9},{2,18},{10... | collective-permute-start | bytes 589832 | tf_op jit(solution)/shard_map/ppermute | solution.py:876
  8.4 29.5 %collective-permute-start.1 = (bf16[1,16,16,384]{3,2,1,0:T(8,128)(2,1)S(1)}, bf16[1,16,16,384]{3,2,1,0:T(8,128)(2,1)S(1)}, u32[]{:S(2)}, u32[]{:S(2)}) collective-permute-start(bf16[1,16,16,384]{3,2,1,0:T(8,128)(2,1)S(1)} %get-tuple-element.59), channel_id=1, source_target_pairs={{0,24},{8,16},{16,8},{24,0},{1,25},{9,17},{17,9},{25,1},{2,26},{10... | collective-permute-start | bytes 589832 | tf_op jit(solution)/shard_map/ppermute | solution.py:876
  11.2 1.2 collective-permute-start.12
  12.4 3.7 %collective-permute-start.13 = (f32[2,1024]{1,0:T(2,128)S(1)}, f32[2,1024]{1,0:T(2,128)S(1)}, u32[]{:S(2)}, u32[]{:S(2)}) collective-permute-start(f32[2,1024]{1,0:T(2,128)S(1)} %pad_maximum_fusion.1), channel_id=1, source_target_pairs={{0,1},{1,0},{16,17},{17,16},{2,3},{3,2},{18,19},{19,18},{4,5},{5,4... | collective-permute-start | bytes 24584 | tf_op jit(solution)/shard_map/ppermute | solution.py:789
  14.0 4.4 %collective-permute-start.14 = (f32[2,1024]{1,0:T(2,128)S(1)}, f32[2,1024]{1,0:T(2,128)S(1)}, u32[]{:S(2)}, u32[]{:S(2)}) collective-permute-start(f32[2,1024]{1,0:T(2,128)S(1)} %pad_maximum_fusion.1), channel_id=1, source_target_pairs={{0,16},{1,17},{16,0},{17,1},{2,18},{3,19},{18,2},{19,3},{4,20},{5,... | collective-permute-start | bytes 24584 | tf_op jit(solution)/shard_map/ppermute | solution.py:789
  15.6 4.5 %collective-permute-start.15 = (f32[2,1024]{1,0:T(2,128)S(1)}, f32[2,1024]{1,0:T(2,128)S(1)}, u32[]{:S(2)}, u32[]{:S(2)}) collective-permute-start(f32[2,1024]{1,0:T(2,128)S(1)} %pad_maximum_fusion.1), channel_id=1, source_target_pairs={{0,17},{1,16},{16,1},{17,0},{2,19},{3,18},{18,3},{19,2},{4,21},{5,... | collective-permute-start | bytes 24584 | tf_op jit(solution)/shard_map/ppermute | solution.py:789
  20.2 11.1 %collective-permute-start.16 = (f32[8,1024]{1,0:T(8,128)S(1)}, f32[8,1024]{1,0:T(8,128)S(1)}, u32[]{:S(2)}, u32[]{:S(2)}) collective-permute-start(f32[8,1024]{1,0:T(8,128)S(1)} %concatenate.25), channel_id=1, source_target_pairs={{0,2},{2,4},{4,6},{6,0},{1,3},{3,5},{5,7},{7,1},{8,10},{10,12},{12... | collective-permute-start | bytes 98312 | tf_op jit(solution)/shard_map/ppermute | solution.py:789
  21.8 9.5 %collective-permute-start.17 = (f32[8,1024]{1,0:T(8,128)S(1)}, f32[8,1024]{1,0:T(8,128)S(1)}, u32[]{:S(2)}, u32[]{:S(2)}) collective-permute-start(f32[8,1024]{1,0:T(8,128)S(1)} %concatenate.25), channel_id=1, source_target_pairs={{0,4},{2,6},{4,0},{6,2},{1,5},{3,7},{5,1},{7,3},{8,12},{10,14},{12... | collective-permute-start | bytes 98312 | tf_op jit(solution)/shard_map/ppermute | solution.py:789
  24.4 6.9 %collective-permute-start.18 = (f32[8,1024]{1,0:T(8,128)S(1)}, f32[8,1024]{1,0:T(8,128)S(1)}, u32[]{:S(2)}, u32[]{:S(2)}) collective-permute-start(f32[8,1024]{1,0:T(8,128)S(1)} %concatenate.25), channel_id=1, source_target_pairs={{0,6},{2,0},{4,2},{6,4},{1,7},{3,1},{5,3},{7,5},{8,14},{10,8},{12,... | collective-permute-start | bytes 98312 | tf_op jit(solution)/shard_map/ppermute | solution.py:789
  31.4 8.4 %collective-permute-start.4 = (bf16[2,16,16,384]{3,2,1,0:T(8,128)(2,1)S(1)}, bf16[2,16,16,384]{3,2,1,0:T(8,128)(2,1)S(1)}, u32[]{:S(2)}, u32[]{:S(2)}) collective-permute-start(bf16[2,16,16,384]{3,2,1,0:T(8,128)(2,1)S(1)} %get-tuple-element.64), channel_id=1, source_target_pairs={{0,8},{8,0},{1,9},{9,1},{2,10},{10,2},{3,11},{11,3},{4,12},{12,4},... | collective-permute-start | bytes 1179656 | tf_op jit(solution)/shard_map/ppermute | solution.py:789
  32.1 22.8 %copy-start.4 = (f32[32,1024]{1,0:T(8,128)}, f32[32,1024]{1,0:T(8,128)S(1)}, u32[]{:S(2)}) copy-start(f32[32,1024]{1,0:T(8,128)S(1)} %broadcast_select_fusion) | copy-start | bytes 393220
  37.8 17.2 %copy-start.9 = (bf16[1,16,16,384]{3,2,1,0:T(8,128)(2,1)}, bf16[1,16,16,384]{3,2,1,0:T(8,128)(2,1)S(1)}, u32[]{:S(2)}) copy-start(bf16[1,16,16,384]{3,2,1,0:T(8,128)(2,1)S(1)} %collective-permute-done.refs_0_) | copy-start | bytes 589828
  37.8 17.2 %copy-start.10 = (bf16[1,16,16,384]{3,2,1,0:T(8,128)(2,1)}, bf16[1,16,16,384]{3,2,1,0:T(8,128)(2,1)S(1)}, u32[]{:S(2)}) copy-start(bf16[1,16,16,384]{3,2,1,0:T(8,128)(2,1)S(1)} %collective-permute-done.1.refs_1_) | copy-start | bytes 589828
  37.8 26.5 %collective-permute-start.2 = (bf16[1,16,16,384]{3,2,1,0:T(8,128)(2,1)S(1)}, bf16[1,16,16,384]{3,2,1,0:T(8,128)(2,1)S(1)}, u32[]{:S(2)}, u32[]{:S(2)}) collective-permute-start(bf16[1,16,16,384]{3,2,1,0:T(8,128)(2,1)S(1)} %get-tuple-element.60), channel_id=1, source_target_pairs={{0,16},{8,24},{16,0},{24,8},{1,17},{9,25},{17,1},{25,9},{2,18},{10... | collective-permute-start | bytes 589832 | tf_op jit(solution)/shard_map/ppermute | solution.py:876
  38.3 26.1 %collective-permute-start.3 = (bf16[1,16,16,384]{3,2,1,0:T(8,128)(2,1)S(1)}, bf16[1,16,16,384]{3,2,1,0:T(8,128)(2,1)S(1)}, u32[]{:S(2)}, u32[]{:S(2)}) collective-permute-start(bf16[1,16,16,384]{3,2,1,0:T(8,128)(2,1)S(1)} %get-tuple-element.61), channel_id=1, source_target_pairs={{0,24},{8,16},{16,8},{24,0},{1,25},{9,17},{17,9},{25,1},{2,26},{10... | collective-permute-start | bytes 589832 | tf_op jit(solution)/shard_map/ppermute | solution.py:876
  65.1 10.7 %slice-start = ((f32[32,1024]{1,0:T(8,128)}), f32[32,32]{1,0:T(8,128)S(1)}, s32[]{:S(2)}) async-start(f32[32,1024]{1,0:T(8,128)} %copy-done.4), calls=%async_computation | async-start | bytes 32768 | tf_op jit(solution)/shard_map/slice | solution.py:931
  75.5 1.2 collective-permute-start.5
  76.7 3.8 %collective-permute-start.6 = (bf16[8,768]{1,0:T(8,128)(2,1)S(1)}, bf16[8,768]{1,0:T(8,128)(2,1)S(1)}, u32[]{:S(2)}, u32[]{:S(2)}) collective-permute-start(bf16[8,768]{1,0:T(8,128)(2,1)S(1)} %pad_maximum_fusion), channel_id=1, source_target_pairs={{0,1},{1,0},{16,17},{17,16},{2,3},{3,2},{18,19},{19,18},{4,5},{5,4... | collective-permute-start | bytes 36872 | tf_op jit(solution)/shard_map/ppermute | solution.py:789
  77.3 3.7 %collective-permute-start.7 = (bf16[8,768]{1,0:T(8,128)(2,1)S(1)}, bf16[8,768]{1,0:T(8,128)(2,1)S(1)}, u32[]{:S(2)}, u32[]{:S(2)}) collective-permute-start(bf16[8,768]{1,0:T(8,128)(2,1)S(1)} %pad_maximum_fusion), channel_id=1, source_target_pairs={{0,16},{1,17},{16,0},{17,1},{2,18},{3,19},{18,2},{19,3},{4,20},{5,... | collective-permute-start | bytes 36872 | tf_op jit(solution)/shard_map/ppermute | solution.py:789
  78.3 4.6 %collective-permute-start.8 = (bf16[8,768]{1,0:T(8,128)(2,1)S(1)}, bf16[8,768]{1,0:T(8,128)(2,1)S(1)}, u32[]{:S(2)}, u32[]{:S(2)}) collective-permute-start(bf16[8,768]{1,0:T(8,128)(2,1)S(1)} %pad_maximum_fusion), channel_id=1, source_target_pairs={{0,17},{1,16},{16,1},{17,0},{2,19},{3,18},{18,3},{19,2},{4,21},{5,... | collective-permute-start | bytes 36872 | tf_op jit(solution)/shard_map/ppermute | solution.py:789
  82.9 6.8 %copy-start.7 = (bf16[32,768]{1,0:T(8,128)(2,1)}, bf16[32,768]{1,0:T(8,128)(2,1)S(1)}, u32[]{:S(2)}) copy-start(bf16[32,768]{1,0:T(8,128)(2,1)S(1)} %concatenate.22.refs_0_) | copy-start | bytes 147460
  82.9 6.0 %collective-permute-start.9 = (bf16[32,768]{1,0:T(8,128)(2,1)S(1)}, bf16[32,768]{1,0:T(8,128)(2,1)S(1)}, u32[]{:S(2)}, u32[]{:S(2)}) collective-permute-start(bf16[32,768]{1,0:T(8,128)(2,1)S(1)} %concatenate.22.refs_0_), channel_id=1, source_target_pairs={{0,2},{2,4},{4,6},{6,0},{1,3},{3,5},{5,7},{7,1},{8,10},{10,12},{12... | collective-permute-start | bytes 147464 | tf_op jit(solution)/shard_map/ppermute | solution.py:789
  83.6 6.0 %collective-permute-start.10 = (bf16[32,768]{1,0:T(8,128)(2,1)S(1)}, bf16[32,768]{1,0:T(8,128)(2,1)S(1)}, u32[]{:S(2)}, u32[]{:S(2)}) collective-permute-start(bf16[32,768]{1,0:T(8,128)(2,1)S(1)} %concatenate.22.refs_0_), channel_id=1, source_target_pairs={{0,4},{2,6},{4,0},{6,2},{1,5},{3,7},{5,1},{7,3},{8,12},{10,14},{12... | collective-permute-start | bytes 147464 | tf_op jit(solution)/shard_map/ppermute | solution.py:789
  84.0 5.7 %collective-permute-start.11 = (bf16[32,768]{1,0:T(8,128)(2,1)S(1)}, bf16[32,768]{1,0:T(8,128)(2,1)S(1)}, u32[]{:S(2)}, u32[]{:S(2)}) collective-permute-start(bf16[32,768]{1,0:T(8,128)(2,1)S(1)} %concatenate.22.refs_0_), channel_id=1, source_target_pairs={{0,6},{2,0},{4,2},{6,4},{1,7},{3,1},{5,3},{7,5},{8,14},{10,8},{12,... | collective-permute-start | bytes 147464 | tf_op jit(solution)/shard_map/ppermute | solution.py:789
  107.9 12.1 %collective-permute-start.25 = (bf16[4,4,48,384]{3,2,1,0:T(8,128)(2,1)}, bf16[4,4,48,384]{3,2,1,0:T(8,128)(2,1)S(1)}, u32[]{:S(2)}, u32[]{:S(2)}) collective-permute-start(bf16[4,4,48,384]{3,2,1,0:T(8,128)(2,1)} %get-tuple-element.98), channel_id=1, source_target_pairs={{0,8},{8,0},{1,9},{9,1},{2,10},{10,2},{3,11},{11,3},{4,12},{12,4},... | collective-permute-start | bytes 1769480 | tf_op jit(solution)/shard_map/ppermute | solution.py:789
  108.0 12.0 %copy-start.6 = (bf16[4,4,48,384]{3,2,1,0:T(8,128)(2,1)S(1)}, bf16[4,4,48,384]{3,2,1,0:T(8,128)(2,1)}, u32[]{:S(2)}) copy-start(bf16[4,4,48,384]{3,2,1,0:T(8,128)(2,1)} %get-tuple-element.97) | copy-start | bytes 1769476
  120.2 14.5 %copy-start.5 = (bf16[4,4,48,384]{3,2,1,0:T(8,128)(2,1)S(1)}, bf16[4,4,48,384]{3,2,1,0:T(8,128)(2,1)}, u32[]{:S(2)}) copy-start(bf16[4,4,48,384]{3,2,1,0:T(8,128)(2,1)} %get-tuple-element.95) | copy-start | bytes 1769476
  128.3 12.3 %copy-start.3 = (bf16[5,16,16,384]{3,2,1,0:T(8,128)(2,1)S(1)}, bf16[5,16,16,384]{3,2,1,0:T(8,128)(2,1)}, u32[]{:S(2)}) copy-start(bf16[5,16,16,384]{3,2,1,0:T(8,128)(2,1)} %get-tuple-element.81) | copy-start | bytes 2949124
  128.3 1.8 %collective-permute-start.31 = (bf16[4,4,16,384]{3,2,1,0:T(8,128)(2,1)}, bf16[4,4,16,384]{3,2,1,0:T(8,128)(2,1)S(1)}, u32[]{:S(2)}, u32[]{:S(2)}) collective-permute-start(bf16[4,4,16,384]{3,2,1,0:T(8,128)(2,1)} %get-tuple-element.104), channel_id=1, source_target_pairs={{0,8},{8,0},{1,9},{9,1},{2,10},{10,2},{3,11},{11,3},{4,12},{12,4},... | collective-permute-start | bytes 589832 | tf_op jit(solution)/shard_map/ppermute | solution.py:789
  128.8 5.9 %collective-permute-start.19 = (bf16[4,4,48,384]{3,2,1,0:T(8,128)(2,1)}, bf16[4,4,48,384]{3,2,1,0:T(8,128)(2,1)S(1)}, u32[]{:S(2)}, u32[]{:S(2)}) collective-permute-start(bf16[4,4,48,384]{3,2,1,0:T(8,128)(2,1)} %get-tuple-element.96), channel_id=1, source_target_pairs={{0,8},{8,0},{1,9},{9,1},{2,10},{10,2},{3,11},{11,3},{4,12},{12,4},... | collective-permute-start | bytes 1769480 | tf_op jit(solution)/shard_map/ppermute | solution.py:789
  131.1 5.1 %collective-permute-start.34 = (bf16[4,16,384]{2,1,0:T(8,128)(2,1)S(1)}, bf16[4,16,384]{2,1,0:T(8,128)(2,1)S(1)}, u32[]{:S(2)}, u32[]{:S(2)}) collective-permute-start(bf16[4,16,384]{2,1,0:T(8,128)(2,1)S(1)} %get-tuple-element.120), channel_id=1, source_target_pairs={{0,17},{1,16},{16,1},{17,0},{2,19},{3,18},{18,3},{19,2},{4,21},{5,... | collective-permute-start | bytes 147464 | tf_op jit(solution)/shard_map/ppermute | solution.py:789
  133.1 4.3 %collective-permute-start.33 = (bf16[4,16,384]{2,1,0:T(8,128)(2,1)S(1)}, bf16[4,16,384]{2,1,0:T(8,128)(2,1)S(1)}, u32[]{:S(2)}, u32[]{:S(2)}) collective-permute-start(bf16[4,16,384]{2,1,0:T(8,128)(2,1)S(1)} %get-tuple-element.121), channel_id=1, source_target_pairs={{0,16},{1,17},{16,0},{17,1},{2,18},{3,19},{18,2},{19,3},{4,20},{5,... | collective-permute-start | bytes 147464 | tf_op jit(solution)/shard_map/ppermute | solution.py:789
  133.4 4.1 %collective-permute-start.32 = (bf16[4,16,384]{2,1,0:T(8,128)(2,1)S(1)}, bf16[4,16,384]{2,1,0:T(8,128)(2,1)S(1)}, u32[]{:S(2)}, u32[]{:S(2)}) collective-permute-start(bf16[4,16,384]{2,1,0:T(8,128)(2,1)S(1)} %get-tuple-element.119), channel_id=1, source_target_pairs={{0,1},{1,0},{16,17},{17,16},{2,3},{3,2},{18,19},{19,18},{4,5},{5,4... | collective-permute-start | bytes 147464 | tf_op jit(solution)/shard_map/ppermute | solution.py:789
  134.8 11.9 %collective-permute-start.20 = (bf16[2,4,48,384]{3,2,1,0:T(8,128)(2,1)S(1)}, bf16[2,4,48,384]{3,2,1,0:T(8,128)(2,1)S(1)}, u32[]{:S(2)}, u32[]{:S(2)}) collective-permute-start(bf16[2,4,48,384]{3,2,1,0:T(8,128)(2,1)S(1)} %get-tuple-element.108), channel_id=1, source_target_pairs={{0,16},{16,0},{1,17},{17,1},{2,18},{18,2},{3,19},{19,3},{4,20},{20... | collective-permute-start | bytes 884744 | tf_op jit(solution)/shard_map/ppermute | solution.py:789
  137.6 5.3 %collective-permute-start.37 = (bf16[16,384]{1,0:T(8,128)(2,1)S(1)}, bf16[16,384]{1,0:T(8,128)(2,1)S(1)}, u32[]{:S(2)}, u32[]{:S(2)}) collective-permute-start(bf16[16,384]{1,0:T(8,128)(2,1)S(1)} %get-tuple-element.123), channel_id=1, source_target_pairs={{0,6},{2,0},{4,2},{6,4},{1,7},{3,1},{5,3},{7,5},{8,14},{10,8},{12,... | collective-permute-start | bytes 36872 | tf_op jit(solution)/shard_map/ppermute | solution.py:789
  139.8 4.6 %collective-permute-start.36 = (bf16[16,384]{1,0:T(8,128)(2,1)S(1)}, bf16[16,384]{1,0:T(8,128)(2,1)S(1)}, u32[]{:S(2)}, u32[]{:S(2)}) collective-permute-start(bf16[16,384]{1,0:T(8,128)(2,1)S(1)} %get-tuple-element.124), channel_id=1, source_target_pairs={{0,4},{2,6},{4,0},{6,2},{1,5},{3,7},{5,1},{7,3},{8,12},{10,14},{12... | collective-permute-start | bytes 36872 | tf_op jit(solution)/shard_map/ppermute | solution.py:789
  140.5 5.5 %collective-permute-start.35 = (bf16[16,384]{1,0:T(8,128)(2,1)S(1)}, bf16[16,384]{1,0:T(8,128)(2,1)S(1)}, u32[]{:S(2)}, u32[]{:S(2)}) collective-permute-start(bf16[16,384]{1,0:T(8,128)(2,1)S(1)} %get-tuple-element.122), channel_id=1, source_target_pairs={{0,2},{2,4},{4,6},{6,0},{1,3},{3,5},{5,7},{7,1},{8,10},{10,12},{12... | collective-permute-start | bytes 36872 | tf_op jit(solution)/shard_map/ppermute | solution.py:789
  141.6 8.9 %collective-permute-start.26 = (bf16[2,4,48,384]{3,2,1,0:T(8,128)(2,1)S(1)}, bf16[2,4,48,384]{3,2,1,0:T(8,128)(2,1)S(1)}, u32[]{:S(2)}, u32[]{:S(2)}) collective-permute-start(bf16[2,4,48,384]{3,2,1,0:T(8,128)(2,1)S(1)} %get-tuple-element.100), channel_id=1, source_target_pairs={{0,1},{1,0},{2,3},{3,2},{4,5},{5,4},{6,7},{7,6},{8,9},{9,8},{10,11... | collective-permute-start | bytes 884744 | tf_op jit(solution)/shard_map/ppermute | solution.py:789
  146.8 5.3 %collective-permute-start.21 = (bf16[4,48,384]{2,1,0:T(8,128)(2,1)S(1)}, bf16[4,48,384]{2,1,0:T(8,128)(2,1)S(1)}, u32[]{:S(2)}, u32[]{:S(2)}) collective-permute-start(bf16[4,48,384]{2,1,0:T(8,128)(2,1)S(1)} %get-tuple-element.112), channel_id=1, source_target_pairs={{0,1},{1,0},{2,3},{3,2},{4,5},{5,4},{6,7},{7,6},{8,9},{9,8},{10,11... | collective-permute-start | bytes 442376 | tf_op jit(solution)/shard_map/ppermute | solution.py:789
  150.6 5.9 %collective-permute-start.27 = (bf16[4,48,384]{2,1,0:T(8,128)(2,1)S(1)}, bf16[4,48,384]{2,1,0:T(8,128)(2,1)S(1)}, u32[]{:S(2)}, u32[]{:S(2)}) collective-permute-start(bf16[4,48,384]{2,1,0:T(8,128)(2,1)S(1)} %get-tuple-element.110), channel_id=1, source_target_pairs={{0,16},{16,0},{1,17},{17,1},{2,18},{18,2},{3,19},{19,3},{4,20},{20... | collective-permute-start | bytes 442376 | tf_op jit(solution)/shard_map/ppermute | solution.py:789
  152.1 8.6 %collective-permute-start.24 = (bf16[48,384]{1,0:T(8,128)(2,1)S(1)}, bf16[48,384]{1,0:T(8,128)(2,1)S(1)}, u32[]{:S(2)}, u32[]{:S(2)}) collective-permute-start(bf16[48,384]{1,0:T(8,128)(2,1)S(1)} %get-tuple-element.117), channel_id=1, source_target_pairs={{0,6},{2,0},{4,2},{6,4},{1,7},{3,1},{5,3},{7,5},{8,14},{10,8},{12,... | collective-permute-start | bytes 110600 | tf_op jit(solution)/shard_map/ppermute | solution.py:789
  155.7 5.1 %collective-permute-start.23 = (bf16[48,384]{1,0:T(8,128)(2,1)S(1)}, bf16[48,384]{1,0:T(8,128)(2,1)S(1)}, u32[]{:S(2)}, u32[]{:S(2)}) collective-permute-start(bf16[48,384]{1,0:T(8,128)(2,1)S(1)} %get-tuple-element.118), channel_id=1, source_target_pairs={{0,4},{2,6},{4,0},{6,2},{1,5},{3,7},{5,1},{7,3},{8,12},{10,14},{12... | collective-permute-start | bytes 110600 | tf_op jit(solution)/shard_map/ppermute | solution.py:789
  156.2 5.8 %collective-permute-start.22 = (bf16[48,384]{1,0:T(8,128)(2,1)S(1)}, bf16[48,384]{1,0:T(8,128)(2,1)S(1)}, u32[]{:S(2)}, u32[]{:S(2)}) collective-permute-start(bf16[48,384]{1,0:T(8,128)(2,1)S(1)} %get-tuple-element.116), channel_id=1, source_target_pairs={{0,2},{2,4},{4,6},{6,0},{1,3},{3,5},{5,7},{7,1},{8,10},{10,12},{12... | collective-permute-start | bytes 110600 | tf_op jit(solution)/shard_map/ppermute | solution.py:789
  156.5 6.2 %collective-permute-start.30 = (bf16[48,384]{1,0:T(8,128)(2,1)S(1)}, bf16[48,384]{1,0:T(8,128)(2,1)S(1)}, u32[]{:S(2)}, u32[]{:S(2)}) collective-permute-start(bf16[48,384]{1,0:T(8,128)(2,1)S(1)} %get-tuple-element.114), channel_id=1, source_target_pairs={{0,6},{2,0},{4,2},{6,4},{1,7},{3,1},{5,3},{7,5},{8,14},{10,8},{12,... | collective-permute-start | bytes 110600 | tf_op jit(solution)/shard_map/ppermute | solution.py:789
  160.1 4.9 %collective-permute-start.29 = (bf16[48,384]{1,0:T(8,128)(2,1)S(1)}, bf16[48,384]{1,0:T(8,128)(2,1)S(1)}, u32[]{:S(2)}, u32[]{:S(2)}) collective-permute-start(bf16[48,384]{1,0:T(8,128)(2,1)S(1)} %get-tuple-element.115), channel_id=1, source_target_pairs={{0,4},{2,6},{4,0},{6,2},{1,5},{3,7},{5,1},{7,3},{8,12},{10,14},{12... | collective-permute-start | bytes 110600 | tf_op jit(solution)/shard_map/ppermute | solution.py:789
  160.7 5.8 %collective-permute-start.28 = (bf16[48,384]{1,0:T(8,128)(2,1)S(1)}, bf16[48,384]{1,0:T(8,128)(2,1)S(1)}, u32[]{:S(2)}, u32[]{:S(2)}) collective-permute-start(bf16[48,384]{1,0:T(8,128)(2,1)S(1)} %get-tuple-element.113), channel_id=1, source_target_pairs={{0,2},{2,4},{4,6},{6,0},{1,3},{3,5},{5,7},{7,1},{8,10},{10,12},{12... | collective-permute-start | bytes 110600 | tf_op jit(solution)/shard_map/ppermute | solution.py:789
  (7 other events, 4.8 us)

commit v3 on v2

--- a/solution.py
+++ b/solution.py
@@ -24,7 +24,7 @@
 LANES = 128
 ROW_UNIT = 16
 DEPTH_ROWS = 4
-VMEM_BYTES = 56 * 1024 * 1024
+MIB = 1024 * 1024
 PART = 32
 WIDTH = 256
 GAIN, SHIFT, SCALE, REDUCE_BIAS, DEPTH_BIAS, EXPAND_BIAS, SLIDE_BIAS = range(7)
@@ -35,7 +35,7 @@
 
 
 def whole(shape):
-    return pl.BlockSpec(shape, lambda *_: (0,) * len(shape))
+    return pl.BlockSpec(shape, lambda *_: (0,) * len(shape), pipeline_mode=pl.Buffered(1))
 
 
 def gelu_and_slope(values):
@@ -191,7 +191,7 @@
             pltpu.SMEM((slides * places,), jnp.int32),
             pltpu.SemaphoreType.DMA((slides * places,)),
         ],
-        compiler_params=pltpu.CompilerParams(vmem_limit_bytes=16 * 1024 * 1024),
+        compiler_params=pltpu.CompilerParams(vmem_limit_bytes=8 * MIB),
         name="pack_tiles",
     )(routing, tile_maps)
     return outs[:-1], outs[-1]
@@ -373,7 +373,7 @@
             ],
         ),
         input_output_aliases={first + index: index for index in range(len(before))},
-        compiler_params=pltpu.CompilerParams(vmem_limit_bytes=VMEM_BYTES),
+        compiler_params=pltpu.CompilerParams(vmem_limit_bytes=20 * MIB),
         cost_estimate=cost(6.0 * min(items, 2)),
         name="forward_block_" + str(kind),
     )(table, *tiles, *consts, *before)
@@ -495,7 +495,7 @@
             pltpu.VMEM((length, embed), jnp.bfloat16),
             pltpu.VMEM((sum(piece.shape[0] for piece in pieces), embed), jnp.bfloat16),
         ],
-        compiler_params=pltpu.CompilerParams(vmem_limit_bytes=VMEM_BYTES),
+        compiler_params=pltpu.CompilerParams(vmem_limit_bytes=16 * MIB),
         cost_estimate=cost(6.0),
         name="slide_grads",
     )(table, *pieces, pick, codes, weight, cot, taps, matrix, vectors)
@@ -544,78 +544,28 @@
     return block.astype(jnp.bfloat16)
 
 
-def reduce_kernel(
+def weights_kernel(
     plan,
     table_ref,
     grad_ref,
     hidden_ref,
     head_slope_ref,
-    vectors_ref,
-    head_ref,
-    eye_ref,
-    grad_mlp_ref,
-    keep_ref,
-    send_ref,
-    hidden_all,
-    grad_mlp_all,
-    grad_head,
-    staged,
-    sems,
-):
-    step = pl.program_id(0)
-    filled = table_ref[FILLED + step]
-    cells, channels = grad_mlp_ref.shape[1:]
-    rows_all = pl.ds(pl.multiple_of(step * cells, cells), cells)
-
-    @pl.when(filled == 0)
-    def _empty():
-        hidden_all[rows_all, :] = jnp.zeros((cells, hidden_all.shape[1]), jnp.bfloat16)
-        grad_mlp_all[:, rows_all] = jnp.zeros((channels, cells), jnp.bfloat16)
-        grad_mlp_ref[...] = jnp.zeros(grad_mlp_ref.shape, jnp.bfloat16)
-
-    @pl.when(filled != 0)
-    def _work():
-        for start in range(0, cells, PART):
-            rows = slice(start, start + PART)
-            grad_head[rows, :] = (
-                (grad_ref[0] * (1.0 / cells)) * head_slope_ref[0, rows, :].astype(jnp.float32)
-            ).astype(jnp.bfloat16)
-        scale = vectors_ref[SCALE : SCALE + 1, 0:channels]
-        grad_mlp = (scale * mix_cols(grad_head[...], head_ref[...])).astype(jnp.bfloat16)
-        grad_mlp_ref[0] = grad_mlp
-        grad_mlp_all[:, rows_all] = mix_cols(eye_ref[...], grad_mlp).astype(jnp.bfloat16)
-        hidden_all[rows_all, :] = hidden_ref[0]
-
-    @pl.when(step == pl.num_programs(0) - 1)
-    def _finish():
-        spots = dict(plan.spots())
-        per_block = channels // plan.reduce_rows
-        for index in range(plan.pieces):
-            cols = slice(index * channels, (index + 1) * channels)
-            total = mix(grad_mlp_all[...], hidden_all[:, cols]).astype(jnp.bfloat16)
-            turned = mix_cols(eye_ref[...], total)
-            for part in range(per_block):
-                block = turned[part * plan.reduce_rows : (part + 1) * plan.reduce_rows]
-                staged[spots[index * per_block + part]] = padded_block(block, plan.block_rows)
-        send_out(staged, sems, (keep_ref, send_ref))
-
-
-def expand_kernel(
-    plan,
-    table_ref,
-    grad_mlp_ref,
     slope_ref,
     unit_ref,
     inv_ref,
     vectors_ref,
+    head_ref,
     expand_ref,
     reduce_ref,
     eye_ref,
     depth_back_ref,
     keep_ref,
     send_ref,
+    hidden_all,
+    grad_mlp_all,
     grad_pre_all,
     normed_all,
+    grad_head,
     grad_norm,
     staged,
     sems,
@@ -632,14 +582,26 @@
 
     @pl.when(filled == 0)
     def _empty():
-        grad_pre_all[rows_all, :] = jnp.zeros((cells, grad_pre_all.shape[1]), jnp.bfloat16)
-        normed_all[:, rows_all] = jnp.zeros((channels, cells), jnp.bfloat16)
+        for ref in (hidden_all, grad_pre_all):
+            ref[rows_all, :] = jnp.zeros((cells, ref.shape[1]), jnp.bfloat16)
+        for ref in (grad_mlp_all, normed_all):
+            ref[:, rows_all] = jnp.zeros((channels, cells), jnp.bfloat16)
 
     @pl.when(filled != 0)
     def _work():
+        for start in range(0, cells, PART):
+            rows = slice(start, start + PART)
+            grad_head[rows, :] = (
+                (grad_ref[0] * (1.0 / cells)) * head_slope_ref[0, rows, :].astype(jnp.float32)
+            ).astype(jnp.bfloat16)
+        grad_mlp = (vector(SCALE, every) * mix_cols(grad_head[...], head_ref[...])).astype(
+            jnp.bfloat16
+        )
+        grad_mlp_all[:, rows_all] = mix_cols(eye_ref[...], grad_mlp).astype(jnp.bfloat16)
+        hidden_all[rows_all, :] = hidden_ref[0]
         for begin in range(0, expand_ref.shape[1], WIDTH):
             cols = slice(begin, begin + WIDTH)
-            grad_hidden = mix_cols(grad_mlp_ref[0], reduce_ref[cols, :])
+            grad_hidden = mix_cols(grad_mlp, reduce_ref[cols, :])
             grad_pre_all[rows_all, cols] = (
                 grad_hidden * slope_ref[0, :, cols].astype(jnp.float32)
             ).astype(jnp.bfloat16)
@@ -662,6 +624,16 @@
     @pl.when(step == pl.num_programs(0) - 1)
     def _finish():
         spots = dict(plan.spots())
+        per_block = channels // plan.reduce_rows
+        tall = plan.block_rows
+        for index in range(plan.pieces):
+            cols = slice(index * channels, (index + 1) * channels)
+            total = mix(grad_mlp_all[...], hidden_all[:, cols]).astype(jnp.bfloat16)
+            turned = mix_cols(eye_ref[...], total)
+            for part in range(per_block):
+                block = turned[part * plan.reduce_rows : (part + 1) * plan.reduce_rows]
+                core, cross, z = spots[index * per_block + part]
+                staged[core, 0, cross, z] = padded_block(block, tall)
         totals = []
         for quarter in range(plan.pieces):
             cols = slice(quarter * channels, (quarter + 1) * channels)
@@ -670,7 +642,8 @@
         for device in range(plan.devices):
             rows = slice(device * size, (device + 1) * size)
             block = jnp.concatenate([total[rows] for total in totals], axis=0)
-            staged[spots[device]] = padded_block(block, plan.block_rows)
+            core, cross, z = spots[device]
+            staged[core, 1, cross, z] = padded_block(block, tall)
         send_out(staged, sems, (keep_ref, send_ref))
 
 
@@ -679,13 +652,10 @@
     table_ref,
     source_ref,
     depth_back,
-    keep_ref,
-    send_ref,
+    out_ref,
     padded,
     tap_sums,
     tap_rows,
-    staged,
-    sems,
 ):
     step = pl.program_id(0)
     filled = table_ref[FILLED + step]
@@ -742,34 +712,75 @@
             lanes = slice(band * LANES, (band + 1) * LANES)
             tap_rows[0 : KS * KS, lanes] = jnp.sum(tap_sums[band], axis=1)
             tap_rows[KS * KS :, lanes] = jnp.zeros((tap_rows.shape[0] - KS * KS, LANES), jnp.float32)
-        for device, spot in plan.spots():
+        for device in range(plan.devices):
             start = device * plan.share // channels
-            staged[spot] = padded_block(tap_rows[start : start + DEPTH_ROWS, :], ROW_UNIT)
-        send_out(staged, sems, (keep_ref, send_ref))
-
-
-def backward_call(plan, kernel, name, micros, rows, table, streams, consts, outs, scratch):
-    def per_slot(shape):
-        return pl.BlockSpec((1,) + tuple(shape), lambda i, table: (i,) + (0,) * len(shape))
-
-    blocks = jax.ShapeDtypeStruct(plan.blocks(rows), jnp.bfloat16)
+            out_ref[device] = tap_rows[start : start + DEPTH_ROWS, :].astype(jnp.bfloat16)
+
+
+def per_slot(array):
+    shape = array.shape[1:]
+    return pl.BlockSpec((1,) + shape, lambda i, table: (i,) + (0,) * len(shape))
+
+
+def weight_grads(plan, table, embed_grad, saved, vectors, head, expand, reduce):
+    unit, inv, hidden, slope, head_slope = saved
+    cells, channels = unit.shape[1:]
+    hid, bands = expand.shape[1], channels // LANES
+    eye = jnp.asarray(np.eye(channels, dtype=np.float32), jnp.bfloat16)
+    streams = (embed_grad, hidden, head_slope, slope, unit, inv)
+    consts = (vectors, head, expand, reduce, eye)
+    back = jax.ShapeDtypeStruct((PROC, bands, cells, LANES), jnp.float32)
+    blocks = jax.ShapeDtypeStruct(
+        (2, plan.cross, plan.g1, plan.block_rows, channels), jnp.bfloat16
+    )
     return pl.pallas_call(
-        functools.partial(kernel, plan),
-        out_shape=tuple(jax.ShapeDtypeStruct((PROC,) + shape, kind) for shape, kind in outs)
-        + (blocks, blocks),
+        functools.partial(weights_kernel, plan),
+        out_shape=(back, blocks, blocks),
         grid_spec=pltpu.PrefetchScalarGridSpec(
             num_scalar_prefetch=1,
             grid=(PROC,),
-            in_specs=[per_slot(stream.shape[1:]) for stream in streams]
+            in_specs=[per_slot(stream) for stream in streams]
             + [whole(const.shape) for const in consts],
-            out_specs=[per_slot(shape) for shape, _ in outs] + [HBM, HBM],
-            scratch_shapes=scratch
-            + [pltpu.VMEM((2,) + blocks.shape, jnp.bfloat16), pltpu.SemaphoreType.DMA((2,))],
+            out_specs=[per_slot(back), HBM, HBM],
+            scratch_shapes=[
+                pltpu.VMEM((PROC * cells, hid), jnp.bfloat16),
+                pltpu.VMEM((channels, PROC * cells), jnp.bfloat16),
+                pltpu.VMEM((PROC * cells, hid), jnp.bfloat16),
+                pltpu.VMEM((channels, PROC * cells), jnp.bfloat16),
+                pltpu.VMEM((cells, head.shape[1]), jnp.bfloat16),
+                pltpu.VMEM((cells, channels), jnp.float32),
+                pltpu.VMEM((2,) + blocks.shape, jnp.bfloat16),
+                pltpu.SemaphoreType.DMA((2,)),
+            ],
         ),
-        compiler_params=pltpu.CompilerParams(vmem_limit_bytes=VMEM_BYTES),
-        cost_estimate=cost(micros),
-        name=name,
+        compiler_params=pltpu.CompilerParams(vmem_limit_bytes=32 * MIB),
+        cost_estimate=cost(16.0),
+        name="weight_grads",
     )(table, *streams, *consts)
+
+
+def tap_grads(plan, table, source, depth_back):
+    side, channels = source.shape[1], source.shape[3]
+    bands = channels // LANES
+    out = (plan.devices, DEPTH_ROWS, channels)
+    return pl.pallas_call(
+        functools.partial(taps_kernel, plan),
+        out_shape=jax.ShapeDtypeStruct(out, jnp.bfloat16),
+        grid_spec=pltpu.PrefetchScalarGridSpec(
+            num_scalar_prefetch=1,
+            grid=(PROC,),
+            in_specs=[per_slot(source), per_slot(depth_back)],
+            out_specs=pl.BlockSpec(out, lambda i, table: (0, 0, 0)),
+            scratch_shapes=[
+                pltpu.VMEM((bands, side, side + ROW_UNIT, LANES), jnp.float32),
+                pltpu.VMEM((bands, KS * KS, 8, LANES), jnp.float32),
+                pltpu.VMEM((KS * KS + 7, channels), jnp.float32),
+            ],
+        ),
+        compiler_params=pltpu.CompilerParams(vmem_limit_bytes=10 * MIB),
+        cost_estimate=cost(8.0),
+        name="tap_grads",
+    )(table, source, depth_back)
 
 
 def shifted(values, names, sizes, shift):
@@ -796,21 +807,8 @@
     return steps
 
 
-def gather_all(plan, values):
-    pair = jnp.concatenate([values, shifted(values, ("core",), (2,), (1,))], axis=0)
-    sizes = (plan.ys, plan.g2)
-    column = jnp.concatenate(
-        [pair] + [shifted(pair, ("y", "g2"), sizes, step) for step in shifts(sizes)[1:]], axis=0
-    )
-    return [column] + [shifted(column, ("g1",), (plan.g1,), (step,)) for step in range(1, plan.g1)]
-
-
-def distance(plan, slide, member):
-    my_core, my_y = lax.axis_index("core"), lax.axis_index("y")
-    my_z, my_x = lax.axis_index("g1"), lax.axis_index("g2")
-    y, core, z, x = slide // 2, slide % 2, member // plan.g2, member % plan.g2
-    cross = (my_y - y) % plan.ys * plan.g2 + (my_x - x) % plan.g2
-    return ((my_z - z) % plan.g1 * plan.cross + cross) * 2 + (core ^ my_core)
+def exchange(values, names):
+    return lax.all_to_all(values, names, split_axis=0, concat_axis=0, tiled=True)
 
 
 def add_all(parts, kind=jnp.bfloat16):
@@ -880,10 +878,22 @@
     arrived = []
     for rank in range(places):
         buffers = packed[1 + rank * (slides - 2) : 1 + (rank + 1) * (slides - 2)]
-        if arrived:
-            held = lax.optimization_barrier((tuple(buffers), tuple(arrived[-1])))
-            buffers, arrived[-1] = held[0], list(held[1])
+        if rank:
+            buffers, from_core = lax.optimization_barrier((buffers, from_core))
         arrived.append(from_other(buffers))
+    held = lax.optimization_barrier((table, routing, cotangent, positions, counts))
+    _, routing, cotangent, positions, counts = held
+    extras = jnp.concatenate(
+        [
+            cotangent[0],
+            routing.reshape(-1).astype(jnp.float32),
+            jnp.zeros((960 - E - slides * slots,), jnp.float32),
+            positions.reshape(-1).astype(jnp.float32),
+            jnp.zeros((1023 - 960 - 2 * slots,), jnp.float32),
+            counts.astype(jnp.float32),
+        ]
+    )
+    extras = exchange(jnp.broadcast_to(extras, (devices, 1024)), ALL)
 
     vectors = jnp.stack(
         [
@@ -908,26 +918,11 @@
     section, tile_embed, unit, inv, hidden, slope, head_slope, source = saved
     filled = table[FILLED : FILLED + PROC] != 0
     tile_embed = jnp.where(filled[:, None], tile_embed[:PROC, 0], 0.0).astype(jnp.bfloat16)
-    embeds = gather_all(plan, tile_embed)
+    tile_embed = jnp.broadcast_to(tile_embed, (devices, PROC, E))
+    tile_embed, extras = lax.optimization_barrier((tile_embed, extras))
+    embeds = exchange(tile_embed, ALL).reshape(devices * PROC, E)
     tile_out = jnp.where(filled[:, None, None, None], section[:PROC], jnp.zeros((), jnp.bfloat16))
 
-    packed_last, routing, cotangent, positions, counts = lax.optimization_barrier(
-        (table, routing, cotangent, positions, counts)
-    )
-    extras = jnp.concatenate(
-        [
-            cotangent[0],
-            routing.reshape(-1).astype(jnp.float32),
-            jnp.zeros((960 - E - slides * slots,), jnp.float32),
-            positions.reshape(-1).astype(jnp.float32),
-            jnp.zeros((1023 - 960 - 2 * slots,), jnp.float32),
-            counts.astype(jnp.float32),
-        ]
-    )
-    extras = jnp.concatenate(gather_all(plan, extras[None, :]), axis=0)
-    ids = jnp.arange(devices, dtype=jnp.int32)
-    spots = distance(plan, ids // members, ids % members)
-    extras = jnp.take(extras, spots, axis=0)
     route_all = extras[:, E : E + slides * slots].astype(jnp.int32)
     route_all = route_all.reshape(slides, members, slides, slots)[0]
     pos_all = extras[:, 960 : 960 + 2 * slots].reshape(slides, members, 2, slots)
@@ -937,9 +932,7 @@
     codes = position_code(pos_all)
     member_ids = jnp.arange(members, dtype=jnp.int32)[:, None, None]
     target = jnp.where(
-        route_all >= 0,
-        distance(plan, route_all // PROC, member_ids) * PROC + route_all % PROC,
-        -1,
+        route_all >= 0, (route_all // PROC * members + member_ids) * PROC + route_all % PROC, -1
     )
     target = target.transpose(1, 2, 0).reshape(slides, length, 1)
     pick = (target == jnp.arange(devices * PROC, dtype=jnp.int32)).astype(jnp.bfloat16)
@@ -947,110 +940,55 @@
     weight = jnp.where(steps < counts_all[:, None, None], 1.0 / counts_all[:, None, None], 0.0)
 
     feature, embed_grad = slide_grads(
-        table, embeds, pick, codes, weight, cot_all, slide_taps, slide_weight, vectors
-    )
-
-    side, hid = tile_maps.shape[1], expand_weight.shape[1]
-    cells, bands = side * side, channels // LANES
-    eye = jnp.asarray(np.eye(channels, dtype=np.float32), jnp.bfloat16)
-    grad_mlp, reduce_kept, reduce_sent = backward_call(
+        table, [embeds], pick, codes, weight, cot_all, slide_taps, slide_weight, vectors
+    )
+    depth_back, kept, sent = weight_grads(
         plan,
-        reduce_kernel,
-        "reduce_grads",
-        5.0,
-        plan.block_rows,
         table,
-        (embed_grad, hidden, head_slope),
-        (vectors, head_weight, eye),
-        (((cells, channels), jnp.bfloat16),),
-        [
-            pltpu.VMEM((PROC * cells, hid), jnp.bfloat16),
-            pltpu.VMEM((channels, PROC * cells), jnp.bfloat16),
-            pltpu.VMEM((cells, E), jnp.bfloat16),
-        ],
-    )
-    reduce_came = other_core(reduce_sent)
-    depth_back, expand_kept, expand_sent = backward_call(
-        plan,
-        expand_kernel,
-        "expand_grads",
-        8.0,
-        plan.block_rows,
-        table,
-        (grad_mlp, slope, unit, inv),
-        (vectors, expand_weight, reduce_weight, eye),
-        (((bands, cells, LANES), jnp.float32),),
-        [
-            pltpu.VMEM((PROC * cells, hid), jnp.bfloat16),
-            pltpu.VMEM((channels, PROC * cells), jnp.bfloat16),
-            pltpu.VMEM((cells, channels), jnp.float32),
-        ],
-    )
-    expand_came = other_core(expand_sent)
-
-    def column(kept, came, wanted):
-        grid = [
-            part.reshape((plan.ys, plan.g2) + part.shape[1:]) for part in (kept, came)
+        embed_grad,
+        (unit, inv, hidden, slope, head_slope),
+        vectors,
+        head_weight,
+        expand_weight,
+        reduce_weight,
+    )
+
+    came = other_core(sent)
+    grid = [
+        part.reshape((2, plan.ys, plan.g2) + part.shape[2:]) for part in (kept, came)
+    ]
+
+    def sums(parts, wanted, count):
+        return add_all([wanted(part)(0) for part in parts]), [
+            add_all([wanted(part)(step) for part in parts]) for step in range(1, count)
         ]
-        return add_all([wanted(part) for part in grid])
-
-    reduce_out = [
-        column(reduce_kept, reduce_came, lambda part: part[:, step]) for step in range(1, plan.g2)
-    ]
-    reduce_stay = column(reduce_kept, reduce_came, lambda part: part[:, 0])
-    depth_back, reduce_out = lax.optimization_barrier((depth_back, reduce_out))
+
+    reduce_stay, reduce_out = sums(grid, lambda part: lambda step: part[0][:, step], plan.g2)
+    expand_stay, expand_out = sums(grid, lambda part: lambda step: part[1][step], plan.ys)
+    held = lax.optimization_barrier((depth_back, reduce_out, expand_out))
+    depth_back, reduce_out, expand_out = held
     reduce_parts = sum_axis(reduce_stay, reduce_out, "g2", plan.g2)
-    depth_kept, depth_sent = backward_call(
-        plan,
-        taps_kernel,
-        "tap_grads",
-        8.0,
-        ROW_UNIT,
-        table,
-        (source, depth_back),
-        (),
-        (),
-        [
-            pltpu.VMEM((bands, side, side + ROW_UNIT, LANES), jnp.float32),
-            pltpu.VMEM((bands, KS * KS, 8, LANES), jnp.float32),
-            pltpu.VMEM((KS * KS + 7, channels), jnp.float32),
-        ],
-    )
-    depth_came = other_core(depth_sent)
-    expand_out = [
-        column(expand_kept, expand_came, lambda part: part[step]) for step in range(1, plan.ys)
-    ]
-    expand_stay = column(expand_kept, expand_came, lambda part: part[0])
     expand_parts = sum_axis(expand_stay, expand_out, "y", plan.ys)
-
-    def finish(parts, name, size):
-        out = [add_all([part[step] for part in parts]) for step in range(1, size)]
-        stay = add_all([part[0] for part in parts])
-        parts = sum_axis(stay, out, name, size)
-        out = [add_all([part[step] for part in parts]) for step in range(1, plan.g1)]
-        stay = add_all([part[0] for part in parts])
-        return add_all(sum_axis(stay, out, "g1", plan.g1), jnp.float32)
-
-    reduce_total = finish(reduce_parts, "y", plan.ys)
-    expand_total = finish(expand_parts, "g2", plan.g2)
-    sizes = (plan.ys, plan.g2)
-    depth_all = add_all([depth_kept, depth_came])
-    depth_parts = [depth_all[0]] + [
-        shifted(depth_all[index], ("y", "g2"), sizes, step)
-        for index, step in enumerate(shifts(sizes))
-        if index
-    ]
-    depth_all = add_all(depth_parts)
-    depth_total = add_all(
-        sum_axis(depth_all[0], [depth_all[step] for step in range(1, plan.g1)], "g1", plan.g1),
-        jnp.float32,
-    )
-
-    expand_share = expand_total[: plan.pieces * plan.expand_rows]
+    taps = exchange(tap_grads(plan, table, source, depth_back), ALL)
+
+    def along(part):
+        return lambda step: part[step]
+
+    reduce_stay, reduce_out = sums(reduce_parts, along, plan.ys)
+    expand_stay, expand_out = sums(expand_parts, along, plan.g2)
+    reduce_parts = sum_axis(reduce_stay, reduce_out, "y", plan.ys)
+    expand_parts = sum_axis(expand_stay, expand_out, "g2", plan.g2)
+    both = jnp.concatenate([add_all(reduce_parts), add_all(expand_parts)], axis=1)
+    total = add_all(
+        sum_axis(both[0], [both[step] for step in range(1, plan.g1)], "g1", plan.g1), jnp.float32
+    )
+    reduce_share = total[: plan.reduce_rows]
+    expand_share = total[plan.block_rows : plan.block_rows + plan.pieces * plan.expand_rows]
     expand_share = expand_share.reshape(plan.pieces, plan.expand_rows, channels).transpose(1, 0, 2)
-    reduce_share = reduce_total[: plan.reduce_rows]
     depth_share = lax.dynamic_slice(
-        depth_total[:DEPTH_ROWS].reshape(-1), (my_device * plan.share % channels,), (plan.share,)
+        jnp.sum(taps.astype(jnp.float32), axis=0).reshape(-1),
+        (my_device * plan.share % channels,),
+        (plan.share,),
     )
     return (tile_out, feature, expand_share.reshape(-1), reduce_share.reshape(-1), depth_share)
 

time: 168 us -> 134 us (0.80)
  Pallas kernels: 73.1 us -> 50.7 us
  starting transfers between devices: 42.9 us -> 27.3 us
  local copies, waits for them, and re-layouts: 15.7 us -> 27.7 us
  waiting for transfers between devices: 24.3 us -> 18.7 us
  other arithmetic: 9.36 us -> 7.26 us
    ppermute x34 -> x9, starting transfers between devices: 37.5 us -> 10.2 us  [shifted(): return lax.ppermute(values, names, pairs)]
    ppermute x34 -> x9, waiting for transfers between devices: 24.3 us -> 11.3 us  [shifted(): return lax.ppermute(values, names, pairs)]
    all_to_all x0 -> x3, starting transfers between devices: none -> 12.2 us  [exchange(): lax.all_to_all(values, names, split_axis=0, concat_axis=0, tiled=True)]
    pallas_call x3 -> x2, Pallas kernels: 30.5 us -> 19 us  [the longest x1 12.2 us: weight_grads(): pl.pallas_call(functools.partial(weights_kernel, plan), out_shape=(back,...]
    unnamed x32 -> x59, local copies, waits for them, and re-layouts: 4.81 us -> 15.8 us
    pallas_call x3, Pallas kernels: 33.5 us -> 23.2 us  [forward_block(): pl.pallas_call(functools.partial(forward_kernel, kind, len(tiles), len(be...]
    all_to_all x0 -> x3, waiting for transfers between devices: none -> 7.35 us  [exchange(): lax.all_to_all(values, names, split_axis=0, concat_axis=0, tiled=True)]
  transfers between devices with their start and end apart: 38 -> 16, of which waited for: 19 -> 7; matrix products, arithmetic and copies ran while one was open for 11% -> 10% of each run, Pallas kernels for 21% -> 18%
where the time goes in v3:
time: 134 us; the launch traced here: 133 us
  Pallas kernels  50.7 us (38%)
  local copies, waits for them, and re-layouts  27.7 us (21%)
  starting transfers between devices  27.3 us (20%)
  waiting for transfers between devices  18.7 us (14%)
  other arithmetic  7.26 us (5%)
  between operations  1.83 us (1%)
    pallas_call x3, Pallas kernels, forward_block(): pl.pallas_call(functools.partial(forward_kernel, kind, len(tiles), len(be...  23.2 us
    unnamed x59, local copies, waits for them, and re-layouts  15.8 us
    all_to_all x3, starting transfers between devices, exchange(): lax.all_to_all(values, names, split_axis=0, concat_axis=0, tiled=True)  12.2 us
    pallas_call x1, Pallas kernels, weight_grads(): pl.pallas_call(functools.partial(weights_kernel, plan), out_shape=(back,...  12.2 us
    ppermute x9, waiting for transfers between devices, shifted(): return lax.ppermute(values, names, pairs)  11.3 us
    ppermute x9, starting transfers between devices, shifted(): return lax.ppermute(values, names, pairs)  10.2 us
    all_to_all x3, waiting for transfers between devices, exchange(): lax.all_to_all(values, names, split_axis=0, concat_axis=0, tiled=True)  7.35 us
    pallas_call x1, Pallas kernels, tap_grads(): pl.pallas_call(functools.partial(taps_kernel, plan), out_shape=jax.ShapeD...  6.8 us
  transfers between devices with their start and end apart: 16, of which 7 were waited for; matrix products, arithmetic and copies ran while one was open for 10% of the time, Pallas kernels for 18%

profile of v3, /device:TPU:0, one launch (start us, length us, event | category | flops | bytes accessed | tf_op | source)
XLA Modules:
  0.0 133.4 jit_solution(13879846298353948079)
XLA Ops:
  0.6 1.4 %copy-done = bf16[8,16,16,384]{3,2,1,0:T(8,128)(2,1)S(1)} copy-done((bf16[8,16,16,384]{3,2,1,0:T(8,128)(2,1)S(1)}, bf16[8,16,16,384]{3,2,1,0:T(8,128)(2,1)}, u32[]{:S(2)}) %copy-start) | copy-done | bytes 1572888
  2.7 3.1 %pack_tiles.1 = (bf16[2,16,16,384]{3,2,1,0:T(8,128)(2,1)S(1)}, bf16[1,16,16,384]{3,2,1,0:T(8,128)(2,1)}, bf16[1,16,16,384]{3,2,1,0:T(8,128)(2,1)}, bf16[1,16,16,...) custom-call(s32[4,1,8]{2,1,0:T(1,128)S(1)} %copy-done.2, bf16[8,16,16,384]{3,2,1,0:T(8,128)(2,1)S(1)} %copy-done), custom_call_target="tpu_custom_call" | custom-call | tf_op jit(solution)/shard_map/pack_tiles/pallas_call | solution.py:181
  6.1 3.4 %collective-permute-start.3 = (bf16[1,16,16,384]{3,2,1,0:T(8,128)(2,1)}, bf16[1,16,16,384]{3,2,1,0:T(8,128)(2,1)}, u32[]{:S(2)}, u32[]{:S(2)}) collective-permute-start(bf16[1,16,16,384]{3,2,1,0:T(8,128)(2,1)} %get-tuple-element.58), channel_id=1, source_target_pairs={{0,16},{8,24},{16,0},{24,8},{1,17},{9,25},{17,1},{25,9},{2,18},{10... | collective-permute-start | bytes 589832 | tf_op jit(solution)/shard_map/ppermute | solution.py:874
  11.0 0.7 reduce
  11.8 0.7 broadcast_in_dim.96
  12.5 6.1 %all-to-all-start = ((f32[32,1,1024]{2,1,0:T(1,128)}), f32[32,1,1024]{2,1,0:T(1,128)S(1)}, u32[]{:S(2)}, u32[]{:S(2)}) async-start(f32[32,1,1024]{2,1,0:T(1,128)} %broadcast_in_dim.96), calls=%async_computation | async-start | bytes 262144 | tf_op jit(solution)/shard_map/all_to_all | solution.py:811
  18.6 0.7 pad.21
  19.3 0.7 pad.22
  21.4 0.7 pad.25
  22.1 0.7 stack.30
  22.8 0.7 pad.26
  23.6 2.7 %all-to-all-done = f32[32,1,1024]{2,1,0:T(1,128)S(1)} async-done(((f32[32,1,1024]{2,1,0:T(1,128)}), f32[32,1,1024]{2,1,0:T(1,128)S(1)}, u32[]{:S(2)}, u32[]{:S(2)}) %all-to-all-start) | async-done | bytes 131104 | tf_op jit(solution)/shard_map/all_to_all | solution.py:811
  26.4 0.7 copy-done.10
  27.1 1.1 collective-permute-start.1
  28.6 1.3 copy-done.4
  29.8 1.3 copy-done.6
  31.1 1.0 copy-done.11
  32.1 5.7 %forward_block_0.1 = (bf16[5,16,16,384]{3,2,1,0:T(8,128)(2,1)S(1)}, f32[5,1,768]{2,1,0:T(1,128)S(1)}, f32[5,256,384]{2,1,0:T(8,128)S(1)}, f32[5,256,128]{2,1,0:T...) custom-call(s32[51]{0:T(128)S(1)} %get-tuple-element.52.table_ref, ...), custom_call_target="tpu_custom_call" | custom-call | flops 12000000000 | bytes 1024 | tf_op jit(solution)/shard_map/forward_block_0/pallas_call | solution.py:359
  37.9 11.7 %forward_block_1.1 = (bf16[5,16,16,384]{3,2,1,0:T(8,128)(2,1)S(1)}, f32[5,1,768]{2,1,0:T(1,128)S(1)}, f32[5,256,384]{2,1,0:T(8,128)S(1)}, f32[5,256,128]{2,1,0:T...) custom-call(s32[51]{0:T(128)S(1)} %get-tuple-element.52.table_ref, ...), custom_call_target="tpu_custom_call", output_to_operand_aliasing={{0}: (8, {}), {1}: (9, {}), {2}: (10, {}), {3}: (11, {}), {... | custom-call | flops 12000000000 | bytes 1024 | tf_op jit(solution)/shard_map/forward_block_1/pallas_call | solution.py:359
  49.6 5.7 %forward_block_2.1 = (bf16[5,16,16,384]{3,2,1,0:T(8,128)(2,1)S(1)}, f32[5,1,768]{2,1,0:T(1,128)S(1)}, f32[5,256,384]{2,1,0:T(8,128)S(1)}, f32[5,256,128]{2,1,0:T...) custom-call(s32[51]{0:T(128)S(1)} %get-tuple-element.52.table_ref, ...), custom_call_target="tpu_custom_call", output_to_operand_aliasing={{0}: (8, {}), {1}: (9, {}), {2}: (10, {}), {3}: (11, {}), {... | custom-call | flops 12000000000 | bytes 1024 | tf_op jit(solution)/shard_map/forward_block_2/pallas_call | solution.py:359
  55.3 1.9 %copy-done.15 = bf16[5,256,1536]{2,1,0:T(8,128)(2,1)} copy-done((bf16[5,256,1536]{2,1,0:T(8,128)(2,1)}, bf16[5,256,1536]{2,1,0:T(8,128)(2,1)S(1)}, u32[]{:S(2)}) %copy-start.15) | copy-done | bytes 3932184
  57.2 1.9 %copy-done.17 = bf16[5,256,1536]{2,1,0:T(8,128)(2,1)} copy-done((bf16[5,256,1536]{2,1,0:T(8,128)(2,1)}, bf16[5,256,1536]{2,1,0:T(8,128)(2,1)S(1)}, u32[]{:S(2)}) %copy-start.17) | copy-done | bytes 3932184
  59.1 1.3 copy-done.19
  60.4 1.3 copy-done.21
  61.7 1.0 copy-done.25
  62.7 0.8 copy-done.27
  63.6 0.7 broadcast_in_dim.93
  64.7 3.5 %all-to-all-start.1 = ((bf16[32,4,768]{2,1,0:T(4,128)(2,1)}), bf16[32,4,768]{2,1,0:T(4,128)(2,1)}, u32[]{:S(2)}, u32[]{:S(2)}) async-start(bf16[32,4,768]{2,1,0:T(4,128)(2,1)} %broadcast_in_dim.93), calls=%async_computation.1 | async-start | bytes 393216 | tf_op jit(solution)/shard_map/all_to_all | solution.py:811
  69.2 2.7 %add_sine_fusion.refs_2_ = f32[4,64,768]{2,1,0:T(8,128)S(1)} fusion(f32[768]{0:T(1024)S(1)} %get-tuple-element.111, f32[768]{0:T(1024)S(1)} %get-tuple-element.110, f32[4,64]{1,0:T(4,128)S(1)} %broadcast_in_dim.100, f32[4,64]{1,0:T(4,128)S(1)} %broadcast_in_dim.98, pred[768]{0:T(1024)(128)(4,1)S(1)} %iota_compare_fusion.1), kind=kLoop, calls=%fused_computation | loop fusion | flops 589824 | bytes 795392 | tf_op jit(solution)/shard_map/sin | solution.py:839
  71.9 4.6 %all-to-all-done.1 = bf16[32,4,768]{2,1,0:T(4,128)(2,1)} async-done(((bf16[32,4,768]{2,1,0:T(4,128)(2,1)}), bf16[32,4,768]{2,1,0:T(4,128)(2,1)}, u32[]{:S(2)}, u32[]{:S(2)}) %all-to-all-start.1) | async-done | bytes 196640 | tf_op jit(solution)/shard_map/all_to_all | solution.py:811
  76.5 1.0 reshape.255.refs_0_
  77.6 5.5 %slide_grads.1 = (f32[1,768]{1,0:T(1,128)}, f32[4,1,768]{2,1,0:T(1,128)S(1)}) custom-call(s32[51]{0:T(128)S(1)} %get-tuple-element.52.table_ref, bf16[128,768]{1,0:T(8,128)(2,1)S(1)} %reshape.255.refs_0_, bf16[4,64,128]{2,1,0:T(8,128)(2,1)S(1)} %fusion.14.refs_1_, f32[4,64,768]{2,1,0:T(8,128)S(1)} %add_sine_fusion.refs_2_, ...), custom_call_target="tpu_custom_call" | custom-call | flops 6000000000 | bytes 1024 | tf_op jit(solution)/shard_map/slide_grads/pallas_call | solution.py:481
  83.1 12.2 %weight_grads.1 = (f32[4,3,256,128]{3,2,1,0:T(8,128)S(1)}, bf16[2,4,4,48,384]{4,3,2,1,0:T(8,128)(2,1)S(1)}, bf16[2,4,4,48,384]{4,3,2,1,0:T(8,128)(2,1)S(1)}) custom-call(s32[51]{0:T(128)S(1)} %get-tuple-element.52.table_ref, f32[4,1,768]{2,1,0:T(1,128)S(1)} %get-tuple-element.86.grad_ref, bf16[5,256,1536]{2,1,0:T(8,128)(2,1)S(1)} %copy-done.16, ...), custom_call_target="tpu_custom_call" | custom-call | flops 16000000000 | bytes 1024 | tf_op jit(solution)/shard_map/weight_grads/pallas_call | solution.py:736
  95.3 1.2 copy-done.23
  96.6 1.0 slice_select_fusion
  97.7 1.8 %collective-permute-done.5 = bf16[2,4,4,48,384]{4,3,2,1,0:T(8,128)(2,1)} collective-permute-done((bf16[2,4,4,48,384]{4,3,2,1,0:T(8,128)(2,1)S(1)}, bf16[2,4,4,48,384]{4,3,2,1,0:T(8,128)(2,1)}, u32[]{:S(2)}, u32[]{:S(2)}) %collective-permute-start.5) | collective-permute-done | bytes 1179680 | tf_op jit(solution)/shard_map/ppermute | solution.py:800
  99.5 1.1 slice.174
  100.8 1.3 %add_convert_fusion = (bf16[1,2,4,48,384]{4,3,2,1,0:T(8,128)(2,1)S(1)}, bf16[2,4,48,384]{3,2,1,0:T(8,128)(2,1)S(1)}) fusion(bf16[2,4,4,48,384]{4,3,2,1,0:T(8,128)(2,1)} %collective-permute-done.5, bf16[2,4,4,48,384]{4,3,2,1,0:T(8,128)(2,1)S(1)} %get-tuple-element.92), kind=kLoop, calls=%fused_computation.2 | loop fusion | flops 1179648 | bytes 1769472 | tf_op jit(solution)/shard_map/convert_element_type | solution.py:818
  102.1 1.8 %collective-permute-start.6 = (bf16[2,4,48,384]{3,2,1,0:T(8,128)(2,1)S(1)}, bf16[2,4,48,384]{3,2,1,0:T(8,128)(2,1)S(1)}, u32[]{:S(2)}, u32[]{:S(2)}) collective-permute-start(bf16[2,4,48,384]{3,2,1,0:T(8,128)(2,1)S(1)} %get-tuple-element.95), channel_id=1, source_target_pairs={{0,1},{1,0},{2,3},{3,2},{4,5},{5,4},{6,7},{7,6},{8,9},{9,8},{10,11... | collective-permute-start | bytes 884744 | tf_op jit(solution)/shard_map/ppermute | solution.py:800
  104.4 6.8 %tap_grads.1 = bf16[32,4,384]{2,1,0:T(4,128)(2,1)} custom-call(s32[51]{0:T(128)S(1)} %get-tuple-element.52.table_ref, bf16[5,16,16,384]{3,2,1,0:T(8,128)(2,1)S(1)} %copy-done.26, f32[4,3,256,128]{3,2,1,0:T(8,128)S(1)} %copy-done.24), custom_call_target="tpu_custom_call" | custom-call | flops 8000000000 | bytes 1024 | tf_op jit(solution)/shard_map/tap_grads/pallas_call | solution.py:766
  111.2 2.7 %all-to-all-start.2 = ((bf16[32,4,384]{2,1,0:T(4,128)(2,1)}), bf16[32,4,384]{2,1,0:T(4,128)(2,1)S(1)}, u32[]{:S(2)}, u32[]{:S(2)}) async-start(bf16[32,4,384]{2,1,0:T(4,128)(2,1)} %tap_grads.1), calls=%async_computation.2 | async-start | bytes 196608 | tf_op jit(solution)/shard_map/all_to_all | solution.py:811
  114.0 1.8 %collective-permute-start.7 = (bf16[4,48,384]{2,1,0:T(8,128)(2,1)S(1)}, bf16[4,48,384]{2,1,0:T(8,128)(2,1)S(1)}, u32[]{:S(2)}, u32[]{:S(2)}) collective-permute-start(bf16[4,48,384]{2,1,0:T(8,128)(2,1)S(1)} %fusion.9), channel_id=1, source_target_pairs={{0,16},{16,0},{1,17},{17,1},{2,18},{18,2},{3,19},{19,3},{4,20},{20... | collective-permute-start | bytes 442376 | tf_op jit(solution)/shard_map/ppermute | solution.py:800
  115.9 1.5 %collective-permute-start.9 = (bf16[4,48,384]{2,1,0:T(8,128)(2,1)S(1)}, bf16[4,48,384]{2,1,0:T(8,128)(2,1)S(1)}, u32[]{:S(2)}, u32[]{:S(2)}) collective-permute-start(bf16[4,48,384]{2,1,0:T(8,128)(2,1)S(1)} %fusion.11), channel_id=1, source_target_pairs={{0,1},{1,0},{2,3},{3,2},{4,5},{5,4},{6,7},{7,6},{8,9},{9,8},{10,11... | collective-permute-start | bytes 442376 | tf_op jit(solution)/shard_map/ppermute | solution.py:800
  117.4 3.6 %collective-permute-done.7 = bf16[4,48,384]{2,1,0:T(8,128)(2,1)S(1)} collective-permute-done((bf16[4,48,384]{2,1,0:T(8,128)(2,1)S(1)}, bf16[4,48,384]{2,1,0:T(8,128)(2,1)S(1)}, u32[]{:S(2)}, u32[]{:S(2)}) %collective-permute-start.7) | collective-permute-done | bytes 147488 | tf_op jit(solution)/shard_map/ppermute | solution.py:800
  121.1 1.1 collective-permute-done.9
  122.3 2.8 %collective-permute-start.12 = (bf16[96,384]{1,0:T(8,128)(2,1)S(1)}, bf16[96,384]{1,0:T(8,128)(2,1)S(1)}, u32[]{:S(2)}, u32[]{:S(2)}) collective-permute-start(bf16[96,384]{1,0:T(8,128)(2,1)S(1)} %get-tuple-element.104), channel_id=1, source_target_pairs={{0,6},{2,0},{4,2},{6,4},{1,7},{3,1},{5,3},{7,5},{8,14},{10,8},{12,... | collective-permute-start | bytes 221192 | tf_op jit(solution)/shard_map/ppermute | solution.py:800
  125.1 1.2 collective-permute-start.10
  127.8 4.2 %collective-permute-done.11 = bf16[96,384]{1,0:T(8,128)(2,1)S(1)} collective-permute-done((bf16[96,384]{1,0:T(8,128)(2,1)S(1)}, bf16[96,384]{1,0:T(8,128)(2,1)S(1)}, u32[]{:S(2)}, u32[]{:S(2)}) %collective-permute-start.11) | collective-permute-done | bytes 73760 | tf_op jit(solution)/shard_map/ppermute | solution.py:800
  (123 shorter events, 9.3 us)
Async XLA Ops:
  0.6 1.4 %copy-start = (bf16[8,16,16,384]{3,2,1,0:T(8,128)(2,1)S(1)}, bf16[8,16,16,384]{3,2,1,0:T(8,128)(2,1)}, u32[]{:S(2)}) copy-start(bf16[8,16,16,384]{3,2,1,0:T(8,128)(2,1)} %refs_0_.1) | copy-start | bytes 4718596
  2.0 0.7 copy-start.2
  2.7 25.8 %copy-start.1 = (bf16[8,16,16,384]{3,2,1,0:T(8,128)(2,1)S(1)}, bf16[8,16,16,384]{3,2,1,0:T(8,128)(2,1)}, u32[]{:S(2)}) copy-start(bf16[8,16,16,384]{3,2,1,0:T(8,128)(2,1)} %refs_0_.1) | copy-start | bytes 4718596
  2.7 25.8 %copy-start.8 = (bf16[384,768]{1,0:T(8,128)(2,1)S(1)}, bf16[384,768]{1,0:T(8,128)(2,1)}, u32[]{:S(2)}) copy-start(bf16[384,768]{1,0:T(8,128)(2,1)} %head_ref.1) | copy-start | bytes 1769476
  2.7 25.8 %copy-start.12 = (f32[49,384]{1,0:T(8,128)S(1)}, f32[49,384]{1,0:T(8,128)}, u32[]{:S(2)}) copy-start(f32[49,384]{1,0:T(8,128)} %refs_2_.5) | copy-start | bytes 225796
  5.8 20.5 %collective-permute-start = (bf16[2,16,16,384]{3,2,1,0:T(8,128)(2,1)S(1)}, bf16[2,16,16,384]{3,2,1,0:T(8,128)(2,1)S(1)}, u32[]{:S(2)}, u32[]{:S(2)}) collective-permute-start(bf16[2,16,16,384]{3,2,1,0:T(8,128)(2,1)S(1)} %get-tuple-element.55), channel_id=1, source_target_pairs={{0,8},{8,0},{1,9},{9,1},{2,10},{10,2},{3,11},{11,3},{4,12},{12,4},... | collective-permute-start | bytes 1179656 | tf_op jit(solution)/shard_map/ppermute | solution.py:800
  6.1 31.8 %collective-permute-start.3 = (bf16[1,16,16,384]{3,2,1,0:T(8,128)(2,1)}, bf16[1,16,16,384]{3,2,1,0:T(8,128)(2,1)}, u32[]{:S(2)}, u32[]{:S(2)}) collective-permute-start(bf16[1,16,16,384]{3,2,1,0:T(8,128)(2,1)} %get-tuple-element.58), channel_id=1, source_target_pairs={{0,16},{8,24},{16,0},{24,8},{1,17},{9,25},{17,1},{25,9},{2,18},{10... | collective-permute-start | bytes 589832 | tf_op jit(solution)/shard_map/ppermute | solution.py:874
  9.4 28.4 %collective-permute-start.4 = (bf16[1,16,16,384]{3,2,1,0:T(8,128)(2,1)}, bf16[1,16,16,384]{3,2,1,0:T(8,128)(2,1)}, u32[]{:S(2)}, u32[]{:S(2)}) collective-permute-start(bf16[1,16,16,384]{3,2,1,0:T(8,128)(2,1)} %get-tuple-element.59), channel_id=1, source_target_pairs={{0,24},{8,16},{16,8},{24,0},{1,25},{9,17},{17,9},{25,1},{2,26},{10... | collective-permute-start | bytes 589832 | tf_op jit(solution)/shard_map/ppermute | solution.py:874
  12.5 13.8 %all-to-all-start = ((f32[32,1,1024]{2,1,0:T(1,128)}), f32[32,1,1024]{2,1,0:T(1,128)S(1)}, u32[]{:S(2)}, u32[]{:S(2)}) async-start(f32[32,1,1024]{2,1,0:T(1,128)} %broadcast_in_dim.96), calls=%async_computation | async-start | bytes 262144 | tf_op jit(solution)/shard_map/all_to_all | solution.py:811
  26.4 0.7 copy-start.10
  27.1 22.5 %collective-permute-start.1 = (bf16[1,16,16,384]{3,2,1,0:T(8,128)(2,1)}, bf16[1,16,16,384]{3,2,1,0:T(8,128)(2,1)S(1)}, u32[]{:S(2)}, u32[]{:S(2)}) collective-permute-start(bf16[1,16,16,384]{3,2,1,0:T(8,128)(2,1)} %get-tuple-element.56), channel_id=1, source_target_pairs={{0,16},{8,24},{16,0},{24,8},{1,17},{9,25},{17,1},{25,9},{2,18},{10... | collective-permute-start | bytes 589832 | tf_op jit(solution)/shard_map/ppermute | solution.py:874
  28.2 21.5 %collective-permute-start.2 = (bf16[1,16,16,384]{3,2,1,0:T(8,128)(2,1)S(1)}, bf16[1,16,16,384]{3,2,1,0:T(8,128)(2,1)S(1)}, u32[]{:S(2)}, u32[]{:S(2)}) collective-permute-start(bf16[1,16,16,384]{3,2,1,0:T(8,128)(2,1)S(1)} %get-tuple-element.57), channel_id=1, source_target_pairs={{0,24},{8,16},{16,8},{24,0},{1,25},{9,17},{17,9},{25,1},{2,26},{10... | collective-permute-start | bytes 589832 | tf_op jit(solution)/shard_map/ppermute | solution.py:874
  28.6 1.3 copy-start.4
  29.8 1.3 copy-start.6
  31.1 1.0 copy-start.11
  55.3 1.9 %copy-start.15 = (bf16[5,256,1536]{2,1,0:T(8,128)(2,1)}, bf16[5,256,1536]{2,1,0:T(8,128)(2,1)S(1)}, u32[]{:S(2)}) copy-start(bf16[5,256,1536]{2,1,0:T(8,128)(2,1)S(1)} %get-tuple-element.87.hidden_ref) | copy-start | bytes 11796484
  57.2 1.9 %copy-start.17 = (bf16[5,256,1536]{2,1,0:T(8,128)(2,1)}, bf16[5,256,1536]{2,1,0:T(8,128)(2,1)S(1)}, u32[]{:S(2)}) copy-start(bf16[5,256,1536]{2,1,0:T(8,128)(2,1)S(1)} %get-tuple-element.89.slope_ref) | copy-start | bytes 11796484
  59.1 1.3 copy-start.19
  60.4 1.3 copy-start.21
  61.7 1.0 copy-start.25
  62.7 0.8 copy-start.27
  63.6 13.9 %copy-start.3 = (bf16[768,768]{1,0:T(8,128)(2,1)S(1)}, bf16[768,768]{1,0:T(8,128)(2,1)}, u32[]{:S(2)}) copy-start(bf16[768,768]{1,0:T(8,128)(2,1)} %refs_6_.7) | copy-start | bytes 3538948
  63.6 13.9 %copy-start.13 = (f32[7,768]{1,0:T(8,128)S(1)}, f32[7,768]{1,0:T(8,128)}, u32[]{:S(2)}) copy-start(f32[7,768]{1,0:T(8,128)} %refs_5_.7) | copy-start | bytes 64516
  64.7 11.8 %all-to-all-start.1 = ((bf16[32,4,768]{2,1,0:T(4,128)(2,1)}), bf16[32,4,768]{2,1,0:T(4,128)(2,1)}, u32[]{:S(2)}, u32[]{:S(2)}) async-start(bf16[32,4,768]{2,1,0:T(4,128)(2,1)} %broadcast_in_dim.93), calls=%async_computation.1 | async-start | bytes 393216 | tf_op jit(solution)/shard_map/all_to_all | solution.py:811
  77.5 5.6 %copy-start.5 = (bf16[384,1536]{1,0:T(8,128)(2,1)S(1)}, bf16[384,1536]{1,0:T(8,128)(2,1)}, u32[]{:S(2)}) copy-start(bf16[384,1536]{1,0:T(8,128)(2,1)} %expand_ref.1) | copy-start | bytes 3538948
  77.5 5.6 %copy-start.7 = (bf16[1536,384]{1,0:T(8,128)(2,1)S(1)}, bf16[1536,384]{1,0:T(8,128)(2,1)}, u32[]{:S(2)}) copy-start(bf16[1536,384]{1,0:T(8,128)(2,1)} %reduce_ref.1) | copy-start | bytes 3538948
  77.5 5.5 %copy-start.9 = (bf16[384,768]{1,0:T(8,128)(2,1)S(1)}, bf16[384,768]{1,0:T(8,128)(2,1)}, u32[]{:S(2)}) copy-start(bf16[384,768]{1,0:T(8,128)(2,1)} %head_ref.1) | copy-start | bytes 1769476
  77.5 5.5 %copy-start.14 = (bf16[384,384]{1,0:T(8,128)(2,1)S(1)}, bf16[384,384]{1,0:T(8,128)(2,1)}, u32[]{:S(2)}) copy-start(bf16[384,384]{1,0:T(8,128)(2,1)} %constant.109.clone.eye_ref) | copy-start | bytes 884740
  77.5 5.5 %copy-start.16 = (bf16[5,256,1536]{2,1,0:T(8,128)(2,1)S(1)}, bf16[5,256,1536]{2,1,0:T(8,128)(2,1)}, u32[]{:S(2)}) copy-start(bf16[5,256,1536]{2,1,0:T(8,128)(2,1)} %copy-done.15) | copy-start | bytes 11796484
  77.6 5.5 %copy-start.18 = (bf16[5,256,1536]{2,1,0:T(8,128)(2,1)S(1)}, bf16[5,256,1536]{2,1,0:T(8,128)(2,1)}, u32[]{:S(2)}) copy-start(bf16[5,256,1536]{2,1,0:T(8,128)(2,1)} %copy-done.17) | copy-start | bytes 11796484
  77.6 5.5 %copy-start.20 = (f32[5,256,384]{2,1,0:T(8,128)S(1)}, f32[5,256,384]{2,1,0:T(8,128)}, u32[]{:S(2)}) copy-start(f32[5,256,384]{2,1,0:T(8,128)} %copy-done.19) | copy-start | bytes 5898244
  77.6 5.5 %copy-start.22 = (bf16[5,256,768]{2,1,0:T(8,128)(2,1)S(1)}, bf16[5,256,768]{2,1,0:T(8,128)(2,1)}, u32[]{:S(2)}) copy-start(bf16[5,256,768]{2,1,0:T(8,128)(2,1)} %copy-done.21) | copy-start | bytes 5898244
  77.6 5.5 %copy-start.28 = (f32[5,256,128]{2,1,0:T(8,128)S(1)}, f32[5,256,128]{2,1,0:T(8,128)}, u32[]{:S(2)}) copy-start(f32[5,256,128]{2,1,0:T(8,128)} %copy-done.27) | copy-start | bytes 1966084
  95.3 1.2 copy-start.23
  96.5 3.0 %collective-permute-start.5 = (bf16[2,4,4,48,384]{4,3,2,1,0:T(8,128)(2,1)S(1)}, bf16[2,4,4,48,384]{4,3,2,1,0:T(8,128)(2,1)}, u32[]{:S(2)}, u32[]{:S(2)}) collective-permute-start(bf16[2,4,4,48,384]{4,3,2,1,0:T(8,128)(2,1)S(1)} %get-tuple-element.93), channel_id=1, source_target_pairs={{0,8},{8,0},{1,9},{9,1},{2,10},{10,2},{3,11},{11,3},{4,12},{12,4},... | collective-permute-start | bytes 3538952 | tf_op jit(solution)/shard_map/ppermute | solution.py:800
  100.6 3.9 %copy-start.24 = (f32[4,3,256,128]{3,2,1,0:T(8,128)S(1)}, f32[4,3,256,128]{3,2,1,0:T(8,128)}, u32[]{:S(2)}) copy-start(f32[4,3,256,128]{3,2,1,0:T(8,128)} %copy-done.23) | copy-start | bytes 4718596
  100.6 3.9 %copy-start.26 = (bf16[5,16,16,384]{3,2,1,0:T(8,128)(2,1)S(1)}, bf16[5,16,16,384]{3,2,1,0:T(8,128)(2,1)}, u32[]{:S(2)}) copy-start(bf16[5,16,16,384]{3,2,1,0:T(8,128)(2,1)} %copy-done.25) | copy-start | bytes 2949124
  102.1 11.9 %collective-permute-start.6 = (bf16[2,4,48,384]{3,2,1,0:T(8,128)(2,1)S(1)}, bf16[2,4,48,384]{3,2,1,0:T(8,128)(2,1)S(1)}, u32[]{:S(2)}, u32[]{:S(2)}) collective-permute-start(bf16[2,4,48,384]{3,2,1,0:T(8,128)(2,1)S(1)} %get-tuple-element.95), channel_id=1, source_target_pairs={{0,1},{1,0},{2,3},{3,2},{4,5},{5,4},{6,7},{7,6},{8,9},{9,8},{10,11... | collective-permute-start | bytes 884744 | tf_op jit(solution)/shard_map/ppermute | solution.py:800
  103.9 11.9 %collective-permute-start.8 = (bf16[2,4,48,384]{3,2,1,0:T(8,128)(2,1)S(1)}, bf16[2,4,48,384]{3,2,1,0:T(8,128)(2,1)S(1)}, u32[]{:S(2)}, u32[]{:S(2)}) collective-permute-start(bf16[2,4,48,384]{3,2,1,0:T(8,128)(2,1)S(1)} %get-tuple-element.96), channel_id=1, source_target_pairs={{0,16},{16,0},{1,17},{17,1},{2,18},{18,2},{3,19},{19,3},{4,20},{20... | collective-permute-start | bytes 884744 | tf_op jit(solution)/shard_map/ppermute | solution.py:800
  111.2 15.2 %all-to-all-start.2 = ((bf16[32,4,384]{2,1,0:T(4,128)(2,1)}), bf16[32,4,384]{2,1,0:T(4,128)(2,1)S(1)}, u32[]{:S(2)}, u32[]{:S(2)}) async-start(bf16[32,4,384]{2,1,0:T(4,128)(2,1)} %tap_grads.1), calls=%async_computation.2 | async-start | bytes 196608 | tf_op jit(solution)/shard_map/all_to_all | solution.py:811
  114.0 7.0 %collective-permute-start.7 = (bf16[4,48,384]{2,1,0:T(8,128)(2,1)S(1)}, bf16[4,48,384]{2,1,0:T(8,128)(2,1)S(1)}, u32[]{:S(2)}, u32[]{:S(2)}) collective-permute-start(bf16[4,48,384]{2,1,0:T(8,128)(2,1)S(1)} %fusion.9), channel_id=1, source_target_pairs={{0,16},{16,0},{1,17},{17,1},{2,18},{18,2},{3,19},{19,3},{4,20},{20... | collective-permute-start | bytes 442376 | tf_op jit(solution)/shard_map/ppermute | solution.py:800
  115.9 6.3 %collective-permute-start.9 = (bf16[4,48,384]{2,1,0:T(8,128)(2,1)S(1)}, bf16[4,48,384]{2,1,0:T(8,128)(2,1)S(1)}, u32[]{:S(2)}, u32[]{:S(2)}) collective-permute-start(bf16[4,48,384]{2,1,0:T(8,128)(2,1)S(1)} %fusion.11), channel_id=1, source_target_pairs={{0,1},{1,0},{2,3},{3,2},{4,5},{5,4},{6,7},{7,6},{8,9},{9,8},{10,11... | collective-permute-start | bytes 442376 | tf_op jit(solution)/shard_map/ppermute | solution.py:800
  122.3 5.5 %collective-permute-start.12 = (bf16[96,384]{1,0:T(8,128)(2,1)S(1)}, bf16[96,384]{1,0:T(8,128)(2,1)S(1)}, u32[]{:S(2)}, u32[]{:S(2)}) collective-permute-start(bf16[96,384]{1,0:T(8,128)(2,1)S(1)} %get-tuple-element.104), channel_id=1, source_target_pairs={{0,6},{2,0},{4,2},{6,4},{1,7},{3,1},{5,3},{7,5},{8,14},{10,8},{12,... | collective-permute-start | bytes 221192 | tf_op jit(solution)/shard_map/ppermute | solution.py:800
  125.1 6.8 %collective-permute-start.11 = (bf16[96,384]{1,0:T(8,128)(2,1)S(1)}, bf16[96,384]{1,0:T(8,128)(2,1)S(1)}, u32[]{:S(2)}, u32[]{:S(2)}) collective-permute-start(bf16[96,384]{1,0:T(8,128)(2,1)S(1)} %get-tuple-element.105), channel_id=1, source_target_pairs={{0,4},{2,6},{4,0},{6,2},{1,5},{3,7},{5,1},{7,3},{8,12},{10,14},{12... | collective-permute-start | bytes 221192 | tf_op jit(solution)/shard_map/ppermute | solution.py:800
  125.1 6.8 %collective-permute-start.10 = (bf16[96,384]{1,0:T(8,128)(2,1)S(1)}, bf16[96,384]{1,0:T(8,128)(2,1)S(1)}, u32[]{:S(2)}, u32[]{:S(2)}) collective-permute-start(bf16[96,384]{1,0:T(8,128)(2,1)S(1)} %get-tuple-element.103), channel_id=1, source_target_pairs={{0,2},{2,4},{4,6},{6,0},{1,3},{3,5},{5,7},{7,1},{8,10},{10,12},{12... | collective-permute-start | bytes 221192 | tf_op jit(solution)/shard_map/ppermute | solution.py:800

commit v4 on v3

--- a/solution.py
+++ b/solution.py
@@ -28,10 +28,13 @@
 PART = 32
 WIDTH = 256
 GAIN, SHIFT, SCALE, REDUCE_BIAS, DEPTH_BIAS, EXPAND_BIAS, SLIDE_BIAS = range(7)
+VECTORS = 7
 ERFC_P = 0.3275911
 ERFC_A = (0.254829592, -0.284496736, 1.421413741, -1.453152027, 1.061405429)
 
 HBM = pl.BlockSpec(memory_space=pl.ANY)
+IN_HBM = pl.BlockSpec(memory_space=pltpu.HBM)
+ROWS_AT, COLS_AT, COUNT_AT, SMALL = E, E + LANES, E + 2 * LANES, E + 3 * LANES
 
 
 def whole(shape):
@@ -73,11 +76,21 @@
 SLOT, FROM, OWN = range(3)
 
 
-def pack_kernel(slides, slots, places, route_ref, tiles_ref, *refs):
-    send_refs, (table_ref, count_ref, slot_ref, sems) = refs[:-4], refs[-4:]
+def pack_kernel(slides, slots, places, counts_ref, route_ref, tiles_ref, pos_ref, cot_ref, *refs):
+    inputs = (pos_ref, cot_ref) + refs[:VECTORS]
+    refs = refs[VECTORS:]
+    held_refs, refs = refs[-len(inputs) - 1 : -1], refs[: -len(inputs) - 1] + refs[-1:]
+    send_refs, refs = refs[:-7], refs[-7:]
+    table_ref, small_ref, vectors_ref, count_ref, slot_ref, sems, input_sems = refs
+    loads = [
+        pltpu.make_async_copy(ref, held, input_sems.at[index])
+        for index, (ref, held) in enumerate(zip(inputs, held_refs))
+    ]
+    for load in loads:
+        load.start()
+    pos_ref, cot_ref = held_refs[:2]
+    vector_refs = held_refs[2:]
     my_slide = lax.axis_index(DP)
-    members = lax.axis_size(GROUP)
-    my_member = lax.axis_index(GROUP)
 
     targets = [(0, rank, rank) for rank in range(places)]
     for rank in range(places):
@@ -113,6 +126,18 @@
         @pl.when(slot >= 0)
         def _start():
             copy_of(index, slot).start()
+
+    for load in loads:
+        load.wait()
+    small_ref[:, 0:E] = cot_ref[...]
+    for row, start in enumerate((ROWS_AT, COLS_AT)):
+        small_ref[:, start : start + LANES] = jnp.zeros((1, LANES), jnp.float32)
+        small_ref[:, start : start + slots] = pos_ref[row : row + 1, :].astype(jnp.float32)
+    small_ref[:, COUNT_AT:SMALL] = jnp.full((1, LANES), counts_ref[0], jnp.int32).astype(jnp.float32)
+    vectors_ref[...] = jnp.zeros(vectors_ref.shape, jnp.float32)
+    for index, ref in enumerate(vector_refs):
+        size = ref.shape[0]
+        vectors_ref[index : index + 1, 0:size] = ref[...].reshape(1, size)
 
     kinds = 1 + places
     for field in range(CLASSES + kinds * CLASS_SIZE):
@@ -134,7 +159,7 @@
                 count_ref[0] = rank + 1
                 table_ref[FILLED + proc] = 1
                 table_ref[SLIDE + proc] = source
-                table_ref[PLACE + proc] = slot * members + my_member
+                table_ref[PLACE + proc] = slot
                 kind = 0 if other < 2 else 1 + rank
                 base = CLASSES + kind * CLASS_SIZE
                 item = table_ref[base]
@@ -172,29 +197,38 @@
             copy_of(index, 0).wait()
 
 
-def pack_tiles(routing, tile_maps, slides, places):
+def pack_tiles(counts, routing, tile_maps, positions, cotangent, vectors, slides, places):
     slots = tile_maps.shape[0]
     smem = pl.BlockSpec(memory_space=pltpu.SMEM)
     vmem = pl.BlockSpec(memory_space=pltpu.VMEM)
     buffers = 1 + places * (slides - 2)
     shapes = [places] + [1] * (buffers - 1)
+    widest = max(vector.shape[0] for vector in vectors)
+    inputs = (positions, cotangent) + vectors
+    pinned = [pltpu.with_memory_space_constraint(x, pltpu.HBM) for x in (tile_maps,) + inputs]
     outs = pl.pallas_call(
         functools.partial(pack_kernel, slides, slots, places),
         out_shape=tuple(
             jax.ShapeDtypeStruct((size,) + tile_maps.shape[1:], tile_maps.dtype) for size in shapes
         )
-        + (jax.ShapeDtypeStruct((CLASSES + (1 + places) * CLASS_SIZE,), jnp.int32),),
-        in_specs=[smem, HBM],
-        out_specs=(vmem,) * buffers + (smem,),
+        + (
+            jax.ShapeDtypeStruct((CLASSES + (1 + places) * CLASS_SIZE,), jnp.int32),
+            jax.ShapeDtypeStruct((1, SMALL), jnp.float32),
+            jax.ShapeDtypeStruct((8, widest), jnp.float32),
+        ),
+        in_specs=[smem, smem] + [IN_HBM] * len(pinned),
+        out_specs=(vmem,) * buffers + (smem, vmem, vmem),
         scratch_shapes=[
             pltpu.SMEM((slides,), jnp.int32),
             pltpu.SMEM((slides * places,), jnp.int32),
             pltpu.SemaphoreType.DMA((slides * places,)),
-        ],
+        ]
+        + [pltpu.VMEM(x.shape, x.dtype) for x in inputs]
+        + [pltpu.SemaphoreType.DMA((len(inputs),))],
         compiler_params=pltpu.CompilerParams(vmem_limit_bytes=8 * MIB),
         name="pack_tiles",
-    )(routing, tile_maps)
-    return outs[:-1], outs[-1]
+    )(counts, routing, *pinned)
+    return outs[:-3], outs[-3:]
 
 
 def forward_kernel(kind, inputs, aliased, table_ref, *refs):
@@ -358,11 +392,11 @@
     first = 1 + len(tiles) + len(consts)
     return pl.pallas_call(
         functools.partial(forward_kernel, kind, len(tiles), len(before)),
-        out_shape=tuple(jax.ShapeDtypeStruct((PROC + 1,) + shape, dtype) for shape, dtype in outs),
+        out_shape=tuple(pltpu.HBM((PROC + 1,) + shape, dtype) for shape, dtype in outs),
         grid_spec=pltpu.PrefetchScalarGridSpec(
             num_scalar_prefetch=1,
             grid=(items,),
-            in_specs=tile_specs + [whole(const.shape) for const in consts] + [HBM] * len(before),
+            in_specs=tile_specs + [whole(const.shape) for const in consts] + [IN_HBM] * len(before),
             out_specs=[per_slot(*shape) for shape, _ in outs],
             scratch_shapes=[
                 pltpu.VMEM((bands, side, side + ROW_UNIT, LANES), jnp.float32),
@@ -383,45 +417,74 @@
     return pl.CostEstimate(flops=int(micros * 1e9), bytes_accessed=1024, transcendentals=0)
 
 
+def rows_kernel(slides, table_ref, embed_ref, *refs):
+    small_refs, out_ref = refs[:slides], refs[slides]
+    my_slide, my_member = lax.axis_index(DP), lax.axis_index(GROUP)
+    devices = out_ref.shape[0]
+    half = E // 2
+    channel = lax.broadcasted_iota(jnp.int32, (1, E), 1)
+    inner = jnp.where(channel < half, channel, channel - half)
+    odd = lax.rem(inner, 2)
+    frequency = jnp.exp((inner - odd).astype(jnp.float32) * (-math.log(10000.0) / half))
+    phase = odd.astype(jnp.float32) * (0.5 * math.pi)
+    lane = lax.broadcasted_iota(jnp.int32, (1, LANES), 1)
+    for proc in range(PROC):
+        filled = table_ref[FILLED + proc]
+        slide = table_ref[SLIDE + proc]
+        slot = table_ref[PLACE + proc]
+        spots = []
+        for start in (ROWS_AT, COLS_AT):
+            held = small_refs[0][:, start : start + LANES]
+            for other in range(1, slides):
+                held = jnp.where(
+                    (slide ^ my_slide) == other, small_refs[other][:, start : start + LANES], held
+                )
+            spots.append(jnp.sum(jnp.where(lane == slot, held, 0.0), axis=1, keepdims=True))
+        spot = jnp.where(channel < half, spots[0], spots[1])
+        embed = embed_ref[proc].astype(jnp.bfloat16).astype(jnp.float32)
+        row = jnp.where(filled != 0, embed + jnp.sin(spot * frequency + phase), 0.0)
+        target = jnp.where(lane == 0, slide, jnp.where(lane == 1, slot, my_member))
+        target = jnp.where(filled != 0, target, jnp.where(lane == 2, -1, 0))
+        target = jnp.where(lane < 3, target, 0)
+        out_ref[0, proc : proc + 1, 0:E] = row.astype(jnp.bfloat16).astype(jnp.float32)
+        out_ref[0, proc : proc + 1, E:] = target.astype(jnp.float32)
+
+
+def tile_rows(table, embeds, smalls, devices):
+    smem = pl.BlockSpec(memory_space=pltpu.SMEM)
+    vmem = pl.BlockSpec(memory_space=pltpu.VMEM)
+    return pl.pallas_call(
+        functools.partial(rows_kernel, len(smalls)),
+        out_shape=jax.ShapeDtypeStruct((1, PROC, E + LANES), jnp.float32),
+        in_specs=[smem] + [vmem] * (1 + len(smalls)),
+        out_specs=vmem,
+        cost_estimate=cost(1.0),
+        name="tile_rows",
+    )(table, embeds, *smalls)
+
+
 def slide_kernel(
     length,
-    slides,
-    pieces,
-    table_ref,
-    *refs,
-):
-    slide_items(length, slides, table_ref, refs[:pieces], *refs[pieces:])
-
-
-def slide_items(
-    length,
+    members,
     slides,
     table_ref,
-    piece_refs,
-    pick_ref,
-    codes_ref,
-    weight_ref,
-    cot_ref,
+    came_ref,
     taps_ref,
     matrix_ref,
     vectors_ref,
-    feature_ref,
-    grad_ref,
-    rows,
-    back,
-    features,
-    mixed,
-    pre,
-    grad_agg,
-    embeds_ref,
+    *refs,
 ):
-    for index, ref in enumerate(piece_refs):
-        size = ref.shape[0]
-        embeds_ref[index * size : (index + 1) * size, :] = ref[...]
+    small_refs = refs[:slides]
+    feature_ref, grad_ref, rows, back, mixed, pre, grad_agg = refs[slides:]
+    my_slide = lax.axis_index(DP)
     border = ROW_UNIT
     edge = jnp.zeros((border, rows.shape[2]), jnp.float32)
     reach = KERNEL_TAPS // 2
-    blocks = [slice(start, start + WIDTH) for start in range(0, rows.shape[2], WIDTH)]
+    blocks = [slice(start, start + WIDTH) for start in range(0, E, WIDTH)]
+    lane = lax.broadcasted_iota(jnp.int32, (8, LANES), 1)
+    scales = jnp.where(lane == 0, length, jnp.where(lane == 1, members, jnp.where(lane == 2, 1, 0)))
+    target = mix_cols(scales.astype(jnp.float32).astype(jnp.bfloat16), came_ref[:, E:])[0:1, :]
+    step = lax.broadcasted_iota(jnp.int32, (length, 1), 0).astype(jnp.float32)
 
     def dilate(ref, slide, direction, cols):
         total = ref[slide, border : border + length, cols]
@@ -430,15 +493,20 @@
             total = total + taps_ref[tap : tap + 1, cols] * ref[slide, start : start + length, cols]
         return total
 
-    def one_slide(slide, carry):
-        here = weight_ref[slide] > 0.0
+    for other in range(slides):
+        slide = my_slide ^ other
+        small = small_refs[other]
+        count = small[:, COUNT_AT : COUNT_AT + 1]
+        here = step < count
+        share = jnp.where(here, 1.0 / count, 0.0)
+        first = lax.convert_element_type(slide * length, jnp.float32)
+        pick = ((target - first) == step).astype(jnp.float32).astype(jnp.bfloat16)
         for ref in (rows, back):
             ref[slide, 0:border, :] = edge
             ref[slide, border + length :, :] = edge
         for cols in blocks:
-            own = mix(pick_ref[slide], embeds_ref[:, cols]) + codes_ref[slide, :, cols]
-            rows[slide, border : border + length, cols] = (
-                jnp.where(here, own, 0.0).astype(jnp.bfloat16).astype(jnp.float32)
+            rows[slide, border : border + length, cols] = jnp.where(
+                here, mix(pick, came_ref[:, cols]), 0.0
             )
             mixed[:, cols] = dilate(rows, slide, 1, cols).astype(jnp.bfloat16)
         for cols in blocks:
@@ -446,14 +514,15 @@
             total = None
             for start in range(0, length, PART):
                 part = slice(start, start + PART)
-                share = weight_ref[slide, part, :]
                 act, slope = gelu_and_slope(
                     pre[part, cols] + vectors_ref[SLIDE_BIAS : SLIDE_BIAS + 1, cols]
                 )
-                grad_agg[part, cols] = (cot_ref[slide, :, cols] * share * slope).astype(jnp.bfloat16)
-                piece = jnp.sum(act * share, axis=0, keepdims=True)
-                total = piece if total is None else total + piece
-            features[pl.ds(slide, 1), cols] = total
+                grad_agg[part, cols] = (small[:, cols] * share[part] * slope).astype(jnp.bfloat16)
+                if other == 0:
+                    piece = jnp.sum(act * share[part], axis=0, keepdims=True)
+                    total = piece if total is None else total + piece
+            if other == 0:
+                feature_ref[:, cols] = total
         for cols in blocks:
             back[slide, border : border + length, cols] = mix_cols(
                 grad_agg[...], matrix_ref[cols, :]
@@ -462,50 +531,44 @@
             rows[slide, border : border + length, cols] = total.astype(jnp.bfloat16).astype(
                 jnp.float32
             )
-        return carry
-
-    lax.fori_loop(0, slides, one_slide, 0)
-    feature_ref[...] = features[pl.ds(lax.axis_index(DP), 1), :]
+    my_member = lax.axis_index(GROUP)
     for proc in range(PROC):
-        filled = table_ref[FILLED + proc]
-        at = border + table_ref[PLACE + proc]
+        at = border + table_ref[PLACE + proc] * members + my_member
         row = rows[table_ref[SLIDE + proc], pl.ds(at, 1), :]
-        grad_ref[proc] = jnp.where(filled != 0, row, 0.0)
-
-
-def slide_grads(table, pieces, pick, codes, weight, cot, taps, matrix, vectors):
-    slides, length, embed = codes.shape
+        grad_ref[proc] = jnp.where(table_ref[FILLED + proc] != 0, row, 0.0)
+
+
+def slide_grads(length, members, table, came, taps, matrix, vectors, smalls):
+    slides = len(smalls)
     smem = pl.BlockSpec(memory_space=pltpu.SMEM)
     vmem = pl.BlockSpec(memory_space=pltpu.VMEM)
-    padded = (slides, length + 2 * ROW_UNIT, embed)
+    padded = (slides, length + 2 * ROW_UNIT, E)
     return pl.pallas_call(
-        functools.partial(slide_kernel, length, slides, len(pieces)),
+        functools.partial(slide_kernel, length, members, slides),
         out_shape=(
-            jax.ShapeDtypeStruct((1, embed), jnp.float32),
-            jax.ShapeDtypeStruct((PROC, 1, embed), jnp.float32),
+            jax.ShapeDtypeStruct((1, E), jnp.float32),
+            jax.ShapeDtypeStruct((PROC, 1, E), jnp.float32),
         ),
-        in_specs=[smem] + [vmem] * (7 + len(pieces)),
+        in_specs=[smem] + [vmem] * (4 + slides),
         out_specs=(vmem, vmem),
         scratch_shapes=[
             pltpu.VMEM(padded, jnp.float32),
             pltpu.VMEM(padded, jnp.float32),
-            pltpu.VMEM((max(slides, 8), embed), jnp.float32),
-            pltpu.VMEM((length, embed), jnp.bfloat16),
-            pltpu.VMEM((length, embed), jnp.float32),
-            pltpu.VMEM((length, embed), jnp.bfloat16),
-            pltpu.VMEM((sum(piece.shape[0] for piece in pieces), embed), jnp.bfloat16),
+            pltpu.VMEM((length, E), jnp.bfloat16),
+            pltpu.VMEM((length, E), jnp.float32),
+            pltpu.VMEM((length, E), jnp.bfloat16),
         ],
-        compiler_params=pltpu.CompilerParams(vmem_limit_bytes=16 * MIB),
+        compiler_params=pltpu.CompilerParams(vmem_limit_bytes=24 * MIB),
         cost_estimate=cost(6.0),
         name="slide_grads",
-    )(table, *pieces, pick, codes, weight, cot, taps, matrix, vectors)
+    )(table, came, taps, matrix, vectors, *smalls)
 
 
 class Plan:
     def __init__(self, slides, members, channels, hid):
         self.devices = slides * members
         self.ys, self.g1, self.g2 = slides // 2, 4, members // 4
-        self.cross = self.ys * self.g2
+        assert self.ys == self.g2
         self.channels = channels
         self.pieces = hid // channels
         self.expand_rows = channels // self.devices
@@ -513,18 +576,18 @@
         self.block_rows = -(-self.reduce_rows // ROW_UNIT) * ROW_UNIT
         self.share = KS * KS * channels // self.devices
 
-    def blocks(self, rows):
-        return (self.cross, self.g1, rows, self.channels)
-
     def spots(self):
         my_core, my_y = lax.axis_index("core"), lax.axis_index("y")
         my_z, my_x = lax.axis_index("g1"), lax.axis_index("g2")
         for device in range(self.devices):
             slide, member = divmod(device, self.g1 * self.g2)
             (y, core), (z, x) = divmod(slide, 2), divmod(member, self.g2)
-            cross = lax.rem(y - my_y + self.ys, self.ys) * self.g2
-            cross = cross + lax.rem(x - my_x + self.g2, self.g2)
-            yield device, (my_core ^ core, cross, lax.rem(z - my_z + self.g1, self.g1))
+            yield (
+                my_core ^ core,
+                lax.rem(y - my_y + self.ys, self.ys),
+                lax.rem(x - my_x + self.g2, self.g2),
+                lax.rem(z - my_z + self.g1, self.g1),
+            )
 
 
 def send_out(staged, sems, refs):
@@ -623,7 +686,7 @@
 
     @pl.when(step == pl.num_programs(0) - 1)
     def _finish():
-        spots = dict(plan.spots())
+        spots = list(plan.spots())
         per_block = channels // plan.reduce_rows
         tall = plan.block_rows
         for index in range(plan.pieces):
@@ -632,8 +695,8 @@
             turned = mix_cols(eye_ref[...], total)
             for part in range(per_block):
                 block = turned[part * plan.reduce_rows : (part + 1) * plan.reduce_rows]
-                core, cross, z = spots[index * per_block + part]
-                staged[core, 0, cross, z] = padded_block(block, tall)
+                core, y, x, z = spots[index * per_block + part]
+                staged[core, 0, x, y, z] = padded_block(block, tall)
         totals = []
         for quarter in range(plan.pieces):
             cols = slice(quarter * channels, (quarter + 1) * channels)
@@ -642,23 +705,26 @@
         for device in range(plan.devices):
             rows = slice(device * size, (device + 1) * size)
             block = jnp.concatenate([total[rows] for total in totals], axis=0)
-            core, cross, z = spots[device]
-            staged[core, 1, cross, z] = padded_block(block, tall)
+            core, y, x, z = spots[device]
+            staged[core, 1, y, x, z] = padded_block(block, tall)
         send_out(staged, sems, (keep_ref, send_ref))
 
 
 def taps_kernel(
     plan,
+    first,
+    last,
     table_ref,
     source_ref,
     depth_back,
+    before_ref,
     out_ref,
     padded,
     tap_sums,
     tap_rows,
 ):
     step = pl.program_id(0)
-    filled = table_ref[FILLED + step]
+    filled = table_ref[FILLED + first + step]
     side, channels = source_ref.shape[1], source_ref.shape[3]
     bands = channels // LANES
     low = ROW_UNIT // 2
@@ -666,7 +732,10 @@
 
     @pl.when(step == 0)
     def _start():
-        tap_sums[...] = jnp.zeros(tap_sums.shape, jnp.float32)
+        if first:
+            tap_sums[...] = before_ref[...]
+        else:
+            tap_sums[...] = jnp.zeros(tap_sums.shape, jnp.float32)
 
     @pl.when(filled != 0)
     def _work():
@@ -708,6 +777,9 @@
 
     @pl.when(step == pl.num_programs(0) - 1)
     def _finish():
+        if not last:
+            out_ref[...] = tap_sums[...]
+            return
         for band in range(bands):
             lanes = slice(band * LANES, (band + 1) * LANES)
             tap_rows[0 : KS * KS, lanes] = jnp.sum(tap_sums[band], axis=1)
@@ -729,9 +801,9 @@
     eye = jnp.asarray(np.eye(channels, dtype=np.float32), jnp.bfloat16)
     streams = (embed_grad, hidden, head_slope, slope, unit, inv)
     consts = (vectors, head, expand, reduce, eye)
-    back = jax.ShapeDtypeStruct((PROC, bands, cells, LANES), jnp.float32)
+    back = pltpu.HBM((PROC, bands, cells, LANES), jnp.float32)
     blocks = jax.ShapeDtypeStruct(
-        (2, plan.cross, plan.g1, plan.block_rows, channels), jnp.bfloat16
+        (2, plan.ys, plan.g2, plan.g1, plan.block_rows, channels), jnp.bfloat16
     )
     return pl.pallas_call(
         functools.partial(weights_kernel, plan),
@@ -741,7 +813,11 @@
             grid=(PROC,),
             in_specs=[per_slot(stream) for stream in streams]
             + [whole(const.shape) for const in consts],
-            out_specs=[per_slot(back), HBM, HBM],
+            out_specs=[
+                pl.BlockSpec((1, bands, cells, LANES), lambda i, table: (i, 0, 0, 0)),
+                HBM,
+                HBM,
+            ],
             scratch_shapes=[
                 pltpu.VMEM((PROC * cells, hid), jnp.bfloat16),
                 pltpu.VMEM((channels, PROC * cells), jnp.bfloat16),
@@ -759,28 +835,34 @@
     )(table, *streams, *consts)
 
 
-def tap_grads(plan, table, source, depth_back):
+def tap_grads(plan, first, last, table, source, depth_back, before):
     side, channels = source.shape[1], source.shape[3]
     bands = channels // LANES
-    out = (plan.devices, DEPTH_ROWS, channels)
+    sums = (bands, KS * KS, 8, LANES)
+    out = (plan.devices, DEPTH_ROWS, channels) if last else sums
+
+    def items(array):
+        shape = array.shape[1:]
+        return pl.BlockSpec((1,) + shape, lambda i, table: (first + i,) + (0,) * len(shape))
+
     return pl.pallas_call(
-        functools.partial(taps_kernel, plan),
-        out_shape=jax.ShapeDtypeStruct(out, jnp.bfloat16),
+        functools.partial(taps_kernel, plan, first, last),
+        out_shape=jax.ShapeDtypeStruct(out, jnp.bfloat16 if last else jnp.float32),
         grid_spec=pltpu.PrefetchScalarGridSpec(
             num_scalar_prefetch=1,
-            grid=(PROC,),
-            in_specs=[per_slot(source), per_slot(depth_back)],
-            out_specs=pl.BlockSpec(out, lambda i, table: (0, 0, 0)),
+            grid=(PROC // 2,),
+            in_specs=[items(source), items(depth_back), whole(before.shape)],
+            out_specs=pl.BlockSpec(out, lambda i, table: (0,) * len(out)),
             scratch_shapes=[
                 pltpu.VMEM((bands, side, side + ROW_UNIT, LANES), jnp.float32),
-                pltpu.VMEM((bands, KS * KS, 8, LANES), jnp.float32),
+                pltpu.VMEM(sums, jnp.float32),
                 pltpu.VMEM((KS * KS + 7, channels), jnp.float32),
             ],
         ),
-        compiler_params=pltpu.CompilerParams(vmem_limit_bytes=10 * MIB),
-        cost_estimate=cost(8.0),
-        name="tap_grads",
-    )(table, source, depth_back)
+        compiler_params=pltpu.CompilerParams(vmem_limit_bytes=12 * MIB),
+        cost_estimate=cost(4.0),
+        name="tap_grads_" + str(first),
+    )(table, source, depth_back, before)
 
 
 def shifted(values, names, sizes, shift):
@@ -824,19 +906,6 @@
 
 def sum_axis(kept, sent, name, size, kind=jnp.bfloat16):
     return [kept] + [shifted(part, (name,), (size,), (step + 1,)) for step, part in enumerate(sent)]
-
-
-def position_code(positions):
-    half_width = E // 2
-    channel_ids = jnp.arange(E, dtype=jnp.int32) % half_width
-    frequency = jnp.exp(
-        (2 * (channel_ids // 2)).astype(jnp.float32) * (-math.log(10000.0) / half_width)
-    )
-    phase = jnp.where(channel_ids % 2 == 0, 0.0, 0.5 * math.pi)
-    rows = jnp.where(
-        jnp.arange(E, dtype=jnp.int32) < half_width, positions[0][..., None], positions[1][..., None]
-    )
-    return jnp.sin(rows.astype(jnp.float32) * frequency + phase)
 
 
 def on_device(
@@ -866,81 +935,47 @@
     devices, length, places = slides * members, slots * members, slots // slides
     plan = Plan(slides, members, channels, expand_weight.shape[1])
 
-    packed, table = pack_tiles(routing, tile_maps, slides, places)
-    from_core = other_core(packed[0])
-
-    def from_other(buffers):
-        return [
-            lax.ppermute(buffer, DP, [(index, index ^ (other + 2)) for index in range(slides)])
-            for other, buffer in enumerate(buffers)
-        ]
-
+    raw = (
+        norm_gain,
+        norm_shift,
+        layer_scale,
+        reduce_bias,
+        depth_bias,
+        expand_bias,
+        slide_bias,
+    )
+    packed, (table, small, vectors) = pack_tiles(
+        counts, routing, tile_maps, positions, cotangent, raw, slides, places
+    )
+
+    def from_other(buffer, other):
+        return lax.ppermute(buffer, DP, [(index, index ^ other) for index in range(slides)])
+
+    from_core = from_other(packed[0], 1)
     arrived = []
     for rank in range(places):
         buffers = packed[1 + rank * (slides - 2) : 1 + (rank + 1) * (slides - 2)]
         if rank:
             buffers, from_core = lax.optimization_barrier((buffers, from_core))
-        arrived.append(from_other(buffers))
-    held = lax.optimization_barrier((table, routing, cotangent, positions, counts))
-    _, routing, cotangent, positions, counts = held
-    extras = jnp.concatenate(
-        [
-            cotangent[0],
-            routing.reshape(-1).astype(jnp.float32),
-            jnp.zeros((960 - E - slides * slots,), jnp.float32),
-            positions.reshape(-1).astype(jnp.float32),
-            jnp.zeros((1023 - 960 - 2 * slots,), jnp.float32),
-            counts.astype(jnp.float32),
-        ]
-    )
-    extras = exchange(jnp.broadcast_to(extras, (devices, 1024)), ALL)
-
-    vectors = jnp.stack(
-        [
-            jnp.pad(vector, (0, expand_bias.shape[0] - vector.shape[0]))
-            for vector in (
-                norm_gain,
-                norm_shift,
-                layer_scale,
-                reduce_bias,
-                depth_bias,
-                expand_bias,
-                slide_bias,
-                slide_bias,
-            )
-        ]
-    )
+        arrived.append([from_other(buffer, other + 2) for other, buffer in enumerate(buffers)])
+    small, from_core = lax.optimization_barrier((small, from_core))
+    smalls = [small] + [from_other(small, other) for other in range(1, slides)]
+
     consts = (depth_kernel, vectors, expand_weight, reduce_weight, head_weight)
     saved = forward_block(0, PROC, table, (tile_maps, from_core), consts, ())
     for rank in range(places):
         items = min(PROC, slides - 2)
         saved = forward_block(1 + rank, items, table, arrived[rank], consts, saved)
     section, tile_embed, unit, inv, hidden, slope, head_slope, source = saved
+    rows = tile_rows(table, tile_embed, smalls, devices).astype(jnp.bfloat16)
+    came = exchange(jnp.broadcast_to(rows, (devices,) + rows.shape[1:]), ALL)
+    came = came.reshape(devices * PROC, rows.shape[2])
     filled = table[FILLED : FILLED + PROC] != 0
-    tile_embed = jnp.where(filled[:, None], tile_embed[:PROC, 0], 0.0).astype(jnp.bfloat16)
-    tile_embed = jnp.broadcast_to(tile_embed, (devices, PROC, E))
-    tile_embed, extras = lax.optimization_barrier((tile_embed, extras))
-    embeds = exchange(tile_embed, ALL).reshape(devices * PROC, E)
     tile_out = jnp.where(filled[:, None, None, None], section[:PROC], jnp.zeros((), jnp.bfloat16))
-
-    route_all = extras[:, E : E + slides * slots].astype(jnp.int32)
-    route_all = route_all.reshape(slides, members, slides, slots)[0]
-    pos_all = extras[:, 960 : 960 + 2 * slots].reshape(slides, members, 2, slots)
-    pos_all = pos_all.transpose(2, 0, 3, 1).reshape(2, slides, length)
-    counts_all = extras[:, 1023].reshape(slides, members)[:, 0]
-    cot_all = extras[:, :E].reshape(slides, members, 1, E)[:, 0]
-    codes = position_code(pos_all)
-    member_ids = jnp.arange(members, dtype=jnp.int32)[:, None, None]
-    target = jnp.where(
-        route_all >= 0, (route_all // PROC * members + member_ids) * PROC + route_all % PROC, -1
-    )
-    target = target.transpose(1, 2, 0).reshape(slides, length, 1)
-    pick = (target == jnp.arange(devices * PROC, dtype=jnp.int32)).astype(jnp.bfloat16)
-    steps = jnp.arange(length, dtype=jnp.int32)[None, :, None].astype(jnp.float32)
-    weight = jnp.where(steps < counts_all[:, None, None], 1.0 / counts_all[:, None, None], 0.0)
+    came, tile_out = lax.optimization_barrier((came, tile_out))
 
     feature, embed_grad = slide_grads(
-        table, [embeds], pick, codes, weight, cot_all, slide_taps, slide_weight, vectors
+        length, members, table, came, slide_taps, slide_weight, vectors, smalls
     )
     depth_back, kept, sent = weight_grads(
         plan,
@@ -953,32 +988,29 @@
         reduce_weight,
     )
 
+    names = ("g2", "y")
+    size = plan.ys
     came = other_core(sent)
-    grid = [
-        part.reshape((2, plan.ys, plan.g2) + part.shape[2:]) for part in (kept, came)
+    none = jnp.zeros((channels // LANES, KS * KS, 8, LANES), jnp.float32)
+    tap_sums = tap_grads(plan, 0, False, table, source, depth_back, none)
+    came, tap_sums = lax.optimization_barrier((came, tap_sums))
+    out = [
+        [add_all([kept[kind, step], came[kind, step]]) for step in range(1, size)]
+        for kind in range(2)
     ]
-
-    def sums(parts, wanted, count):
-        return add_all([wanted(part)(0) for part in parts]), [
-            add_all([wanted(part)(step) for part in parts]) for step in range(1, count)
-        ]
-
-    reduce_stay, reduce_out = sums(grid, lambda part: lambda step: part[0][:, step], plan.g2)
-    expand_stay, expand_out = sums(grid, lambda part: lambda step: part[1][step], plan.ys)
-    held = lax.optimization_barrier((depth_back, reduce_out, expand_out))
-    depth_back, reduce_out, expand_out = held
-    reduce_parts = sum_axis(reduce_stay, reduce_out, "g2", plan.g2)
-    expand_parts = sum_axis(expand_stay, expand_out, "y", plan.ys)
-    taps = exchange(tap_grads(plan, table, source, depth_back), ALL)
-
-    def along(part):
-        return lambda step: part[step]
-
-    reduce_stay, reduce_out = sums(reduce_parts, along, plan.ys)
-    expand_stay, expand_out = sums(expand_parts, along, plan.g2)
-    reduce_parts = sum_axis(reduce_stay, reduce_out, "y", plan.ys)
-    expand_parts = sum_axis(expand_stay, expand_out, "g2", plan.g2)
-    both = jnp.concatenate([add_all(reduce_parts), add_all(expand_parts)], axis=1)
+    stay = [add_all([kept[kind, 0], came[kind, 0]]) for kind in range(2)]
+    out, tap_sums = lax.optimization_barrier((out, tap_sums))
+    parts = [sum_axis(stay[kind], out[kind], names[kind], size) for kind in range(2)]
+    taps = tap_grads(plan, PROC // 2, True, table, source, depth_back, tap_sums)
+    out = [
+        [add_all([part[step] for part in parts[kind]]) for step in range(1, size)]
+        for kind in range(2)
+    ]
+    stay = [add_all([part[0] for part in parts[kind]]) for kind in range(2)]
+    out, taps = lax.optimization_barrier((out, taps))
+    taps = exchange(taps, ALL)
+    parts = [sum_axis(stay[kind], out[kind], names[1 - kind], size) for kind in range(2)]
+    both = jnp.concatenate([add_all(parts[0]), add_all(parts[1])], axis=1)
     total = add_all(
         sum_axis(both[0], [both[step] for step in range(1, plan.g1)], "g1", plan.g1), jnp.float32
     )

time: 134 us -> 123 us (0.918)
  local copies, waits for them, and re-layouts: 27.7 us -> 11.7 us
  Pallas kernels: 50.7 us -> 56.9 us
  other arithmetic: 7.26 us -> 3.59 us
  starting transfers between devices: 27.3 us -> 29.4 us
  waiting for transfers between devices: 18.7 us -> 20.4 us
    ppermute x4 -> x8, starting transfers between devices: 4.81 us -> 12 us  [from_other(): lax.ppermute(buffer, DP, [(index, index ^ other) for index in range(slide...]
    unnamed x59 -> x62, local copies, waits for them, and re-layouts: 15.8 us -> 8.82 us
    pad x6 -> x0, local copies, waits for them, and re-layouts: 4.11 us -> none  [on_device(): jnp.pad(vector, (0, expand_bias.shape[0] - vector.shape[0]))]
    pallas_call x3, Pallas kernels: 23.2 us -> 27 us  [forward_block(): pl.pallas_call(functools.partial(forward_kernel, kind, len(tiles), len(be...]
    ppermute x9 -> x8, starting transfers between devices: 10.2 us -> 6.53 us  [shifted(): return lax.ppermute(values, names, pairs)]
    all_to_all x3 -> x2, waiting for transfers between devices: 7.35 us -> 10.3 us  [exchange(): lax.all_to_all(values, names, split_axis=0, concat_axis=0, tiled=True)]
    sin x1 -> x0, other arithmetic: 2.66 us -> none  [position_code(): return jnp.sin(rows.astype(jnp.float32) * frequency + phase)]
    pallas_call x2 -> x4, Pallas kernels: 12.3 us -> 14.1 us  [the longest x2 7.47 us: tap_grads(): pl.pallas_call(functools.partial(taps_kernel, plan, first, last), out_sha...]
  transfers between devices with their start and end apart: 16 -> 18, of which waited for: 7 -> 8; matrix products, arithmetic and copies ran while one was open for 10% -> 3% of each run, Pallas kernels for 18% -> 28%
where the time goes in v4:
time: 123 us; the launch traced here: 124 us
  Pallas kernels  56.9 us (46%)
  starting transfers between devices  29.4 us (24%)
  waiting for transfers between devices  20.4 us (17%)
  local copies, waits for them, and re-layouts  11.7 us (10%)
  other arithmetic  3.59 us (3%)
  between operations  1.73 us (1%)
    pallas_call x3, Pallas kernels, forward_block(): pl.pallas_call(functools.partial(forward_kernel, kind, len(tiles), len(be...  27 us
    pallas_call x1, Pallas kernels, weight_grads(): pl.pallas_call(functools.partial(weights_kernel, plan), out_shape=(back,...  13 us
    ppermute x8, starting transfers between devices, from_other(): lax.ppermute(buffer, DP, [(index, index ^ other) for index in range(slide...  12 us
    all_to_all x2, starting transfers between devices, exchange(): lax.all_to_all(values, names, split_axis=0, concat_axis=0, tiled=True)  10.8 us
    all_to_all x2, waiting for transfers between devices, exchange(): lax.all_to_all(values, names, split_axis=0, concat_axis=0, tiled=True)  10.3 us
    ppermute x8, waiting for transfers between devices, shifted(): return lax.ppermute(values, names, pairs)  9.84 us
    unnamed x62, local copies, waits for them, and re-layouts  8.82 us
    pallas_call x2, Pallas kernels, tap_grads(): pl.pallas_call(functools.partial(taps_kernel, plan, first, last), out_sha...  7.47 us
  transfers between devices with their start and end apart: 18, of which 8 were waited for; matrix products, arithmetic and copies ran while one was open for 3% of the time, Pallas kernels for 28%

profile of v4, /device:TPU:0, one launch (start us, length us, event | category | flops | bytes accessed | tf_op | source)
XLA Modules:
  0.0 123.6 jit_solution(16462245527520731429)
XLA Ops:
  1.3 0.7 copy-done.1
  2.0 2.8 %pack_tiles.1 = (bf16[2,16,16,384]{3,2,1,0:T(8,128)(2,1)S(1)}, bf16[1,16,16,384]{3,2,1,0:T(8,128)(2,1)S(1)}, bf16[1,16,16,384]{3,2,1,0:T(8,128)(2,1)S(1)}, bf16[...) custom-call(s32[1]{0:T(128)S(6)} %copy.57.counts_ref, ...), custom_call_target="tpu_custom_call" | custom-call | tf_op jit(solution)/shard_map/pack_tiles/pallas_call | solution.py:209
  4.7 0.5 collective-permute-start
  5.3 2.7 %collective-permute-start.3 = (bf16[1,16,16,384]{3,2,1,0:T(8,128)(2,1)S(1)}, bf16[1,16,16,384]{3,2,1,0:T(8,128)(2,1)S(1)}, u32[]{:S(2)}, u32[]{:S(2)}) collective-permute-start(bf16[1,16,16,384]{3,2,1,0:T(8,128)(2,1)S(1)} %get-tuple-element.64), channel_id=1, source_target_pairs={{0,16},{8,24},{16,0},{24,8},{1,17},{9,25},{17,1},{25,9},{2,18},{10... | collective-permute-start | bytes 589832 | tf_op jit(solution)/shard_map/ppermute | solution.py:952
  8.0 0.1 collective-permute-start.5
  8.1 1.9 %collective-permute-start.6 = (f32[1,1152]{1,0:T(1,128)S(1)}, f32[1,1152]{1,0:T(1,128)S(1)}, u32[]{:S(2)}, u32[]{:S(2)}) collective-permute-start(f32[1,1152]{1,0:T(1,128)S(1)} %get-tuple-element.86.refs_0_), channel_id=1, source_target_pairs={{0,16},{8,24},{16,0},{24,8},{1,17},{9,25},{17,1},{25,9},{2,18},{10... | collective-permute-start | bytes 13832 | tf_op jit(solution)/shard_map/ppermute | solution.py:952
  10.1 1.4 %copy-done = bf16[8,16,16,384]{3,2,1,0:T(8,128)(2,1)S(1)} copy-done((bf16[8,16,16,384]{3,2,1,0:T(8,128)(2,1)S(1)}, bf16[8,16,16,384]{3,2,1,0:T(8,128)(2,1)}, u32[]{:S(2)}) %copy-start) | copy-done | bytes 1572888
  11.5 1.3 %copy-done.3 = bf16[384,1536]{1,0:T(8,128)(2,1)S(1)} copy-done((bf16[384,1536]{1,0:T(8,128)(2,1)S(1)}, bf16[384,1536]{1,0:T(8,128)(2,1)}, u32[]{:S(2)}) %copy-start.3) | copy-done | bytes 1179672
  12.8 1.3 %copy-done.5 = bf16[1536,384]{1,0:T(8,128)(2,1)S(1)} copy-done((bf16[1536,384]{1,0:T(8,128)(2,1)S(1)}, bf16[1536,384]{1,0:T(8,128)(2,1)}, u32[]{:S(2)}) %copy-start.5) | copy-done | bytes 1179672
  14.0 1.1 copy-done.8
  15.1 0.9 copy-done.10
  16.0 12.4 %forward_block_0.1 = (bf16[5,16,16,384]{3,2,1,0:T(8,128)(2,1)}, f32[5,1,768]{2,1,0:T(1,128)}, f32[5,256,384]{2,1,0:T(8,128)}, f32[5,256,128]{2,1,0:T(8,128)}, bf...) custom-call(s32[51]{0:T(128)S(1)} %get-tuple-element.57.table_ref, ...), custom_call_target="tpu_custom_call" | custom-call | flops 12000000000 | bytes 1024 | tf_op jit(solution)/shard_map/forward_block_0/pallas_call | solution.py:393
  28.4 1.6 %collective-permute-start.1 = (bf16[1,16,16,384]{3,2,1,0:T(8,128)(2,1)S(1)}, bf16[1,16,16,384]{3,2,1,0:T(8,128)(2,1)S(1)}, u32[]{:S(2)}, u32[]{:S(2)}) collective-permute-start(bf16[1,16,16,384]{3,2,1,0:T(8,128)(2,1)S(1)} %get-tuple-element.61), channel_id=1, source_target_pairs={{0,16},{8,24},{16,0},{24,8},{1,17},{9,25},{17,1},{25,9},{2,18},{10... | collective-permute-start | bytes 589832 | tf_op jit(solution)/shard_map/ppermute | solution.py:952
  29.9 5.1 %collective-permute-start.2 = (bf16[1,16,16,384]{3,2,1,0:T(8,128)(2,1)S(1)}, bf16[1,16,16,384]{3,2,1,0:T(8,128)(2,1)S(1)}, u32[]{:S(2)}, u32[]{:S(2)}) collective-permute-start(bf16[1,16,16,384]{3,2,1,0:T(8,128)(2,1)S(1)} %get-tuple-element.62), channel_id=1, source_target_pairs={{0,24},{8,16},{16,8},{24,0},{1,25},{9,17},{17,9},{25,1},{2,26},{10... | collective-permute-start | bytes 589832 | tf_op jit(solution)/shard_map/ppermute | solution.py:952
  35.1 7.2 %forward_block_1.1 = (bf16[5,16,16,384]{3,2,1,0:T(8,128)(2,1)}, f32[5,1,768]{2,1,0:T(1,128)}, f32[5,256,384]{2,1,0:T(8,128)}, f32[5,256,128]{2,1,0:T(8,128)}, bf...) custom-call(s32[51]{0:T(128)S(1)} %get-tuple-element.57.table_ref, ...), custom_call_target="tpu_custom_call", output_to_operand_aliasing={{0}: (8, {}), {1}: (9, {}), {2}: (10, {}), {3}: (11, {}), {... | custom-call | flops 12000000000 | bytes 1024 | tf_op jit(solution)/shard_map/forward_block_1/pallas_call | solution.py:393
  42.3 0.2 collective-permute-done.2.refs_1_
  42.5 7.4 %forward_block_2.1 = (bf16[5,16,16,384]{3,2,1,0:T(8,128)(2,1)}, f32[5,1,768]{2,1,0:T(1,128)}, f32[5,256,384]{2,1,0:T(8,128)}, f32[5,256,128]{2,1,0:T(8,128)}, bf...) custom-call(s32[51]{0:T(128)S(1)} %get-tuple-element.57.table_ref, ...), custom_call_target="tpu_custom_call", output_to_operand_aliasing={{0}: (8, {}), {1}: (9, {}), {2}: (10, {}), {3}: (11, {}), {... | custom-call | flops 12000000000 | bytes 1024 | tf_op jit(solution)/shard_map/forward_block_2/pallas_call | solution.py:393
  50.0 0.5 copy-done.14
  50.6 1.9 %tile_rows.1 = f32[1,4,896]{2,1,0:T(4,128)} custom-call(s32[51]{0:T(128)} %copy-done.20, f32[5,1,768]{2,1,0:T(1,128)} %get-tuple-element.85.embed_ref, f32[1,1152]{1,0:T(1,128)} %copy-done.12, f32[1,1152]{1,0:T(1,128)} %copy-done.14, f32[1,1152]{1,0:T(1,128)} %copy-done.16, f32[1,1152]{1,0:T(1,128)} %copy-done.18), custom_call_target="tpu_custom_call" | custom-call | flops 1000000000 | bytes 1024 | tf_op jit(solution)/shard_map/tile_rows/pallas_call | solution.py:456
  52.5 0.8 convert_bitcast_fusion
  53.3 0.8 broadcast_in_dim.24
  54.1 8.3 %all-to-all-start = ((bf16[32,4,896]{2,1,0:T(4,128)(2,1)}), bf16[32,4,896]{2,1,0:T(4,128)(2,1)S(1)}, u32[]{:S(2)}, u32[]{:S(2)}) async-start(bf16[32,4,896]{2,1,0:T(4,128)(2,1)} %broadcast_in_dim.24), calls=%async_computation | async-start | bytes 458752 | tf_op jit(solution)/shard_map/all_to_all | solution.py:893
  62.4 2.2 %slice_select_fusion = bf16[4,16,16,384]{3,2,1,0:T(8,128)(2,1)} fusion(bf16[5,16,16,384]{3,2,1,0:T(8,128)(2,1)} %get-tuple-element.87, pred[4]{0:T(512)(128)(4,1)S(1)} %slice_compare_fusion), kind=kLoop, calls=%fused_computation | loop fusion | flops 393216 | bytes 1572868 | tf_op jit(solution)/shard_map/jit(_where)/select_n | solution.py:974
  64.5 7.6 %all-to-all-done = bf16[32,4,896]{2,1,0:T(4,128)(2,1)S(1)} async-done(((bf16[32,4,896]{2,1,0:T(4,128)(2,1)}), bf16[32,4,896]{2,1,0:T(4,128)(2,1)S(1)}, u32[]{:S(2)}, u32[]{:S(2)}) %all-to-all-start) | async-done | bytes 229408 | tf_op jit(solution)/shard_map/all_to_all | solution.py:893
  72.4 4.8 %slide_grads.1 = (f32[1,768]{1,0:T(1,128)}, f32[4,1,768]{2,1,0:T(1,128)S(1)}) custom-call(s32[51]{0:T(128)S(1)} %copy-done.21, bf16[128,896]{1,0:T(8,128)(2,1)S(1)} %reshape.76.came_ref, f32[7,768]{1,0:T(8,128)S(1)} %copy-done.11, bf16[768,768]{1,0:T(8,128)(2,1)S(1)} %copy-done.2, f32[8,1536]{1,0:T(8,128)S(1)} %get-tuple-element.63.refs_3_.vectors_ref, ...), custom_call_target="tpu_custom_call" | custom-call | flops 6000000000 | bytes 1024 | tf_op jit(solution)/shard_map/slide_grads/pallas_call | solution.py:546
  77.2 0.1 copy-done.29
  77.3 0.1 copy-done.30
  77.4 13.0 %weight_grads.1 = (f32[4,3,256,128]{3,2,1,0:T(8,128)}, bf16[2,2,2,4,48,384]{5,4,3,2,1,0:T(8,128)(2,1)S(1)}, bf16[2,2,2,4,48,384]{5,4,3,2,1,0:T(8,128)(2,1)S(1)}) custom-call(s32[51]{0:T(128)S(1)} %copy-done.21, f32[4,1,768]{2,1,0:T(1,128)S(1)} %get-tuple-element.91.grad_ref, bf16[5,256,1536]{2,1,0:T(8,128)(2,1)S(1)} %copy-done.26, ...), custom_call_target="tpu_custom_call" | custom-call | flops 16000000000 | bytes 1024 | tf_op jit(solution)/shard_map/weight_grads/pallas_call | solution.py:808
  90.5 1.4 %copy-done.23 = f32[4,3,256,128]{3,2,1,0:T(8,128)S(1)} copy-done((f32[4,3,256,128]{3,2,1,0:T(8,128)S(1)}, f32[4,3,256,128]{3,2,1,0:T(8,128)}, u32[]{:S(2)}) %copy-start.23) | copy-done | bytes 1572888
  91.9 3.3 %tap_grads_0.1.before_ref = f32[3,49,8,128]{3,2,1,0:T(8,128)S(1)} custom-call(s32[51]{0:T(128)S(1)} %copy-done.21, bf16[5,16,16,384]{3,2,1,0:T(8,128)(2,1)S(1)} %copy-done.25, f32[4,3,256,128]{3,2,1,0:T(8,128)S(1)} %copy-done.23, f32[3,49,8,128]{3,2,1,0:T(8,128)S(1)} %broadcast_in_dim.27.before_ref), custom_call_target="tpu_custom_call" | custom-call | flops 4000000000 | bytes 1024 | tf_op jit(solution)/shard_map/tap_grads_0/pallas_call | solution.py:848
  95.2 0.3 add_convert_fusion
  95.5 1.3 %collective-permute-start.9 = (bf16[2,4,48,384]{3,2,1,0:T(8,128)(2,1)S(1)}, bf16[2,4,48,384]{3,2,1,0:T(8,128)(2,1)S(1)}, u32[]{:S(2)}, u32[]{:S(2)}) collective-permute-start(bf16[2,4,48,384]{3,2,1,0:T(8,128)(2,1)S(1)} %get-tuple-element.103), channel_id=1, source_target_pairs={{0,1},{1,0},{2,3},{3,2},{4,5},{5,4},{6,7},{7,6},{8,9},{9,8},{10,11... | collective-permute-start | bytes 884744 | tf_op jit(solution)/shard_map/ppermute | solution.py:882
  96.9 0.6 collective-permute-start.10
  97.4 4.2 %tap_grads_2.1 = bf16[32,4,384]{2,1,0:T(4,128)(2,1)} custom-call(s32[51]{0:T(128)S(1)} %copy-done.21, bf16[5,16,16,384]{3,2,1,0:T(8,128)(2,1)S(1)} %copy-done.25, f32[4,3,256,128]{3,2,1,0:T(8,128)S(1)} %copy-done.24, f32[3,49,8,128]{3,2,1,0:T(8,128)S(1)} %tap_grads_0.1.before_ref), custom_call_target="tpu_custom_call" | custom-call | flops 4000000000 | bytes 1024 | tf_op jit(solution)/shard_map/tap_grads_2/pallas_call | solution.py:848
  101.6 3.4 %collective-permute-done.9 = bf16[2,4,48,384]{3,2,1,0:T(8,128)(2,1)S(1)} collective-permute-done((bf16[2,4,48,384]{3,2,1,0:T(8,128)(2,1)S(1)}, bf16[2,4,48,384]{3,2,1,0:T(8,128)(2,1)S(1)}, u32[]{:S(2)}, u32[]{:S(2)}) %collective-permute-start.9) | collective-permute-done | bytes 294944 | tf_op jit(solution)/shard_map/ppermute | solution.py:882
  105.0 0.9 collective-permute-done.10
  106.0 0.6 collective-permute-start.11
  106.6 0.9 collective-permute-start.12
  107.4 2.6 %all-to-all-start.1 = ((bf16[32,4,384]{2,1,0:T(4,128)(2,1)}), bf16[32,4,384]{2,1,0:T(4,128)(2,1)S(1)}, u32[]{:S(2)}, u32[]{:S(2)}) async-start(bf16[32,4,384]{2,1,0:T(4,128)(2,1)} %tap_grads_2.1), calls=%async_computation.1 | async-start | bytes 196608 | tf_op jit(solution)/shard_map/all_to_all | solution.py:893
  110.0 1.2 collective-permute-done.11
  111.2 0.5 collective-permute-done.12
  111.8 2.0 %collective-permute-start.15 = (bf16[96,384]{1,0:T(8,128)(2,1)S(1)}, bf16[96,384]{1,0:T(8,128)(2,1)S(1)}, u32[]{:S(2)}, u32[]{:S(2)}) collective-permute-start(bf16[96,384]{1,0:T(8,128)(2,1)S(1)} %get-tuple-element.114), channel_id=1, source_target_pairs={{0,6},{2,0},{4,2},{6,4},{1,7},{3,1},{5,3},{7,5},{8,14},{10,8},{12,... | collective-permute-start | bytes 221192 | tf_op jit(solution)/shard_map/ppermute | solution.py:882
  113.9 1.1 collective-permute-start.13
  114.9 2.6 %all-to-all-done.1 = bf16[32,4,384]{2,1,0:T(4,128)(2,1)S(1)} async-done(((bf16[32,4,384]{2,1,0:T(4,128)(2,1)}), bf16[32,4,384]{2,1,0:T(4,128)(2,1)S(1)}, u32[]{:S(2)}, u32[]{:S(2)}) %all-to-all-start.1) | async-done | bytes 98336 | tf_op jit(solution)/shard_map/all_to_all | solution.py:893
  117.7 0.7 dynamic_slice.3
  118.3 3.9 %collective-permute-done.14 = bf16[96,384]{1,0:T(8,128)(2,1)S(1)} collective-permute-done((bf16[96,384]{1,0:T(8,128)(2,1)S(1)}, bf16[96,384]{1,0:T(8,128)(2,1)S(1)}, u32[]{:S(2)}, u32[]{:S(2)}) %collective-permute-start.14) | collective-permute-done | bytes 73760 | tf_op jit(solution)/shard_map/ppermute | solution.py:882
  122.3 0.7 reshape.78
  123.0 0.6 reshape.79
  (80 shorter events, 0.8 us)
Async XLA Ops:
  1.3 0.7 copy-start.1
  4.7 23.6 %copy-start.12 = (f32[1,1152]{1,0:T(1,128)}, f32[1,1152]{1,0:T(1,128)S(1)}, u32[]{:S(2)}) copy-start(f32[1,1152]{1,0:T(1,128)S(1)} %get-tuple-element.86.refs_0_) | copy-start | bytes 13828
  4.7 37.8 %copy-start.20 = (s32[51]{0:T(128)}, s32[51]{0:T(128)S(1)}, u32[]{:S(2)}) copy-start(s32[51]{0:T(128)S(1)} %get-tuple-element.57.table_ref) | copy-start | bytes 616
  4.7 3.3 %collective-permute-start = (bf16[2,16,16,384]{3,2,1,0:T(8,128)(2,1)S(1)}, bf16[2,16,16,384]{3,2,1,0:T(8,128)(2,1)S(1)}, u32[]{:S(2)}, u32[]{:S(2)}) collective-permute-start(bf16[2,16,16,384]{3,2,1,0:T(8,128)(2,1)S(1)} %get-tuple-element.60), channel_id=1, source_target_pairs={{0,8},{8,0},{16,24},{24,16},{1,9},{9,1},{17,25},{25,17},{2,10},{10... | collective-permute-start | bytes 1179656 | tf_op jit(solution)/shard_map/ppermute | solution.py:952
  5.3 23.1 %collective-permute-start.3 = (bf16[1,16,16,384]{3,2,1,0:T(8,128)(2,1)S(1)}, bf16[1,16,16,384]{3,2,1,0:T(8,128)(2,1)S(1)}, u32[]{:S(2)}, u32[]{:S(2)}) collective-permute-start(bf16[1,16,16,384]{3,2,1,0:T(8,128)(2,1)S(1)} %get-tuple-element.64), channel_id=1, source_target_pairs={{0,16},{8,24},{16,0},{24,8},{1,17},{9,25},{17,1},{25,9},{2,18},{10... | collective-permute-start | bytes 589832 | tf_op jit(solution)/shard_map/ppermute | solution.py:952
  7.9 22.0 %collective-permute-start.4 = (bf16[1,16,16,384]{3,2,1,0:T(8,128)(2,1)S(1)}, bf16[1,16,16,384]{3,2,1,0:T(8,128)(2,1)S(1)}, u32[]{:S(2)}, u32[]{:S(2)}) collective-permute-start(bf16[1,16,16,384]{3,2,1,0:T(8,128)(2,1)S(1)} %get-tuple-element.65), channel_id=1, source_target_pairs={{0,24},{8,16},{16,8},{24,0},{1,25},{9,17},{17,9},{25,1},{2,26},{10... | collective-permute-start | bytes 589832 | tf_op jit(solution)/shard_map/ppermute | solution.py:952
  8.0 42.0 %collective-permute-start.5 = (f32[1,1152]{1,0:T(1,128)S(1)}, f32[1,1152]{1,0:T(1,128)S(1)}, u32[]{:S(2)}, u32[]{:S(2)}) collective-permute-start(f32[1,1152]{1,0:T(1,128)S(1)} %get-tuple-element.86.refs_0_), channel_id=1, source_target_pairs={{0,8},{8,0},{16,24},{24,16},{1,9},{9,1},{17,25},{25,17},{2,10},{10... | collective-permute-start | bytes 13832 | tf_op jit(solution)/shard_map/ppermute | solution.py:952
  8.1 41.8 %collective-permute-start.6 = (f32[1,1152]{1,0:T(1,128)S(1)}, f32[1,1152]{1,0:T(1,128)S(1)}, u32[]{:S(2)}, u32[]{:S(2)}) collective-permute-start(f32[1,1152]{1,0:T(1,128)S(1)} %get-tuple-element.86.refs_0_), channel_id=1, source_target_pairs={{0,16},{8,24},{16,0},{24,8},{1,17},{9,25},{17,1},{25,9},{2,18},{10... | collective-permute-start | bytes 13832 | tf_op jit(solution)/shard_map/ppermute | solution.py:952
  10.1 39.9 %collective-permute-start.7 = (f32[1,1152]{1,0:T(1,128)S(1)}, f32[1,1152]{1,0:T(1,128)S(1)}, u32[]{:S(2)}, u32[]{:S(2)}) collective-permute-start(f32[1,1152]{1,0:T(1,128)S(1)} %get-tuple-element.86.refs_0_), channel_id=1, source_target_pairs={{0,24},{8,16},{16,8},{24,0},{1,25},{9,17},{17,9},{25,1},{2,26},{10... | collective-permute-start | bytes 13832 | tf_op jit(solution)/shard_map/ppermute | solution.py:952
  10.1 1.4 %copy-start = (bf16[8,16,16,384]{3,2,1,0:T(8,128)(2,1)S(1)}, bf16[8,16,16,384]{3,2,1,0:T(8,128)(2,1)}, u32[]{:S(2)}) copy-start(bf16[8,16,16,384]{3,2,1,0:T(8,128)(2,1)} %refs_0_.3) | copy-start | bytes 4718596
  11.5 1.3 %copy-start.3 = (bf16[384,1536]{1,0:T(8,128)(2,1)S(1)}, bf16[384,1536]{1,0:T(8,128)(2,1)}, u32[]{:S(2)}) copy-start(bf16[384,1536]{1,0:T(8,128)(2,1)} %expand_ref.1) | copy-start | bytes 3538948
  12.8 1.3 %copy-start.5 = (bf16[1536,384]{1,0:T(8,128)(2,1)S(1)}, bf16[1536,384]{1,0:T(8,128)(2,1)}, u32[]{:S(2)}) copy-start(bf16[1536,384]{1,0:T(8,128)(2,1)} %reduce_ref.1) | copy-start | bytes 3538948
  14.0 1.1 copy-start.8
  15.1 0.9 copy-start.10
  16.0 19.1 %copy-start.4 = (bf16[384,1536]{1,0:T(8,128)(2,1)S(1)}, bf16[384,1536]{1,0:T(8,128)(2,1)}, u32[]{:S(2)}) copy-start(bf16[384,1536]{1,0:T(8,128)(2,1)} %expand_ref.1) | copy-start | bytes 3538948
  16.0 19.1 %copy-start.6 = (bf16[1536,384]{1,0:T(8,128)(2,1)S(1)}, bf16[1536,384]{1,0:T(8,128)(2,1)}, u32[]{:S(2)}) copy-start(bf16[1536,384]{1,0:T(8,128)(2,1)} %reduce_ref.1) | copy-start | bytes 3538948
  28.4 14.0 %collective-permute-start.1 = (bf16[1,16,16,384]{3,2,1,0:T(8,128)(2,1)S(1)}, bf16[1,16,16,384]{3,2,1,0:T(8,128)(2,1)S(1)}, u32[]{:S(2)}, u32[]{:S(2)}) collective-permute-start(bf16[1,16,16,384]{3,2,1,0:T(8,128)(2,1)S(1)} %get-tuple-element.61), channel_id=1, source_target_pairs={{0,16},{8,24},{16,0},{24,8},{1,17},{9,25},{17,1},{25,9},{2,18},{10... | collective-permute-start | bytes 589832 | tf_op jit(solution)/shard_map/ppermute | solution.py:952
  29.9 12.6 %collective-permute-start.2 = (bf16[1,16,16,384]{3,2,1,0:T(8,128)(2,1)S(1)}, bf16[1,16,16,384]{3,2,1,0:T(8,128)(2,1)S(1)}, u32[]{:S(2)}, u32[]{:S(2)}) collective-permute-start(bf16[1,16,16,384]{3,2,1,0:T(8,128)(2,1)S(1)} %get-tuple-element.62), channel_id=1, source_target_pairs={{0,24},{8,16},{16,8},{24,0},{1,25},{9,17},{17,9},{25,1},{2,26},{10... | collective-permute-start | bytes 589832 | tf_op jit(solution)/shard_map/ppermute | solution.py:952
  50.0 0.6 copy-start.14
  50.0 0.6 copy-start.16
  50.6 11.7 %copy-start.21 = (s32[51]{0:T(128)S(1)}, s32[51]{0:T(128)}, u32[]{:S(2)}) copy-start(s32[51]{0:T(128)} %copy-done.20) | copy-start | bytes 616
  52.5 19.7 %copy-start.2 = (bf16[768,768]{1,0:T(8,128)(2,1)S(1)}, bf16[768,768]{1,0:T(8,128)(2,1)}, u32[]{:S(2)}) copy-start(bf16[768,768]{1,0:T(8,128)(2,1)} %matrix_ref.1) | copy-start | bytes 3538948
  52.5 19.7 %copy-start.11 = (f32[7,768]{1,0:T(8,128)S(1)}, f32[7,768]{1,0:T(8,128)}, u32[]{:S(2)}) copy-start(f32[7,768]{1,0:T(8,128)} %taps_ref.1) | copy-start | bytes 64516
  52.5 19.7 %copy-start.13 = (f32[1,1152]{1,0:T(1,128)S(1)}, f32[1,1152]{1,0:T(1,128)}, u32[]{:S(2)}) copy-start(f32[1,1152]{1,0:T(1,128)} %copy-done.12) | copy-start | bytes 13828
  52.5 19.8 %copy-start.15 = (f32[1,1152]{1,0:T(1,128)S(1)}, f32[1,1152]{1,0:T(1,128)}, u32[]{:S(2)}) copy-start(f32[1,1152]{1,0:T(1,128)} %copy-done.14) | copy-start | bytes 13828
  52.5 19.8 %copy-start.17 = (f32[1,1152]{1,0:T(1,128)S(1)}, f32[1,1152]{1,0:T(1,128)}, u32[]{:S(2)}) copy-start(f32[1,1152]{1,0:T(1,128)} %copy-done.16) | copy-start | bytes 13828
  52.5 19.8 %copy-start.19 = (f32[1,1152]{1,0:T(1,128)S(1)}, f32[1,1152]{1,0:T(1,128)}, u32[]{:S(2)}) copy-start(f32[1,1152]{1,0:T(1,128)} %copy-done.18) | copy-start | bytes 13828
  54.1 18.1 %all-to-all-start = ((bf16[32,4,896]{2,1,0:T(4,128)(2,1)}), bf16[32,4,896]{2,1,0:T(4,128)(2,1)S(1)}, u32[]{:S(2)}, u32[]{:S(2)}) async-start(bf16[32,4,896]{2,1,0:T(4,128)(2,1)} %broadcast_in_dim.24), calls=%async_computation | async-start | bytes 458752 | tf_op jit(solution)/shard_map/all_to_all | solution.py:893
  72.3 4.9 %copy-start.7 = (bf16[1536,384]{1,0:T(8,128)(2,1)S(1)}, bf16[1536,384]{1,0:T(8,128)(2,1)}, u32[]{:S(2)}) copy-start(bf16[1536,384]{1,0:T(8,128)(2,1)} %reduce_ref.1) | copy-start | bytes 3538948
  72.3 4.9 %copy-start.9 = (bf16[384,768]{1,0:T(8,128)(2,1)S(1)}, bf16[384,768]{1,0:T(8,128)(2,1)}, u32[]{:S(2)}) copy-start(bf16[384,768]{1,0:T(8,128)(2,1)} %head_ref.1) | copy-start | bytes 1769476
  72.3 4.9 %copy-start.22 = (bf16[384,384]{1,0:T(8,128)(2,1)S(1)}, bf16[384,384]{1,0:T(8,128)(2,1)}, u32[]{:S(2)}) copy-start(bf16[384,384]{1,0:T(8,128)(2,1)} %constant.44.clone.eye_ref) | copy-start | bytes 884740
  72.3 4.9 %copy-start.26 = (bf16[5,256,1536]{2,1,0:T(8,128)(2,1)S(1)}, bf16[5,256,1536]{2,1,0:T(8,128)(2,1)}, u32[]{:S(2)}) copy-start(bf16[5,256,1536]{2,1,0:T(8,128)(2,1)} %get-tuple-element.92.hidden_ref) | copy-start | bytes 11796484
  72.3 4.9 %copy-start.27 = (bf16[5,256,1536]{2,1,0:T(8,128)(2,1)S(1)}, bf16[5,256,1536]{2,1,0:T(8,128)(2,1)}, u32[]{:S(2)}) copy-start(bf16[5,256,1536]{2,1,0:T(8,128)(2,1)} %get-tuple-element.94.slope_ref) | copy-start | bytes 11796484
  72.3 4.9 %copy-start.28 = (f32[5,256,384]{2,1,0:T(8,128)S(1)}, f32[5,256,384]{2,1,0:T(8,128)}, u32[]{:S(2)}) copy-start(f32[5,256,384]{2,1,0:T(8,128)} %get-tuple-element.95.unit_ref) | copy-start | bytes 5898244
  72.3 5.0 %copy-start.29 = (bf16[5,256,768]{2,1,0:T(8,128)(2,1)S(1)}, bf16[5,256,768]{2,1,0:T(8,128)(2,1)}, u32[]{:S(2)}) copy-start(bf16[5,256,768]{2,1,0:T(8,128)(2,1)} %get-tuple-element.93.head_slope_ref) | copy-start | bytes 5898244
  72.3 5.0 %copy-start.30 = (f32[5,256,128]{2,1,0:T(8,128)S(1)}, f32[5,256,128]{2,1,0:T(8,128)}, u32[]{:S(2)}) copy-start(f32[5,256,128]{2,1,0:T(8,128)} %get-tuple-element.96.inv_ref) | copy-start | bytes 1966084
  77.4 13.1 %copy-start.25 = (bf16[5,16,16,384]{3,2,1,0:T(8,128)(2,1)S(1)}, bf16[5,16,16,384]{3,2,1,0:T(8,128)(2,1)}, u32[]{:S(2)}) copy-start(bf16[5,16,16,384]{3,2,1,0:T(8,128)(2,1)} %get-tuple-element.99.source_ref) | copy-start | bytes 2949124
  90.3 4.9 %collective-permute-start.8 = (bf16[2,2,2,4,48,384]{5,4,3,2,1,0:T(8,128)(2,1)S(1)}, bf16[2,2,2,4,48,384]{5,4,3,2,1,0:T(8,128)(2,1)S(1)}, u32[]{:S(2)}, u32[]{:S(2)}) collective-permute-start(bf16[2,2,2,4,48,384]{5,4,3,2,1,0:T(8,128)(2,1)S(1)} %get-tuple-element.98), channel_id=1, source_target_pairs={{0,8},{8,0},{1,9},{9,1},{2,10},{10,2},{3,11},{11,3},{4,12},{12,4},... | collective-permute-start | bytes 3538952 | tf_op jit(solution)/shard_map/ppermute | solution.py:882
  90.5 1.4 %copy-start.23 = (f32[4,3,256,128]{3,2,1,0:T(8,128)S(1)}, f32[4,3,256,128]{3,2,1,0:T(8,128)}, u32[]{:S(2)}) copy-start(f32[4,3,256,128]{3,2,1,0:T(8,128)} %get-tuple-element.100.depth_back) | copy-start | bytes 4718596
  95.2 2.2 %copy-start.24 = (f32[4,3,256,128]{3,2,1,0:T(8,128)S(1)}, f32[4,3,256,128]{3,2,1,0:T(8,128)}, u32[]{:S(2)}) copy-start(f32[4,3,256,128]{3,2,1,0:T(8,128)} %get-tuple-element.100.depth_back) | copy-start | bytes 4718596
  95.5 9.5 %collective-permute-start.9 = (bf16[2,4,48,384]{3,2,1,0:T(8,128)(2,1)S(1)}, bf16[2,4,48,384]{3,2,1,0:T(8,128)(2,1)S(1)}, u32[]{:S(2)}, u32[]{:S(2)}) collective-permute-start(bf16[2,4,48,384]{3,2,1,0:T(8,128)(2,1)S(1)} %get-tuple-element.103), channel_id=1, source_target_pairs={{0,1},{1,0},{2,3},{3,2},{4,5},{5,4},{6,7},{7,6},{8,9},{9,8},{10,11... | collective-permute-start | bytes 884744 | tf_op jit(solution)/shard_map/ppermute | solution.py:882
  96.9 9.1 %collective-permute-start.10 = (bf16[2,4,48,384]{3,2,1,0:T(8,128)(2,1)S(1)}, bf16[2,4,48,384]{3,2,1,0:T(8,128)(2,1)S(1)}, u32[]{:S(2)}, u32[]{:S(2)}) collective-permute-start(bf16[2,4,48,384]{3,2,1,0:T(8,128)(2,1)S(1)} %get-tuple-element.104), channel_id=1, source_target_pairs={{0,16},{16,0},{1,17},{17,1},{2,18},{18,2},{3,19},{19,3},{4,20},{20... | collective-permute-start | bytes 884744 | tf_op jit(solution)/shard_map/ppermute | solution.py:882
  106.0 5.2 %collective-permute-start.11 = (bf16[4,48,384]{2,1,0:T(8,128)(2,1)S(1)}, bf16[4,48,384]{2,1,0:T(8,128)(2,1)S(1)}, u32[]{:S(2)}, u32[]{:S(2)}) collective-permute-start(bf16[4,48,384]{2,1,0:T(8,128)(2,1)S(1)} %fusion.9), channel_id=1, source_target_pairs={{0,16},{16,0},{1,17},{17,1},{2,18},{18,2},{3,19},{19,3},{4,20},{20... | collective-permute-start | bytes 442376 | tf_op jit(solution)/shard_map/ppermute | solution.py:882
  106.6 5.1 %collective-permute-start.12 = (bf16[4,48,384]{2,1,0:T(8,128)(2,1)S(1)}, bf16[4,48,384]{2,1,0:T(8,128)(2,1)S(1)}, u32[]{:S(2)}, u32[]{:S(2)}) collective-permute-start(bf16[4,48,384]{2,1,0:T(8,128)(2,1)S(1)} %fusion.10), channel_id=1, source_target_pairs={{0,1},{1,0},{2,3},{3,2},{4,5},{5,4},{6,7},{7,6},{8,9},{9,8},{10,11... | collective-permute-start | bytes 442376 | tf_op jit(solution)/shard_map/ppermute | solution.py:882
  107.4 10.1 %all-to-all-start.1 = ((bf16[32,4,384]{2,1,0:T(4,128)(2,1)}), bf16[32,4,384]{2,1,0:T(4,128)(2,1)S(1)}, u32[]{:S(2)}, u32[]{:S(2)}) async-start(bf16[32,4,384]{2,1,0:T(4,128)(2,1)} %tap_grads_2.1), calls=%async_computation.1 | async-start | bytes 196608 | tf_op jit(solution)/shard_map/all_to_all | solution.py:893
  111.8 6.5 %collective-permute-start.15 = (bf16[96,384]{1,0:T(8,128)(2,1)S(1)}, bf16[96,384]{1,0:T(8,128)(2,1)S(1)}, u32[]{:S(2)}, u32[]{:S(2)}) collective-permute-start(bf16[96,384]{1,0:T(8,128)(2,1)S(1)} %get-tuple-element.114), channel_id=1, source_target_pairs={{0,6},{2,0},{4,2},{6,4},{1,7},{3,1},{5,3},{7,5},{8,14},{10,8},{12,... | collective-permute-start | bytes 221192 | tf_op jit(solution)/shard_map/ppermute | solution.py:882
  113.9 8.3 %collective-permute-start.14 = (bf16[96,384]{1,0:T(8,128)(2,1)S(1)}, bf16[96,384]{1,0:T(8,128)(2,1)S(1)}, u32[]{:S(2)}, u32[]{:S(2)}) collective-permute-start(bf16[96,384]{1,0:T(8,128)(2,1)S(1)} %get-tuple-element.115), channel_id=1, source_target_pairs={{0,4},{2,6},{4,0},{6,2},{1,5},{3,7},{5,1},{7,3},{8,12},{10,14},{12... | collective-permute-start | bytes 221192 | tf_op jit(solution)/shard_map/ppermute | solution.py:882
  113.9 8.3 %collective-permute-start.13 = (bf16[96,384]{1,0:T(8,128)(2,1)S(1)}, bf16[96,384]{1,0:T(8,128)(2,1)S(1)}, u32[]{:S(2)}, u32[]{:S(2)}) collective-permute-start(bf16[96,384]{1,0:T(8,128)(2,1)S(1)} %get-tuple-element.113), channel_id=1, source_target_pairs={{0,2},{2,4},{4,6},{6,0},{1,3},{3,5},{5,7},{7,1},{8,10},{10,12},{12... | collective-permute-start | bytes 221192 | tf_op jit(solution)/shard_map/ppermute | solution.py:882
  (1 other events, 0.6 us)

commit v5 on v4

--- a/solution.py
+++ b/solution.py
@@ -3,7 +3,6 @@
 
 import jax
 import jax.numpy as jnp
-import numpy as np
 from jax import lax
 from jax.experimental import pallas as pl
 from jax.experimental.pallas import tpu as pltpu
@@ -21,6 +20,7 @@
 EPSILON = 1e-06
 HALF_ROOT = 0.7071067811865476
 INV_ROOT_TAU = 0.3989422804014327
+BELL_SCALE = -0.7213475204444817
 LANES = 128
 ROW_UNIT = 16
 DEPTH_ROWS = 4
@@ -44,9 +44,8 @@
 def gelu_and_slope(values):
     size = jnp.abs(values)
     divisor = 1.0 + (ERFC_P * HALF_ROOT) * size
-    guess = pl.reciprocal(divisor, approx=True)
-    t = guess * (2.0 - divisor * guess)
-    bell = jnp.exp(-0.5 * values * values)
+    t = pl.reciprocal(divisor, approx=True)
+    bell = jnp.exp2(values * (values * BELL_SCALE))
     poly = 0.5 * ERFC_A[4]
     for coefficient in ERFC_A[3::-1]:
         poly = poly * t + 0.5 * coefficient
@@ -205,7 +204,7 @@
     shapes = [places] + [1] * (buffers - 1)
     widest = max(vector.shape[0] for vector in vectors)
     inputs = (positions, cotangent) + vectors
-    pinned = [pltpu.with_memory_space_constraint(x, pltpu.HBM) for x in (tile_maps,) + inputs]
+    fixed = [pinned(x) for x in (tile_maps,) + inputs]
     outs = pl.pallas_call(
         functools.partial(pack_kernel, slides, slots, places),
         out_shape=tuple(
@@ -216,7 +215,7 @@
             jax.ShapeDtypeStruct((1, SMALL), jnp.float32),
             jax.ShapeDtypeStruct((8, widest), jnp.float32),
         ),
-        in_specs=[smem, smem] + [IN_HBM] * len(pinned),
+        in_specs=[smem, smem] + [IN_HBM] * len(fixed),
         out_specs=(vmem,) * buffers + (smem, vmem, vmem),
         scratch_shapes=[
             pltpu.SMEM((slides,), jnp.int32),
@@ -227,65 +226,94 @@
         + [pltpu.SemaphoreType.DMA((len(inputs),))],
         compiler_params=pltpu.CompilerParams(vmem_limit_bytes=8 * MIB),
         name="pack_tiles",
-    )(counts, routing, *pinned)
+    )(counts, routing, *fixed)
     return outs[:-3], outs[-3:]
 
 
-def forward_kernel(kind, inputs, aliased, table_ref, *refs):
-    forward_items(kind, table_ref, refs[:inputs], *refs[inputs : inputs + 5], *refs[inputs + 5 + aliased :])
-
-
-def forward_items(
-    kind,
-    table_ref,
-    tile_refs,
-    taps_ref,
-    vectors_ref,
-    expand_ref,
-    reduce_ref,
-    head_ref,
-    out_ref,
-    embed_ref,
-    unit_ref,
-    inv_ref,
-    hidden_ref,
-    slope_ref,
-    head_slope_ref,
-    source_ref,
-    padded,
-    depth_out,
-    normed,
-    pre,
-    section,
-):
-    item = pl.program_id(0)
-    side = out_ref.shape[1]
-    channels = out_ref.shape[3]
+def forward_kernel(kind, last, inputs, kept, table_ref, *refs):
+    tile_refs, refs = refs[:inputs], refs[inputs:]
+    taps_hbm, vectors_ref, expand_hbm, reduce_hbm, head_hbm = refs[:5]
+    refs = refs[5 + (0 if kind == 0 else kept) :]
+    out_hbms, refs = refs[:kept], refs[kept:]
+    held, refs = refs[:kept], refs[kept:]
+    taps_ref, expand_ref, reduce_ref, head_ref, padded, depth_out, normed, pre, load_sems = refs[:9]
+    tile_sems, out_sems = refs[9:]
+    out_s, embed_s, unit_s, inv_s, hidden_s, slope_s, head_slope_s, source_s = held
+    items = table_ref[class_field(kind, -1)]
+    side, channels = out_s.shape[1], out_s.shape[3]
     cells = side * side
     bands = channels // LANES
     low = ROW_UNIT // 2
     reach = KS // 2
-
-    @pl.when(item < table_ref[class_field(kind, -1)])
-    def _work():
+    constants = [
+        pltpu.make_async_copy(source, target, load_sems.at[index])
+        for index, (source, target) in enumerate(
+            (
+                (taps_hbm, taps_ref),
+                (expand_hbm, expand_ref),
+                (reduce_hbm, reduce_ref),
+                (head_hbm, head_ref),
+            )
+        )
+    ]
+
+    def tile_copy(ref, row, buffer):
+        return pltpu.make_async_copy(ref.at[row], source_s.at[buffer], tile_sems.at[buffer])
+
+    def load(item, buffer):
         origin = table_ref[class_field(kind, FROM) + item]
+        place = 0
+        for index, ref in enumerate(tile_refs):
+            own = kind == 0 and index == 0
+            for row in range(1 if own else ref.shape[0]):
+
+                @pl.when(origin == place)
+                def _load():
+                    at = table_ref[class_field(kind, OWN) + item] if own else row
+                    tile_copy(ref, at, buffer).start()
+
+                place += 1
+
+    def keep(part, slot, buffer):
+        return pltpu.make_async_copy(
+            held[part].at[buffer], out_hbms[part].at[slot], out_sems.at[part, buffer]
+        )
+
+    def wait_kept(buffer):
+        for part in range(kept - 1):
+            keep(part, 0, buffer).wait()
+
+    def vector(index, lanes):
+        return vectors_ref[index : index + 1, lanes]
+
+    @pl.when(items > 0)
+    def _first():
+        load(0, 0)
+        for copy in constants:
+            copy.start()
         edge = jnp.zeros((side, low, LANES), jnp.float32)
         for band in range(bands):
             padded[band, :, 0:low, :] = edge
             padded[band, :, low + side :, :] = edge
-        place = 0
-        for ref in tile_refs:
-            for row in range(ref.shape[0]):
-
-                @pl.when(origin == place)
-                def _load():
-                    source_ref[0] = ref[row]
-
-                place += 1
+
+    def one_item(item, carry):
+        buffer = lax.rem(item, 2)
+        slot = table_ref[class_field(kind, SLOT) + item]
+
+        @pl.when(item >= 2)
+        def _free():
+            wait_kept(buffer)
+
+        tile_copy(tile_refs[0], 0, buffer).wait()
+
+        @pl.when(item == 0)
+        def _taps():
+            constants[0].wait()
+
         for band in range(bands):
             for at in range(side):
-                padded[band, at, low : low + side, :] = source_ref[
-                    0, at, :, band * LANES : (band + 1) * LANES
+                padded[band, at, low : low + side, :] = source_s[
+                    buffer, at, :, band * LANES : (band + 1) * LANES
                 ].astype(jnp.float32)
 
         def convolve(band, carry):
@@ -308,10 +336,6 @@
             return carry
 
         lax.fori_loop(0, bands, convolve, 0)
-
-        def vector(index, lanes):
-            return vectors_ref[index : index + 1, lanes]
-
         for start in range(0, cells, PART):
             rows = slice(start, start + PART)
             pieces = [depth_out[band, rows, :] for band in range(bands)]
@@ -319,63 +343,101 @@
             pieces = [piece - mean for piece in pieces]
             var = jnp.sum(sum(p * p for p in pieces), axis=1, keepdims=True) * (1.0 / channels)
             inv = lax.rsqrt(var + EPSILON)
-            inv_ref[0, rows, :] = jnp.broadcast_to(inv, (PART, LANES))
+            inv_s[buffer, rows, :] = jnp.broadcast_to(inv, (PART, LANES))
             for band in range(bands):
                 lanes = slice(band * LANES, (band + 1) * LANES)
                 unit = pieces[band] * inv
-                unit_ref[0, rows, lanes] = unit
+                unit_s[buffer, rows, lanes] = unit
                 normed[rows, lanes] = (unit * vector(GAIN, lanes) + vector(SHIFT, lanes)).astype(
                     jnp.bfloat16
                 )
 
+        @pl.when(item == 0)
+        def _weights():
+            for copy in constants[1:]:
+                copy.wait()
+
+        @pl.when(item + 1 < items)
+        def _next():
+            @pl.when(item >= 1)
+            def _source_free():
+                keep(kept - 1, 0, 1 - buffer).wait()
+
+            load(item + 1, 1 - buffer)
+
+        for part in (2, 3):
+            keep(part, slot, buffer).start()
         for index, begin in enumerate(range(0, expand_ref.shape[1], WIDTH)):
             cols = slice(begin, begin + WIDTH)
-            buffer = index % pre.shape[0]
-            pre[buffer] = mix(normed[...], expand_ref[:, cols])
+            at = index % pre.shape[0]
+            pre[at] = mix(normed[...], expand_ref[:, cols])
             for start in range(0, cells, PART):
                 rows = slice(start, start + PART)
-                act, slope = gelu_and_slope(pre[buffer, rows, :] + vector(EXPAND_BIAS, cols))
-                hidden_ref[0, rows, cols] = act.astype(jnp.bfloat16)
-                slope_ref[0, rows, cols] = slope.astype(jnp.bfloat16)
+                act, slope = gelu_and_slope(pre[at, rows, :] + vector(EXPAND_BIAS, cols))
+                hidden_s[buffer, rows, cols] = act.astype(jnp.bfloat16)
+                slope_s[buffer, rows, cols] = slope.astype(jnp.bfloat16)
+        for part in (4, 5):
+            keep(part, slot, buffer).start()
         lanes = slice(0, channels)
-        depth_rows = mix(hidden_ref[0], reduce_ref[...])
+        depth_rows = mix(hidden_s[buffer], reduce_ref[...])
         for at in range(side):
             rows = slice(at * side, (at + 1) * side)
             branch = vector(SCALE, lanes) * (depth_rows[rows] + vector(REDUCE_BIAS, lanes))
-            line = (source_ref[0, at].astype(jnp.float32) + branch).astype(jnp.bfloat16)
-            section[rows, :] = line
-            out_ref[0, at] = line
+            line = (source_s[buffer, at].astype(jnp.float32) + branch).astype(jnp.bfloat16)
+            normed[rows, :] = line
+            out_s[buffer, at] = line
+        for part in (0, 7):
+            keep(part, slot, buffer).start()
         for index, begin in enumerate(range(0, head_ref.shape[1], WIDTH)):
             cols = slice(begin, begin + WIDTH)
-            buffer = index % pre.shape[0]
-            pre[buffer] = mix(section[...], head_ref[:, cols])
+            at = index % pre.shape[0]
+            pre[at] = mix(normed[...], head_ref[:, cols])
             total = None
             for start in range(0, cells, PART):
                 rows = slice(start, start + PART)
-                act, slope = gelu_and_slope(pre[buffer, rows, :])
-                head_slope_ref[0, rows, cols] = slope.astype(jnp.bfloat16)
+                act, slope = gelu_and_slope(pre[at, rows, :])
+                head_slope_s[buffer, rows, cols] = slope.astype(jnp.bfloat16)
                 folded = act[0:8]
                 for piece in range(8, PART, 8):
                     folded = folded + act[piece : piece + 8]
                 total = folded if total is None else total + folded
-            embed_ref[0, :, cols] = jnp.sum(total, axis=0, keepdims=True) * (1.0 / cells)
-
-
-def forward_block(kind, items, table, tiles, consts, before):
+            mean = jnp.sum(total, axis=0, keepdims=True) * (1.0 / cells)
+            embed_s[buffer, :, cols] = jnp.broadcast_to(mean, (8, WIDTH))
+        for part in (1, 6):
+            keep(part, slot, buffer).start()
+        return carry
+
+    lax.fori_loop(0, items, one_item, 0)
+    for back in (1, 2):
+
+        @pl.when(items >= back)
+        def _drain():
+            buffer = lax.rem(items - back, 2)
+            for part in range(kept):
+                keep(part, 0, buffer).wait()
+
+    if last:
+        out_s[0] = jnp.zeros(out_s.shape[1:], out_s.dtype)
+        for proc in range(PROC):
+
+            @pl.when(table_ref[FILLED + proc] == 0)
+            def _empty():
+                copy = keep(0, proc, 0)
+                copy.start()
+                copy.wait()
+
+
+def pinned(array):
+    return pltpu.with_memory_space_constraint(array, pltpu.HBM)
+
+
+def forward_block(kind, last, table, tiles, taps, vectors, expand, reduce, head, before):
     side, channels = tiles[0].shape[1], tiles[0].shape[3]
-    taps, vectors, expand, reduce, head = consts
     cells, hid, embed = side * side, expand.shape[1], head.shape[1]
     bands = channels // LANES
-
-    def per_slot(*shape):
-        return pl.BlockSpec(
-            (1,) + shape,
-            lambda i, table: (table[class_field(kind, SLOT) + i],) + (0,) * len(shape),
-        )
-
     outs = (
         ((side, side, channels), jnp.bfloat16),
-        ((1, embed), jnp.float32),
+        ((8, embed), jnp.float32),
         ((cells, channels), jnp.float32),
         ((cells, LANES), jnp.float32),
         ((cells, hid), jnp.bfloat16),
@@ -383,34 +445,38 @@
         ((cells, embed), jnp.bfloat16),
         ((side, side, channels), jnp.bfloat16),
     )
-    tile_specs = [whole(tile.shape) for tile in tiles]
+    smem = pl.BlockSpec(memory_space=pltpu.SMEM)
+    vmem = pl.BlockSpec(memory_space=pltpu.VMEM)
     if kind == 0:
-        tile_specs[0] = pl.BlockSpec(
-            (1, side, side, channels),
-            lambda i, table: (table[class_field(kind, OWN) + i], 0, 0, 0),
-        )
-    first = 1 + len(tiles) + len(consts)
+        tiles = (pinned(tiles[0]),) + tuple(tiles[1:])
+    first = 1 + len(tiles) + 5
     return pl.pallas_call(
-        functools.partial(forward_kernel, kind, len(tiles), len(before)),
-        out_shape=tuple(pltpu.HBM((PROC + 1,) + shape, dtype) for shape, dtype in outs),
-        grid_spec=pltpu.PrefetchScalarGridSpec(
-            num_scalar_prefetch=1,
-            grid=(items,),
-            in_specs=tile_specs + [whole(const.shape) for const in consts] + [IN_HBM] * len(before),
-            out_specs=[per_slot(*shape) for shape, _ in outs],
-            scratch_shapes=[
-                pltpu.VMEM((bands, side, side + ROW_UNIT, LANES), jnp.float32),
-                pltpu.VMEM((bands, cells, LANES), jnp.float32),
-                pltpu.VMEM((cells, channels), jnp.bfloat16),
-                pltpu.VMEM((3, cells, WIDTH), jnp.float32),
-                pltpu.VMEM((cells, channels), jnp.bfloat16),
-            ],
-        ),
+        functools.partial(forward_kernel, kind, last, len(tiles), len(outs)),
+        out_shape=tuple(pltpu.HBM((PROC,) + shape, dtype) for shape, dtype in outs),
+        in_specs=[smem]
+        + [HBM] * len(tiles)
+        + [IN_HBM, vmem, IN_HBM, IN_HBM, IN_HBM]
+        + [IN_HBM] * len(before),
+        out_specs=(IN_HBM,) * len(outs),
+        scratch_shapes=[pltpu.VMEM((2,) + shape, dtype) for shape, dtype in outs]
+        + [
+            pltpu.VMEM(taps.shape, jnp.float32),
+            pltpu.VMEM(expand.shape, jnp.bfloat16),
+            pltpu.VMEM(reduce.shape, jnp.bfloat16),
+            pltpu.VMEM(head.shape, jnp.bfloat16),
+            pltpu.VMEM((bands, side, side + ROW_UNIT, LANES), jnp.float32),
+            pltpu.VMEM((bands, cells, LANES), jnp.float32),
+            pltpu.VMEM((cells, channels), jnp.bfloat16),
+            pltpu.VMEM((3, cells, WIDTH), jnp.float32),
+            pltpu.SemaphoreType.DMA((4,)),
+            pltpu.SemaphoreType.DMA((2,)),
+            pltpu.SemaphoreType.DMA((len(outs), 2)),
+        ],
         input_output_aliases={first + index: index for index in range(len(before))},
-        compiler_params=pltpu.CompilerParams(vmem_limit_bytes=20 * MIB),
-        cost_estimate=cost(6.0 * min(items, 2)),
+        compiler_params=pltpu.CompilerParams(vmem_limit_bytes=24 * MIB),
+        cost_estimate=cost(1.0),
         name="forward_block_" + str(kind),
-    )(table, *tiles, *consts, *before)
+    )(table, *tiles, pinned(taps), vectors, pinned(expand), pinned(reduce), pinned(head), *before)
 
 
 def cost(micros):
@@ -418,7 +484,7 @@
 
 
 def rows_kernel(slides, table_ref, embed_ref, *refs):
-    small_refs, out_ref = refs[:slides], refs[slides]
+    small_refs, (out_ref, rows_ref) = refs[:slides], refs[slides:]
     my_slide, my_member = lax.axis_index(DP), lax.axis_index(GROUP)
     devices = out_ref.shape[0]
     half = E // 2
@@ -441,13 +507,16 @@
                 )
             spots.append(jnp.sum(jnp.where(lane == slot, held, 0.0), axis=1, keepdims=True))
         spot = jnp.where(channel < half, spots[0], spots[1])
-        embed = embed_ref[proc].astype(jnp.bfloat16).astype(jnp.float32)
+        embed = embed_ref[proc, 0:1, :].astype(jnp.bfloat16).astype(jnp.float32)
         row = jnp.where(filled != 0, embed + jnp.sin(spot * frequency + phase), 0.0)
         target = jnp.where(lane == 0, slide, jnp.where(lane == 1, slot, my_member))
         target = jnp.where(filled != 0, target, jnp.where(lane == 2, -1, 0))
         target = jnp.where(lane < 3, target, 0)
-        out_ref[0, proc : proc + 1, 0:E] = row.astype(jnp.bfloat16).astype(jnp.float32)
-        out_ref[0, proc : proc + 1, E:] = target.astype(jnp.float32)
+        rows_ref[proc : proc + 1, 0:E] = row
+        rows_ref[proc : proc + 1, E:] = target.astype(jnp.float32)
+    sent = rows_ref[...].astype(jnp.bfloat16)
+    for device in range(devices):
+        out_ref[device] = sent
 
 
 def tile_rows(table, embeds, smalls, devices):
@@ -455,9 +524,10 @@
     vmem = pl.BlockSpec(memory_space=pltpu.VMEM)
     return pl.pallas_call(
         functools.partial(rows_kernel, len(smalls)),
-        out_shape=jax.ShapeDtypeStruct((1, PROC, E + LANES), jnp.float32),
+        out_shape=jax.ShapeDtypeStruct((devices, PROC, E + LANES), jnp.bfloat16),
         in_specs=[smem] + [vmem] * (1 + len(smalls)),
         out_specs=vmem,
+        scratch_shapes=[pltpu.VMEM((PROC, E + LANES), jnp.float32)],
         cost_estimate=cost(1.0),
         name="tile_rows",
     )(table, embeds, *smalls)
@@ -615,13 +685,10 @@
     head_slope_ref,
     slope_ref,
     unit_ref,
-    inv_ref,
     vectors_ref,
     head_ref,
-    expand_ref,
     reduce_ref,
-    eye_ref,
-    depth_back_ref,
+    grad_pre_ref,
     keep_ref,
     send_ref,
     hidden_all,
@@ -629,19 +696,24 @@
     grad_pre_all,
     normed_all,
     grad_head,
-    grad_norm,
+    eye_ref,
     staged,
     sems,
 ):
     step = pl.program_id(0)
     filled = table_ref[FILLED + step]
     cells, channels = unit_ref.shape[1:]
-    bands = channels // LANES
     rows_all = pl.ds(pl.multiple_of(step * cells, cells), cells)
     every = slice(0, channels)
 
     def vector(index, lanes):
         return vectors_ref[index : index + 1, lanes]
+
+    @pl.when(step == 0)
+    def _start():
+        spot = lax.broadcasted_iota(jnp.int32, eye_ref.shape, 0)
+        same = spot == lax.broadcasted_iota(jnp.int32, eye_ref.shape, 1)
+        eye_ref[...] = same.astype(jnp.float32).astype(jnp.bfloat16)
 
     @pl.when(filled == 0)
     def _empty():
@@ -662,27 +734,16 @@
         )
         grad_mlp_all[:, rows_all] = mix_cols(eye_ref[...], grad_mlp).astype(jnp.bfloat16)
         hidden_all[rows_all, :] = hidden_ref[0]
-        for begin in range(0, expand_ref.shape[1], WIDTH):
+        for begin in range(0, reduce_ref.shape[0], WIDTH):
             cols = slice(begin, begin + WIDTH)
             grad_hidden = mix_cols(grad_mlp, reduce_ref[cols, :])
-            grad_pre_all[rows_all, cols] = (
-                grad_hidden * slope_ref[0, :, cols].astype(jnp.float32)
-            ).astype(jnp.bfloat16)
-        grad_norm[...] = mix_cols(grad_pre_all[rows_all, :], expand_ref[...])
+            grad_pre = (grad_hidden * slope_ref[0, :, cols].astype(jnp.float32)).astype(
+                jnp.bfloat16
+            )
+            grad_pre_all[rows_all, cols] = grad_pre
+            grad_pre_ref[0, :, cols] = grad_pre
         normed = (unit_ref[0] * vector(GAIN, every) + vector(SHIFT, every)).astype(jnp.bfloat16)
         normed_all[:, rows_all] = mix_cols(eye_ref[...], normed).astype(jnp.bfloat16)
-        for start in range(0, cells, PART):
-            rows = slice(start, start + PART)
-            scaled = grad_norm[rows, :] * vector(GAIN, every)
-            unit = unit_ref[0, rows, :]
-            mean = jnp.sum(scaled, axis=1, keepdims=True) * (1.0 / channels)
-            mean_unit = jnp.sum(scaled * unit, axis=1, keepdims=True) * (1.0 / channels)
-            inv = inv_ref[0, rows, 0:1]
-            for band in range(bands):
-                lanes = slice(band * LANES, (band + 1) * LANES)
-                depth_back_ref[0, band, rows, :] = inv * (
-                    scaled[:, lanes] - mean - unit[:, lanes] * mean_unit
-                )
 
     @pl.when(step == pl.num_programs(0) - 1)
     def _finish():
@@ -716,12 +777,18 @@
     last,
     table_ref,
     source_ref,
-    depth_back,
+    grad_pre_ref,
+    unit_ref,
+    inv_ref,
     before_ref,
+    vectors_ref,
+    expand_ref,
     out_ref,
     padded,
     tap_sums,
     tap_rows,
+    grad_norm,
+    depth_back,
 ):
     step = pl.program_id(0)
     filled = table_ref[FILLED + first + step]
@@ -739,6 +806,21 @@
 
     @pl.when(filled != 0)
     def _work():
+        cells = side * side
+        gain = vectors_ref[GAIN : GAIN + 1, 0:channels]
+        grad_norm[...] = mix_cols(grad_pre_ref[0], expand_ref[...])
+        for start in range(0, cells, PART):
+            rows = slice(start, start + PART)
+            scaled = grad_norm[rows, :] * gain
+            unit = unit_ref[0, rows, :]
+            mean = jnp.sum(scaled, axis=1, keepdims=True) * (1.0 / channels)
+            mean_unit = jnp.sum(scaled * unit, axis=1, keepdims=True) * (1.0 / channels)
+            inv = inv_ref[0, rows, 0:1]
+            for band in range(bands):
+                lanes = slice(band * LANES, (band + 1) * LANES)
+                depth_back[band, rows, :] = inv * (
+                    scaled[:, lanes] - mean - unit[:, lanes] * mean_unit
+                )
         edge = jnp.zeros((side, low, LANES), jnp.float32)
         for band in range(bands):
             lanes = slice(band * LANES, (band + 1) * LANES)
@@ -761,7 +843,7 @@
                         if 0 <= place < side:
                             if place not in grads:
                                 grads[place] = depth_back[
-                                    0, band, place * side : (place + 1) * side, :
+                                    band, place * side : (place + 1) * side, :
                                 ]
                             term = line * grads[place]
                             sums[row] = term if sums[row] is None else sums[row] + term
@@ -794,14 +876,13 @@
     return pl.BlockSpec((1,) + shape, lambda i, table: (i,) + (0,) * len(shape))
 
 
-def weight_grads(plan, table, embed_grad, saved, vectors, head, expand, reduce):
-    unit, inv, hidden, slope, head_slope = saved
+def weight_grads(plan, table, embed_grad, saved, vectors, head, reduce):
+    unit, hidden, slope, head_slope = saved
     cells, channels = unit.shape[1:]
-    hid, bands = expand.shape[1], channels // LANES
-    eye = jnp.asarray(np.eye(channels, dtype=np.float32), jnp.bfloat16)
-    streams = (embed_grad, hidden, head_slope, slope, unit, inv)
-    consts = (vectors, head, expand, reduce, eye)
-    back = pltpu.HBM((PROC, bands, cells, LANES), jnp.float32)
+    hid = reduce.shape[0]
+    streams = (embed_grad, hidden, head_slope, slope, unit)
+    consts = (vectors, head, reduce)
+    back = pltpu.HBM((PROC, cells, hid), jnp.bfloat16)
     blocks = jax.ShapeDtypeStruct(
         (2, plan.ys, plan.g2, plan.g1, plan.block_rows, channels), jnp.bfloat16
     )
@@ -814,7 +895,7 @@
             in_specs=[per_slot(stream) for stream in streams]
             + [whole(const.shape) for const in consts],
             out_specs=[
-                pl.BlockSpec((1, bands, cells, LANES), lambda i, table: (i, 0, 0, 0)),
+                pl.BlockSpec((1, cells, hid), lambda i, table: (i, 0, 0)),
                 HBM,
                 HBM,
             ],
@@ -824,7 +905,7 @@
                 pltpu.VMEM((PROC * cells, hid), jnp.bfloat16),
                 pltpu.VMEM((channels, PROC * cells), jnp.bfloat16),
                 pltpu.VMEM((cells, head.shape[1]), jnp.bfloat16),
-                pltpu.VMEM((cells, channels), jnp.float32),
+                pltpu.VMEM((channels, channels), jnp.bfloat16),
                 pltpu.VMEM((2,) + blocks.shape, jnp.bfloat16),
                 pltpu.SemaphoreType.DMA((2,)),
             ],
@@ -835,8 +916,8 @@
     )(table, *streams, *consts)
 
 
-def tap_grads(plan, first, last, table, source, depth_back, before):
-    side, channels = source.shape[1], source.shape[3]
+def tap_grads(plan, first, last, table, streams, before, vectors, expand):
+    side, channels = streams[0].shape[1], streams[0].shape[3]
     bands = channels // LANES
     sums = (bands, KS * KS, 8, LANES)
     out = (plan.devices, DEPTH_ROWS, channels) if last else sums
@@ -851,18 +932,21 @@
         grid_spec=pltpu.PrefetchScalarGridSpec(
             num_scalar_prefetch=1,
             grid=(PROC // 2,),
-            in_specs=[items(source), items(depth_back), whole(before.shape)],
+            in_specs=[items(stream) for stream in streams]
+            + [whole(before.shape), whole(vectors.shape), whole(expand.shape)],
             out_specs=pl.BlockSpec(out, lambda i, table: (0,) * len(out)),
             scratch_shapes=[
                 pltpu.VMEM((bands, side, side + ROW_UNIT, LANES), jnp.float32),
                 pltpu.VMEM(sums, jnp.float32),
                 pltpu.VMEM((KS * KS + 7, channels), jnp.float32),
+                pltpu.VMEM((side * side, channels), jnp.float32),
+                pltpu.VMEM((bands, side * side, LANES), jnp.float32),
             ],
         ),
-        compiler_params=pltpu.CompilerParams(vmem_limit_bytes=12 * MIB),
+        compiler_params=pltpu.CompilerParams(vmem_limit_bytes=16 * MIB),
         cost_estimate=cost(4.0),
         name="tap_grads_" + str(first),
-    )(table, source, depth_back, before)
+    )(table, *streams, before, vectors, expand)
 
 
 def shifted(values, names, sizes, shift):
@@ -962,37 +1046,32 @@
     smalls = [small] + [from_other(small, other) for other in range(1, slides)]
 
     consts = (depth_kernel, vectors, expand_weight, reduce_weight, head_weight)
-    saved = forward_block(0, PROC, table, (tile_maps, from_core), consts, ())
+    saved = forward_block(0, False, table, (tile_maps, from_core), *consts, ())
     for rank in range(places):
-        items = min(PROC, slides - 2)
-        saved = forward_block(1 + rank, items, table, arrived[rank], consts, saved)
-    section, tile_embed, unit, inv, hidden, slope, head_slope, source = saved
-    rows = tile_rows(table, tile_embed, smalls, devices).astype(jnp.bfloat16)
-    came = exchange(jnp.broadcast_to(rows, (devices,) + rows.shape[1:]), ALL)
-    came = came.reshape(devices * PROC, rows.shape[2])
-    filled = table[FILLED : FILLED + PROC] != 0
-    tile_out = jnp.where(filled[:, None, None, None], section[:PROC], jnp.zeros((), jnp.bfloat16))
-    came, tile_out = lax.optimization_barrier((came, tile_out))
+        saved = forward_block(1 + rank, rank + 1 == places, table, arrived[rank], *consts, saved)
+    tile_out, tile_embed, unit, inv, hidden, slope, head_slope, source = saved
+    came = exchange(tile_rows(table, tile_embed, smalls, devices), ALL)
+    came = came.reshape(devices * PROC, came.shape[2])
 
     feature, embed_grad = slide_grads(
         length, members, table, came, slide_taps, slide_weight, vectors, smalls
     )
-    depth_back, kept, sent = weight_grads(
+    grad_pre, kept, sent = weight_grads(
         plan,
         table,
         embed_grad,
-        (unit, inv, hidden, slope, head_slope),
+        (unit, hidden, slope, head_slope),
         vectors,
         head_weight,
-        expand_weight,
         reduce_weight,
     )
+    streams = (source, pinned(grad_pre), unit, inv)
 
     names = ("g2", "y")
     size = plan.ys
     came = other_core(sent)
     none = jnp.zeros((channels // LANES, KS * KS, 8, LANES), jnp.float32)
-    tap_sums = tap_grads(plan, 0, False, table, source, depth_back, none)
+    tap_sums = tap_grads(plan, 0, False, table, streams, none, vectors, expand_weight)
     came, tap_sums = lax.optimization_barrier((came, tap_sums))
     out = [
         [add_all([kept[kind, step], came[kind, step]]) for step in range(1, size)]
@@ -1001,7 +1080,7 @@
     stay = [add_all([kept[kind, 0], came[kind, 0]]) for kind in range(2)]
     out, tap_sums = lax.optimization_barrier((out, tap_sums))
     parts = [sum_axis(stay[kind], out[kind], names[kind], size) for kind in range(2)]
-    taps = tap_grads(plan, PROC // 2, True, table, source, depth_back, tap_sums)
+    taps = tap_grads(plan, PROC // 2, True, table, streams, tap_sums, vectors, expand_weight)
     out = [
         [add_all([part[step] for part in parts[kind]]) for step in range(1, size)]
         for kind in range(2)

time: 123 us -> 121 us (0.984); the launches traced: 124 us -> 120 us
  blocking collectives: 0 us -> 27 us
  starting transfers between devices: 29.4 us -> 16.2 us
  waiting for transfers between devices: 20.4 us -> 10.1 us
  local copies, waits for them, and re-layouts: 11.7 us -> 5.52 us
  other arithmetic: 3.59 us -> 0.63 us
  Pallas kernels: 56.9 us -> 58.5 us
    all_to_all x0 -> x1, blocking collectives: none -> 27 us  [exchange(): lax.all_to_all(values, names, split_axis=0, concat_axis=0, tiled=True)]
    all_to_all x2 -> x1, starting transfers between devices: 10.8 us -> 2.56 us  [exchange(): lax.all_to_all(values, names, split_axis=0, concat_axis=0, tiled=True)]
    all_to_all x2 -> x1, waiting for transfers between devices: 10.3 us -> 2.64 us  [exchange(): lax.all_to_all(values, names, split_axis=0, concat_axis=0, tiled=True)]
    unnamed x62 -> x44, local copies, waits for them, and re-layouts: 8.82 us -> 3.39 us
    ppermute x8, starting transfers between devices: 12 us -> 6.96 us  [from_other(): lax.ppermute(buffer, DP, [(index, index ^ other) for index in range(slide...]
    pallas_call x2, Pallas kernels: 7.47 us -> 12.3 us  [tap_grads(): pl.pallas_call(functools.partial(taps_kernel, plan, first, last), out_sha...]
    ppermute x8, waiting for transfers between devices: 9.84 us -> 7.4 us  [shifted(): return lax.ppermute(values, names, pairs)]
    pallas_call x3, Pallas kernels: 27 us -> 24.9 us  [forward_block(): pl.pallas_call(functools.partial(forward_kernel, kind, last, len(tiles),...]
  transfers between devices with their start and end apart: 18 -> 17, of which waited for: 8 -> 6; matrix products, arithmetic and copies ran while one was open for 3% -> 1% of each run, Pallas kernels for 28% -> 31%
where the time goes in v5:
time: 121 us; the launch traced here: 120 us
  Pallas kernels  58.5 us (48%)
  blocking collectives  27 us (22%)
  starting transfers between devices  16.2 us (13%)
  waiting for transfers between devices  10.1 us (8%)
  local copies, waits for them, and re-layouts  5.52 us (5%)
  between operations  1.73 us (1%)
    all_to_all x1, blocking collectives, exchange(): lax.all_to_all(values, names, split_axis=0, concat_axis=0, tiled=True)  27 us
    pallas_call x3, Pallas kernels, forward_block(): pl.pallas_call(functools.partial(forward_kernel, kind, last, len(tiles),...  24.9 us
    pallas_call x2, Pallas kernels, tap_grads(): pl.pallas_call(functools.partial(taps_kernel, plan, first, last), out_sha...  12.3 us
    pallas_call x1, Pallas kernels, weight_grads(): pl.pallas_call(functools.partial(weights_kernel, plan), out_shape=(back,...  11.6 us
    ppermute x8, waiting for transfers between devices, shifted(): return lax.ppermute(values, names, pairs)  7.4 us
    ppermute x8, starting transfers between devices, from_other(): lax.ppermute(buffer, DP, [(index, index ^ other) for index in range(slide...  6.96 us
    ppermute x8, starting transfers between devices, shifted(): return lax.ppermute(values, names, pairs)  6.68 us
    pallas_call x1, Pallas kernels, slide_grads(): pl.pallas_call(functools.partial(slide_kernel, length, members, slides),...  4.67 us
  transfers between devices with their start and end apart: 17, of which 6 were waited for; matrix products, arithmetic and copies ran while one was open for 1% of the time, Pallas kernels for 31%

profile of v5, /device:TPU:0, one launch (start us, length us, event | category | flops | bytes accessed | tf_op | source)
XLA Modules:
  0.0 119.6 jit_solution(2621391607158864058)
XLA Ops:
  1.3 0.7 copy-done.11
  2.0 2.8 %pack_tiles.1 = (bf16[2,16,16,384]{3,2,1,0:T(8,128)(2,1)S(1)}, bf16[1,16,16,384]{3,2,1,0:T(8,128)(2,1)S(1)}, bf16[1,16,16,384]{3,2,1,0:T(8,128)(2,1)S(1)}, bf16[...) custom-call(s32[1]{0:T(128)S(6)} %copy.56.counts_ref, ...), custom_call_target="tpu_custom_call" | custom-call | tf_op jit(solution)/shard_map/pack_tiles/pallas_call | solution.py:208
  4.8 0.0 copy-start.14
  4.8 0.0 copy-start.9
  4.8 0.4 collective-permute-start
  5.3 2.6 %collective-permute-start.3 = (bf16[1,16,16,384]{3,2,1,0:T(8,128)(2,1)S(1)}, bf16[1,16,16,384]{3,2,1,0:T(8,128)(2,1)S(1)}, u32[]{:S(2)}, u32[]{:S(2)}) collective-permute-start(bf16[1,16,16,384]{3,2,1,0:T(8,128)(2,1)S(1)} %get-tuple-element.62), channel_id=1, source_target_pairs={{0,16},{8,24},{16,0},{24,8},{1,17},{9,25},{17,1},{25,9},{2,18},{10... | collective-permute-start | bytes 589832 | tf_op jit(solution)/shard_map/ppermute | solution.py:1036
  7.9 0.1 collective-permute-start.4
  7.9 1.7 %collective-permute-start.1 = (bf16[1,16,16,384]{3,2,1,0:T(8,128)(2,1)S(1)}, bf16[1,16,16,384]{3,2,1,0:T(8,128)(2,1)S(1)}, u32[]{:S(2)}, u32[]{:S(2)}) collective-permute-start(bf16[1,16,16,384]{3,2,1,0:T(8,128)(2,1)S(1)} %get-tuple-element.59), channel_id=1, source_target_pairs={{0,16},{8,24},{16,0},{24,8},{1,17},{9,25},{17,1},{25,9},{2,18},{10... | collective-permute-start | bytes 589832 | tf_op jit(solution)/shard_map/ppermute | solution.py:1036
  9.7 0.4 collective-permute-start.5
  10.1 16.7 %forward_block_0.1 = (bf16[4,16,16,384]{3,2,1,0:T(8,128)(2,1)}, f32[4,8,768]{2,1,0:T(8,128)}, f32[4,256,384]{2,1,0:T(8,128)}, f32[4,256,128]{2,1,0:T(8,128)}, bf...) custom-call(s32[51]{0:T(128)S(1)} %get-tuple-element.55.table_ref, ...), custom_call_target="tpu_custom_call" | custom-call | flops 1000000000 | bytes 1024 | tf_op jit(solution)/shard_map/forward_block_0/pallas_call | solution.py:453
  26.8 0.1 collective-permute-start.6
  26.9 1.6 %collective-permute-start.7 = (f32[1,1152]{1,0:T(1,128)S(1)}, f32[1,1152]{1,0:T(1,128)S(1)}, u32[]{:S(2)}, u32[]{:S(2)}) collective-permute-start(f32[1,1152]{1,0:T(1,128)S(1)} %get-tuple-element.85.refs_0_), channel_id=1, source_target_pairs={{0,24},{8,16},{16,8},{24,0},{1,25},{9,17},{17,9},{25,1},{2,26},{10... | collective-permute-start | bytes 13832 | tf_op jit(solution)/shard_map/ppermute | solution.py:1036
  28.5 7.3 %forward_block_1.1 = (bf16[4,16,16,384]{3,2,1,0:T(8,128)(2,1)}, f32[4,8,768]{2,1,0:T(8,128)}, f32[4,256,384]{2,1,0:T(8,128)}, f32[4,256,128]{2,1,0:T(8,128)}, bf...) custom-call(s32[51]{0:T(128)S(1)} %get-tuple-element.55.table_ref, ...), custom_call_target="tpu_custom_call", output_to_operand_aliasing={{0}: (8, {}), {1}: (9, {}), {2}: (10, {}), {3}: (11, {}), {... | custom-call | flops 1000000000 | bytes 1024 | tf_op jit(solution)/shard_map/forward_block_1/pallas_call | solution.py:453
  35.9 0.8 forward_block_2.1
  36.8 0.5 copy-done.16
  37.3 0.0 copy-done.18
  37.4 0.0 copy-done.20
  37.4 2.2 %tile_rows.1 = bf16[32,4,896]{2,1,0:T(4,128)(2,1)} custom-call(s32[51]{0:T(128)} %copy-done.9, f32[4,8,768]{2,1,0:T(8,128)} %get-tuple-element.84.embed_ref, f32[1,1152]{1,0:T(1,128)} %copy-done.14, f32[1,1152]{1,0:T(1,128)} %copy-done.16, f32[1,1152]{1,0:T(1,128)} %copy-done.18, f32[1,1152]{1,0:T(1,128)} %copy-done.20), custom_call_target="tpu_custom_call" | custom-call | flops 1000000000 | bytes 1024 | tf_op jit(solution)/shard_map/tile_rows/pallas_call | solution.py:525
  39.6 27.0 %all_to_all.10 = bf16[32,4,896]{2,1,0:T(4,128)(2,1)S(1)} all-to-all(bf16[32,4,896]{2,1,0:T(4,128)(2,1)} %tile_rows.1), channel_id=1, replica_groups=mesh['y'=2,'core'=2,'g1'=4,'g2'=2] {'y','core','g1','g2'}, dimensions={0} | all-to-all | bytes 458752 | tf_op jit(solution)/shard_map/all_to_all | solution.py:977
  66.6 0.1 reshape.75.came_ref
  66.7 0.7 copy-done.17
  67.4 0.7 copy-done.19
  68.1 0.7 copy-done.21
  68.8 4.7 %slide_grads.1 = (f32[1,768]{1,0:T(1,128)}, f32[4,1,768]{2,1,0:T(1,128)S(1)}) custom-call(s32[51]{0:T(128)S(1)} %copy-done.10, bf16[128,896]{1,0:T(8,128)(2,1)S(1)} %reshape.75.came_ref, f32[7,768]{1,0:T(8,128)S(1)} %copy-done.13, bf16[768,768]{1,0:T(8,128)(2,1)S(1)} %copy-done.12, f32[8,1536]{1,0:T(8,128)S(1)} %get-tuple-element.61.refs_3_.vectors_ref, ...), custom_call_target="tpu_custom_call" | custom-call | flops 6000000000 | bytes 1024 | tf_op jit(solution)/shard_map/slide_grads/pallas_call | solution.py:616
  73.5 11.6 %weight_grads.1 = (bf16[4,256,1536]{2,1,0:T(8,128)(2,1)}, bf16[2,2,2,4,48,384]{5,4,3,2,1,0:T(8,128)(2,1)S(1)}, bf16[2,2,2,4,48,384]{5,4,3,2,1,0:T(8,128)(2,1)S(1)}) custom-call(s32[51]{0:T(128)S(1)} %copy-done.10, f32[4,1,768]{2,1,0:T(1,128)S(1)} %get-tuple-element.87.grad_ref, bf16[4,256,1536]{2,1,0:T(8,128)(2,1)S(1)} %copy-done, ...), custom_call_target="tpu_custom_call" | custom-call | flops 16000000000 | bytes 1024 | tf_op jit(solution)/shard_map/weight_grads/pallas_call | solution.py:889
  85.2 0.1 collective-permute-start.8
  85.3 5.8 %tap_grads_0.1.before_ref = f32[3,49,8,128]{3,2,1,0:T(8,128)S(1)} custom-call(s32[51]{0:T(128)S(1)} %copy-done.10, bf16[4,16,16,384]{3,2,1,0:T(8,128)(2,1)S(1)} %copy-done.7, bf16[4,256,1536]{2,1,0:T(8,128)(2,1)} %get-tuple-element.95.grad_pre_ref, f32[4,256,384]{2,1,0:T(8,128)S(1)} %copy-done.4, f32[4,256,128]{2,1,0:T(8,128)S(1)} %copy-done.8, ...), custom_call_target="tpu_custom_call" | custom-call | flops 4000000000 | bytes 1024 | tf_op jit(solution)/shard_map/tap_grads_0/pallas_call | solution.py:929
  91.2 0.3 add_convert_fusion
  91.5 1.4 %collective-permute-start.9 = (bf16[2,4,48,384]{3,2,1,0:T(8,128)(2,1)S(1)}, bf16[2,4,48,384]{3,2,1,0:T(8,128)(2,1)S(1)}, u32[]{:S(2)}, u32[]{:S(2)}) collective-permute-start(bf16[2,4,48,384]{3,2,1,0:T(8,128)(2,1)S(1)} %get-tuple-element.99), channel_id=1, source_target_pairs={{0,1},{1,0},{2,3},{3,2},{4,5},{5,4},{6,7},{7,6},{8,9},{9,8},{10,11... | collective-permute-start | bytes 884744 | tf_op jit(solution)/shard_map/ppermute | solution.py:966
  92.9 0.6 collective-permute-start.10
  93.4 6.5 %tap_grads_2.1 = bf16[32,4,384]{2,1,0:T(4,128)(2,1)} custom-call(s32[51]{0:T(128)S(1)} %copy-done.10, bf16[4,16,16,384]{3,2,1,0:T(8,128)(2,1)S(1)} %copy-done.7, bf16[4,256,1536]{2,1,0:T(8,128)(2,1)} %get-tuple-element.95.grad_pre_ref, f32[4,256,384]{2,1,0:T(8,128)S(1)} %copy-done.4, f32[4,256,128]{2,1,0:T(8,128)S(1)} %copy-done.8, ...), custom_call_target="tpu_custom_call" | custom-call | flops 4000000000 | bytes 1024 | tf_op jit(solution)/shard_map/tap_grads_2/pallas_call | solution.py:929
  99.9 1.1 collective-permute-done.9
  101.0 0.9 collective-permute-done.10
  101.9 0.6 collective-permute-start.11
  102.5 0.9 collective-permute-start.12
  103.4 2.6 %all-to-all-start.1 = ((bf16[32,4,384]{2,1,0:T(4,128)(2,1)}), bf16[32,4,384]{2,1,0:T(4,128)(2,1)S(1)}, u32[]{:S(2)}, u32[]{:S(2)}) async-start(bf16[32,4,384]{2,1,0:T(4,128)(2,1)} %tap_grads_2.1), calls=%async_computation.1 | async-start | bytes 196608 | tf_op jit(solution)/shard_map/all_to_all | solution.py:977
  106.0 1.1 collective-permute-done.11
  107.1 0.1 fusion.6
  107.2 0.5 collective-permute-done.12
  107.7 0.1 fusion.2
  107.8 2.1 %collective-permute-start.15 = (bf16[96,384]{1,0:T(8,128)(2,1)S(1)}, bf16[96,384]{1,0:T(8,128)(2,1)S(1)}, u32[]{:S(2)}, u32[]{:S(2)}) collective-permute-start(bf16[96,384]{1,0:T(8,128)(2,1)S(1)} %get-tuple-element.110), channel_id=1, source_target_pairs={{0,6},{2,0},{4,2},{6,4},{1,7},{3,1},{5,3},{7,5},{8,14},{10,8},{12,... | collective-permute-start | bytes 221192 | tf_op jit(solution)/shard_map/ppermute | solution.py:966
  109.9 1.1 collective-permute-start.13
  110.9 2.6 %all-to-all-done.1 = bf16[32,4,384]{2,1,0:T(4,128)(2,1)S(1)} async-done(((bf16[32,4,384]{2,1,0:T(4,128)(2,1)}), bf16[32,4,384]{2,1,0:T(4,128)(2,1)S(1)}, u32[]{:S(2)}, u32[]{:S(2)}) %all-to-all-start.1) | async-done | bytes 98336 | tf_op jit(solution)/shard_map/all_to_all | solution.py:977
  113.6 0.1 convert_reduce_fusion
  113.6 0.7 dynamic_slice.3
  114.3 3.9 %collective-permute-done.14 = bf16[96,384]{1,0:T(8,128)(2,1)S(1)} collective-permute-done((bf16[96,384]{1,0:T(8,128)(2,1)S(1)}, bf16[96,384]{1,0:T(8,128)(2,1)S(1)}, u32[]{:S(2)}, u32[]{:S(2)}) %collective-permute-start.14) | collective-permute-done | bytes 73760 | tf_op jit(solution)/shard_map/ppermute | solution.py:966
  118.3 0.7 reshape.77
  119.0 0.6 reshape.78
  (57 shorter events, 0.4 us)
Async XLA Ops:
  1.3 0.7 copy-start.11
  4.8 22.1 %copy-start.14 = (f32[1,1152]{1,0:T(1,128)}, f32[1,1152]{1,0:T(1,128)S(1)}, u32[]{:S(2)}) copy-start(f32[1,1152]{1,0:T(1,128)S(1)} %get-tuple-element.85.refs_0_) | copy-start | bytes 13828
  4.8 31.1 %copy-start.9 = (s32[51]{0:T(128)}, s32[51]{0:T(128)S(1)}, u32[]{:S(2)}) copy-start(s32[51]{0:T(128)S(1)} %get-tuple-element.55.table_ref) | copy-start | bytes 616
  4.8 3.1 %collective-permute-start = (bf16[2,16,16,384]{3,2,1,0:T(8,128)(2,1)S(1)}, bf16[2,16,16,384]{3,2,1,0:T(8,128)(2,1)S(1)}, u32[]{:S(2)}, u32[]{:S(2)}) collective-permute-start(bf16[2,16,16,384]{3,2,1,0:T(8,128)(2,1)S(1)} %get-tuple-element.58), channel_id=1, source_target_pairs={{0,8},{8,0},{16,24},{24,16},{1,9},{9,1},{17,25},{25,17},{2,10},{10... | collective-permute-start | bytes 1179656 | tf_op jit(solution)/shard_map/ppermute | solution.py:1036
  5.3 21.5 %collective-permute-start.3 = (bf16[1,16,16,384]{3,2,1,0:T(8,128)(2,1)S(1)}, bf16[1,16,16,384]{3,2,1,0:T(8,128)(2,1)S(1)}, u32[]{:S(2)}, u32[]{:S(2)}) collective-permute-start(bf16[1,16,16,384]{3,2,1,0:T(8,128)(2,1)S(1)} %get-tuple-element.62), channel_id=1, source_target_pairs={{0,16},{8,24},{16,0},{24,8},{1,17},{9,25},{17,1},{25,9},{2,18},{10... | collective-permute-start | bytes 589832 | tf_op jit(solution)/shard_map/ppermute | solution.py:1036
  7.9 19.0 %collective-permute-start.4 = (bf16[1,16,16,384]{3,2,1,0:T(8,128)(2,1)S(1)}, bf16[1,16,16,384]{3,2,1,0:T(8,128)(2,1)S(1)}, u32[]{:S(2)}, u32[]{:S(2)}) collective-permute-start(bf16[1,16,16,384]{3,2,1,0:T(8,128)(2,1)S(1)} %get-tuple-element.63), channel_id=1, source_target_pairs={{0,24},{8,16},{16,8},{24,0},{1,25},{9,17},{17,9},{25,1},{2,26},{10... | collective-permute-start | bytes 589832 | tf_op jit(solution)/shard_map/ppermute | solution.py:1036
  7.9 27.9 %collective-permute-start.1 = (bf16[1,16,16,384]{3,2,1,0:T(8,128)(2,1)S(1)}, bf16[1,16,16,384]{3,2,1,0:T(8,128)(2,1)S(1)}, u32[]{:S(2)}, u32[]{:S(2)}) collective-permute-start(bf16[1,16,16,384]{3,2,1,0:T(8,128)(2,1)S(1)} %get-tuple-element.59), channel_id=1, source_target_pairs={{0,16},{8,24},{16,0},{24,8},{1,17},{9,25},{17,1},{25,9},{2,18},{10... | collective-permute-start | bytes 589832 | tf_op jit(solution)/shard_map/ppermute | solution.py:1036
  9.7 26.2 %collective-permute-start.2 = (bf16[1,16,16,384]{3,2,1,0:T(8,128)(2,1)S(1)}, bf16[1,16,16,384]{3,2,1,0:T(8,128)(2,1)S(1)}, u32[]{:S(2)}, u32[]{:S(2)}) collective-permute-start(bf16[1,16,16,384]{3,2,1,0:T(8,128)(2,1)S(1)} %get-tuple-element.60), channel_id=1, source_target_pairs={{0,24},{8,16},{16,8},{24,0},{1,25},{9,17},{17,9},{25,1},{2,26},{10... | collective-permute-start | bytes 589832 | tf_op jit(solution)/shard_map/ppermute | solution.py:1036
  9.7 27.1 %collective-permute-start.5 = (f32[1,1152]{1,0:T(1,128)S(1)}, f32[1,1152]{1,0:T(1,128)S(1)}, u32[]{:S(2)}, u32[]{:S(2)}) collective-permute-start(f32[1,1152]{1,0:T(1,128)S(1)} %get-tuple-element.85.refs_0_), channel_id=1, source_target_pairs={{0,8},{8,0},{16,24},{24,16},{1,9},{9,1},{17,25},{25,17},{2,10},{10... | collective-permute-start | bytes 13832 | tf_op jit(solution)/shard_map/ppermute | solution.py:1036
  26.8 9.9 %collective-permute-start.6 = (f32[1,1152]{1,0:T(1,128)S(1)}, f32[1,1152]{1,0:T(1,128)S(1)}, u32[]{:S(2)}, u32[]{:S(2)}) collective-permute-start(f32[1,1152]{1,0:T(1,128)S(1)} %get-tuple-element.85.refs_0_), channel_id=1, source_target_pairs={{0,16},{8,24},{16,0},{24,8},{1,17},{9,25},{17,1},{25,9},{2,18},{10... | collective-permute-start | bytes 13832 | tf_op jit(solution)/shard_map/ppermute | solution.py:1036
  26.9 9.9 %collective-permute-start.7 = (f32[1,1152]{1,0:T(1,128)S(1)}, f32[1,1152]{1,0:T(1,128)S(1)}, u32[]{:S(2)}, u32[]{:S(2)}) collective-permute-start(f32[1,1152]{1,0:T(1,128)S(1)} %get-tuple-element.85.refs_0_), channel_id=1, source_target_pairs={{0,24},{8,16},{16,8},{24,0},{1,25},{9,17},{17,9},{25,1},{2,26},{10... | collective-permute-start | bytes 13832 | tf_op jit(solution)/shard_map/ppermute | solution.py:1036
  36.7 0.6 copy-start.16
  36.8 0.6 copy-start.18
  36.8 0.6 copy-start.20
  37.4 29.3 %copy-start.10 = (s32[51]{0:T(128)S(1)}, s32[51]{0:T(128)}, u32[]{:S(2)}) copy-start(s32[51]{0:T(128)} %copy-done.9) | copy-start | bytes 616
  37.4 29.3 %copy-start.12 = (bf16[768,768]{1,0:T(8,128)(2,1)S(1)}, bf16[768,768]{1,0:T(8,128)(2,1)}, u32[]{:S(2)}) copy-start(bf16[768,768]{1,0:T(8,128)(2,1)} %matrix_ref.1) | copy-start | bytes 3538948
  37.4 29.3 %copy-start.13 = (f32[7,768]{1,0:T(8,128)S(1)}, f32[7,768]{1,0:T(8,128)}, u32[]{:S(2)}) copy-start(f32[7,768]{1,0:T(8,128)} %taps_ref.1) | copy-start | bytes 64516
  37.4 29.3 %copy-start.15 = (f32[1,1152]{1,0:T(1,128)S(1)}, f32[1,1152]{1,0:T(1,128)}, u32[]{:S(2)}) copy-start(f32[1,1152]{1,0:T(1,128)} %copy-done.14) | copy-start | bytes 13828
  66.7 0.7 copy-start.17
  67.4 0.7 copy-start.19
  68.1 0.7 copy-start.21
  68.7 4.7 %copy-start = (bf16[4,256,1536]{2,1,0:T(8,128)(2,1)S(1)}, bf16[4,256,1536]{2,1,0:T(8,128)(2,1)}, u32[]{:S(2)}) copy-start(bf16[4,256,1536]{2,1,0:T(8,128)(2,1)} %get-tuple-element.88.hidden_ref) | copy-start | bytes 9437188
  68.7 4.7 %copy-start.1 = (bf16[4,256,1536]{2,1,0:T(8,128)(2,1)S(1)}, bf16[4,256,1536]{2,1,0:T(8,128)(2,1)}, u32[]{:S(2)}) copy-start(bf16[4,256,1536]{2,1,0:T(8,128)(2,1)} %get-tuple-element.90.slope_ref) | copy-start | bytes 9437188
  68.7 4.7 %copy-start.2 = (bf16[1536,384]{1,0:T(8,128)(2,1)S(1)}, bf16[1536,384]{1,0:T(8,128)(2,1)}, u32[]{:S(2)}) copy-start(bf16[1536,384]{1,0:T(8,128)(2,1)} %reduce_ref.1) | copy-start | bytes 3538948
  68.8 4.7 %copy-start.4 = (f32[4,256,384]{2,1,0:T(8,128)S(1)}, f32[4,256,384]{2,1,0:T(8,128)}, u32[]{:S(2)}) copy-start(f32[4,256,384]{2,1,0:T(8,128)} %get-tuple-element.91.unit_ref) | copy-start | bytes 4718596
  68.8 4.7 %copy-start.5 = (bf16[4,256,768]{2,1,0:T(8,128)(2,1)S(1)}, bf16[4,256,768]{2,1,0:T(8,128)(2,1)}, u32[]{:S(2)}) copy-start(bf16[4,256,768]{2,1,0:T(8,128)(2,1)} %get-tuple-element.89.head_slope_ref) | copy-start | bytes 4718596
  68.8 4.7 %copy-start.6 = (bf16[384,768]{1,0:T(8,128)(2,1)S(1)}, bf16[384,768]{1,0:T(8,128)(2,1)}, u32[]{:S(2)}) copy-start(bf16[384,768]{1,0:T(8,128)(2,1)} %head_ref.1) | copy-start | bytes 1769476
  73.5 11.8 %copy-start.3 = (bf16[384,1536]{1,0:T(8,128)(2,1)S(1)}, bf16[384,1536]{1,0:T(8,128)(2,1)}, u32[]{:S(2)}) copy-start(bf16[384,1536]{1,0:T(8,128)(2,1)} %expand_ref.3) | copy-start | bytes 3538948
  73.5 11.8 %copy-start.7 = (bf16[4,16,16,384]{3,2,1,0:T(8,128)(2,1)S(1)}, bf16[4,16,16,384]{3,2,1,0:T(8,128)(2,1)}, u32[]{:S(2)}) copy-start(bf16[4,16,16,384]{3,2,1,0:T(8,128)(2,1)} %get-tuple-element.94.source_ref) | copy-start | bytes 2359300
  73.5 11.8 %copy-start.8 = (f32[4,256,128]{2,1,0:T(8,128)S(1)}, f32[4,256,128]{2,1,0:T(8,128)}, u32[]{:S(2)}) copy-start(f32[4,256,128]{2,1,0:T(8,128)} %get-tuple-element.96.inv_ref) | copy-start | bytes 1572868
  85.2 6.0 %collective-permute-start.8 = (bf16[2,2,2,4,48,384]{5,4,3,2,1,0:T(8,128)(2,1)S(1)}, bf16[2,2,2,4,48,384]{5,4,3,2,1,0:T(8,128)(2,1)S(1)}, u32[]{:S(2)}, u32[]{:S(2)}) collective-permute-start(bf16[2,2,2,4,48,384]{5,4,3,2,1,0:T(8,128)(2,1)S(1)} %get-tuple-element.93), channel_id=1, source_target_pairs={{0,8},{8,0},{1,9},{9,1},{2,10},{10,2},{3,11},{11,3},{4,12},{12,4},... | collective-permute-start | bytes 3538952 | tf_op jit(solution)/shard_map/ppermute | solution.py:966
  91.5 9.5 %collective-permute-start.9 = (bf16[2,4,48,384]{3,2,1,0:T(8,128)(2,1)S(1)}, bf16[2,4,48,384]{3,2,1,0:T(8,128)(2,1)S(1)}, u32[]{:S(2)}, u32[]{:S(2)}) collective-permute-start(bf16[2,4,48,384]{3,2,1,0:T(8,128)(2,1)S(1)} %get-tuple-element.99), channel_id=1, source_target_pairs={{0,1},{1,0},{2,3},{3,2},{4,5},{5,4},{6,7},{7,6},{8,9},{9,8},{10,11... | collective-permute-start | bytes 884744 | tf_op jit(solution)/shard_map/ppermute | solution.py:966
  92.9 9.0 %collective-permute-start.10 = (bf16[2,4,48,384]{3,2,1,0:T(8,128)(2,1)S(1)}, bf16[2,4,48,384]{3,2,1,0:T(8,128)(2,1)S(1)}, u32[]{:S(2)}, u32[]{:S(2)}) collective-permute-start(bf16[2,4,48,384]{3,2,1,0:T(8,128)(2,1)S(1)} %get-tuple-element.100), channel_id=1, source_target_pairs={{0,16},{16,0},{1,17},{17,1},{2,18},{18,2},{3,19},{19,3},{4,20},{20... | collective-permute-start | bytes 884744 | tf_op jit(solution)/shard_map/ppermute | solution.py:966
  101.9 5.2 %collective-permute-start.11 = (bf16[4,48,384]{2,1,0:T(8,128)(2,1)S(1)}, bf16[4,48,384]{2,1,0:T(8,128)(2,1)S(1)}, u32[]{:S(2)}, u32[]{:S(2)}) collective-permute-start(bf16[4,48,384]{2,1,0:T(8,128)(2,1)S(1)} %fusion.9), channel_id=1, source_target_pairs={{0,16},{16,0},{1,17},{17,1},{2,18},{18,2},{3,19},{19,3},{4,20},{20... | collective-permute-start | bytes 442376 | tf_op jit(solution)/shard_map/ppermute | solution.py:966
  102.5 5.1 %collective-permute-start.12 = (bf16[4,48,384]{2,1,0:T(8,128)(2,1)S(1)}, bf16[4,48,384]{2,1,0:T(8,128)(2,1)S(1)}, u32[]{:S(2)}, u32[]{:S(2)}) collective-permute-start(bf16[4,48,384]{2,1,0:T(8,128)(2,1)S(1)} %fusion.10), channel_id=1, source_target_pairs={{0,1},{1,0},{2,3},{3,2},{4,5},{5,4},{6,7},{7,6},{8,9},{9,8},{10,11... | collective-permute-start | bytes 442376 | tf_op jit(solution)/shard_map/ppermute | solution.py:966
  103.4 10.1 %all-to-all-start.1 = ((bf16[32,4,384]{2,1,0:T(4,128)(2,1)}), bf16[32,4,384]{2,1,0:T(4,128)(2,1)S(1)}, u32[]{:S(2)}, u32[]{:S(2)}) async-start(bf16[32,4,384]{2,1,0:T(4,128)(2,1)} %tap_grads_2.1), calls=%async_computation.1 | async-start | bytes 196608 | tf_op jit(solution)/shard_map/all_to_all | solution.py:977
  107.8 6.6 %collective-permute-start.15 = (bf16[96,384]{1,0:T(8,128)(2,1)S(1)}, bf16[96,384]{1,0:T(8,128)(2,1)S(1)}, u32[]{:S(2)}, u32[]{:S(2)}) collective-permute-start(bf16[96,384]{1,0:T(8,128)(2,1)S(1)} %get-tuple-element.110), channel_id=1, source_target_pairs={{0,6},{2,0},{4,2},{6,4},{1,7},{3,1},{5,3},{7,5},{8,14},{10,8},{12,... | collective-permute-start | bytes 221192 | tf_op jit(solution)/shard_map/ppermute | solution.py:966
  109.9 8.3 %collective-permute-start.14 = (bf16[96,384]{1,0:T(8,128)(2,1)S(1)}, bf16[96,384]{1,0:T(8,128)(2,1)S(1)}, u32[]{:S(2)}, u32[]{:S(2)}) collective-permute-start(bf16[96,384]{1,0:T(8,128)(2,1)S(1)} %get-tuple-element.111), channel_id=1, source_target_pairs={{0,4},{2,6},{4,0},{6,2},{1,5},{3,7},{5,1},{7,3},{8,12},{10,14},{12... | collective-permute-start | bytes 221192 | tf_op jit(solution)/shard_map/ppermute | solution.py:966
  109.9 8.3 %collective-permute-start.13 = (bf16[96,384]{1,0:T(8,128)(2,1)S(1)}, bf16[96,384]{1,0:T(8,128)(2,1)S(1)}, u32[]{:S(2)}, u32[]{:S(2)}) collective-permute-start(bf16[96,384]{1,0:T(8,128)(2,1)S(1)} %get-tuple-element.109), channel_id=1, source_target_pairs={{0,2},{2,4},{4,6},{6,0},{1,3},{3,5},{5,7},{7,1},{8,10},{10,12},{12... | collective-permute-start | bytes 221192 | tf_op jit(solution)/shard_map/ppermute | solution.py:966

commit v6 on v5

--- a/solution.py
+++ b/solution.py
@@ -24,6 +24,7 @@
 LANES = 128
 ROW_UNIT = 16
 DEPTH_ROWS = 4
+TAP_ROWS = 8
 MIB = 1024 * 1024
 PART = 32
 WIDTH = 256
@@ -35,6 +36,7 @@
 HBM = pl.BlockSpec(memory_space=pl.ANY)
 IN_HBM = pl.BlockSpec(memory_space=pltpu.HBM)
 ROWS_AT, COLS_AT, COUNT_AT, SMALL = E, E + LANES, E + 2 * LANES, E + 3 * LANES
+PIECES = 3
 
 
 def whole(shape):
@@ -99,7 +101,9 @@
 
     def copy_of(index, slot):
         buffer, row, _ = targets[index]
-        return pltpu.make_async_copy(tiles_ref.at[slot], send_refs[buffer].at[row], sems.at[index])
+        side = tiles_ref.shape[1]
+        lines = send_refs[buffer].at[pl.ds(row * side, side)]
+        return pltpu.make_async_copy(tiles_ref.at[slot], lines, sems.at[index])
 
     for index in range(slides):
         count_ref[index] = 0
@@ -133,6 +137,17 @@
         small_ref[:, start : start + LANES] = jnp.zeros((1, LANES), jnp.float32)
         small_ref[:, start : start + slots] = pos_ref[row : row + 1, :].astype(jnp.float32)
     small_ref[:, COUNT_AT:SMALL] = jnp.full((1, LANES), counts_ref[0], jnp.int32).astype(jnp.float32)
+    channels = tiles_ref.shape[3]
+    extra = []
+    rest = small_ref[...]
+    for piece in range(PIECES):
+        part = rest.astype(jnp.bfloat16).astype(jnp.float32)
+        rest = rest - part
+        extra += [part[:, at : at + channels] for at in range(0, SMALL, channels)]
+    extra.append(jnp.zeros((ROW_UNIT - len(extra), channels), jnp.float32))
+    extra = jnp.concatenate(extra, axis=0).astype(jnp.bfloat16)
+    for ref in send_refs[: slides - 1]:
+        ref[ref.shape[0] - 1] = extra
     vectors_ref[...] = jnp.zeros(vectors_ref.shape, jnp.float32)
     for index, ref in enumerate(vector_refs):
         size = ref.shape[0]
@@ -201,14 +216,15 @@
     smem = pl.BlockSpec(memory_space=pltpu.SMEM)
     vmem = pl.BlockSpec(memory_space=pltpu.VMEM)
     buffers = 1 + places * (slides - 2)
-    shapes = [places] + [1] * (buffers - 1)
+    side = tile_maps.shape[1]
+    shapes = [places * side + 1] + [side + 1] * (slides - 2) + [side] * (buffers - slides + 1)
     widest = max(vector.shape[0] for vector in vectors)
     inputs = (positions, cotangent) + vectors
     fixed = [pinned(x) for x in (tile_maps,) + inputs]
     outs = pl.pallas_call(
         functools.partial(pack_kernel, slides, slots, places),
         out_shape=tuple(
-            jax.ShapeDtypeStruct((size,) + tile_maps.shape[1:], tile_maps.dtype) for size in shapes
+            jax.ShapeDtypeStruct((size,) + tile_maps.shape[2:], tile_maps.dtype) for size in shapes
         )
         + (
             jax.ShapeDtypeStruct((CLASSES + (1 + places) * CLASS_SIZE,), jnp.int32),
@@ -258,14 +274,15 @@
     ]
 
     def tile_copy(ref, row, buffer):
-        return pltpu.make_async_copy(ref.at[row], source_s.at[buffer], tile_sems.at[buffer])
+        lines = ref.at[row] if len(ref.shape) == 4 else ref.at[pl.ds(row * side, side)]
+        return pltpu.make_async_copy(lines, source_s.at[buffer], tile_sems.at[buffer])
 
     def load(item, buffer):
         origin = table_ref[class_field(kind, FROM) + item]
         place = 0
         for index, ref in enumerate(tile_refs):
             own = kind == 0 and index == 0
-            for row in range(1 if own else ref.shape[0]):
+            for row in range(1 if own else ref.shape[0] // side):
 
                 @pl.when(origin == place)
                 def _load():
@@ -417,14 +434,21 @@
                 keep(part, 0, buffer).wait()
 
     if last:
-        out_s[0] = jnp.zeros(out_s.shape[1:], out_s.dtype)
+        filled = sum(table_ref[FILLED + proc] for proc in range(PROC))
+
+        @pl.when(filled < PROC)
+        def _zeros():
+            for ref in held:
+                ref[0] = jnp.zeros(ref.shape[1:], ref.dtype)
+
         for proc in range(PROC):
 
             @pl.when(table_ref[FILLED + proc] == 0)
             def _empty():
-                copy = keep(0, proc, 0)
-                copy.start()
-                copy.wait()
+                for part in range(kept):
+                    keep(part, proc, 0).start()
+                wait_kept(0)
+                keep(kept - 1, proc, 0).wait()
 
 
 def pinned(array):
@@ -432,7 +456,7 @@
 
 
 def forward_block(kind, last, table, tiles, taps, vectors, expand, reduce, head, before):
-    side, channels = tiles[0].shape[1], tiles[0].shape[3]
+    side, channels = tiles[0].shape[-2:]
     cells, hid, embed = side * side, expand.shape[1], head.shape[1]
     bands = channels // LANES
     outs = (
@@ -483,10 +507,16 @@
     return pl.CostEstimate(flops=int(micros * 1e9), bytes_accessed=1024, transcendentals=0)
 
 
-def rows_kernel(slides, table_ref, embed_ref, *refs):
-    small_refs, (out_ref, rows_ref) = refs[:slides], refs[slides:]
+def rows_kernel(slides, table_ref, embed_ref, small_ref, *refs):
+    buffer_refs, (out_ref, smalls_ref, rows_ref, extra_ref, sems) = refs[: slides - 1], refs[slides - 1 :]
+    copies = [
+        pltpu.make_async_copy(ref.at[ref.shape[0] - 1], extra_ref.at[index], sems.at[index])
+        for index, ref in enumerate(buffer_refs)
+    ]
+    for copy in copies:
+        copy.start()
     my_slide, my_member = lax.axis_index(DP), lax.axis_index(GROUP)
-    devices = out_ref.shape[0]
+    channels = extra_ref.shape[2]
     half = E // 2
     channel = lax.broadcasted_iota(jnp.int32, (1, E), 1)
     inner = jnp.where(channel < half, channel, channel - half)
@@ -494,43 +524,61 @@
     frequency = jnp.exp((inner - odd).astype(jnp.float32) * (-math.log(10000.0) / half))
     phase = odd.astype(jnp.float32) * (0.5 * math.pi)
     lane = lax.broadcasted_iota(jnp.int32, (1, LANES), 1)
+    smalls_ref[0] = small_ref[...]
+    lines = SMALL // channels
+    for index, copy in enumerate(copies):
+        copy.wait()
+        extra = extra_ref[index].astype(jnp.float32)
+        for line in range(lines):
+            total = extra[line : line + 1]
+            for piece in range(1, PIECES):
+                total = total + extra[piece * lines + line : piece * lines + line + 1]
+            smalls_ref[1 + index, :, line * channels : (line + 1) * channels] = total
     for proc in range(PROC):
         filled = table_ref[FILLED + proc]
         slide = table_ref[SLIDE + proc]
         slot = table_ref[PLACE + proc]
-        spots = []
-        for start in (ROWS_AT, COLS_AT):
-            held = small_refs[0][:, start : start + LANES]
-            for other in range(1, slides):
-                held = jnp.where(
-                    (slide ^ my_slide) == other, small_refs[other][:, start : start + LANES], held
-                )
-            spots.append(jnp.sum(jnp.where(lane == slot, held, 0.0), axis=1, keepdims=True))
+        held = smalls_ref[0]
+        for other in range(1, slides):
+            held = jnp.where((slide ^ my_slide) == other, smalls_ref[other], held)
+        spots = [
+            jnp.sum(jnp.where(lane == slot, held[:, at : at + LANES], 0.0), axis=1, keepdims=True)
+            for at in (ROWS_AT, COLS_AT)
+        ]
         spot = jnp.where(channel < half, spots[0], spots[1])
         embed = embed_ref[proc, 0:1, :].astype(jnp.bfloat16).astype(jnp.float32)
         row = jnp.where(filled != 0, embed + jnp.sin(spot * frequency + phase), 0.0)
         target = jnp.where(lane == 0, slide, jnp.where(lane == 1, slot, my_member))
         target = jnp.where(filled != 0, target, jnp.where(lane == 2, -1, 0))
         target = jnp.where(lane < 3, target, 0)
-        rows_ref[proc : proc + 1, 0:E] = row
-        rows_ref[proc : proc + 1, E:] = target.astype(jnp.float32)
+        for copied in range(proc, ROW_UNIT, PROC):
+            rows_ref[copied : copied + 1, 0:E] = row
+            rows_ref[copied : copied + 1, E:] = target.astype(jnp.float32)
     sent = rows_ref[...].astype(jnp.bfloat16)
-    for device in range(devices):
-        out_ref[device] = sent
-
-
-def tile_rows(table, embeds, smalls, devices):
+    for start in range(0, out_ref.shape[0], ROW_UNIT):
+        out_ref[start : start + ROW_UNIT, :] = sent
+
+
+def tile_rows(table, embeds, small, buffers, devices):
     smem = pl.BlockSpec(memory_space=pltpu.SMEM)
     vmem = pl.BlockSpec(memory_space=pltpu.VMEM)
+    slides = 1 + len(buffers)
     return pl.pallas_call(
-        functools.partial(rows_kernel, len(smalls)),
-        out_shape=jax.ShapeDtypeStruct((devices, PROC, E + LANES), jnp.bfloat16),
-        in_specs=[smem] + [vmem] * (1 + len(smalls)),
-        out_specs=vmem,
-        scratch_shapes=[pltpu.VMEM((PROC, E + LANES), jnp.float32)],
+        functools.partial(rows_kernel, slides),
+        out_shape=(
+            jax.ShapeDtypeStruct((devices * PROC, E + LANES), jnp.bfloat16),
+            jax.ShapeDtypeStruct((slides, 1, SMALL), jnp.float32),
+        ),
+        in_specs=[smem, vmem, vmem] + [HBM] * len(buffers),
+        out_specs=(vmem, vmem),
+        scratch_shapes=[
+            pltpu.VMEM((ROW_UNIT, E + LANES), jnp.float32),
+            pltpu.VMEM((len(buffers),) + buffers[0].shape[1:], jnp.bfloat16),
+            pltpu.SemaphoreType.DMA((len(buffers),)),
+        ],
         cost_estimate=cost(1.0),
         name="tile_rows",
-    )(table, embeds, *smalls)
+    )(table, embeds, small, *buffers)
 
 
 def slide_kernel(
@@ -539,13 +587,27 @@
     slides,
     table_ref,
     came_ref,
+    taps_hbm,
+    matrix_hbm,
+    vectors_ref,
+    smalls_ref,
+    feature_ref,
+    grad_ref,
+    rows,
+    back,
+    mixed,
+    pre,
+    grad_agg,
     taps_ref,
     matrix_ref,
-    vectors_ref,
-    *refs,
+    sems,
 ):
-    small_refs = refs[:slides]
-    feature_ref, grad_ref, rows, back, mixed, pre, grad_agg = refs[slides:]
+    loads = [
+        pltpu.make_async_copy(taps_hbm, taps_ref, sems.at[0]),
+        pltpu.make_async_copy(matrix_hbm, matrix_ref, sems.at[1]),
+    ]
+    for load in loads:
+        load.start()
     my_slide = lax.axis_index(DP)
     border = ROW_UNIT
     edge = jnp.zeros((border, rows.shape[2]), jnp.float32)
@@ -565,7 +627,7 @@
 
     for other in range(slides):
         slide = my_slide ^ other
-        small = small_refs[other]
+        small = smalls_ref[other]
         count = small[:, COUNT_AT : COUNT_AT + 1]
         here = step < count
         share = jnp.where(here, 1.0 / count, 0.0)
@@ -574,11 +636,15 @@
         for ref in (rows, back):
             ref[slide, 0:border, :] = edge
             ref[slide, border + length :, :] = edge
+        if other == 0:
+            loads[0].wait()
         for cols in blocks:
             rows[slide, border : border + length, cols] = jnp.where(
                 here, mix(pick, came_ref[:, cols]), 0.0
             )
             mixed[:, cols] = dilate(rows, slide, 1, cols).astype(jnp.bfloat16)
+        if other == 0:
+            loads[1].wait()
         for cols in blocks:
             pre[:, cols] = mix(mixed[...], matrix_ref[:, cols])
             total = None
@@ -609,7 +675,7 @@
 
 
 def slide_grads(length, members, table, came, taps, matrix, vectors, smalls):
-    slides = len(smalls)
+    slides = smalls.shape[0]
     smem = pl.BlockSpec(memory_space=pltpu.SMEM)
     vmem = pl.BlockSpec(memory_space=pltpu.VMEM)
     padded = (slides, length + 2 * ROW_UNIT, E)
@@ -619,7 +685,7 @@
             jax.ShapeDtypeStruct((1, E), jnp.float32),
             jax.ShapeDtypeStruct((PROC, 1, E), jnp.float32),
         ),
-        in_specs=[smem] + [vmem] * (4 + slides),
+        in_specs=[smem, vmem, IN_HBM, IN_HBM, vmem, vmem],
         out_specs=(vmem, vmem),
         scratch_shapes=[
             pltpu.VMEM(padded, jnp.float32),
@@ -627,11 +693,14 @@
             pltpu.VMEM((length, E), jnp.bfloat16),
             pltpu.VMEM((length, E), jnp.float32),
             pltpu.VMEM((length, E), jnp.bfloat16),
+            pltpu.VMEM(taps.shape, jnp.float32),
+            pltpu.VMEM(matrix.shape, jnp.bfloat16),
+            pltpu.SemaphoreType.DMA((2,)),
         ],
         compiler_params=pltpu.CompilerParams(vmem_limit_bytes=24 * MIB),
         cost_estimate=cost(6.0),
         name="slide_grads",
-    )(table, came, taps, matrix, vectors, *smalls)
+    )(table, came, pinned(taps), pinned(matrix), vectors, smalls)
 
 
 class Plan:
@@ -679,7 +748,6 @@
 
 def weights_kernel(
     plan,
-    table_ref,
     grad_ref,
     hidden_ref,
     head_slope_ref,
@@ -688,87 +756,86 @@
     vectors_ref,
     head_ref,
     reduce_ref,
-    grad_pre_ref,
+    grad_pre_hbm,
     keep_ref,
     send_ref,
-    hidden_all,
-    grad_mlp_all,
-    grad_pre_all,
-    normed_all,
+    grad_pre,
+    turned,
+    normed,
     grad_head,
     eye_ref,
     staged,
     sems,
+    pre_sems,
 ):
-    step = pl.program_id(0)
-    filled = table_ref[FILLED + step]
     cells, channels = unit_ref.shape[1:]
-    rows_all = pl.ds(pl.multiple_of(step * cells, cells), cells)
+    hid = reduce_ref.shape[0]
     every = slice(0, channels)
 
     def vector(index, lanes):
         return vectors_ref[index : index + 1, lanes]
 
-    @pl.when(step == 0)
-    def _start():
-        spot = lax.broadcasted_iota(jnp.int32, eye_ref.shape, 0)
-        same = spot == lax.broadcasted_iota(jnp.int32, eye_ref.shape, 1)
-        eye_ref[...] = same.astype(jnp.float32).astype(jnp.bfloat16)
-
-    @pl.when(filled == 0)
-    def _empty():
-        for ref in (hidden_all, grad_pre_all):
-            ref[rows_all, :] = jnp.zeros((cells, ref.shape[1]), jnp.bfloat16)
-        for ref in (grad_mlp_all, normed_all):
-            ref[:, rows_all] = jnp.zeros((channels, cells), jnp.bfloat16)
-
-    @pl.when(filled != 0)
-    def _work():
+    spot = lax.broadcasted_iota(jnp.int32, eye_ref.shape, 0)
+    same = spot == lax.broadcasted_iota(jnp.int32, eye_ref.shape, 1)
+    eye_ref[...] = same.astype(jnp.float32).astype(jnp.bfloat16)
+
+    def one_slot(slot, carry):
+        rows_all = pl.ds(pl.multiple_of(slot * cells, cells), cells)
+        row = grad_ref[slot] * (1.0 / cells)
         for start in range(0, cells, PART):
             rows = slice(start, start + PART)
-            grad_head[rows, :] = (
-                (grad_ref[0] * (1.0 / cells)) * head_slope_ref[0, rows, :].astype(jnp.float32)
+            grad_head[rows, :] = (row * head_slope_ref[slot, rows, :].astype(jnp.float32)).astype(
+                jnp.bfloat16
+            )
+            normed[rows, :] = (
+                unit_ref[slot, rows, :] * vector(GAIN, every) + vector(SHIFT, every)
             ).astype(jnp.bfloat16)
         grad_mlp = (vector(SCALE, every) * mix_cols(grad_head[...], head_ref[...])).astype(
             jnp.bfloat16
         )
-        grad_mlp_all[:, rows_all] = mix_cols(eye_ref[...], grad_mlp).astype(jnp.bfloat16)
-        hidden_all[rows_all, :] = hidden_ref[0]
-        for begin in range(0, reduce_ref.shape[0], WIDTH):
+        turned[0, :, rows_all] = mix_cols(eye_ref[...], grad_mlp).astype(jnp.bfloat16)
+        turned[1, :, rows_all] = mix_cols(eye_ref[...], normed[...]).astype(jnp.bfloat16)
+        for begin in range(0, hid, WIDTH):
             cols = slice(begin, begin + WIDTH)
             grad_hidden = mix_cols(grad_mlp, reduce_ref[cols, :])
-            grad_pre = (grad_hidden * slope_ref[0, :, cols].astype(jnp.float32)).astype(
-                jnp.bfloat16
-            )
-            grad_pre_all[rows_all, cols] = grad_pre
-            grad_pre_ref[0, :, cols] = grad_pre
-        normed = (unit_ref[0] * vector(GAIN, every) + vector(SHIFT, every)).astype(jnp.bfloat16)
-        normed_all[:, rows_all] = mix_cols(eye_ref[...], normed).astype(jnp.bfloat16)
-
-    @pl.when(step == pl.num_programs(0) - 1)
-    def _finish():
-        spots = list(plan.spots())
-        per_block = channels // plan.reduce_rows
-        tall = plan.block_rows
-        for index in range(plan.pieces):
-            cols = slice(index * channels, (index + 1) * channels)
-            total = mix(grad_mlp_all[...], hidden_all[:, cols]).astype(jnp.bfloat16)
-            turned = mix_cols(eye_ref[...], total)
-            for part in range(per_block):
-                block = turned[part * plan.reduce_rows : (part + 1) * plan.reduce_rows]
-                core, y, x, z = spots[index * per_block + part]
-                staged[core, 0, x, y, z] = padded_block(block, tall)
-        totals = []
-        for quarter in range(plan.pieces):
-            cols = slice(quarter * channels, (quarter + 1) * channels)
-            totals.append(mix(normed_all[...], grad_pre_all[:, cols]))
-        size = plan.expand_rows
-        for device in range(plan.devices):
-            rows = slice(device * size, (device + 1) * size)
-            block = jnp.concatenate([total[rows] for total in totals], axis=0)
-            core, y, x, z = spots[device]
-            staged[core, 1, y, x, z] = padded_block(block, tall)
-        send_out(staged, sems, (keep_ref, send_ref))
+            grad_pre[rows_all, cols] = (
+                grad_hidden * slope_ref[slot, :, cols].astype(jnp.float32)
+            ).astype(jnp.bfloat16)
+        return carry
+
+    lax.fori_loop(0, PROC, one_slot, 0)
+    writes = [
+        pltpu.make_async_copy(
+            grad_pre.at[pl.ds(slot * cells, cells)], grad_pre_hbm.at[slot], pre_sems.at[slot]
+        )
+        for slot in range(PROC)
+    ]
+    for write in writes:
+        write.start()
+    spots = list(plan.spots())
+    per_block = channels // plan.reduce_rows
+    tall = plan.block_rows
+    for index in range(plan.pieces):
+        cols = slice(index * channels, (index + 1) * channels)
+        total = mix(turned[0], hidden_ref[:, cols]).astype(jnp.bfloat16)
+        back = mix_cols(eye_ref[...], total)
+        for part in range(per_block):
+            block = back[part * plan.reduce_rows : (part + 1) * plan.reduce_rows]
+            core, y, x, z = spots[index * per_block + part]
+            staged[core, 0, x, y, z] = padded_block(block, tall)
+    totals = []
+    for quarter in range(plan.pieces):
+        cols = slice(quarter * channels, (quarter + 1) * channels)
+        totals.append(mix(turned[1], grad_pre[:, cols]))
+    size = plan.expand_rows
+    for device in range(plan.devices):
+        rows = slice(device * size, (device + 1) * size)
+        block = jnp.concatenate([total[rows] for total in totals], axis=0)
+        core, y, x, z = spots[device]
+        staged[core, 1, y, x, z] = padded_block(block, tall)
+    send_out(staged, sems, (keep_ref, send_ref))
+    for write in writes:
+        write.wait()
 
 
 def taps_kernel(
@@ -866,9 +933,15 @@
             lanes = slice(band * LANES, (band + 1) * LANES)
             tap_rows[0 : KS * KS, lanes] = jnp.sum(tap_sums[band], axis=1)
             tap_rows[KS * KS :, lanes] = jnp.zeros((tap_rows.shape[0] - KS * KS, LANES), jnp.float32)
-        for device in range(plan.devices):
-            start = device * plan.share // channels
-            out_ref[device] = tap_rows[start : start + DEPTH_ROWS, :].astype(jnp.bfloat16)
+        my_z = lax.axis_index("g1")
+        for part in range(2 * plan.ys * plan.g2):
+            cross, core = divmod(part, 2)
+            y, x = divmod(cross, plan.g2)
+            for z in range(plan.g1):
+                away = lax.rem(z - my_z + plan.g1, plan.g1)
+                device = ((y * 2 + core) * plan.g1 + z) * plan.g2 + x
+                start = device * plan.share // channels
+                out_ref[part, away] = tap_rows[start : start + TAP_ROWS, :]
 
 
 def per_slot(array):
@@ -876,51 +949,40 @@
     return pl.BlockSpec((1,) + shape, lambda i, table: (i,) + (0,) * len(shape))
 
 
-def weight_grads(plan, table, embed_grad, saved, vectors, head, reduce):
+def weight_grads(plan, embed_grad, saved, vectors, head, reduce):
     unit, hidden, slope, head_slope = saved
     cells, channels = unit.shape[1:]
     hid = reduce.shape[0]
-    streams = (embed_grad, hidden, head_slope, slope, unit)
-    consts = (vectors, head, reduce)
-    back = pltpu.HBM((PROC, cells, hid), jnp.bfloat16)
+    vmem = pl.BlockSpec(memory_space=pltpu.VMEM)
     blocks = jax.ShapeDtypeStruct(
         (2, plan.ys, plan.g2, plan.g1, plan.block_rows, channels), jnp.bfloat16
     )
     return pl.pallas_call(
         functools.partial(weights_kernel, plan),
-        out_shape=(back, blocks, blocks),
-        grid_spec=pltpu.PrefetchScalarGridSpec(
-            num_scalar_prefetch=1,
-            grid=(PROC,),
-            in_specs=[per_slot(stream) for stream in streams]
-            + [whole(const.shape) for const in consts],
-            out_specs=[
-                pl.BlockSpec((1, cells, hid), lambda i, table: (i, 0, 0)),
-                HBM,
-                HBM,
-            ],
-            scratch_shapes=[
-                pltpu.VMEM((PROC * cells, hid), jnp.bfloat16),
-                pltpu.VMEM((channels, PROC * cells), jnp.bfloat16),
-                pltpu.VMEM((PROC * cells, hid), jnp.bfloat16),
-                pltpu.VMEM((channels, PROC * cells), jnp.bfloat16),
-                pltpu.VMEM((cells, head.shape[1]), jnp.bfloat16),
-                pltpu.VMEM((channels, channels), jnp.bfloat16),
-                pltpu.VMEM((2,) + blocks.shape, jnp.bfloat16),
-                pltpu.SemaphoreType.DMA((2,)),
-            ],
-        ),
-        compiler_params=pltpu.CompilerParams(vmem_limit_bytes=32 * MIB),
-        cost_estimate=cost(16.0),
+        out_shape=(pltpu.HBM((PROC, cells, hid), jnp.bfloat16), blocks, blocks),
+        in_specs=[vmem] * 8,
+        out_specs=(IN_HBM, HBM, HBM),
+        scratch_shapes=[
+            pltpu.VMEM((PROC * cells, hid), jnp.bfloat16),
+            pltpu.VMEM((2, channels, PROC * cells), jnp.bfloat16),
+            pltpu.VMEM((cells, channels), jnp.bfloat16),
+            pltpu.VMEM((cells, head.shape[1]), jnp.bfloat16),
+            pltpu.VMEM((channels, channels), jnp.bfloat16),
+            pltpu.VMEM((2,) + blocks.shape, jnp.bfloat16),
+            pltpu.SemaphoreType.DMA((2,)),
+            pltpu.SemaphoreType.DMA((PROC,)),
+        ],
+        compiler_params=pltpu.CompilerParams(vmem_limit_bytes=36 * MIB),
+        cost_estimate=cost(12.0),
         name="weight_grads",
-    )(table, *streams, *consts)
+    )(embed_grad, hidden.reshape(PROC * cells, hid), head_slope, slope, unit, vectors, head, reduce)
 
 
 def tap_grads(plan, first, last, table, streams, before, vectors, expand):
     side, channels = streams[0].shape[1], streams[0].shape[3]
     bands = channels // LANES
     sums = (bands, KS * KS, 8, LANES)
-    out = (plan.devices, DEPTH_ROWS, channels) if last else sums
+    out = (2 * plan.ys * plan.g2, plan.g1, TAP_ROWS, channels) if last else sums
 
     def items(array):
         shape = array.shape[1:]
@@ -928,7 +990,7 @@
 
     return pl.pallas_call(
         functools.partial(taps_kernel, plan, first, last),
-        out_shape=jax.ShapeDtypeStruct(out, jnp.bfloat16 if last else jnp.float32),
+        out_shape=jax.ShapeDtypeStruct(out, jnp.float32),
         grid_spec=pltpu.PrefetchScalarGridSpec(
             num_scalar_prefetch=1,
             grid=(PROC // 2,),
@@ -1042,23 +1104,20 @@
         if rank:
             buffers, from_core = lax.optimization_barrier((buffers, from_core))
         arrived.append([from_other(buffer, other + 2) for other, buffer in enumerate(buffers)])
-    small, from_core = lax.optimization_barrier((small, from_core))
-    smalls = [small] + [from_other(small, other) for other in range(1, slides)]
 
     consts = (depth_kernel, vectors, expand_weight, reduce_weight, head_weight)
     saved = forward_block(0, False, table, (tile_maps, from_core), *consts, ())
     for rank in range(places):
         saved = forward_block(1 + rank, rank + 1 == places, table, arrived[rank], *consts, saved)
     tile_out, tile_embed, unit, inv, hidden, slope, head_slope, source = saved
-    came = exchange(tile_rows(table, tile_embed, smalls, devices), ALL)
-    came = came.reshape(devices * PROC, came.shape[2])
+    came, smalls = tile_rows(table, tile_embed, small, [from_core] + arrived[0], devices)
+    came = exchange(came, ALL)
 
     feature, embed_grad = slide_grads(
         length, members, table, came, slide_taps, slide_weight, vectors, smalls
     )
     grad_pre, kept, sent = weight_grads(
         plan,
-        table,
         embed_grad,
         (unit, hidden, slope, head_slope),
         vectors,
@@ -1087,9 +1146,10 @@
     ]
     stay = [add_all([part[0] for part in parts[kind]]) for kind in range(2)]
     out, taps = lax.optimization_barrier((out, taps))
-    taps = exchange(taps, ALL)
     parts = [sum_axis(stay[kind], out[kind], names[1 - kind], size) for kind in range(2)]
-    both = jnp.concatenate([add_all(parts[0]), add_all(parts[1])], axis=1)
+    taps = exchange(taps[:, :, :DEPTH_ROWS].astype(jnp.bfloat16), ("y", "g2", "core"))
+    taps = jnp.sum(taps.astype(jnp.float32), axis=0).astype(jnp.bfloat16)
+    both = jnp.concatenate([add_all(parts[0]), add_all(parts[1]), taps], axis=1)
     total = add_all(
         sum_axis(both[0], [both[step] for step in range(1, plan.g1)], "g1", plan.g1), jnp.float32
     )
@@ -1097,7 +1157,7 @@
     expand_share = total[plan.block_rows : plan.block_rows + plan.pieces * plan.expand_rows]
     expand_share = expand_share.reshape(plan.pieces, plan.expand_rows, channels).transpose(1, 0, 2)
     depth_share = lax.dynamic_slice(
-        jnp.sum(taps.astype(jnp.float32), axis=0).reshape(-1),
+        total[2 * plan.block_rows :].reshape(-1),
         (my_device * plan.share % channels,),
         (plan.share,),
     )

time: 121 us -> 119 us (0.983)
  blocking collectives: 27 us -> 20.1 us
  waiting for transfers between devices: 10.1 us -> 15.4 us
    all_to_all x1, blocking collectives: 27 us -> 20.1 us  [exchange(): lax.all_to_all(values, names, split_axis=0, concat_axis=0, tiled=True)]
    ppermute x8, waiting for transfers between devices: 7.4 us -> 12.1 us  [shifted(): return lax.ppermute(values, names, pairs)]
    ppermute x8 -> x5, starting transfers between devices: 6.96 us -> 4.88 us  [from_other(): lax.ppermute(buffer, DP, [(index, index ^ other) for index in range(slide...]
    unnamed x44 -> x34, local copies, waits for them, and re-layouts: 3.39 us -> 1.46 us
    pallas_call x1, Pallas kernels: 4.67 us -> 6 us  [slide_grads(): pl.pallas_call(functools.partial(slide_kernel, length, members, slides),...]
  transfers between devices with their start and end apart: 17 -> 14, of which waited for: 6 -> 6; matrix products, arithmetic and copies ran while one was open for 1% -> 1% of each run, Pallas kernels for 31% -> 30%
where the time goes in v6:
time: 119 us; the launch traced here: 118 us
  Pallas kernels  59.2 us (50%)
  blocking collectives  20.1 us (17%)
  starting transfers between devices  15.7 us (13%)
  waiting for transfers between devices  15.4 us (13%)
  local copies, waits for them, and re-layouts  5.28 us (4%)
  between operations  1.74 us (1%)
    pallas_call x3, Pallas kernels, forward_block(): pl.pallas_call(functools.partial(forward_kernel, kind, last, len(tiles),...  25.1 us
    all_to_all x1, blocking collectives, exchange(): lax.all_to_all(values, names, split_axis=0, concat_axis=0, tiled=True)  20.1 us
    ppermute x8, waiting for transfers between devices, shifted(): return lax.ppermute(values, names, pairs)  12.1 us
    pallas_call x2, Pallas kernels, tap_grads(): pl.pallas_call(functools.partial(taps_kernel, plan, first, last), out_sha...  11.7 us
    pallas_call x1, Pallas kernels, weight_grads(): pl.pallas_call(functools.partial(weights_kernel, plan), out_shape=(pltpu....  10.8 us
    ppermute x8, starting transfers between devices, shifted(): return lax.ppermute(values, names, pairs)  7.48 us
    pallas_call x1, Pallas kernels, slide_grads(): pl.pallas_call(functools.partial(slide_kernel, length, members, slides),...  6 us
    ppermute x5, starting transfers between devices, from_other(): lax.ppermute(buffer, DP, [(index, index ^ other) for index in range(slide...  4.88 us
  transfers between devices with their start and end apart: 14, of which 6 were waited for; matrix products, arithmetic and copies ran while one was open for 1% of the time, Pallas kernels for 30%

profile of v6, /device:TPU:0, one launch (start us, length us, event | category | flops | bytes accessed | tf_op | source)
XLA Modules:
  0.0 118.1 jit_solution(14485242710542933013)
XLA Ops:
  1.3 0.7 copy-done.14
  2.0 2.8 %pack_tiles.1 = (bf16[33,16,384]{2,1,0:T(8,128)(2,1)S(1)}, bf16[17,16,384]{2,1,0:T(8,128)(2,1)S(1)}, bf16[17,16,384]{2,1,0:T(8,128)(2,1)S(1)}, bf16[16,16,384]{2...) custom-call(s32[1]{0:T(128)S(6)} %copy.56.counts_ref, ...), custom_call_target="tpu_custom_call" | custom-call | tf_op jit(solution)/shard_map/pack_tiles/pallas_call | solution.py:224
  4.8 0.0 copy-start.15
  4.8 0.0 copy-start.12
  4.8 0.5 collective-permute-start
  5.3 2.6 %collective-permute-start.3 = (bf16[17,16,384]{2,1,0:T(8,128)(2,1)S(1)}, bf16[17,16,384]{2,1,0:T(8,128)(2,1)S(1)}, u32[]{:S(2)}, u32[]{:S(2)}) collective-permute-start(bf16[17,16,384]{2,1,0:T(8,128)(2,1)S(1)} %get-tuple-element.62), channel_id=1, source_target_pairs={{0,16},{8,24},{16,0},{24,8},{1,17},{9,25},{17,1},{25,9},{2,18},{10... | collective-permute-start | bytes 626696 | tf_op jit(solution)/shard_map/ppermute | solution.py:1098
  7.9 0.1 collective-permute-start.4
  7.9 0.0 collective-permute-done.refs_1_.refs_0_
  8.0 1.7 %collective-permute-start.1 = (bf16[16,16,384]{2,1,0:T(8,128)(2,1)S(1)}, bf16[16,16,384]{2,1,0:T(8,128)(2,1)S(1)}, u32[]{:S(2)}, u32[]{:S(2)}) collective-permute-start(bf16[16,16,384]{2,1,0:T(8,128)(2,1)S(1)} %get-tuple-element.59), channel_id=1, source_target_pairs={{0,16},{8,24},{16,0},{24,8},{1,17},{9,25},{17,1},{25,9},{2,18},{10... | collective-permute-start | bytes 589832 | tf_op jit(solution)/shard_map/ppermute | solution.py:1098
  9.7 0.0 collective-permute-start.2
  9.7 16.7 %forward_block_0.1 = (bf16[4,16,16,384]{3,2,1,0:T(8,128)(2,1)}, f32[4,8,768]{2,1,0:T(8,128)}, f32[4,256,384]{2,1,0:T(8,128)}, f32[4,256,128]{2,1,0:T(8,128)}, bf...) custom-call(s32[51]{0:T(128)S(1)} %get-tuple-element.55.table_ref, ...), custom_call_target="tpu_custom_call" | custom-call | flops 1000000000 | bytes 1024 | tf_op jit(solution)/shard_map/forward_block_0/pallas_call | solution.py:477
  26.4 7.4 %forward_block_1.1 = (bf16[4,16,16,384]{3,2,1,0:T(8,128)(2,1)}, f32[4,8,768]{2,1,0:T(8,128)}, f32[4,256,384]{2,1,0:T(8,128)}, f32[4,256,128]{2,1,0:T(8,128)}, bf...) custom-call(s32[51]{0:T(128)S(1)} %get-tuple-element.55.table_ref, ...), custom_call_target="tpu_custom_call", output_to_operand_aliasing={{0}: (8, {}), {1}: (9, {}), {2}: (10, {}), {3}: (11, {}), {... | custom-call | flops 1000000000 | bytes 1024 | tf_op jit(solution)/shard_map/forward_block_1/pallas_call | solution.py:477
  33.9 1.1 forward_block_2.1
  35.0 0.0 copy-start.13
  35.0 2.8 %tile_rows.1 = (bf16[128,896]{1,0:T(8,128)(2,1)}, f32[4,1,1152]{2,1,0:T(1,128)}) custom-call(s32[51]{0:T(128)} %copy-done.12, f32[4,8,768]{2,1,0:T(8,128)} %get-tuple-element.82.embed_ref, f32[1,1152]{1,0:T(1,128)} %copy-done.15, bf16[33,16,384]{2,1,0:T(8,128)(2,1)} %copy-done.9, bf16[17,16,384]{2,1,0:T(8,128)(2,1)} %copy-done.10, ...), custom_call_target="tpu_custom_call" | custom-call | flops 1000000000 | bytes 1024 | tf_op jit(solution)/shard_map/tile_rows/pallas_call | solution.py:566
  37.8 1.0 all_to_all.10
  38.8 20.1 %all_to_all.16 = bf16[32,4,896]{2,1,0:T(4,128)(2,1)S(1)} all-to-all(bf16[32,4,896]{2,1,0:T(4,128)(2,1)S(1)} %all_to_all.10), channel_id=1, replica_groups=mesh['y'=2,'core'=2,'g1'=4,'g2'=2] {'y','core','g1','g2'}, dimensions={0} | all-to-all | bytes 458752 | tf_op jit(solution)/shard_map/all_to_all | solution.py:1039
  58.9 0.1 all_to_all.12.came_ref
  59.0 0.0 copy-start.16
  59.0 0.7 copy-done.16
  59.7 0.0 copy-start.6
  59.8 6.0 %slide_grads.1 = (f32[1,768]{1,0:T(1,128)}, f32[4,1,768]{2,1,0:T(1,128)S(1)}) custom-call(s32[51]{0:T(128)S(1)} %copy-done.13, bf16[128,896]{1,0:T(8,128)(2,1)S(1)} %all_to_all.12.came_ref, f32[7,768]{1,0:T(8,128)} %taps_hbm.1, bf16[768,768]{1,0:T(8,128)(2,1)} %matrix_hbm.1, f32[8,1536]{1,0:T(8,128)S(1)} %get-tuple-element.61.refs_3_.vectors_ref, ...), custom_call_target="tpu_custom_call" | custom-call | flops 6000000000 | bytes 1024 | tf_op jit(solution)/shard_map/slide_grads/pallas_call | solution.py:682
  65.8 0.0 copy-start.3
  65.9 10.8 %weight_grads.1 = (bf16[4,256,1536]{2,1,0:T(8,128)(2,1)}, bf16[2,2,2,4,48,384]{5,4,3,2,1,0:T(8,128)(2,1)S(1)}, bf16[2,2,2,4,48,384]{5,4,3,2,1,0:T(8,128)(2,1)S(1)}) custom-call(f32[4,1,768]{2,1,0:T(1,128)S(1)} %get-tuple-element.87.grad_ref, bf16[1024,1536]{1,0:T(8,128)(2,1)S(1)} %bitcast.51, bf16[4,256,768]{2,1,0:T(8,128)(2,1)S(1)} %copy-done.5, ...), custom_call_target="tpu_custom_call" | custom-call | flops 12000000000 | bytes 1024 | tf_op jit(solution)/shard_map/weight_grads/pallas_call | solution.py:960
  76.7 0.1 collective-permute-start.5
  76.8 5.8 %tap_grads_0.1.before_ref = f32[3,49,8,128]{3,2,1,0:T(8,128)S(1)} custom-call(s32[51]{0:T(128)S(1)} %copy-done.13, bf16[4,16,16,384]{3,2,1,0:T(8,128)(2,1)S(1)} %copy-done.7, bf16[4,256,1536]{2,1,0:T(8,128)(2,1)} %get-tuple-element.95.grad_pre_ref, f32[4,256,384]{2,1,0:T(8,128)S(1)} %copy-done.4, f32[4,256,128]{2,1,0:T(8,128)S(1)} %copy-done.8, ...), custom_call_target="tpu_custom_call" | custom-call | flops 4000000000 | bytes 1024 | tf_op jit(solution)/shard_map/tap_grads_0/pallas_call | solution.py:991
  82.7 0.3 add_convert_fusion
  83.0 1.4 %collective-permute-start.6 = (bf16[2,4,48,384]{3,2,1,0:T(8,128)(2,1)S(1)}, bf16[2,4,48,384]{3,2,1,0:T(8,128)(2,1)S(1)}, u32[]{:S(2)}, u32[]{:S(2)}) collective-permute-start(bf16[2,4,48,384]{3,2,1,0:T(8,128)(2,1)S(1)} %get-tuple-element.99), channel_id=1, source_target_pairs={{0,1},{1,0},{2,3},{3,2},{4,5},{5,4},{6,7},{7,6},{8,9},{9,8},{10,11... | collective-permute-start | bytes 884744 | tf_op jit(solution)/shard_map/ppermute | solution.py:1028
  84.4 0.6 collective-permute-start.7
  84.9 5.8 %tap_grads_2.1 = f32[8,4,8,384]{3,2,1,0:T(8,128)S(1)} custom-call(s32[51]{0:T(128)S(1)} %copy-done.13, bf16[4,16,16,384]{3,2,1,0:T(8,128)(2,1)S(1)} %copy-done.7, bf16[4,256,1536]{2,1,0:T(8,128)(2,1)} %get-tuple-element.95.grad_pre_ref, f32[4,256,384]{2,1,0:T(8,128)S(1)} %copy-done.4, f32[4,256,128]{2,1,0:T(8,128)S(1)} %copy-done.8, ...), custom_call_target="tpu_custom_call" | custom-call | flops 4000000000 | bytes 1024 | tf_op jit(solution)/shard_map/tap_grads_2/pallas_call | solution.py:991
  90.8 1.7 %collective-permute-done.6 = bf16[2,4,48,384]{3,2,1,0:T(8,128)(2,1)S(1)} collective-permute-done((bf16[2,4,48,384]{3,2,1,0:T(8,128)(2,1)S(1)}, bf16[2,4,48,384]{3,2,1,0:T(8,128)(2,1)S(1)}, u32[]{:S(2)}, u32[]{:S(2)}) %collective-permute-start.6) | collective-permute-done | bytes 294944 | tf_op jit(solution)/shard_map/ppermute | solution.py:1028
  92.5 0.9 collective-permute-done.7
  93.4 0.9 collective-permute-start.9
  94.3 0.7 slice.148
  95.0 3.4 %all-to-all-start.1 = ((bf16[8,4,4,384]{3,2,1,0:T(4,128)(2,1)}), bf16[8,4,4,384]{3,2,1,0:T(4,128)(2,1)S(1)}, u32[]{:S(2)}, u32[]{:S(2)}) async-start(bf16[8,4,4,384]{3,2,1,0:T(4,128)(2,1)} %slice.148), calls=%async_computation.1 | async-start | bytes 196608 | tf_op jit(solution)/shard_map/all_to_all | solution.py:1039
  98.3 1.9 %collective-permute-start.8 = (bf16[4,48,384]{2,1,0:T(8,128)(2,1)S(1)}, bf16[4,48,384]{2,1,0:T(8,128)(2,1)S(1)}, u32[]{:S(2)}, u32[]{:S(2)}) collective-permute-start(bf16[4,48,384]{2,1,0:T(8,128)(2,1)S(1)} %fusion.11), channel_id=1, source_target_pairs={{0,16},{16,0},{1,17},{17,1},{2,18},{18,2},{3,19},{19,3},{4,20},{20... | collective-permute-start | bytes 442376 | tf_op jit(solution)/shard_map/ppermute | solution.py:1028
  100.3 3.2 %all-to-all-done.1 = bf16[8,4,4,384]{3,2,1,0:T(4,128)(2,1)S(1)} async-done(((bf16[8,4,4,384]{3,2,1,0:T(4,128)(2,1)}), bf16[8,4,4,384]{3,2,1,0:T(4,128)(2,1)S(1)}, u32[]{:S(2)}, u32[]{:S(2)}) %all-to-all-start.1) | async-done | bytes 98336 | tf_op jit(solution)/shard_map/all_to_all | solution.py:1039
  103.5 0.1 reduce_sum.12
  103.5 0.1 fusion.2
  103.6 2.1 %collective-permute-done.8 = bf16[4,48,384]{2,1,0:T(8,128)(2,1)S(1)} collective-permute-done((bf16[4,48,384]{2,1,0:T(8,128)(2,1)S(1)}, bf16[4,48,384]{2,1,0:T(8,128)(2,1)S(1)}, u32[]{:S(2)}, u32[]{:S(2)}) %collective-permute-start.8) | collective-permute-done | bytes 147488 | tf_op jit(solution)/shard_map/ppermute | solution.py:1028
  105.7 0.1 fusion.6
  105.8 1.3 %collective-permute-start.12 = (bf16[100,384]{1,0:T(8,128)(2,1)S(1)}, bf16[100,384]{1,0:T(8,128)(2,1)S(1)}, u32[]{:S(2)}, u32[]{:S(2)}) collective-permute-start(bf16[100,384]{1,0:T(8,128)(2,1)S(1)} %get-tuple-element.110), channel_id=1, source_target_pairs={{0,6},{2,0},{4,2},{6,4},{1,7},{3,1},{5,3},{7,5},{8,14},{10,8},{12,... | collective-permute-start | bytes 230408 | tf_op jit(solution)/shard_map/ppermute | solution.py:1028
  107.1 1.3 %collective-permute-start.11 = (bf16[100,384]{1,0:T(8,128)(2,1)S(1)}, bf16[100,384]{1,0:T(8,128)(2,1)S(1)}, u32[]{:S(2)}, u32[]{:S(2)}) collective-permute-start(bf16[100,384]{1,0:T(8,128)(2,1)S(1)} %get-tuple-element.111), channel_id=1, source_target_pairs={{0,4},{2,6},{4,0},{6,2},{1,5},{3,7},{5,1},{7,3},{8,12},{10,14},{12... | collective-permute-start | bytes 230408 | tf_op jit(solution)/shard_map/ppermute | solution.py:1028
  108.5 2.0 %collective-permute-done.12 = bf16[100,384]{1,0:T(8,128)(2,1)S(1)} collective-permute-done((bf16[100,384]{1,0:T(8,128)(2,1)S(1)}, bf16[100,384]{1,0:T(8,128)(2,1)S(1)}, u32[]{:S(2)}, u32[]{:S(2)}) %collective-permute-start.12) | collective-permute-done | bytes 76832 | tf_op jit(solution)/shard_map/ppermute | solution.py:1028
  110.5 5.5 %collective-permute-done.11 = bf16[100,384]{1,0:T(8,128)(2,1)S(1)} collective-permute-done((bf16[100,384]{1,0:T(8,128)(2,1)S(1)}, bf16[100,384]{1,0:T(8,128)(2,1)S(1)}, u32[]{:S(2)}, u32[]{:S(2)}) %collective-permute-start.11) | collective-permute-done | bytes 76832 | tf_op jit(solution)/shard_map/ppermute | solution.py:1028
  116.1 0.7 reshape.79
  116.8 0.6 reshape.80
  117.4 0.7 dynamic_slice.3
  (45 shorter events, 0.4 us)
Async XLA Ops:
  1.3 0.7 copy-start.14
  4.8 21.6 %copy-start.15 = (f32[1,1152]{1,0:T(1,128)}, f32[1,1152]{1,0:T(1,128)S(1)}, u32[]{:S(2)}) copy-start(f32[1,1152]{1,0:T(1,128)S(1)} %get-tuple-element.83.small_ref) | copy-start | bytes 13828
  4.8 29.1 %copy-start.12 = (s32[51]{0:T(128)}, s32[51]{0:T(128)S(1)}, u32[]{:S(2)}) copy-start(s32[51]{0:T(128)S(1)} %get-tuple-element.55.table_ref) | copy-start | bytes 616
  4.8 3.1 %collective-permute-start = (bf16[33,16,384]{2,1,0:T(8,128)(2,1)S(1)}, bf16[33,16,384]{2,1,0:T(8,128)(2,1)S(1)}, u32[]{:S(2)}, u32[]{:S(2)}) collective-permute-start(bf16[33,16,384]{2,1,0:T(8,128)(2,1)S(1)} %get-tuple-element.58), channel_id=1, source_target_pairs={{0,8},{8,0},{16,24},{24,16},{1,9},{9,1},{17,25},{25,17},{2,10},{10... | collective-permute-start | bytes 1216520 | tf_op jit(solution)/shard_map/ppermute | solution.py:1098
  5.3 21.1 %collective-permute-start.3 = (bf16[17,16,384]{2,1,0:T(8,128)(2,1)S(1)}, bf16[17,16,384]{2,1,0:T(8,128)(2,1)S(1)}, u32[]{:S(2)}, u32[]{:S(2)}) collective-permute-start(bf16[17,16,384]{2,1,0:T(8,128)(2,1)S(1)} %get-tuple-element.62), channel_id=1, source_target_pairs={{0,16},{8,24},{16,0},{24,8},{1,17},{9,25},{17,1},{25,9},{2,18},{10... | collective-permute-start | bytes 626696 | tf_op jit(solution)/shard_map/ppermute | solution.py:1098
  7.9 18.6 %collective-permute-start.4 = (bf16[17,16,384]{2,1,0:T(8,128)(2,1)S(1)}, bf16[17,16,384]{2,1,0:T(8,128)(2,1)S(1)}, u32[]{:S(2)}, u32[]{:S(2)}) collective-permute-start(bf16[17,16,384]{2,1,0:T(8,128)(2,1)S(1)} %get-tuple-element.63), channel_id=1, source_target_pairs={{0,24},{8,16},{16,8},{24,0},{1,25},{9,17},{17,9},{25,1},{2,26},{10... | collective-permute-start | bytes 626696 | tf_op jit(solution)/shard_map/ppermute | solution.py:1098
  7.9 18.5 %copy-start.9 = (bf16[33,16,384]{2,1,0:T(8,128)(2,1)}, bf16[33,16,384]{2,1,0:T(8,128)(2,1)S(1)}, u32[]{:S(2)}) copy-start(bf16[33,16,384]{2,1,0:T(8,128)(2,1)S(1)} %collective-permute-done.refs_1_.refs_0_) | copy-start | bytes 1216516
  8.0 25.9 %collective-permute-start.1 = (bf16[16,16,384]{2,1,0:T(8,128)(2,1)S(1)}, bf16[16,16,384]{2,1,0:T(8,128)(2,1)S(1)}, u32[]{:S(2)}, u32[]{:S(2)}) collective-permute-start(bf16[16,16,384]{2,1,0:T(8,128)(2,1)S(1)} %get-tuple-element.59), channel_id=1, source_target_pairs={{0,16},{8,24},{16,0},{24,8},{1,17},{9,25},{17,1},{25,9},{2,18},{10... | collective-permute-start | bytes 589832 | tf_op jit(solution)/shard_map/ppermute | solution.py:1098
  9.7 24.2 %collective-permute-start.2 = (bf16[16,16,384]{2,1,0:T(8,128)(2,1)S(1)}, bf16[16,16,384]{2,1,0:T(8,128)(2,1)S(1)}, u32[]{:S(2)}, u32[]{:S(2)}) collective-permute-start(bf16[16,16,384]{2,1,0:T(8,128)(2,1)S(1)} %get-tuple-element.60), channel_id=1, source_target_pairs={{0,24},{8,16},{16,8},{24,0},{1,25},{9,17},{17,9},{25,1},{2,26},{10... | collective-permute-start | bytes 589832 | tf_op jit(solution)/shard_map/ppermute | solution.py:1098
  26.4 7.4 %copy-start.10 = (bf16[17,16,384]{2,1,0:T(8,128)(2,1)}, bf16[17,16,384]{2,1,0:T(8,128)(2,1)S(1)}, u32[]{:S(2)}) copy-start(bf16[17,16,384]{2,1,0:T(8,128)(2,1)S(1)} %collective-permute-done.3.refs_0_.refs_1_) | copy-start | bytes 626692
  26.4 7.4 %copy-start.11 = (bf16[17,16,384]{2,1,0:T(8,128)(2,1)}, bf16[17,16,384]{2,1,0:T(8,128)(2,1)S(1)}, u32[]{:S(2)}) copy-start(bf16[17,16,384]{2,1,0:T(8,128)(2,1)S(1)} %collective-permute-done.4.refs_1_.refs_2_) | copy-start | bytes 626692
  35.0 24.0 %copy-start.13 = (s32[51]{0:T(128)S(1)}, s32[51]{0:T(128)}, u32[]{:S(2)}) copy-start(s32[51]{0:T(128)} %copy-done.12) | copy-start | bytes 616
  59.0 0.7 copy-start.16
  59.7 6.0 %copy-start = (bf16[4,256,1536]{2,1,0:T(8,128)(2,1)S(1)}, bf16[4,256,1536]{2,1,0:T(8,128)(2,1)}, u32[]{:S(2)}) copy-start(bf16[4,256,1536]{2,1,0:T(8,128)(2,1)} %get-tuple-element.88) | copy-start | bytes 9437188
  59.7 6.0 %copy-start.1 = (bf16[4,256,1536]{2,1,0:T(8,128)(2,1)S(1)}, bf16[4,256,1536]{2,1,0:T(8,128)(2,1)}, u32[]{:S(2)}) copy-start(bf16[4,256,1536]{2,1,0:T(8,128)(2,1)} %get-tuple-element.90.slope_ref) | copy-start | bytes 9437188
  59.7 6.1 %copy-start.2 = (bf16[1536,384]{1,0:T(8,128)(2,1)S(1)}, bf16[1536,384]{1,0:T(8,128)(2,1)}, u32[]{:S(2)}) copy-start(bf16[1536,384]{1,0:T(8,128)(2,1)} %reduce_ref.1) | copy-start | bytes 3538948
  59.7 6.1 %copy-start.4 = (f32[4,256,384]{2,1,0:T(8,128)S(1)}, f32[4,256,384]{2,1,0:T(8,128)}, u32[]{:S(2)}) copy-start(f32[4,256,384]{2,1,0:T(8,128)} %get-tuple-element.91.unit_ref) | copy-start | bytes 4718596
  59.7 6.1 %copy-start.5 = (bf16[4,256,768]{2,1,0:T(8,128)(2,1)S(1)}, bf16[4,256,768]{2,1,0:T(8,128)(2,1)}, u32[]{:S(2)}) copy-start(bf16[4,256,768]{2,1,0:T(8,128)(2,1)} %get-tuple-element.89.head_slope_ref) | copy-start | bytes 4718596
  59.7 6.1 %copy-start.6 = (bf16[384,768]{1,0:T(8,128)(2,1)S(1)}, bf16[384,768]{1,0:T(8,128)(2,1)}, u32[]{:S(2)}) copy-start(bf16[384,768]{1,0:T(8,128)(2,1)} %head_ref.1) | copy-start | bytes 1769476
  65.8 11.0 %copy-start.3 = (bf16[384,1536]{1,0:T(8,128)(2,1)S(1)}, bf16[384,1536]{1,0:T(8,128)(2,1)}, u32[]{:S(2)}) copy-start(bf16[384,1536]{1,0:T(8,128)(2,1)} %expand_ref.3) | copy-start | bytes 3538948
  65.8 11.0 %copy-start.7 = (bf16[4,16,16,384]{3,2,1,0:T(8,128)(2,1)S(1)}, bf16[4,16,16,384]{3,2,1,0:T(8,128)(2,1)}, u32[]{:S(2)}) copy-start(bf16[4,16,16,384]{3,2,1,0:T(8,128)(2,1)} %get-tuple-element.94.source_ref) | copy-start | bytes 2359300
  65.8 11.0 %copy-start.8 = (f32[4,256,128]{2,1,0:T(8,128)S(1)}, f32[4,256,128]{2,1,0:T(8,128)}, u32[]{:S(2)}) copy-start(f32[4,256,128]{2,1,0:T(8,128)} %get-tuple-element.96.inv_ref) | copy-start | bytes 1572868
  76.7 6.0 %collective-permute-start.5 = (bf16[2,2,2,4,48,384]{5,4,3,2,1,0:T(8,128)(2,1)S(1)}, bf16[2,2,2,4,48,384]{5,4,3,2,1,0:T(8,128)(2,1)S(1)}, u32[]{:S(2)}, u32[]{:S(2)}) collective-permute-start(bf16[2,2,2,4,48,384]{5,4,3,2,1,0:T(8,128)(2,1)S(1)} %get-tuple-element.93), channel_id=1, source_target_pairs={{0,8},{8,0},{1,9},{9,1},{2,10},{10,2},{3,11},{11,3},{4,12},{12,4},... | collective-permute-start | bytes 3538952 | tf_op jit(solution)/shard_map/ppermute | solution.py:1028
  83.0 9.5 %collective-permute-start.6 = (bf16[2,4,48,384]{3,2,1,0:T(8,128)(2,1)S(1)}, bf16[2,4,48,384]{3,2,1,0:T(8,128)(2,1)S(1)}, u32[]{:S(2)}, u32[]{:S(2)}) collective-permute-start(bf16[2,4,48,384]{3,2,1,0:T(8,128)(2,1)S(1)} %get-tuple-element.99), channel_id=1, source_target_pairs={{0,1},{1,0},{2,3},{3,2},{4,5},{5,4},{6,7},{7,6},{8,9},{9,8},{10,11... | collective-permute-start | bytes 884744 | tf_op jit(solution)/shard_map/ppermute | solution.py:1028
  84.4 9.0 %collective-permute-start.7 = (bf16[2,4,48,384]{3,2,1,0:T(8,128)(2,1)S(1)}, bf16[2,4,48,384]{3,2,1,0:T(8,128)(2,1)S(1)}, u32[]{:S(2)}, u32[]{:S(2)}) collective-permute-start(bf16[2,4,48,384]{3,2,1,0:T(8,128)(2,1)S(1)} %get-tuple-element.100), channel_id=1, source_target_pairs={{0,16},{16,0},{1,17},{17,1},{2,18},{18,2},{3,19},{19,3},{4,20},{20... | collective-permute-start | bytes 884744 | tf_op jit(solution)/shard_map/ppermute | solution.py:1028
  93.4 10.1 %collective-permute-start.9 = (bf16[4,48,384]{2,1,0:T(8,128)(2,1)S(1)}, bf16[4,48,384]{2,1,0:T(8,128)(2,1)S(1)}, u32[]{:S(2)}, u32[]{:S(2)}) collective-permute-start(bf16[4,48,384]{2,1,0:T(8,128)(2,1)S(1)} %fusion.12), channel_id=1, source_target_pairs={{0,1},{1,0},{2,3},{3,2},{4,5},{5,4},{6,7},{7,6},{8,9},{9,8},{10,11... | collective-permute-start | bytes 442376 | tf_op jit(solution)/shard_map/ppermute | solution.py:1028
  95.0 8.5 %all-to-all-start.1 = ((bf16[8,4,4,384]{3,2,1,0:T(4,128)(2,1)}), bf16[8,4,4,384]{3,2,1,0:T(4,128)(2,1)S(1)}, u32[]{:S(2)}, u32[]{:S(2)}) async-start(bf16[8,4,4,384]{3,2,1,0:T(4,128)(2,1)} %slice.148), calls=%async_computation.1 | async-start | bytes 196608 | tf_op jit(solution)/shard_map/all_to_all | solution.py:1039
  98.3 7.4 %collective-permute-start.8 = (bf16[4,48,384]{2,1,0:T(8,128)(2,1)S(1)}, bf16[4,48,384]{2,1,0:T(8,128)(2,1)S(1)}, u32[]{:S(2)}, u32[]{:S(2)}) collective-permute-start(bf16[4,48,384]{2,1,0:T(8,128)(2,1)S(1)} %fusion.11), channel_id=1, source_target_pairs={{0,16},{16,0},{1,17},{17,1},{2,18},{18,2},{3,19},{19,3},{4,20},{20... | collective-permute-start | bytes 442376 | tf_op jit(solution)/shard_map/ppermute | solution.py:1028
  105.8 4.7 %collective-permute-start.12 = (bf16[100,384]{1,0:T(8,128)(2,1)S(1)}, bf16[100,384]{1,0:T(8,128)(2,1)S(1)}, u32[]{:S(2)}, u32[]{:S(2)}) collective-permute-start(bf16[100,384]{1,0:T(8,128)(2,1)S(1)} %get-tuple-element.110), channel_id=1, source_target_pairs={{0,6},{2,0},{4,2},{6,4},{1,7},{3,1},{5,3},{7,5},{8,14},{10,8},{12,... | collective-permute-start | bytes 230408 | tf_op jit(solution)/shard_map/ppermute | solution.py:1028
  107.1 8.8 %collective-permute-start.11 = (bf16[100,384]{1,0:T(8,128)(2,1)S(1)}, bf16[100,384]{1,0:T(8,128)(2,1)S(1)}, u32[]{:S(2)}, u32[]{:S(2)}) collective-permute-start(bf16[100,384]{1,0:T(8,128)(2,1)S(1)} %get-tuple-element.111), channel_id=1, source_target_pairs={{0,4},{2,6},{4,0},{6,2},{1,5},{3,7},{5,1},{7,3},{8,12},{10,14},{12... | collective-permute-start | bytes 230408 | tf_op jit(solution)/shard_map/ppermute | solution.py:1028
  108.5 7.5 %collective-permute-start.10 = (bf16[100,384]{1,0:T(8,128)(2,1)S(1)}, bf16[100,384]{1,0:T(8,128)(2,1)S(1)}, u32[]{:S(2)}, u32[]{:S(2)}) collective-permute-start(bf16[100,384]{1,0:T(8,128)(2,1)S(1)} %get-tuple-element.109), channel_id=1, source_target_pairs={{0,2},{2,4},{4,6},{6,0},{1,3},{3,5},{5,7},{7,1},{8,10},{10,12},{12... | collective-permute-start | bytes 230408 | tf_op jit(solution)/shard_map/ppermute | solution.py:1028

commit v7 on v6

--- a/solution.py
+++ b/solution.py
@@ -340,14 +340,21 @@
             for col in range(KS):
                 start = low - reach + col
                 weights = [
-                    taps_ref[row * KS + col : row * KS + col + 1, lanes] for row in range(KS)
+                    jnp.broadcast_to(
+                        taps_ref[row * KS + col : row * KS + col + 1, lanes], (side, LANES)
+                    ).astype(jnp.bfloat16)
+                    for row in range(KS)
                 ]
+                sums = [None] * side
                 for at in range(side):
-                    line = padded[band, at, start : start + side, :]
+                    line = padded[band, at, start : start + side, :].astype(jnp.bfloat16)
                     for row in range(KS):
                         place = at - row + reach
                         if 0 <= place < side:
-                            totals[place] = totals[place] + weights[row] * line
+                            term = weights[row] * line
+                            sums[place] = term if sums[place] is None else sums[place] + term
+                for place in range(side):
+                    totals[place] = totals[place] + sums[place].astype(jnp.float32)
             for place in range(side):
                 depth_out[band, place * side : (place + 1) * side, :] = totals[place]
             return carry
@@ -545,15 +552,24 @@
             jnp.sum(jnp.where(lane == slot, held[:, at : at + LANES], 0.0), axis=1, keepdims=True)
             for at in (ROWS_AT, COLS_AT)
         ]
-        spot = jnp.where(channel < half, spots[0], spots[1])
-        embed = embed_ref[proc, 0:1, :].astype(jnp.bfloat16).astype(jnp.float32)
-        row = jnp.where(filled != 0, embed + jnp.sin(spot * frequency + phase), 0.0)
+        angle = jnp.where(channel < half, spots[0], spots[1]) * frequency + phase
         target = jnp.where(lane == 0, slide, jnp.where(lane == 1, slot, my_member))
         target = jnp.where(filled != 0, target, jnp.where(lane == 2, -1, 0))
         target = jnp.where(lane < 3, target, 0)
+        rows_ref[proc : proc + 1, 0:E] = angle
+        rows_ref[2 * PROC + proc : 2 * PROC + proc + 1, 0:E] = embed_ref[proc, 0:1, :]
         for copied in range(proc, ROW_UNIT, PROC):
-            rows_ref[copied : copied + 1, 0:E] = row
             rows_ref[copied : copied + 1, E:] = target.astype(jnp.float32)
+    code = jnp.sin(rows_ref[0 : 2 * PROC, 0:E])
+    embed = rows_ref[2 * PROC : 4 * PROC, 0:E].astype(jnp.bfloat16).astype(jnp.float32)
+    row_id = lax.broadcasted_iota(jnp.int32, (2 * PROC, E), 0)
+    there = row_id < 0
+    for proc in range(PROC):
+        there = there | ((row_id == proc) & (table_ref[FILLED + proc] != 0))
+    total = jnp.where(there, embed + code, 0.0)
+    rows_ref[0 : 2 * PROC, 0:E] = total
+    for copied in range(PROC, ROW_UNIT):
+        rows_ref[copied : copied + 1, 0:E] = rows_ref[copied - PROC : copied - PROC + 1, 0:E]
     sent = rows_ref[...].astype(jnp.bfloat16)
     for start in range(0, out_ref.shape[0], ROW_UNIT):
         out_ref[start : start + ROW_UNIT, :] = sent
@@ -572,7 +588,7 @@
         in_specs=[smem, vmem, vmem] + [HBM] * len(buffers),
         out_specs=(vmem, vmem),
         scratch_shapes=[
-            pltpu.VMEM((ROW_UNIT, E + LANES), jnp.float32),
+            pltpu.VMEM((4 * PROC, E + LANES), jnp.float32),
             pltpu.VMEM((len(buffers),) + buffers[0].shape[1:], jnp.bfloat16),
             pltpu.SemaphoreType.DMA((len(buffers),)),
         ],
@@ -630,7 +646,6 @@
         small = smalls_ref[other]
         count = small[:, COUNT_AT : COUNT_AT + 1]
         here = step < count
-        share = jnp.where(here, 1.0 / count, 0.0)
         first = lax.convert_element_type(slide * length, jnp.float32)
         pick = ((target - first) == step).astype(jnp.float32).astype(jnp.bfloat16)
         for ref in (rows, back):
@@ -642,11 +657,15 @@
             rows[slide, border : border + length, cols] = jnp.where(
                 here, mix(pick, came_ref[:, cols]), 0.0
             )
-            mixed[:, cols] = dilate(rows, slide, 1, cols).astype(jnp.bfloat16)
-        if other == 0:
-            loads[1].wait()
+            mixed[other, :, cols] = dilate(rows, slide, 1, cols).astype(jnp.bfloat16)
+    loads[1].wait()
+    for other in range(slides):
+        slide = my_slide ^ other
+        small = smalls_ref[other]
+        here = step < small[:, COUNT_AT : COUNT_AT + 1]
+        share = jnp.where(here, 1.0 / small[:, COUNT_AT : COUNT_AT + 1], 0.0)
         for cols in blocks:
-            pre[:, cols] = mix(mixed[...], matrix_ref[:, cols])
+            pre[:, cols] = mix(mixed[other], matrix_ref[:, cols])
             total = None
             for start in range(0, length, PART):
                 part = slice(start, start + PART)
@@ -690,7 +709,7 @@
         scratch_shapes=[
             pltpu.VMEM(padded, jnp.float32),
             pltpu.VMEM(padded, jnp.float32),
-            pltpu.VMEM((length, E), jnp.bfloat16),
+            pltpu.VMEM((slides, length, E), jnp.bfloat16),
             pltpu.VMEM((length, E), jnp.float32),
             pltpu.VMEM((length, E), jnp.bfloat16),
             pltpu.VMEM(taps.shape, jnp.float32),
@@ -885,9 +904,9 @@
             inv = inv_ref[0, rows, 0:1]
             for band in range(bands):
                 lanes = slice(band * LANES, (band + 1) * LANES)
-                depth_back[band, rows, :] = inv * (
-                    scaled[:, lanes] - mean - unit[:, lanes] * mean_unit
-                )
+                depth_back[band, rows, :] = (
+                    inv * (scaled[:, lanes] - mean - unit[:, lanes] * mean_unit)
+                ).astype(jnp.bfloat16)
         edge = jnp.zeros((side, low, LANES), jnp.float32)
         for band in range(bands):
             lanes = slice(band * LANES, (band + 1) * LANES)
@@ -901,25 +920,28 @@
         def taps_of(band, carry):
             for col in range(KS):
                 start = low - reach + col
-                sums = [None] * KS
+                folded = [None] * KS
                 grads = {}
-                for at in range(side):
-                    line = padded[band, at, start : start + side, :]
+                for half in range(2):
+                    sums = [None] * KS
+                    for at in range(half * side // 2, (half + 1) * side // 2):
+                        line = padded[band, at, start : start + side, :].astype(jnp.bfloat16)
+                        for row in range(KS):
+                            place = at - row + reach
+                            if 0 <= place < side:
+                                if place not in grads:
+                                    grads[place] = depth_back[
+                                        band, place * side : (place + 1) * side, :
+                                    ]
+                                term = line * grads[place]
+                                sums[row] = term if sums[row] is None else sums[row] + term
                     for row in range(KS):
-                        place = at - row + reach
-                        if 0 <= place < side:
-                            if place not in grads:
-                                grads[place] = depth_back[
-                                    band, place * side : (place + 1) * side, :
-                                ]
-                            term = line * grads[place]
-                            sums[row] = term if sums[row] is None else sums[row] + term
+                        total = sums[row].astype(jnp.float32)
+                        for piece in range(0, side, 8):
+                            block = total[piece : piece + 8, :]
+                            folded[row] = block if folded[row] is None else folded[row] + block
                 for row in range(KS):
-                    total = sums[row]
-                    folded = total[0:8, :]
-                    for piece in range(8, side, 8):
-                        folded = folded + total[piece : piece + 8, :]
-                    tap_sums[band, row * KS + col] = tap_sums[band, row * KS + col] + folded
+                    tap_sums[band, row * KS + col] = tap_sums[band, row * KS + col] + folded[row]
             return carry
 
         lax.fori_loop(0, bands, taps_of, 0)
@@ -933,15 +955,9 @@
             lanes = slice(band * LANES, (band + 1) * LANES)
             tap_rows[0 : KS * KS, lanes] = jnp.sum(tap_sums[band], axis=1)
             tap_rows[KS * KS :, lanes] = jnp.zeros((tap_rows.shape[0] - KS * KS, LANES), jnp.float32)
-        my_z = lax.axis_index("g1")
-        for part in range(2 * plan.ys * plan.g2):
-            cross, core = divmod(part, 2)
-            y, x = divmod(cross, plan.g2)
-            for z in range(plan.g1):
-                away = lax.rem(z - my_z + plan.g1, plan.g1)
-                device = ((y * 2 + core) * plan.g1 + z) * plan.g2 + x
-                start = device * plan.share // channels
-                out_ref[part, away] = tap_rows[start : start + TAP_ROWS, :]
+        for device in range(plan.devices):
+            start = device * plan.share // channels
+            out_ref[device] = tap_rows[start : start + TAP_ROWS, :]
 
 
 def per_slot(array):
@@ -982,7 +998,7 @@
     side, channels = streams[0].shape[1], streams[0].shape[3]
     bands = channels // LANES
     sums = (bands, KS * KS, 8, LANES)
-    out = (2 * plan.ys * plan.g2, plan.g1, TAP_ROWS, channels) if last else sums
+    out = (plan.devices, TAP_ROWS, channels) if last else sums
 
     def items(array):
         shape = array.shape[1:]
@@ -1002,7 +1018,7 @@
                 pltpu.VMEM(sums, jnp.float32),
                 pltpu.VMEM((KS * KS + 7, channels), jnp.float32),
                 pltpu.VMEM((side * side, channels), jnp.float32),
-                pltpu.VMEM((bands, side * side, LANES), jnp.float32),
+                pltpu.VMEM((bands, side * side, LANES), jnp.bfloat16),
             ],
         ),
         compiler_params=pltpu.CompilerParams(vmem_limit_bytes=16 * MIB),
@@ -1145,11 +1161,11 @@
         for kind in range(2)
     ]
     stay = [add_all([part[0] for part in parts[kind]]) for kind in range(2)]
+    taps = taps[:, :DEPTH_ROWS].astype(jnp.bfloat16)
     out, taps = lax.optimization_barrier((out, taps))
     parts = [sum_axis(stay[kind], out[kind], names[1 - kind], size) for kind in range(2)]
-    taps = exchange(taps[:, :, :DEPTH_ROWS].astype(jnp.bfloat16), ("y", "g2", "core"))
-    taps = jnp.sum(taps.astype(jnp.float32), axis=0).astype(jnp.bfloat16)
-    both = jnp.concatenate([add_all(parts[0]), add_all(parts[1]), taps], axis=1)
+    taps = exchange(taps, ALL)
+    both = jnp.concatenate([add_all(parts[0]), add_all(parts[1])], axis=1)
     total = add_all(
         sum_axis(both[0], [both[step] for step in range(1, plan.g1)], "g1", plan.g1), jnp.float32
     )
@@ -1157,7 +1173,7 @@
     expand_share = total[plan.block_rows : plan.block_rows + plan.pieces * plan.expand_rows]
     expand_share = expand_share.reshape(plan.pieces, plan.expand_rows, channels).transpose(1, 0, 2)
     depth_share = lax.dynamic_slice(
-        total[2 * plan.block_rows :].reshape(-1),
+        jnp.sum(taps.astype(jnp.float32), axis=0).reshape(-1),
         (my_device * plan.share % channels,),
         (plan.share,),
     )

time: 119 us -> 107 us (0.90)
  Pallas kernels: 59.2 us -> 53.4 us
  waiting for transfers between devices: 15.4 us -> 10.2 us
  blocking collectives: 20.1 us -> 18.5 us
    ppermute x8, waiting for transfers between devices: 12.1 us -> 7.56 us  [shifted(): return lax.ppermute(values, names, pairs)]
    pallas_call x3, Pallas kernels: 25.1 us -> 21.9 us  [forward_block(): pl.pallas_call(functools.partial(forward_kernel, kind, last, len(tiles),...]
    pallas_call x2, Pallas kernels: 11.7 us -> 9.78 us  [tap_grads(): pl.pallas_call(functools.partial(taps_kernel, plan, first, last), out_sha...]
    all_to_all x1, blocking collectives: 20.1 us -> 18.5 us  [exchange(): lax.all_to_all(values, names, split_axis=0, concat_axis=0, tiled=True)]
  transfers between devices with their start and end apart: 14 -> 14, of which waited for: 6 -> 6; matrix products, arithmetic and copies ran while one was open for 1% -> 2% of each run, Pallas kernels for 30% -> 29%
where the time goes in v7:
time: 107 us; the launch traced here: 105 us
  Pallas kernels  53.4 us (50%)
  blocking collectives  18.5 us (17%)
  starting transfers between devices  15.6 us (15%)
  waiting for transfers between devices  10.2 us (10%)
  local copies, waits for them, and re-layouts  5.26 us (5%)
  between operations  1.71 us (2%)
    pallas_call x3, Pallas kernels, forward_block(): pl.pallas_call(functools.partial(forward_kernel, kind, last, len(tiles),...  21.9 us
    all_to_all x1, blocking collectives, exchange(): lax.all_to_all(values, names, split_axis=0, concat_axis=0, tiled=True)  18.5 us
    pallas_call x1, Pallas kernels, weight_grads(): pl.pallas_call(functools.partial(weights_kernel, plan), out_shape=(pltpu....  10.8 us
    pallas_call x2, Pallas kernels, tap_grads(): pl.pallas_call(functools.partial(taps_kernel, plan, first, last), out_sha...  9.78 us
    ppermute x8, waiting for transfers between devices, shifted(): return lax.ppermute(values, names, pairs)  7.56 us
    ppermute x8, starting transfers between devices, shifted(): return lax.ppermute(values, names, pairs)  7.4 us
    pallas_call x1, Pallas kernels, slide_grads(): pl.pallas_call(functools.partial(slide_kernel, length, members, slides),...  5.49 us
    ppermute x5, starting transfers between devices, from_other(): lax.ppermute(buffer, DP, [(index, index ^ other) for index in range(slide...  4.88 us
  transfers between devices with their start and end apart: 14, of which 6 were waited for; matrix products, arithmetic and copies ran while one was open for 2% of the time, Pallas kernels for 29%

profile of v7, /device:TPU:0, one launch (start us, length us, event | category | flops | bytes accessed | tf_op | source)
XLA Modules:
  0.0 105.3 jit_solution(1175860444987136011)
XLA Ops:
  1.3 0.7 copy-done.14
  2.0 2.8 %pack_tiles.1 = (bf16[33,16,384]{2,1,0:T(8,128)(2,1)S(1)}, bf16[17,16,384]{2,1,0:T(8,128)(2,1)S(1)}, bf16[17,16,384]{2,1,0:T(8,128)(2,1)S(1)}, bf16[16,16,384]{2...) custom-call(s32[1]{0:T(128)S(6)} %copy.56.counts_ref, ...), custom_call_target="tpu_custom_call" | custom-call | tf_op jit(solution)/shard_map/pack_tiles/pallas_call | solution.py:224
  4.8 0.0 copy-start.15
  4.8 0.0 copy-start.12
  4.8 0.5 collective-permute-start
  5.3 2.6 %collective-permute-start.3 = (bf16[17,16,384]{2,1,0:T(8,128)(2,1)S(1)}, bf16[17,16,384]{2,1,0:T(8,128)(2,1)S(1)}, u32[]{:S(2)}, u32[]{:S(2)}) collective-permute-start(bf16[17,16,384]{2,1,0:T(8,128)(2,1)S(1)} %get-tuple-element.62), channel_id=1, source_target_pairs={{0,16},{8,24},{16,0},{24,8},{1,17},{9,25},{17,1},{25,9},{2,18},{10... | collective-permute-start | bytes 626696 | tf_op jit(solution)/shard_map/ppermute | solution.py:1114
  7.9 0.1 collective-permute-start.4
  8.0 1.7 %collective-permute-start.1 = (bf16[16,16,384]{2,1,0:T(8,128)(2,1)S(1)}, bf16[16,16,384]{2,1,0:T(8,128)(2,1)S(1)}, u32[]{:S(2)}, u32[]{:S(2)}) collective-permute-start(bf16[16,16,384]{2,1,0:T(8,128)(2,1)S(1)} %get-tuple-element.59), channel_id=1, source_target_pairs={{0,16},{8,24},{16,0},{24,8},{1,17},{9,25},{17,1},{25,9},{2,18},{10... | collective-permute-start | bytes 589832 | tf_op jit(solution)/shard_map/ppermute | solution.py:1114
  9.7 0.0 collective-permute-start.2
  9.7 14.4 %forward_block_0.1 = (bf16[4,16,16,384]{3,2,1,0:T(8,128)(2,1)}, f32[4,8,768]{2,1,0:T(8,128)}, f32[4,256,384]{2,1,0:T(8,128)}, f32[4,256,128]{2,1,0:T(8,128)}, bf...) custom-call(s32[51]{0:T(128)S(1)} %get-tuple-element.55.table_ref, ...), custom_call_target="tpu_custom_call" | custom-call | flops 1000000000 | bytes 1024 | tf_op jit(solution)/shard_map/forward_block_0/pallas_call | solution.py:484
  24.1 0.0 collective-permute-done.3.refs_0_.refs_1_
  24.2 6.6 %forward_block_1.1 = (bf16[4,16,16,384]{3,2,1,0:T(8,128)(2,1)}, f32[4,8,768]{2,1,0:T(8,128)}, f32[4,256,384]{2,1,0:T(8,128)}, f32[4,256,128]{2,1,0:T(8,128)}, bf...) custom-call(s32[51]{0:T(128)S(1)} %get-tuple-element.55.table_ref, ...), custom_call_target="tpu_custom_call", output_to_operand_aliasing={{0}: (8, {}), {1}: (9, {}), {2}: (10, {}), {3}: (11, {}), {... | custom-call | flops 1000000000 | bytes 1024 | tf_op jit(solution)/shard_map/forward_block_1/pallas_call | solution.py:484
  30.9 0.9 forward_block_2.1
  31.8 0.0 copy-start.13
  31.8 2.6 %tile_rows.1 = (bf16[128,896]{1,0:T(8,128)(2,1)}, f32[4,1,1152]{2,1,0:T(1,128)}) custom-call(s32[51]{0:T(128)} %copy-done.12, f32[4,8,768]{2,1,0:T(8,128)} %get-tuple-element.82.embed_ref, f32[1,1152]{1,0:T(1,128)} %copy-done.15, bf16[33,16,384]{2,1,0:T(8,128)(2,1)} %copy-done.9, bf16[17,16,384]{2,1,0:T(8,128)(2,1)} %copy-done.10, ...), custom_call_target="tpu_custom_call" | custom-call | flops 1000000000 | bytes 1024 | tf_op jit(solution)/shard_map/tile_rows/pallas_call | solution.py:582
  34.4 1.0 all_to_all.10
  35.4 18.5 %all_to_all.16 = bf16[32,4,896]{2,1,0:T(4,128)(2,1)S(1)} all-to-all(bf16[32,4,896]{2,1,0:T(4,128)(2,1)S(1)} %all_to_all.10), channel_id=1, replica_groups=mesh['y'=2,'core'=2,'g1'=4,'g2'=2] {'y','core','g1','g2'}, dimensions={0} | all-to-all | bytes 458752 | tf_op jit(solution)/shard_map/all_to_all | solution.py:1055
  53.9 0.1 all_to_all.12.came_ref
  53.9 0.0 copy-start.16
  54.0 0.7 copy-done.16
  54.7 0.0 copy-start.6
  54.7 5.5 %slide_grads.1 = (f32[1,768]{1,0:T(1,128)}, f32[4,1,768]{2,1,0:T(1,128)S(1)}) custom-call(s32[51]{0:T(128)S(1)} %copy-done.13, bf16[128,896]{1,0:T(8,128)(2,1)S(1)} %all_to_all.12.came_ref, f32[7,768]{1,0:T(8,128)} %taps_hbm.1, bf16[768,768]{1,0:T(8,128)(2,1)} %matrix_hbm.1, f32[8,1536]{1,0:T(8,128)S(1)} %get-tuple-element.61.refs_3_.vectors_ref, ...), custom_call_target="tpu_custom_call" | custom-call | flops 6000000000 | bytes 1024 | tf_op jit(solution)/shard_map/slide_grads/pallas_call | solution.py:701
  60.3 0.0 copy-start.3
  60.3 10.8 %weight_grads.1 = (bf16[4,256,1536]{2,1,0:T(8,128)(2,1)}, bf16[2,2,2,4,48,384]{5,4,3,2,1,0:T(8,128)(2,1)S(1)}, bf16[2,2,2,4,48,384]{5,4,3,2,1,0:T(8,128)(2,1)S(1)}) custom-call(f32[4,1,768]{2,1,0:T(1,128)S(1)} %get-tuple-element.87.grad_ref, bf16[1024,1536]{1,0:T(8,128)(2,1)S(1)} %bitcast.51, bf16[4,256,768]{2,1,0:T(8,128)(2,1)S(1)} %copy-done.5, ...), custom_call_target="tpu_custom_call" | custom-call | flops 12000000000 | bytes 1024 | tf_op jit(solution)/shard_map/weight_grads/pallas_call | solution.py:976
  71.1 0.1 collective-permute-start.5
  71.3 4.8 %tap_grads_0.1.before_ref = f32[3,49,8,128]{3,2,1,0:T(8,128)S(1)} custom-call(s32[51]{0:T(128)S(1)} %copy-done.13, bf16[4,16,16,384]{3,2,1,0:T(8,128)(2,1)S(1)} %copy-done.7, bf16[4,256,1536]{2,1,0:T(8,128)(2,1)} %get-tuple-element.95.grad_pre_ref, f32[4,256,384]{2,1,0:T(8,128)S(1)} %copy-done.4, f32[4,256,128]{2,1,0:T(8,128)S(1)} %copy-done.8, ...), custom_call_target="tpu_custom_call" | custom-call | flops 4000000000 | bytes 1024 | tf_op jit(solution)/shard_map/tap_grads_0/pallas_call | solution.py:1007
  76.1 0.3 add_convert_fusion
  76.4 1.4 %collective-permute-start.6 = (bf16[2,4,48,384]{3,2,1,0:T(8,128)(2,1)S(1)}, bf16[2,4,48,384]{3,2,1,0:T(8,128)(2,1)S(1)}, u32[]{:S(2)}, u32[]{:S(2)}) collective-permute-start(bf16[2,4,48,384]{3,2,1,0:T(8,128)(2,1)S(1)} %get-tuple-element.99), channel_id=1, source_target_pairs={{0,1},{1,0},{2,3},{3,2},{4,5},{5,4},{6,7},{7,6},{8,9},{9,8},{10,11... | collective-permute-start | bytes 884744 | tf_op jit(solution)/shard_map/ppermute | solution.py:1044
  77.8 0.6 collective-permute-start.7
  78.4 4.9 %tap_grads_2.1 = f32[32,8,384]{2,1,0:T(8,128)S(1)} custom-call(s32[51]{0:T(128)S(1)} %copy-done.13, bf16[4,16,16,384]{3,2,1,0:T(8,128)(2,1)S(1)} %copy-done.7, bf16[4,256,1536]{2,1,0:T(8,128)(2,1)} %get-tuple-element.95.grad_pre_ref, f32[4,256,384]{2,1,0:T(8,128)S(1)} %copy-done.4, f32[4,256,128]{2,1,0:T(8,128)S(1)} %copy-done.8, ...), custom_call_target="tpu_custom_call" | custom-call | flops 4000000000 | bytes 1024 | tf_op jit(solution)/shard_map/tap_grads_2/pallas_call | solution.py:1007
  83.3 0.7 slice.165
  84.0 1.9 %collective-permute-done.6 = bf16[2,4,48,384]{3,2,1,0:T(8,128)(2,1)S(1)} collective-permute-done((bf16[2,4,48,384]{3,2,1,0:T(8,128)(2,1)S(1)}, bf16[2,4,48,384]{3,2,1,0:T(8,128)(2,1)S(1)}, u32[]{:S(2)}, u32[]{:S(2)}) %collective-permute-start.6) | collective-permute-done | bytes 294944 | tf_op jit(solution)/shard_map/ppermute | solution.py:1044
  85.9 0.9 collective-permute-done.7
  86.8 0.6 collective-permute-start.8
  87.5 0.9 collective-permute-start.9
  88.4 3.3 %all-to-all-start.1 = ((bf16[32,4,384]{2,1,0:T(4,128)(2,1)}), bf16[32,4,384]{2,1,0:T(4,128)(2,1)S(1)}, u32[]{:S(2)}, u32[]{:S(2)}) async-start(bf16[32,4,384]{2,1,0:T(4,128)(2,1)} %slice.165), calls=%async_computation.1 | async-start | bytes 196608 | tf_op jit(solution)/shard_map/all_to_all | solution.py:1055
  91.6 0.4 collective-permute-done.8
  92.0 0.1 fusion.6
  92.1 0.5 collective-permute-done.9
  92.6 0.1 fusion.2
  92.7 2.8 %collective-permute-start.12 = (bf16[96,384]{1,0:T(8,128)(2,1)S(1)}, bf16[96,384]{1,0:T(8,128)(2,1)S(1)}, u32[]{:S(2)}, u32[]{:S(2)}) collective-permute-start(bf16[96,384]{1,0:T(8,128)(2,1)S(1)} %get-tuple-element.110), channel_id=1, source_target_pairs={{0,6},{2,0},{4,2},{6,4},{1,7},{3,1},{5,3},{7,5},{8,14},{10,8},{12,... | collective-permute-start | bytes 221192 | tf_op jit(solution)/shard_map/ppermute | solution.py:1044
  95.5 1.1 %collective-permute-start.10 = (bf16[96,384]{1,0:T(8,128)(2,1)S(1)}, bf16[96,384]{1,0:T(8,128)(2,1)S(1)}, u32[]{:S(2)}, u32[]{:S(2)}) collective-permute-start(bf16[96,384]{1,0:T(8,128)(2,1)S(1)} %get-tuple-element.109), channel_id=1, source_target_pairs={{0,2},{2,4},{4,6},{6,0},{1,3},{3,5},{5,7},{7,1},{8,10},{10,12},{12... | collective-permute-start | bytes 221192 | tf_op jit(solution)/shard_map/ppermute | solution.py:1044
  96.6 2.6 %all-to-all-done.1 = bf16[32,4,384]{2,1,0:T(4,128)(2,1)S(1)} async-done(((bf16[32,4,384]{2,1,0:T(4,128)(2,1)}), bf16[32,4,384]{2,1,0:T(4,128)(2,1)S(1)}, u32[]{:S(2)}, u32[]{:S(2)}) %all-to-all-start.1) | async-done | bytes 98336 | tf_op jit(solution)/shard_map/all_to_all | solution.py:1055
  99.2 0.1 convert_reduce_fusion
  99.3 0.7 dynamic_slice.3
  100.0 3.9 %collective-permute-done.11 = bf16[96,384]{1,0:T(8,128)(2,1)S(1)} collective-permute-done((bf16[96,384]{1,0:T(8,128)(2,1)S(1)}, bf16[96,384]{1,0:T(8,128)(2,1)S(1)}, u32[]{:S(2)}, u32[]{:S(2)}) %collective-permute-start.11) | collective-permute-done | bytes 73760 | tf_op jit(solution)/shard_map/ppermute | solution.py:1044
  104.0 0.7 reshape.79
  104.6 0.6 reshape.80
  (43 shorter events, 0.3 us)
Async XLA Ops:
  1.3 0.7 copy-start.14
  4.8 19.3 %copy-start.15 = (f32[1,1152]{1,0:T(1,128)}, f32[1,1152]{1,0:T(1,128)S(1)}, u32[]{:S(2)}) copy-start(f32[1,1152]{1,0:T(1,128)S(1)} %get-tuple-element.83.small_ref) | copy-start | bytes 13828
  4.8 26.1 %copy-start.12 = (s32[51]{0:T(128)}, s32[51]{0:T(128)S(1)}, u32[]{:S(2)}) copy-start(s32[51]{0:T(128)S(1)} %get-tuple-element.55.table_ref) | copy-start | bytes 616
  4.8 3.1 %collective-permute-start = (bf16[33,16,384]{2,1,0:T(8,128)(2,1)S(1)}, bf16[33,16,384]{2,1,0:T(8,128)(2,1)S(1)}, u32[]{:S(2)}, u32[]{:S(2)}) collective-permute-start(bf16[33,16,384]{2,1,0:T(8,128)(2,1)S(1)} %get-tuple-element.58), channel_id=1, source_target_pairs={{0,8},{8,0},{16,24},{24,16},{1,9},{9,1},{17,25},{25,17},{2,10},{10... | collective-permute-start | bytes 1216520 | tf_op jit(solution)/shard_map/ppermute | solution.py:1114
  5.3 18.9 %collective-permute-start.3 = (bf16[17,16,384]{2,1,0:T(8,128)(2,1)S(1)}, bf16[17,16,384]{2,1,0:T(8,128)(2,1)S(1)}, u32[]{:S(2)}, u32[]{:S(2)}) collective-permute-start(bf16[17,16,384]{2,1,0:T(8,128)(2,1)S(1)} %get-tuple-element.62), channel_id=1, source_target_pairs={{0,16},{8,24},{16,0},{24,8},{1,17},{9,25},{17,1},{25,9},{2,18},{10... | collective-permute-start | bytes 626696 | tf_op jit(solution)/shard_map/ppermute | solution.py:1114
  7.9 16.3 %collective-permute-start.4 = (bf16[17,16,384]{2,1,0:T(8,128)(2,1)S(1)}, bf16[17,16,384]{2,1,0:T(8,128)(2,1)S(1)}, u32[]{:S(2)}, u32[]{:S(2)}) collective-permute-start(bf16[17,16,384]{2,1,0:T(8,128)(2,1)S(1)} %get-tuple-element.63), channel_id=1, source_target_pairs={{0,24},{8,16},{16,8},{24,0},{1,25},{9,17},{17,9},{25,1},{2,26},{10... | collective-permute-start | bytes 626696 | tf_op jit(solution)/shard_map/ppermute | solution.py:1114
  7.9 16.2 %copy-start.9 = (bf16[33,16,384]{2,1,0:T(8,128)(2,1)}, bf16[33,16,384]{2,1,0:T(8,128)(2,1)S(1)}, u32[]{:S(2)}) copy-start(bf16[33,16,384]{2,1,0:T(8,128)(2,1)S(1)} %collective-permute-done.refs_1_.refs_0_) | copy-start | bytes 1216516
  8.0 22.9 %collective-permute-start.1 = (bf16[16,16,384]{2,1,0:T(8,128)(2,1)S(1)}, bf16[16,16,384]{2,1,0:T(8,128)(2,1)S(1)}, u32[]{:S(2)}, u32[]{:S(2)}) collective-permute-start(bf16[16,16,384]{2,1,0:T(8,128)(2,1)S(1)} %get-tuple-element.59), channel_id=1, source_target_pairs={{0,16},{8,24},{16,0},{24,8},{1,17},{9,25},{17,1},{25,9},{2,18},{10... | collective-permute-start | bytes 589832 | tf_op jit(solution)/shard_map/ppermute | solution.py:1114
  9.7 21.2 %collective-permute-start.2 = (bf16[16,16,384]{2,1,0:T(8,128)(2,1)S(1)}, bf16[16,16,384]{2,1,0:T(8,128)(2,1)S(1)}, u32[]{:S(2)}, u32[]{:S(2)}) collective-permute-start(bf16[16,16,384]{2,1,0:T(8,128)(2,1)S(1)} %get-tuple-element.60), channel_id=1, source_target_pairs={{0,24},{8,16},{16,8},{24,0},{1,25},{9,17},{17,9},{25,1},{2,26},{10... | collective-permute-start | bytes 589832 | tf_op jit(solution)/shard_map/ppermute | solution.py:1114
  24.2 6.7 %copy-start.10 = (bf16[17,16,384]{2,1,0:T(8,128)(2,1)}, bf16[17,16,384]{2,1,0:T(8,128)(2,1)S(1)}, u32[]{:S(2)}) copy-start(bf16[17,16,384]{2,1,0:T(8,128)(2,1)S(1)} %collective-permute-done.3.refs_0_.refs_1_) | copy-start | bytes 626692
  24.2 6.7 %copy-start.11 = (bf16[17,16,384]{2,1,0:T(8,128)(2,1)}, bf16[17,16,384]{2,1,0:T(8,128)(2,1)S(1)}, u32[]{:S(2)}) copy-start(bf16[17,16,384]{2,1,0:T(8,128)(2,1)S(1)} %collective-permute-done.4.refs_1_.refs_2_) | copy-start | bytes 626692
  31.8 22.2 %copy-start.13 = (s32[51]{0:T(128)S(1)}, s32[51]{0:T(128)}, u32[]{:S(2)}) copy-start(s32[51]{0:T(128)} %copy-done.12) | copy-start | bytes 616
  53.9 0.7 copy-start.16
  54.7 5.5 %copy-start = (bf16[4,256,1536]{2,1,0:T(8,128)(2,1)S(1)}, bf16[4,256,1536]{2,1,0:T(8,128)(2,1)}, u32[]{:S(2)}) copy-start(bf16[4,256,1536]{2,1,0:T(8,128)(2,1)} %get-tuple-element.88) | copy-start | bytes 9437188
  54.7 5.5 %copy-start.1 = (bf16[4,256,1536]{2,1,0:T(8,128)(2,1)S(1)}, bf16[4,256,1536]{2,1,0:T(8,128)(2,1)}, u32[]{:S(2)}) copy-start(bf16[4,256,1536]{2,1,0:T(8,128)(2,1)} %get-tuple-element.90.slope_ref) | copy-start | bytes 9437188
  54.7 5.6 %copy-start.2 = (bf16[1536,384]{1,0:T(8,128)(2,1)S(1)}, bf16[1536,384]{1,0:T(8,128)(2,1)}, u32[]{:S(2)}) copy-start(bf16[1536,384]{1,0:T(8,128)(2,1)} %reduce_ref.1) | copy-start | bytes 3538948
  54.7 5.6 %copy-start.4 = (f32[4,256,384]{2,1,0:T(8,128)S(1)}, f32[4,256,384]{2,1,0:T(8,128)}, u32[]{:S(2)}) copy-start(f32[4,256,384]{2,1,0:T(8,128)} %get-tuple-element.91.unit_ref) | copy-start | bytes 4718596
  54.7 5.6 %copy-start.5 = (bf16[4,256,768]{2,1,0:T(8,128)(2,1)S(1)}, bf16[4,256,768]{2,1,0:T(8,128)(2,1)}, u32[]{:S(2)}) copy-start(bf16[4,256,768]{2,1,0:T(8,128)(2,1)} %get-tuple-element.89.head_slope_ref) | copy-start | bytes 4718596
  54.7 5.6 %copy-start.6 = (bf16[384,768]{1,0:T(8,128)(2,1)S(1)}, bf16[384,768]{1,0:T(8,128)(2,1)}, u32[]{:S(2)}) copy-start(bf16[384,768]{1,0:T(8,128)(2,1)} %head_ref.1) | copy-start | bytes 1769476
  60.3 11.0 %copy-start.3 = (bf16[384,1536]{1,0:T(8,128)(2,1)S(1)}, bf16[384,1536]{1,0:T(8,128)(2,1)}, u32[]{:S(2)}) copy-start(bf16[384,1536]{1,0:T(8,128)(2,1)} %expand_ref.3) | copy-start | bytes 3538948
  60.3 11.0 %copy-start.7 = (bf16[4,16,16,384]{3,2,1,0:T(8,128)(2,1)S(1)}, bf16[4,16,16,384]{3,2,1,0:T(8,128)(2,1)}, u32[]{:S(2)}) copy-start(bf16[4,16,16,384]{3,2,1,0:T(8,128)(2,1)} %get-tuple-element.94.source_ref) | copy-start | bytes 2359300
  60.3 11.0 %copy-start.8 = (f32[4,256,128]{2,1,0:T(8,128)S(1)}, f32[4,256,128]{2,1,0:T(8,128)}, u32[]{:S(2)}) copy-start(f32[4,256,128]{2,1,0:T(8,128)} %get-tuple-element.96.inv_ref) | copy-start | bytes 1572868
  71.1 5.0 %collective-permute-start.5 = (bf16[2,2,2,4,48,384]{5,4,3,2,1,0:T(8,128)(2,1)S(1)}, bf16[2,2,2,4,48,384]{5,4,3,2,1,0:T(8,128)(2,1)S(1)}, u32[]{:S(2)}, u32[]{:S(2)}) collective-permute-start(bf16[2,2,2,4,48,384]{5,4,3,2,1,0:T(8,128)(2,1)S(1)} %get-tuple-element.93), channel_id=1, source_target_pairs={{0,8},{8,0},{1,9},{9,1},{2,10},{10,2},{3,11},{11,3},{4,12},{12,4},... | collective-permute-start | bytes 3538952 | tf_op jit(solution)/shard_map/ppermute | solution.py:1044
  76.4 9.5 %collective-permute-start.6 = (bf16[2,4,48,384]{3,2,1,0:T(8,128)(2,1)S(1)}, bf16[2,4,48,384]{3,2,1,0:T(8,128)(2,1)S(1)}, u32[]{:S(2)}, u32[]{:S(2)}) collective-permute-start(bf16[2,4,48,384]{3,2,1,0:T(8,128)(2,1)S(1)} %get-tuple-element.99), channel_id=1, source_target_pairs={{0,1},{1,0},{2,3},{3,2},{4,5},{5,4},{6,7},{7,6},{8,9},{9,8},{10,11... | collective-permute-start | bytes 884744 | tf_op jit(solution)/shard_map/ppermute | solution.py:1044
  77.8 9.0 %collective-permute-start.7 = (bf16[2,4,48,384]{3,2,1,0:T(8,128)(2,1)S(1)}, bf16[2,4,48,384]{3,2,1,0:T(8,128)(2,1)S(1)}, u32[]{:S(2)}, u32[]{:S(2)}) collective-permute-start(bf16[2,4,48,384]{3,2,1,0:T(8,128)(2,1)S(1)} %get-tuple-element.100), channel_id=1, source_target_pairs={{0,16},{16,0},{1,17},{17,1},{2,18},{18,2},{3,19},{19,3},{4,20},{20... | collective-permute-start | bytes 884744 | tf_op jit(solution)/shard_map/ppermute | solution.py:1044
  86.8 5.2 %collective-permute-start.8 = (bf16[4,48,384]{2,1,0:T(8,128)(2,1)S(1)}, bf16[4,48,384]{2,1,0:T(8,128)(2,1)S(1)}, u32[]{:S(2)}, u32[]{:S(2)}) collective-permute-start(bf16[4,48,384]{2,1,0:T(8,128)(2,1)S(1)} %fusion.9), channel_id=1, source_target_pairs={{0,16},{16,0},{1,17},{17,1},{2,18},{18,2},{3,19},{19,3},{4,20},{20... | collective-permute-start | bytes 442376 | tf_op jit(solution)/shard_map/ppermute | solution.py:1044
  87.5 5.1 %collective-permute-start.9 = (bf16[4,48,384]{2,1,0:T(8,128)(2,1)S(1)}, bf16[4,48,384]{2,1,0:T(8,128)(2,1)S(1)}, u32[]{:S(2)}, u32[]{:S(2)}) collective-permute-start(bf16[4,48,384]{2,1,0:T(8,128)(2,1)S(1)} %fusion.10), channel_id=1, source_target_pairs={{0,1},{1,0},{2,3},{3,2},{4,5},{5,4},{6,7},{7,6},{8,9},{9,8},{10,11... | collective-permute-start | bytes 442376 | tf_op jit(solution)/shard_map/ppermute | solution.py:1044
  88.4 10.9 %all-to-all-start.1 = ((bf16[32,4,384]{2,1,0:T(4,128)(2,1)}), bf16[32,4,384]{2,1,0:T(4,128)(2,1)S(1)}, u32[]{:S(2)}, u32[]{:S(2)}) async-start(bf16[32,4,384]{2,1,0:T(4,128)(2,1)} %slice.165), calls=%async_computation.1 | async-start | bytes 196608 | tf_op jit(solution)/shard_map/all_to_all | solution.py:1055
  92.7 7.3 %collective-permute-start.12 = (bf16[96,384]{1,0:T(8,128)(2,1)S(1)}, bf16[96,384]{1,0:T(8,128)(2,1)S(1)}, u32[]{:S(2)}, u32[]{:S(2)}) collective-permute-start(bf16[96,384]{1,0:T(8,128)(2,1)S(1)} %get-tuple-element.110), channel_id=1, source_target_pairs={{0,6},{2,0},{4,2},{6,4},{1,7},{3,1},{5,3},{7,5},{8,14},{10,8},{12,... | collective-permute-start | bytes 221192 | tf_op jit(solution)/shard_map/ppermute | solution.py:1044
  95.5 8.3 %collective-permute-start.11 = (bf16[96,384]{1,0:T(8,128)(2,1)S(1)}, bf16[96,384]{1,0:T(8,128)(2,1)S(1)}, u32[]{:S(2)}, u32[]{:S(2)}) collective-permute-start(bf16[96,384]{1,0:T(8,128)(2,1)S(1)} %get-tuple-element.111), channel_id=1, source_target_pairs={{0,4},{2,6},{4,0},{6,2},{1,5},{3,7},{5,1},{7,3},{8,12},{10,14},{12... | collective-permute-start | bytes 221192 | tf_op jit(solution)/shard_map/ppermute | solution.py:1044
  95.5 8.3 %collective-permute-start.10 = (bf16[96,384]{1,0:T(8,128)(2,1)S(1)}, bf16[96,384]{1,0:T(8,128)(2,1)S(1)}, u32[]{:S(2)}, u32[]{:S(2)}) collective-permute-start(bf16[96,384]{1,0:T(8,128)(2,1)S(1)} %get-tuple-element.109), channel_id=1, source_target_pairs={{0,2},{2,4},{4,6},{6,0},{1,3},{3,5},{5,7},{7,1},{8,10},{10,12},{12... | collective-permute-start | bytes 221192 | tf_op jit(solution)/shard_map/ppermute | solution.py:1044

commit v8 on v7

--- a/solution.py
+++ b/solution.py
@@ -37,6 +37,7 @@
 IN_HBM = pl.BlockSpec(memory_space=pltpu.HBM)
 ROWS_AT, COLS_AT, COUNT_AT, SMALL = E, E + LANES, E + 2 * LANES, E + 3 * LANES
 PIECES = 3
+HALF = 512
 
 
 def whole(shape):
@@ -515,7 +516,10 @@
 
 
 def rows_kernel(slides, table_ref, embed_ref, small_ref, *refs):
-    buffer_refs, (out_ref, smalls_ref, rows_ref, extra_ref, sems) = refs[: slides - 1], refs[slides - 1 :]
+    buffer_refs, (out_ref, smalls_ref, rows_ref, lines_ref, extra_ref, sems) = (
+        refs[: slides - 1],
+        refs[slides - 1 :],
+    )
     copies = [
         pltpu.make_async_copy(ref.at[ref.shape[0] - 1], extra_ref.at[index], sems.at[index])
         for index, ref in enumerate(buffer_refs)
@@ -558,8 +562,7 @@
         target = jnp.where(lane < 3, target, 0)
         rows_ref[proc : proc + 1, 0:E] = angle
         rows_ref[2 * PROC + proc : 2 * PROC + proc + 1, 0:E] = embed_ref[proc, 0:1, :]
-        for copied in range(proc, ROW_UNIT, PROC):
-            rows_ref[copied : copied + 1, E:] = target.astype(jnp.float32)
+        rows_ref[proc : proc + 1, E:] = target.astype(jnp.float32)
     code = jnp.sin(rows_ref[0 : 2 * PROC, 0:E])
     embed = rows_ref[2 * PROC : 4 * PROC, 0:E].astype(jnp.bfloat16).astype(jnp.float32)
     row_id = lax.broadcasted_iota(jnp.int32, (2 * PROC, E), 0)
@@ -568,9 +571,11 @@
         there = there | ((row_id == proc) & (table_ref[FILLED + proc] != 0))
     total = jnp.where(there, embed + code, 0.0)
     rows_ref[0 : 2 * PROC, 0:E] = total
-    for copied in range(PROC, ROW_UNIT):
-        rows_ref[copied : copied + 1, 0:E] = rows_ref[copied - PROC : copied - PROC + 1, 0:E]
-    sent = rows_ref[...].astype(jnp.bfloat16)
+    lines_ref[...] = jnp.zeros(lines_ref.shape, jnp.float32)
+    for copied in range(0, ROW_UNIT, 2 * PROC):
+        lines_ref[copied : copied + PROC, :] = rows_ref[0:PROC, 0:HALF]
+        lines_ref[copied + PROC : copied + 2 * PROC, 0 : E + LANES - HALF] = rows_ref[0:PROC, HALF:]
+    sent = lines_ref[...].astype(jnp.bfloat16)
     for start in range(0, out_ref.shape[0], ROW_UNIT):
         out_ref[start : start + ROW_UNIT, :] = sent
 
@@ -582,13 +587,14 @@
     return pl.pallas_call(
         functools.partial(rows_kernel, slides),
         out_shape=(
-            jax.ShapeDtypeStruct((devices * PROC, E + LANES), jnp.bfloat16),
+            jax.ShapeDtypeStruct((devices * 2 * PROC, HALF), jnp.bfloat16),
             jax.ShapeDtypeStruct((slides, 1, SMALL), jnp.float32),
         ),
         in_specs=[smem, vmem, vmem] + [HBM] * len(buffers),
         out_specs=(vmem, vmem),
         scratch_shapes=[
             pltpu.VMEM((4 * PROC, E + LANES), jnp.float32),
+            pltpu.VMEM((ROW_UNIT, HALF), jnp.float32),
             pltpu.VMEM((len(buffers),) + buffers[0].shape[1:], jnp.bfloat16),
             pltpu.SemaphoreType.DMA((len(buffers),)),
         ],
@@ -631,7 +637,11 @@
     blocks = [slice(start, start + WIDTH) for start in range(0, E, WIDTH)]
     lane = lax.broadcasted_iota(jnp.int32, (8, LANES), 1)
     scales = jnp.where(lane == 0, length, jnp.where(lane == 1, members, jnp.where(lane == 2, 1, 0)))
-    target = mix_cols(scales.astype(jnp.float32).astype(jnp.bfloat16), came_ref[:, E:])[0:1, :]
+    tail = came_ref[:, E - HALF : E - HALF + LANES]
+    target = mix_cols(scales.astype(jnp.float32).astype(jnp.bfloat16), tail)[0:1, :]
+    lines = came_ref.shape[0]
+    second = lax.rem(lax.broadcasted_iota(jnp.int32, (1, lines), 1), 2 * PROC) >= PROC
+    target = jnp.where(second, target, -1.0)
     step = lax.broadcasted_iota(jnp.int32, (length, 1), 0).astype(jnp.float32)
 
     def dilate(ref, slide, direction, cols):
@@ -641,47 +651,58 @@
             total = total + taps_ref[tap : tap + 1, cols] * ref[slide, start : start + length, cols]
         return total
 
+    def seen(other):
+        count = smalls_ref[other][:, COUNT_AT : COUNT_AT + 1]
+        here = step < count
+        return here, jnp.where(here, 1.0 / count, 0.0)
+
     for other in range(slides):
         slide = my_slide ^ other
-        small = smalls_ref[other]
-        count = small[:, COUNT_AT : COUNT_AT + 1]
-        here = step < count
+        here, _ = seen(other)
         first = lax.convert_element_type(slide * length, jnp.float32)
-        pick = ((target - first) == step).astype(jnp.float32).astype(jnp.bfloat16)
+        late = ((target - first) == step).astype(jnp.float32)
+        early = pltpu.roll(late, lines - PROC, axis=1).astype(jnp.bfloat16)
+        late = late.astype(jnp.bfloat16)
         for ref in (rows, back):
             ref[slide, 0:border, :] = edge
             ref[slide, border + length :, :] = edge
         if other == 0:
             loads[0].wait()
         for cols in blocks:
+            pick, at = (early, cols.start) if cols.start < HALF else (late, cols.start - HALF)
             rows[slide, border : border + length, cols] = jnp.where(
-                here, mix(pick, came_ref[:, cols]), 0.0
+                here, mix(pick, came_ref[:, at : at + WIDTH]), 0.0
             )
-            mixed[other, :, cols] = dilate(rows, slide, 1, cols).astype(jnp.bfloat16)
+            mixed[other * length : (other + 1) * length, cols] = dilate(
+                rows, slide, 1, cols
+            ).astype(jnp.bfloat16)
     loads[1].wait()
-    for other in range(slides):
-        slide = my_slide ^ other
-        small = smalls_ref[other]
-        here = step < small[:, COUNT_AT : COUNT_AT + 1]
-        share = jnp.where(here, 1.0 / small[:, COUNT_AT : COUNT_AT + 1], 0.0)
-        for cols in blocks:
-            pre[:, cols] = mix(mixed[other], matrix_ref[:, cols])
+    for cols in blocks:
+        pre[:, cols] = mix(mixed[...], matrix_ref[:, cols])
+        for other in range(slides):
+            small = smalls_ref[other]
+            _, share = seen(other)
             total = None
             for start in range(0, length, PART):
-                part = slice(start, start + PART)
+                part = slice(other * length + start, other * length + start + PART)
+                weight = share[start : start + PART]
                 act, slope = gelu_and_slope(
                     pre[part, cols] + vectors_ref[SLIDE_BIAS : SLIDE_BIAS + 1, cols]
                 )
-                grad_agg[part, cols] = (small[:, cols] * share[part] * slope).astype(jnp.bfloat16)
+                grad_agg[part, cols] = (small[:, cols] * weight * slope).astype(jnp.bfloat16)
                 if other == 0:
-                    piece = jnp.sum(act * share[part], axis=0, keepdims=True)
+                    piece = jnp.sum(act * weight, axis=0, keepdims=True)
                     total = piece if total is None else total + piece
             if other == 0:
                 feature_ref[:, cols] = total
-        for cols in blocks:
-            back[slide, border : border + length, cols] = mix_cols(
-                grad_agg[...], matrix_ref[cols, :]
-            )
+    for cols in blocks:
+        pre[:, cols] = mix_cols(grad_agg[...], matrix_ref[cols, :])
+        for other in range(slides):
+            slide = my_slide ^ other
+            here, _ = seen(other)
+            back[slide, border : border + length, cols] = pre[
+                other * length : (other + 1) * length, cols
+            ]
             total = jnp.where(here, dilate(back, slide, -1, cols), 0.0)
             rows[slide, border : border + length, cols] = total.astype(jnp.bfloat16).astype(
                 jnp.float32
@@ -709,9 +730,9 @@
         scratch_shapes=[
             pltpu.VMEM(padded, jnp.float32),
             pltpu.VMEM(padded, jnp.float32),
-            pltpu.VMEM((slides, length, E), jnp.bfloat16),
-            pltpu.VMEM((length, E), jnp.float32),
-            pltpu.VMEM((length, E), jnp.bfloat16),
+            pltpu.VMEM((slides * length, E), jnp.bfloat16),
+            pltpu.VMEM((slides * length, E), jnp.float32),
+            pltpu.VMEM((slides * length, E), jnp.bfloat16),
             pltpu.VMEM(taps.shape, jnp.float32),
             pltpu.VMEM(matrix.shape, jnp.bfloat16),
             pltpu.SemaphoreType.DMA((2,)),
@@ -765,13 +786,48 @@
     return block.astype(jnp.bfloat16)
 
 
+def turn_kernel(unit_ref, vectors_ref, out_ref, normed, eye_ref):
+    cells, channels = unit_ref.shape[1:]
+    eye_ref[...] = unit_matrix(channels)
+    for start in range(0, cells, PART):
+        rows = slice(start, start + PART)
+        gain = vectors_ref[GAIN : GAIN + 1, 0:channels]
+        shift = vectors_ref[SHIFT : SHIFT + 1, 0:channels]
+        normed[rows, :] = (unit_ref[0, rows, :] * gain + shift).astype(jnp.bfloat16)
+    out_ref[...] = mix_cols(eye_ref[...], normed[...]).astype(jnp.bfloat16)
+
+
+def unit_matrix(size):
+    spot = lax.broadcasted_iota(jnp.int32, (size, size), 0)
+    same = spot == lax.broadcasted_iota(jnp.int32, (size, size), 1)
+    return same.astype(jnp.float32).astype(jnp.bfloat16)
+
+
+def turned_normed(unit, vectors):
+    cells, channels = unit.shape[1:]
+    return pl.pallas_call(
+        turn_kernel,
+        out_shape=jax.ShapeDtypeStruct((channels, PROC * cells), jnp.bfloat16),
+        grid=(PROC,),
+        in_specs=[pl.BlockSpec((1, cells, channels), lambda i: (i, 0, 0)), whole(vectors.shape)],
+        out_specs=pl.BlockSpec((channels, cells), lambda i: (0, i)),
+        scratch_shapes=[
+            pltpu.VMEM((cells, channels), jnp.bfloat16),
+            pltpu.VMEM((channels, channels), jnp.bfloat16),
+        ],
+        compiler_params=pltpu.CompilerParams(vmem_limit_bytes=8 * MIB),
+        cost_estimate=cost(3.0),
+        name="turned_normed",
+    )(unit, vectors)
+
+
 def weights_kernel(
     plan,
     grad_ref,
     hidden_ref,
     head_slope_ref,
     slope_ref,
-    unit_ref,
+    normed_ref,
     vectors_ref,
     head_ref,
     reduce_ref,
@@ -780,23 +836,20 @@
     send_ref,
     grad_pre,
     turned,
-    normed,
     grad_head,
     eye_ref,
     staged,
     sems,
     pre_sems,
 ):
-    cells, channels = unit_ref.shape[1:]
+    cells, channels = slope_ref.shape[1], normed_ref.shape[0]
     hid = reduce_ref.shape[0]
     every = slice(0, channels)
 
     def vector(index, lanes):
         return vectors_ref[index : index + 1, lanes]
 
-    spot = lax.broadcasted_iota(jnp.int32, eye_ref.shape, 0)
-    same = spot == lax.broadcasted_iota(jnp.int32, eye_ref.shape, 1)
-    eye_ref[...] = same.astype(jnp.float32).astype(jnp.bfloat16)
+    eye_ref[...] = unit_matrix(channels)
 
     def one_slot(slot, carry):
         rows_all = pl.ds(pl.multiple_of(slot * cells, cells), cells)
@@ -806,14 +859,10 @@
             grad_head[rows, :] = (row * head_slope_ref[slot, rows, :].astype(jnp.float32)).astype(
                 jnp.bfloat16
             )
-            normed[rows, :] = (
-                unit_ref[slot, rows, :] * vector(GAIN, every) + vector(SHIFT, every)
-            ).astype(jnp.bfloat16)
         grad_mlp = (vector(SCALE, every) * mix_cols(grad_head[...], head_ref[...])).astype(
             jnp.bfloat16
         )
-        turned[0, :, rows_all] = mix_cols(eye_ref[...], grad_mlp).astype(jnp.bfloat16)
-        turned[1, :, rows_all] = mix_cols(eye_ref[...], normed[...]).astype(jnp.bfloat16)
+        turned[:, rows_all] = mix_cols(eye_ref[...], grad_mlp).astype(jnp.bfloat16)
         for begin in range(0, hid, WIDTH):
             cols = slice(begin, begin + WIDTH)
             grad_hidden = mix_cols(grad_mlp, reduce_ref[cols, :])
@@ -836,7 +885,7 @@
     tall = plan.block_rows
     for index in range(plan.pieces):
         cols = slice(index * channels, (index + 1) * channels)
-        total = mix(turned[0], hidden_ref[:, cols]).astype(jnp.bfloat16)
+        total = mix(turned[...], hidden_ref[:, cols]).astype(jnp.bfloat16)
         back = mix_cols(eye_ref[...], total)
         for part in range(per_block):
             block = back[part * plan.reduce_rows : (part + 1) * plan.reduce_rows]
@@ -845,7 +894,7 @@
     totals = []
     for quarter in range(plan.pieces):
         cols = slice(quarter * channels, (quarter + 1) * channels)
-        totals.append(mix(turned[1], grad_pre[:, cols]))
+        totals.append(mix(normed_ref[...], grad_pre[:, cols]))
     size = plan.expand_rows
     for device in range(plan.devices):
         rows = slice(device * size, (device + 1) * size)
@@ -966,8 +1015,8 @@
 
 
 def weight_grads(plan, embed_grad, saved, vectors, head, reduce):
-    unit, hidden, slope, head_slope = saved
-    cells, channels = unit.shape[1:]
+    normed, hidden, slope, head_slope = saved
+    cells, channels = slope.shape[1], normed.shape[0]
     hid = reduce.shape[0]
     vmem = pl.BlockSpec(memory_space=pltpu.VMEM)
     blocks = jax.ShapeDtypeStruct(
@@ -980,8 +1029,7 @@
         out_specs=(IN_HBM, HBM, HBM),
         scratch_shapes=[
             pltpu.VMEM((PROC * cells, hid), jnp.bfloat16),
-            pltpu.VMEM((2, channels, PROC * cells), jnp.bfloat16),
-            pltpu.VMEM((cells, channels), jnp.bfloat16),
+            pltpu.VMEM((channels, PROC * cells), jnp.bfloat16),
             pltpu.VMEM((cells, head.shape[1]), jnp.bfloat16),
             pltpu.VMEM((channels, channels), jnp.bfloat16),
             pltpu.VMEM((2,) + blocks.shape, jnp.bfloat16),
@@ -991,7 +1039,7 @@
         compiler_params=pltpu.CompilerParams(vmem_limit_bytes=36 * MIB),
         cost_estimate=cost(12.0),
         name="weight_grads",
-    )(embed_grad, hidden.reshape(PROC * cells, hid), head_slope, slope, unit, vectors, head, reduce)
+    )(embed_grad, hidden.reshape(PROC * cells, hid), head_slope, slope, normed, vectors, head, reduce)
 
 
 def tap_grads(plan, first, last, table, streams, before, vectors, expand):
@@ -1128,6 +1176,8 @@
     tile_out, tile_embed, unit, inv, hidden, slope, head_slope, source = saved
     came, smalls = tile_rows(table, tile_embed, small, [from_core] + arrived[0], devices)
     came = exchange(came, ALL)
+    normed = turned_normed(unit, vectors)
+    came, normed = lax.optimization_barrier((came, normed))
 
     feature, embed_grad = slide_grads(
         length, members, table, came, slide_taps, slide_weight, vectors, smalls
@@ -1135,7 +1185,7 @@
     grad_pre, kept, sent = weight_grads(
         plan,
         embed_grad,
-        (unit, hidden, slope, head_slope),
+        (normed, hidden, slope, head_slope),
         vectors,
         head_weight,
         reduce_weight,

time: 107 us -> 105 us (0.981); the launches traced: 105 us -> 106 us
  blocking collectives: 18.5 us -> 0 us
  starting transfers between devices: 15.6 us -> 27.4 us
  waiting for transfers between devices: 10.2 us -> 18.7 us
  local copies, waits for them, and re-layouts: 5.26 us -> 3.48 us
    all_to_all x1 -> x0, blocking collectives: 18.5 us -> none  [exchange(): lax.all_to_all(values, names, split_axis=0, concat_axis=0, tiled=True)]
    all_to_all x1 -> x2, starting transfers between devices: 3.28 us -> 14.6 us  [exchange(): lax.all_to_all(values, names, split_axis=0, concat_axis=0, tiled=True)]
    all_to_all x1 -> x2, waiting for transfers between devices: 2.63 us -> 11.7 us  [exchange(): lax.all_to_all(values, names, split_axis=0, concat_axis=0, tiled=True)]
    pallas_call x0 -> x1, Pallas kernels: none -> 1.32 us  [turned_normed(): pl.pallas_call(turn_kernel, out_shape=jax.ShapeDtypeStruct((channels, PRO...]
  transfers between devices with their start and end apart: 14 -> 15, of which waited for: 6 -> 5; matrix products, arithmetic and copies ran while one was open for 2% -> 2% of each run, Pallas kernels for 29% -> 30%
where the time goes in v8:
time: 105 us; the launch traced here: 106 us
  Pallas kernels  54.2 us (52%)
  starting transfers between devices  27.4 us (26%)
  waiting for transfers between devices  18.7 us (18%)
  local copies, waits for them, and re-layouts  3.48 us (3%)
  between operations  1.73 us (2%)
    pallas_call x3, Pallas kernels, forward_block(): pl.pallas_call(functools.partial(forward_kernel, kind, last, len(tiles),...  21.9 us
    all_to_all x2, starting transfers between devices, exchange(): lax.all_to_all(values, names, split_axis=0, concat_axis=0, tiled=True)  14.6 us
    all_to_all x2, waiting for transfers between devices, exchange(): lax.all_to_all(values, names, split_axis=0, concat_axis=0, tiled=True)  11.7 us
    pallas_call x1, Pallas kernels, weight_grads(): pl.pallas_call(functools.partial(weights_kernel, plan), out_shape=(pltpu....  10.4 us
    pallas_call x2, Pallas kernels, tap_grads(): pl.pallas_call(functools.partial(taps_kernel, plan, first, last), out_sha...  9.76 us
    ppermute x8, starting transfers between devices, shifted(): return lax.ppermute(values, names, pairs)  7.91 us
    ppermute x8, waiting for transfers between devices, shifted(): return lax.ppermute(values, names, pairs)  6.98 us
    pallas_call x1, Pallas kernels, slide_grads(): pl.pallas_call(functools.partial(slide_kernel, length, members, slides),...  5.29 us
  transfers between devices with their start and end apart: 15, of which 5 were waited for; matrix products, arithmetic and copies ran while one was open for 2% of the time, Pallas kernels for 30%

profile of v8, /device:TPU:0, one launch (start us, length us, event | category | flops | bytes accessed | tf_op | source)
XLA Modules:
  0.0 106.2 jit_solution(10087886719882652611)
XLA Ops:
  1.3 0.7 copy-done.14
  2.0 2.8 %pack_tiles.1 = (bf16[33,16,384]{2,1,0:T(8,128)(2,1)S(1)}, bf16[17,16,384]{2,1,0:T(8,128)(2,1)S(1)}, bf16[17,16,384]{2,1,0:T(8,128)(2,1)S(1)}, bf16[16,16,384]{2...) custom-call(s32[1]{0:T(128)S(6)} %copy.56.counts_ref, ...), custom_call_target="tpu_custom_call" | custom-call | tf_op jit(solution)/shard_map/pack_tiles/pallas_call | solution.py:225
  4.8 0.0 copy-start.15
  4.8 0.0 copy-start.12
  4.8 0.5 collective-permute-start
  5.3 2.6 %collective-permute-start.3 = (bf16[17,16,384]{2,1,0:T(8,128)(2,1)S(1)}, bf16[17,16,384]{2,1,0:T(8,128)(2,1)S(1)}, u32[]{:S(2)}, u32[]{:S(2)}) collective-permute-start(bf16[17,16,384]{2,1,0:T(8,128)(2,1)S(1)} %get-tuple-element.64), channel_id=1, source_target_pairs={{0,16},{8,24},{16,0},{24,8},{1,17},{9,25},{17,1},{25,9},{2,18},{10... | collective-permute-start | bytes 626696 | tf_op jit(solution)/shard_map/ppermute | solution.py:1162
  7.9 0.1 collective-permute-start.4
  8.0 1.7 %collective-permute-start.1 = (bf16[16,16,384]{2,1,0:T(8,128)(2,1)S(1)}, bf16[16,16,384]{2,1,0:T(8,128)(2,1)S(1)}, u32[]{:S(2)}, u32[]{:S(2)}) collective-permute-start(bf16[16,16,384]{2,1,0:T(8,128)(2,1)S(1)} %get-tuple-element.61), channel_id=1, source_target_pairs={{0,16},{8,24},{16,0},{24,8},{1,17},{9,25},{17,1},{25,9},{2,18},{10... | collective-permute-start | bytes 589832 | tf_op jit(solution)/shard_map/ppermute | solution.py:1162
  9.7 0.0 collective-permute-start.2
  9.7 14.4 %forward_block_0.1 = (bf16[4,16,16,384]{3,2,1,0:T(8,128)(2,1)}, f32[4,8,768]{2,1,0:T(8,128)}, f32[4,256,384]{2,1,0:T(8,128)}, f32[4,256,128]{2,1,0:T(8,128)}, bf...) custom-call(s32[51]{0:T(128)S(1)} %get-tuple-element.57.table_ref, ...), custom_call_target="tpu_custom_call" | custom-call | flops 1000000000 | bytes 1024 | tf_op jit(solution)/shard_map/forward_block_0/pallas_call | solution.py:485
  24.1 0.0 collective-permute-done.3.refs_0_.refs_1_
  24.2 6.6 %forward_block_1.1 = (bf16[4,16,16,384]{3,2,1,0:T(8,128)(2,1)}, f32[4,8,768]{2,1,0:T(8,128)}, f32[4,256,384]{2,1,0:T(8,128)}, f32[4,256,128]{2,1,0:T(8,128)}, bf...) custom-call(s32[51]{0:T(128)S(1)} %get-tuple-element.57.table_ref, ...), custom_call_target="tpu_custom_call", output_to_operand_aliasing={{0}: (8, {}), {1}: (9, {}), {2}: (10, {}), {3}: (11, {}), {... | custom-call | flops 1000000000 | bytes 1024 | tf_op jit(solution)/shard_map/forward_block_1/pallas_call | solution.py:485
  30.9 0.9 forward_block_2.1
  31.8 2.8 %tile_rows.1 = (bf16[256,512]{1,0:T(8,128)(2,1)}, f32[4,1,1152]{2,1,0:T(1,128)}) custom-call(s32[51]{0:T(128)} %copy-done.12, f32[4,8,768]{2,1,0:T(8,128)} %get-tuple-element.84.embed_ref, f32[1,1152]{1,0:T(1,128)} %copy-done.15, bf16[33,16,384]{2,1,0:T(8,128)(2,1)} %copy-done.9, bf16[17,16,384]{2,1,0:T(8,128)(2,1)} %copy-done.10, ...), custom_call_target="tpu_custom_call" | custom-call | flops 1000000000 | bytes 1024 | tf_op jit(solution)/shard_map/tile_rows/pallas_call | solution.py:587
  34.5 11.4 %all-to-all-start = ((bf16[32,8,512]{2,1,0:T(8,128)(2,1)}), bf16[32,8,512]{2,1,0:T(8,128)(2,1)S(1)}, u32[]{:S(2)}, u32[]{:S(2)}) async-start(bf16[32,8,512]{2,1,0:T(8,128)(2,1)} %bitcast.56), calls=%async_computation | async-start | bytes 524288 | tf_op jit(solution)/shard_map/all_to_all | solution.py:1103
  46.0 0.0 copy-start.13
  46.0 0.0 copy-start.16
  46.0 1.3 %turned_normed.1.normed_ref = bf16[384,1024]{1,0:T(8,128)(2,1)S(1)} custom-call(f32[4,256,384]{2,1,0:T(8,128)S(1)} %copy-done.4, f32[8,1536]{1,0:T(8,128)S(1)} %get-tuple-element.63.refs_3_.vectors_ref), custom_call_target="tpu_custom_call" | custom-call | flops 3000000000 | bytes 1024 | tf_op jit(solution)/shard_map/turned_normed/pallas_call | solution.py:808
  47.3 9.1 %all-to-all-done = bf16[32,8,512]{2,1,0:T(8,128)(2,1)S(1)} async-done(((bf16[32,8,512]{2,1,0:T(8,128)(2,1)}), bf16[32,8,512]{2,1,0:T(8,128)(2,1)S(1)}, u32[]{:S(2)}, u32[]{:S(2)}) %all-to-all-start) | async-done | bytes 262176 | tf_op jit(solution)/shard_map/all_to_all | solution.py:1103
  56.4 0.0 copy-start.2
  56.4 0.0 copy-start.6
  56.5 5.3 %slide_grads.1 = (f32[1,768]{1,0:T(1,128)}, f32[4,1,768]{2,1,0:T(1,128)S(1)}) custom-call(s32[51]{0:T(128)S(1)} %copy-done.13, bf16[256,512]{1,0:T(8,128)(2,1)S(1)} %bitcast.54, f32[7,768]{1,0:T(8,128)} %taps_hbm.1, bf16[768,768]{1,0:T(8,128)(2,1)} %matrix_hbm.1, f32[8,1536]{1,0:T(8,128)S(1)} %get-tuple-element.63.refs_3_.vectors_ref, ...), custom_call_target="tpu_custom_call" | custom-call | flops 6000000000 | bytes 1024 | tf_op jit(solution)/shard_map/slide_grads/pallas_call | solution.py:722
  61.8 0.0 copy-start.3
  61.8 10.4 %weight_grads.1 = (bf16[4,256,1536]{2,1,0:T(8,128)(2,1)}, bf16[2,2,2,4,48,384]{5,4,3,2,1,0:T(8,128)(2,1)S(1)}, bf16[2,2,2,4,48,384]{5,4,3,2,1,0:T(8,128)(2,1)S(1)}) custom-call(f32[4,1,768]{2,1,0:T(1,128)S(1)} %get-tuple-element.91.grad_ref, bf16[1024,1536]{1,0:T(8,128)(2,1)S(1)} %bitcast.53, bf16[4,256,768]{2,1,0:T(8,128)(2,1)S(1)} %copy-done.5, ...), custom_call_target="tpu_custom_call" | custom-call | flops 12000000000 | bytes 1024 | tf_op jit(solution)/shard_map/weight_grads/pallas_call | solution.py:1025
  72.2 0.1 collective-permute-start.5
  72.4 4.8 %tap_grads_0.1.before_ref = f32[3,49,8,128]{3,2,1,0:T(8,128)S(1)} custom-call(s32[51]{0:T(128)S(1)} %copy-done.13, bf16[4,16,16,384]{3,2,1,0:T(8,128)(2,1)S(1)} %copy-done.7, bf16[4,256,1536]{2,1,0:T(8,128)(2,1)} %get-tuple-element.99.grad_pre_ref, f32[4,256,384]{2,1,0:T(8,128)S(1)} %copy-done.4, f32[4,256,128]{2,1,0:T(8,128)S(1)} %copy-done.8, ...), custom_call_target="tpu_custom_call" | custom-call | flops 4000000000 | bytes 1024 | tf_op jit(solution)/shard_map/tap_grads_0/pallas_call | solution.py:1055
  77.2 0.3 add_convert_fusion
  77.5 1.2 %collective-permute-start.6 = (bf16[2,4,48,384]{3,2,1,0:T(8,128)(2,1)S(1)}, bf16[2,4,48,384]{3,2,1,0:T(8,128)(2,1)S(1)}, u32[]{:S(2)}, u32[]{:S(2)}) collective-permute-start(bf16[2,4,48,384]{3,2,1,0:T(8,128)(2,1)S(1)} %get-tuple-element.103), channel_id=1, source_target_pairs={{0,1},{1,0},{2,3},{3,2},{4,5},{5,4},{6,7},{7,6},{8,9},{9,8},{10,11... | collective-permute-start | bytes 884744 | tf_op jit(solution)/shard_map/ppermute | solution.py:1092
  78.7 0.5 collective-permute-start.7
  79.3 4.9 %tap_grads_2.1 = f32[32,8,384]{2,1,0:T(8,128)S(1)} custom-call(s32[51]{0:T(128)S(1)} %copy-done.13, bf16[4,16,16,384]{3,2,1,0:T(8,128)(2,1)S(1)} %copy-done.7, bf16[4,256,1536]{2,1,0:T(8,128)(2,1)} %get-tuple-element.99.grad_pre_ref, f32[4,256,384]{2,1,0:T(8,128)S(1)} %copy-done.4, f32[4,256,128]{2,1,0:T(8,128)S(1)} %copy-done.8, ...), custom_call_target="tpu_custom_call" | custom-call | flops 4000000000 | bytes 1024 | tf_op jit(solution)/shard_map/tap_grads_2/pallas_call | solution.py:1055
  84.2 0.7 slice.165
  84.9 2.1 %collective-permute-done.6 = bf16[2,4,48,384]{3,2,1,0:T(8,128)(2,1)S(1)} collective-permute-done((bf16[2,4,48,384]{3,2,1,0:T(8,128)(2,1)S(1)}, bf16[2,4,48,384]{3,2,1,0:T(8,128)(2,1)S(1)}, u32[]{:S(2)}, u32[]{:S(2)}) %collective-permute-start.6) | collective-permute-done | bytes 294944 | tf_op jit(solution)/shard_map/ppermute | solution.py:1092
  87.0 0.0 collective-permute-done.7
  87.1 1.3 %collective-permute-start.8 = (bf16[4,48,384]{2,1,0:T(8,128)(2,1)S(1)}, bf16[4,48,384]{2,1,0:T(8,128)(2,1)S(1)}, u32[]{:S(2)}, u32[]{:S(2)}) collective-permute-start(bf16[4,48,384]{2,1,0:T(8,128)(2,1)S(1)} %fusion.9), channel_id=1, source_target_pairs={{0,16},{16,0},{1,17},{17,1},{2,18},{18,2},{3,19},{19,3},{4,20},{20... | collective-permute-start | bytes 442376 | tf_op jit(solution)/shard_map/ppermute | solution.py:1092
  88.4 0.9 collective-permute-start.9
  89.4 3.2 %all-to-all-start.1 = ((bf16[32,4,384]{2,1,0:T(4,128)(2,1)}), bf16[32,4,384]{2,1,0:T(4,128)(2,1)S(1)}, u32[]{:S(2)}, u32[]{:S(2)}) async-start(bf16[32,4,384]{2,1,0:T(4,128)(2,1)} %slice.165), calls=%async_computation.1 | async-start | bytes 196608 | tf_op jit(solution)/shard_map/all_to_all | solution.py:1103
  92.6 0.0 collective-permute-done.8
  92.6 0.1 fusion.6
  92.7 0.9 collective-permute-done.9
  93.6 0.1 fusion.2
  93.7 2.8 %collective-permute-start.12 = (bf16[96,384]{1,0:T(8,128)(2,1)S(1)}, bf16[96,384]{1,0:T(8,128)(2,1)S(1)}, u32[]{:S(2)}, u32[]{:S(2)}) collective-permute-start(bf16[96,384]{1,0:T(8,128)(2,1)S(1)} %get-tuple-element.114), channel_id=1, source_target_pairs={{0,6},{2,0},{4,2},{6,4},{1,7},{3,1},{5,3},{7,5},{8,14},{10,8},{12,... | collective-permute-start | bytes 221192 | tf_op jit(solution)/shard_map/ppermute | solution.py:1092
  96.5 1.1 %collective-permute-start.10 = (bf16[96,384]{1,0:T(8,128)(2,1)S(1)}, bf16[96,384]{1,0:T(8,128)(2,1)S(1)}, u32[]{:S(2)}, u32[]{:S(2)}) collective-permute-start(bf16[96,384]{1,0:T(8,128)(2,1)S(1)} %get-tuple-element.113), channel_id=1, source_target_pairs={{0,2},{2,4},{4,6},{6,0},{1,3},{3,5},{5,7},{7,1},{8,10},{10,12},{12... | collective-permute-start | bytes 221192 | tf_op jit(solution)/shard_map/ppermute | solution.py:1092
  97.5 2.6 %all-to-all-done.1 = bf16[32,4,384]{2,1,0:T(4,128)(2,1)S(1)} async-done(((bf16[32,4,384]{2,1,0:T(4,128)(2,1)}), bf16[32,4,384]{2,1,0:T(4,128)(2,1)S(1)}, u32[]{:S(2)}, u32[]{:S(2)}) %all-to-all-start.1) | async-done | bytes 98336 | tf_op jit(solution)/shard_map/all_to_all | solution.py:1103
  100.2 0.1 convert_reduce_fusion
  100.2 0.7 dynamic_slice.3
  100.9 3.9 %collective-permute-done.11 = bf16[96,384]{1,0:T(8,128)(2,1)S(1)} collective-permute-done((bf16[96,384]{1,0:T(8,128)(2,1)S(1)}, bf16[96,384]{1,0:T(8,128)(2,1)S(1)}, u32[]{:S(2)}, u32[]{:S(2)}) %collective-permute-start.11) | collective-permute-done | bytes 73760 | tf_op jit(solution)/shard_map/ppermute | solution.py:1092
  104.9 0.7 reshape.79
  105.6 0.6 reshape.80
  (43 shorter events, 0.3 us)
Async XLA Ops:
  1.3 0.7 copy-start.14
  4.8 19.3 %copy-start.15 = (f32[1,1152]{1,0:T(1,128)}, f32[1,1152]{1,0:T(1,128)S(1)}, u32[]{:S(2)}) copy-start(f32[1,1152]{1,0:T(1,128)S(1)} %get-tuple-element.85.small_ref) | copy-start | bytes 13828
  4.8 26.1 %copy-start.12 = (s32[51]{0:T(128)}, s32[51]{0:T(128)S(1)}, u32[]{:S(2)}) copy-start(s32[51]{0:T(128)S(1)} %get-tuple-element.57.table_ref) | copy-start | bytes 616
  4.8 3.1 %collective-permute-start = (bf16[33,16,384]{2,1,0:T(8,128)(2,1)S(1)}, bf16[33,16,384]{2,1,0:T(8,128)(2,1)S(1)}, u32[]{:S(2)}, u32[]{:S(2)}) collective-permute-start(bf16[33,16,384]{2,1,0:T(8,128)(2,1)S(1)} %get-tuple-element.60), channel_id=1, source_target_pairs={{0,8},{8,0},{16,24},{24,16},{1,9},{9,1},{17,25},{25,17},{2,10},{10... | collective-permute-start | bytes 1216520 | tf_op jit(solution)/shard_map/ppermute | solution.py:1162
  5.3 18.9 %collective-permute-start.3 = (bf16[17,16,384]{2,1,0:T(8,128)(2,1)S(1)}, bf16[17,16,384]{2,1,0:T(8,128)(2,1)S(1)}, u32[]{:S(2)}, u32[]{:S(2)}) collective-permute-start(bf16[17,16,384]{2,1,0:T(8,128)(2,1)S(1)} %get-tuple-element.64), channel_id=1, source_target_pairs={{0,16},{8,24},{16,0},{24,8},{1,17},{9,25},{17,1},{25,9},{2,18},{10... | collective-permute-start | bytes 626696 | tf_op jit(solution)/shard_map/ppermute | solution.py:1162
  7.9 16.3 %collective-permute-start.4 = (bf16[17,16,384]{2,1,0:T(8,128)(2,1)S(1)}, bf16[17,16,384]{2,1,0:T(8,128)(2,1)S(1)}, u32[]{:S(2)}, u32[]{:S(2)}) collective-permute-start(bf16[17,16,384]{2,1,0:T(8,128)(2,1)S(1)} %get-tuple-element.65), channel_id=1, source_target_pairs={{0,24},{8,16},{16,8},{24,0},{1,25},{9,17},{17,9},{25,1},{2,26},{10... | collective-permute-start | bytes 626696 | tf_op jit(solution)/shard_map/ppermute | solution.py:1162
  7.9 16.2 %copy-start.9 = (bf16[33,16,384]{2,1,0:T(8,128)(2,1)}, bf16[33,16,384]{2,1,0:T(8,128)(2,1)S(1)}, u32[]{:S(2)}) copy-start(bf16[33,16,384]{2,1,0:T(8,128)(2,1)S(1)} %collective-permute-done.refs_1_.refs_0_) | copy-start | bytes 1216516
  8.0 22.9 %collective-permute-start.1 = (bf16[16,16,384]{2,1,0:T(8,128)(2,1)S(1)}, bf16[16,16,384]{2,1,0:T(8,128)(2,1)S(1)}, u32[]{:S(2)}, u32[]{:S(2)}) collective-permute-start(bf16[16,16,384]{2,1,0:T(8,128)(2,1)S(1)} %get-tuple-element.61), channel_id=1, source_target_pairs={{0,16},{8,24},{16,0},{24,8},{1,17},{9,25},{17,1},{25,9},{2,18},{10... | collective-permute-start | bytes 589832 | tf_op jit(solution)/shard_map/ppermute | solution.py:1162
  9.7 21.2 %collective-permute-start.2 = (bf16[16,16,384]{2,1,0:T(8,128)(2,1)S(1)}, bf16[16,16,384]{2,1,0:T(8,128)(2,1)S(1)}, u32[]{:S(2)}, u32[]{:S(2)}) collective-permute-start(bf16[16,16,384]{2,1,0:T(8,128)(2,1)S(1)} %get-tuple-element.62), channel_id=1, source_target_pairs={{0,24},{8,16},{16,8},{24,0},{1,25},{9,17},{17,9},{25,1},{2,26},{10... | collective-permute-start | bytes 589832 | tf_op jit(solution)/shard_map/ppermute | solution.py:1162
  24.2 6.7 %copy-start.10 = (bf16[17,16,384]{2,1,0:T(8,128)(2,1)}, bf16[17,16,384]{2,1,0:T(8,128)(2,1)S(1)}, u32[]{:S(2)}) copy-start(bf16[17,16,384]{2,1,0:T(8,128)(2,1)S(1)} %collective-permute-done.3.refs_0_.refs_1_) | copy-start | bytes 626692
  24.2 6.7 %copy-start.11 = (bf16[17,16,384]{2,1,0:T(8,128)(2,1)}, bf16[17,16,384]{2,1,0:T(8,128)(2,1)S(1)}, u32[]{:S(2)}) copy-start(bf16[17,16,384]{2,1,0:T(8,128)(2,1)S(1)} %collective-permute-done.4.refs_1_.refs_2_) | copy-start | bytes 626692
  31.8 14.2 %copy-start.4 = (f32[4,256,384]{2,1,0:T(8,128)S(1)}, f32[4,256,384]{2,1,0:T(8,128)}, u32[]{:S(2)}) copy-start(f32[4,256,384]{2,1,0:T(8,128)} %get-tuple-element.87.unit_ref) | copy-start | bytes 4718596
  34.5 21.9 %all-to-all-start = ((bf16[32,8,512]{2,1,0:T(8,128)(2,1)}), bf16[32,8,512]{2,1,0:T(8,128)(2,1)S(1)}, u32[]{:S(2)}, u32[]{:S(2)}) async-start(bf16[32,8,512]{2,1,0:T(8,128)(2,1)} %bitcast.56), calls=%async_computation | async-start | bytes 524288 | tf_op jit(solution)/shard_map/all_to_all | solution.py:1103
  46.0 10.5 %copy-start.13 = (s32[51]{0:T(128)S(1)}, s32[51]{0:T(128)}, u32[]{:S(2)}) copy-start(s32[51]{0:T(128)} %copy-done.12) | copy-start | bytes 616
  46.0 10.4 %copy-start.16 = (f32[4,1,1152]{2,1,0:T(1,128)S(1)}, f32[4,1,1152]{2,1,0:T(1,128)}, u32[]{:S(2)}) copy-start(f32[4,1,1152]{2,1,0:T(1,128)} %get-tuple-element.89.smalls_ref) | copy-start | bytes 55300
  56.4 5.3 %copy-start = (bf16[4,256,1536]{2,1,0:T(8,128)(2,1)S(1)}, bf16[4,256,1536]{2,1,0:T(8,128)(2,1)}, u32[]{:S(2)}) copy-start(bf16[4,256,1536]{2,1,0:T(8,128)(2,1)} %get-tuple-element.92) | copy-start | bytes 9437188
  56.4 5.4 %copy-start.1 = (bf16[4,256,1536]{2,1,0:T(8,128)(2,1)S(1)}, bf16[4,256,1536]{2,1,0:T(8,128)(2,1)}, u32[]{:S(2)}) copy-start(bf16[4,256,1536]{2,1,0:T(8,128)(2,1)} %get-tuple-element.94.slope_ref) | copy-start | bytes 9437188
  56.4 5.4 %copy-start.2 = (bf16[1536,384]{1,0:T(8,128)(2,1)S(1)}, bf16[1536,384]{1,0:T(8,128)(2,1)}, u32[]{:S(2)}) copy-start(bf16[1536,384]{1,0:T(8,128)(2,1)} %reduce_ref.1) | copy-start | bytes 3538948
  56.4 5.4 %copy-start.5 = (bf16[4,256,768]{2,1,0:T(8,128)(2,1)S(1)}, bf16[4,256,768]{2,1,0:T(8,128)(2,1)}, u32[]{:S(2)}) copy-start(bf16[4,256,768]{2,1,0:T(8,128)(2,1)} %get-tuple-element.93.head_slope_ref) | copy-start | bytes 4718596
  56.4 5.4 %copy-start.6 = (bf16[384,768]{1,0:T(8,128)(2,1)S(1)}, bf16[384,768]{1,0:T(8,128)(2,1)}, u32[]{:S(2)}) copy-start(bf16[384,768]{1,0:T(8,128)(2,1)} %head_ref.1) | copy-start | bytes 1769476
  61.8 10.5 %copy-start.3 = (bf16[384,1536]{1,0:T(8,128)(2,1)S(1)}, bf16[384,1536]{1,0:T(8,128)(2,1)}, u32[]{:S(2)}) copy-start(bf16[384,1536]{1,0:T(8,128)(2,1)} %expand_ref.3) | copy-start | bytes 3538948
  61.8 10.5 %copy-start.7 = (bf16[4,16,16,384]{3,2,1,0:T(8,128)(2,1)S(1)}, bf16[4,16,16,384]{3,2,1,0:T(8,128)(2,1)}, u32[]{:S(2)}) copy-start(bf16[4,16,16,384]{3,2,1,0:T(8,128)(2,1)} %get-tuple-element.98.source_ref) | copy-start | bytes 2359300
  61.8 10.5 %copy-start.8 = (f32[4,256,128]{2,1,0:T(8,128)S(1)}, f32[4,256,128]{2,1,0:T(8,128)}, u32[]{:S(2)}) copy-start(f32[4,256,128]{2,1,0:T(8,128)} %get-tuple-element.100.inv_ref) | copy-start | bytes 1572868
  72.2 5.0 %collective-permute-start.5 = (bf16[2,2,2,4,48,384]{5,4,3,2,1,0:T(8,128)(2,1)S(1)}, bf16[2,2,2,4,48,384]{5,4,3,2,1,0:T(8,128)(2,1)S(1)}, u32[]{:S(2)}, u32[]{:S(2)}) collective-permute-start(bf16[2,2,2,4,48,384]{5,4,3,2,1,0:T(8,128)(2,1)S(1)} %get-tuple-element.97), channel_id=1, source_target_pairs={{0,8},{8,0},{1,9},{9,1},{2,10},{10,2},{3,11},{11,3},{4,12},{12,4},... | collective-permute-start | bytes 3538952 | tf_op jit(solution)/shard_map/ppermute | solution.py:1092
  77.5 9.5 %collective-permute-start.6 = (bf16[2,4,48,384]{3,2,1,0:T(8,128)(2,1)S(1)}, bf16[2,4,48,384]{3,2,1,0:T(8,128)(2,1)S(1)}, u32[]{:S(2)}, u32[]{:S(2)}) collective-permute-start(bf16[2,4,48,384]{3,2,1,0:T(8,128)(2,1)S(1)} %get-tuple-element.103), channel_id=1, source_target_pairs={{0,1},{1,0},{2,3},{3,2},{4,5},{5,4},{6,7},{7,6},{8,9},{9,8},{10,11... | collective-permute-start | bytes 884744 | tf_op jit(solution)/shard_map/ppermute | solution.py:1092
  78.7 8.4 %collective-permute-start.7 = (bf16[2,4,48,384]{3,2,1,0:T(8,128)(2,1)S(1)}, bf16[2,4,48,384]{3,2,1,0:T(8,128)(2,1)S(1)}, u32[]{:S(2)}, u32[]{:S(2)}) collective-permute-start(bf16[2,4,48,384]{3,2,1,0:T(8,128)(2,1)S(1)} %get-tuple-element.104), channel_id=1, source_target_pairs={{0,16},{16,0},{1,17},{17,1},{2,18},{18,2},{3,19},{19,3},{4,20},{20... | collective-permute-start | bytes 884744 | tf_op jit(solution)/shard_map/ppermute | solution.py:1092
  87.1 5.5 %collective-permute-start.8 = (bf16[4,48,384]{2,1,0:T(8,128)(2,1)S(1)}, bf16[4,48,384]{2,1,0:T(8,128)(2,1)S(1)}, u32[]{:S(2)}, u32[]{:S(2)}) collective-permute-start(bf16[4,48,384]{2,1,0:T(8,128)(2,1)S(1)} %fusion.9), channel_id=1, source_target_pairs={{0,16},{16,0},{1,17},{17,1},{2,18},{18,2},{3,19},{19,3},{4,20},{20... | collective-permute-start | bytes 442376 | tf_op jit(solution)/shard_map/ppermute | solution.py:1092
  88.4 5.1 %collective-permute-start.9 = (bf16[4,48,384]{2,1,0:T(8,128)(2,1)S(1)}, bf16[4,48,384]{2,1,0:T(8,128)(2,1)S(1)}, u32[]{:S(2)}, u32[]{:S(2)}) collective-permute-start(bf16[4,48,384]{2,1,0:T(8,128)(2,1)S(1)} %fusion.10), channel_id=1, source_target_pairs={{0,1},{1,0},{2,3},{3,2},{4,5},{5,4},{6,7},{7,6},{8,9},{9,8},{10,11... | collective-permute-start | bytes 442376 | tf_op jit(solution)/shard_map/ppermute | solution.py:1092
  89.4 10.8 %all-to-all-start.1 = ((bf16[32,4,384]{2,1,0:T(4,128)(2,1)}), bf16[32,4,384]{2,1,0:T(4,128)(2,1)S(1)}, u32[]{:S(2)}, u32[]{:S(2)}) async-start(bf16[32,4,384]{2,1,0:T(4,128)(2,1)} %slice.165), calls=%async_computation.1 | async-start | bytes 196608 | tf_op jit(solution)/shard_map/all_to_all | solution.py:1103
  93.7 7.2 %collective-permute-start.12 = (bf16[96,384]{1,0:T(8,128)(2,1)S(1)}, bf16[96,384]{1,0:T(8,128)(2,1)S(1)}, u32[]{:S(2)}, u32[]{:S(2)}) collective-permute-start(bf16[96,384]{1,0:T(8,128)(2,1)S(1)} %get-tuple-element.114), channel_id=1, source_target_pairs={{0,6},{2,0},{4,2},{6,4},{1,7},{3,1},{5,3},{7,5},{8,14},{10,8},{12,... | collective-permute-start | bytes 221192 | tf_op jit(solution)/shard_map/ppermute | solution.py:1092
  96.5 8.3 %collective-permute-start.11 = (bf16[96,384]{1,0:T(8,128)(2,1)S(1)}, bf16[96,384]{1,0:T(8,128)(2,1)S(1)}, u32[]{:S(2)}, u32[]{:S(2)}) collective-permute-start(bf16[96,384]{1,0:T(8,128)(2,1)S(1)} %get-tuple-element.115), channel_id=1, source_target_pairs={{0,4},{2,6},{4,0},{6,2},{1,5},{3,7},{5,1},{7,3},{8,12},{10,14},{12... | collective-permute-start | bytes 221192 | tf_op jit(solution)/shard_map/ppermute | solution.py:1092
  96.5 8.3 %collective-permute-start.10 = (bf16[96,384]{1,0:T(8,128)(2,1)S(1)}, bf16[96,384]{1,0:T(8,128)(2,1)S(1)}, u32[]{:S(2)}, u32[]{:S(2)}) collective-permute-start(bf16[96,384]{1,0:T(8,128)(2,1)S(1)} %get-tuple-element.113), channel_id=1, source_target_pairs={{0,2},{2,4},{4,6},{6,0},{1,3},{3,5},{5,7},{7,1},{8,10},{10,12},{12... | collective-permute-start | bytes 221192 | tf_op jit(solution)/shard_map/ppermute | solution.py:1092

commit v9 on v8

--- a/solution.py
+++ b/solution.py
@@ -615,10 +615,10 @@
     smalls_ref,
     feature_ref,
     grad_ref,
-    rows,
-    back,
+    picks,
+    own_rows,
+    tile_rows,
     mixed,
-    pre,
     grad_agg,
     taps_ref,
     matrix_ref,
@@ -630,9 +630,8 @@
     ]
     for load in loads:
         load.start()
-    my_slide = lax.axis_index(DP)
+    my_slide, my_member = lax.axis_index(DP), lax.axis_index(GROUP)
     border = ROW_UNIT
-    edge = jnp.zeros((border, rows.shape[2]), jnp.float32)
     reach = KERNEL_TAPS // 2
     blocks = [slice(start, start + WIDTH) for start in range(0, E, WIDTH)]
     lane = lax.broadcasted_iota(jnp.int32, (8, LANES), 1)
@@ -642,83 +641,92 @@
     lines = came_ref.shape[0]
     second = lax.rem(lax.broadcasted_iota(jnp.int32, (1, lines), 1), 2 * PROC) >= PROC
     target = jnp.where(second, target, -1.0)
-    step = lax.broadcasted_iota(jnp.int32, (length, 1), 0).astype(jnp.float32)
-
-    def dilate(ref, slide, direction, cols):
-        total = ref[slide, border : border + length, cols]
-        for tap in range(KERNEL_TAPS):
-            start = border + direction * (tap - reach) * TILE_DILATION
-            total = total + taps_ref[tap : tap + 1, cols] * ref[slide, start : start + length, cols]
-        return total
-
-    def seen(other):
-        count = smalls_ref[other][:, COUNT_AT : COUNT_AT + 1]
-        here = step < count
-        return here, jnp.where(here, 1.0 / count, 0.0)
-
-    for other in range(slides):
-        slide = my_slide ^ other
-        here, _ = seen(other)
-        first = lax.convert_element_type(slide * length, jnp.float32)
-        late = ((target - first) == step).astype(jnp.float32)
-        early = pltpu.roll(late, lines - PROC, axis=1).astype(jnp.bfloat16)
-        late = late.astype(jnp.bfloat16)
-        for ref in (rows, back):
-            ref[slide, 0:border, :] = edge
-            ref[slide, border + length :, :] = edge
-        if other == 0:
-            loads[0].wait()
-        for cols in blocks:
-            pick, at = (early, cols.start) if cols.start < HALF else (late, cols.start - HALF)
-            rows[slide, border : border + length, cols] = jnp.where(
-                here, mix(pick, came_ref[:, at : at + WIDTH]), 0.0
-            )
-            mixed[other * length : (other + 1) * length, cols] = dilate(
-                rows, slide, 1, cols
-            ).astype(jnp.bfloat16)
+    step = lax.broadcasted_iota(jnp.int32, (length, 1), 0)
+
+    want = (my_slide * length + step).astype(jnp.float32)
+    picks[0:length, :] = (target == want).astype(jnp.float32)
+    index = lax.broadcasted_iota(jnp.int32, (ROW_UNIT, 1), 0)
+    short = lax.broadcasted_iota(jnp.int32, (8, 1), 0)
+    helds, shares = [], []
+    for proc in range(PROC):
+        filled = table_ref[FILLED + proc]
+        slide = table_ref[SLIDE + proc]
+        place = table_ref[PLACE + proc] * members + my_member
+        at = place + (index - 2 * reach) * TILE_DILATION
+        inside = (at >= 0) & (at < length) & (index <= 4 * reach) & (filled != 0)
+        want = jnp.where(inside, slide * length + at, -2).astype(jnp.float32)
+        start = length + proc * ROW_UNIT
+        picks[start : start + ROW_UNIT, :] = (target == want).astype(jnp.float32)
+        held = smalls_ref[0]
+        for other in range(1, slides):
+            held = jnp.where((slide ^ my_slide) == other, smalls_ref[other], held)
+        helds.append(held)
+        count = held[:, COUNT_AT : COUNT_AT + 1]
+        at = (place + (short - reach) * TILE_DILATION).astype(jnp.float32)
+        shares.append(jnp.where((at >= 0.0) & (at < count), 1.0 / count, 0.0))
+    late = picks[...]
+    early = pltpu.roll(late, lines - PROC, axis=1).astype(jnp.bfloat16)
+    late = late.astype(jnp.bfloat16)
+    edge = jnp.zeros((border, E), jnp.float32)
+    own_rows[0:border, :] = edge
+    own_rows[border + length :, :] = edge
+    loads[0].wait()
+
+    def tap(number, cols):
+        return taps_ref[number : number + 1, cols]
+
+    for cols in blocks:
+        pick, at = (early, cols.start) if cols.start < HALF else (late, cols.start - HALF)
+        found = mix(pick, came_ref[:, at : at + WIDTH])
+        own_rows[border : border + length, cols] = found[0:length]
+        tile_rows[:, cols] = found[length:]
+        total = found[0:length]
+        for number in range(KERNEL_TAPS):
+            start = border + (number - reach) * TILE_DILATION
+            total = total + tap(number, cols) * own_rows[start : start + length, cols]
+        mixed[0:length, cols] = total.astype(jnp.bfloat16)
+        totals = []
+        for proc in range(PROC):
+            base = proc * ROW_UNIT
+            total = tile_rows[base + reach : base + reach + 8, cols]
+            for number in range(KERNEL_TAPS):
+                total = total + tap(number, cols) * tile_rows[base + number : base + number + 8, cols]
+            totals.append(total)
+        mixed[length:, cols] = jnp.concatenate(totals, axis=0).astype(jnp.bfloat16)
+    count = smalls_ref[0][:, COUNT_AT : COUNT_AT + 1]
+    share = jnp.where(step.astype(jnp.float32) < count, 1.0 / count, 0.0)
     loads[1].wait()
     for cols in blocks:
-        pre[:, cols] = mix(mixed[...], matrix_ref[:, cols])
-        for other in range(slides):
-            small = smalls_ref[other]
-            _, share = seen(other)
-            total = None
-            for start in range(0, length, PART):
-                part = slice(other * length + start, other * length + start + PART)
-                weight = share[start : start + PART]
-                act, slope = gelu_and_slope(
-                    pre[part, cols] + vectors_ref[SLIDE_BIAS : SLIDE_BIAS + 1, cols]
-                )
-                grad_agg[part, cols] = (small[:, cols] * weight * slope).astype(jnp.bfloat16)
-                if other == 0:
-                    piece = jnp.sum(act * weight, axis=0, keepdims=True)
-                    total = piece if total is None else total + piece
-            if other == 0:
-                feature_ref[:, cols] = total
+        bias = vectors_ref[SLIDE_BIAS : SLIDE_BIAS + 1, cols]
+        pre = mix(mixed[...], matrix_ref[:, cols]) + bias
+        total = None
+        for start in range(0, length, PART):
+            act, _ = gelu_and_slope(pre[start : start + PART])
+            piece = jnp.sum(act * share[start : start + PART], axis=0, keepdims=True)
+            total = piece if total is None else total + piece
+        feature_ref[:, cols] = total
+        _, slope = gelu_and_slope(pre[length:])
+        parts = [
+            helds[proc][:, cols] * shares[proc] * slope[proc * 8 : (proc + 1) * 8]
+            for proc in range(PROC)
+        ]
+        grad_agg[:, cols] = jnp.concatenate(parts, axis=0).astype(jnp.bfloat16)
     for cols in blocks:
-        pre[:, cols] = mix_cols(grad_agg[...], matrix_ref[cols, :])
-        for other in range(slides):
-            slide = my_slide ^ other
-            here, _ = seen(other)
-            back[slide, border : border + length, cols] = pre[
-                other * length : (other + 1) * length, cols
-            ]
-            total = jnp.where(here, dilate(back, slide, -1, cols), 0.0)
-            rows[slide, border : border + length, cols] = total.astype(jnp.bfloat16).astype(
-                jnp.float32
-            )
-    my_member = lax.axis_index(GROUP)
-    for proc in range(PROC):
-        at = border + table_ref[PLACE + proc] * members + my_member
-        row = rows[table_ref[SLIDE + proc], pl.ds(at, 1), :]
-        grad_ref[proc] = jnp.where(table_ref[FILLED + proc] != 0, row, 0.0)
+        grads = mix_cols(grad_agg[...], matrix_ref[cols, :])
+        for proc in range(PROC):
+            block = grads[proc * 8 : (proc + 1) * 8]
+            total = block[reach : reach + 1]
+            for number in range(KERNEL_TAPS):
+                at = 2 * reach - number
+                total = total + tap(number, cols) * block[at : at + 1]
+            total = jnp.where(table_ref[FILLED + proc] != 0, total, 0.0)
+            grad_ref[proc, :, cols] = total.astype(jnp.bfloat16).astype(jnp.float32)
 
 
 def slide_grads(length, members, table, came, taps, matrix, vectors, smalls):
     slides = smalls.shape[0]
     smem = pl.BlockSpec(memory_space=pltpu.SMEM)
     vmem = pl.BlockSpec(memory_space=pltpu.VMEM)
-    padded = (slides, length + 2 * ROW_UNIT, E)
     return pl.pallas_call(
         functools.partial(slide_kernel, length, members, slides),
         out_shape=(
@@ -728,17 +736,17 @@
         in_specs=[smem, vmem, IN_HBM, IN_HBM, vmem, vmem],
         out_specs=(vmem, vmem),
         scratch_shapes=[
-            pltpu.VMEM(padded, jnp.float32),
-            pltpu.VMEM(padded, jnp.float32),
-            pltpu.VMEM((slides * length, E), jnp.bfloat16),
-            pltpu.VMEM((slides * length, E), jnp.float32),
-            pltpu.VMEM((slides * length, E), jnp.bfloat16),
+            pltpu.VMEM((length + PROC * ROW_UNIT, came.shape[0]), jnp.float32),
+            pltpu.VMEM((length + 2 * ROW_UNIT, E), jnp.float32),
+            pltpu.VMEM((PROC * ROW_UNIT, E), jnp.float32),
+            pltpu.VMEM((length + PROC * 8, E), jnp.bfloat16),
+            pltpu.VMEM((PROC * 8, E), jnp.bfloat16),
             pltpu.VMEM(taps.shape, jnp.float32),
             pltpu.VMEM(matrix.shape, jnp.bfloat16),
             pltpu.SemaphoreType.DMA((2,)),
         ],
-        compiler_params=pltpu.CompilerParams(vmem_limit_bytes=24 * MIB),
-        cost_estimate=cost(6.0),
+        compiler_params=pltpu.CompilerParams(vmem_limit_bytes=16 * MIB),
+        cost_estimate=cost(3.0),
         name="slide_grads",
     )(table, came, pinned(taps), pinned(matrix), vectors, smalls)
 

time: 105 us -> 104 us (level)
  Pallas kernels: 54.2 us -> 52.2 us
    pallas_call x1, Pallas kernels: 5.29 us -> 3.29 us  [slide_grads(): pl.pallas_call(functools.partial(slide_kernel, length, members, slides),...]
  transfers between devices with their start and end apart: 15 -> 15, of which waited for: 5 -> 7; matrix products, arithmetic and copies ran while one was open for 2% -> 2% of each run, Pallas kernels for 30% -> 31%
where the time goes in v9:
time: 104 us; the launch traced here: 105 us
  Pallas kernels  52.2 us (50%)
  starting transfers between devices  27.2 us (26%)
  waiting for transfers between devices  19.3 us (19%)
  local copies, waits for them, and re-layouts  4.18 us (4%)
  between operations  1.68 us (2%)
    pallas_call x3, Pallas kernels, forward_block(): pl.pallas_call(functools.partial(forward_kernel, kind, last, len(tiles),...  21.9 us
    all_to_all x2, starting transfers between devices, exchange(): lax.all_to_all(values, names, split_axis=0, concat_axis=0, tiled=True)  15 us
    all_to_all x2, waiting for transfers between devices, exchange(): lax.all_to_all(values, names, split_axis=0, concat_axis=0, tiled=True)  11.7 us
    pallas_call x1, Pallas kernels, weight_grads(): pl.pallas_call(functools.partial(weights_kernel, plan), out_shape=(pltpu....  10.4 us
    pallas_call x2, Pallas kernels, tap_grads(): pl.pallas_call(functools.partial(taps_kernel, plan, first, last), out_sha...  9.75 us
    ppermute x8, waiting for transfers between devices, shifted(): return lax.ppermute(values, names, pairs)  7.58 us
    ppermute x8, starting transfers between devices, shifted(): return lax.ppermute(values, names, pairs)  7.32 us
    ppermute x5, starting transfers between devices, from_other(): lax.ppermute(buffer, DP, [(index, index ^ other) for index in range(slide...  4.88 us
  transfers between devices with their start and end apart: 15, of which 7 were waited for; matrix products, arithmetic and copies ran while one was open for 2% of the time, Pallas kernels for 31%

profile of v9, /device:TPU:0, one launch (start us, length us, event | category | flops | bytes accessed | tf_op | source)
XLA Modules:
  0.0 105.2 jit_solution(13136899049596424088)
XLA Ops:
  1.3 0.7 copy-done.14
  2.0 2.8 %pack_tiles.1 = (bf16[33,16,384]{2,1,0:T(8,128)(2,1)S(1)}, bf16[17,16,384]{2,1,0:T(8,128)(2,1)S(1)}, bf16[17,16,384]{2,1,0:T(8,128)(2,1)S(1)}, bf16[16,16,384]{2...) custom-call(s32[1]{0:T(128)S(6)} %copy.56.counts_ref, ...), custom_call_target="tpu_custom_call" | custom-call | tf_op jit(solution)/shard_map/pack_tiles/pallas_call | solution.py:225
  4.8 0.0 copy-start.15
  4.8 0.0 copy-start.12
  4.8 0.5 collective-permute-start
  5.3 2.6 %collective-permute-start.3 = (bf16[17,16,384]{2,1,0:T(8,128)(2,1)S(1)}, bf16[17,16,384]{2,1,0:T(8,128)(2,1)S(1)}, u32[]{:S(2)}, u32[]{:S(2)}) collective-permute-start(bf16[17,16,384]{2,1,0:T(8,128)(2,1)S(1)} %get-tuple-element.64), channel_id=1, source_target_pairs={{0,16},{8,24},{16,0},{24,8},{1,17},{9,25},{17,1},{25,9},{2,18},{10... | collective-permute-start | bytes 626696 | tf_op jit(solution)/shard_map/ppermute | solution.py:1170
  7.9 0.1 collective-permute-start.4
  8.0 1.7 %collective-permute-start.1 = (bf16[16,16,384]{2,1,0:T(8,128)(2,1)S(1)}, bf16[16,16,384]{2,1,0:T(8,128)(2,1)S(1)}, u32[]{:S(2)}, u32[]{:S(2)}) collective-permute-start(bf16[16,16,384]{2,1,0:T(8,128)(2,1)S(1)} %get-tuple-element.61), channel_id=1, source_target_pairs={{0,16},{8,24},{16,0},{24,8},{1,17},{9,25},{17,1},{25,9},{2,18},{10... | collective-permute-start | bytes 589832 | tf_op jit(solution)/shard_map/ppermute | solution.py:1170
  9.7 0.0 collective-permute-start.2
  9.7 14.4 %forward_block_0.1 = (bf16[4,16,16,384]{3,2,1,0:T(8,128)(2,1)}, f32[4,8,768]{2,1,0:T(8,128)}, f32[4,256,384]{2,1,0:T(8,128)}, f32[4,256,128]{2,1,0:T(8,128)}, bf...) custom-call(s32[51]{0:T(128)S(1)} %get-tuple-element.57.table_ref, ...), custom_call_target="tpu_custom_call" | custom-call | flops 1000000000 | bytes 1024 | tf_op jit(solution)/shard_map/forward_block_0/pallas_call | solution.py:485
  24.2 6.6 %forward_block_1.1 = (bf16[4,16,16,384]{3,2,1,0:T(8,128)(2,1)}, f32[4,8,768]{2,1,0:T(8,128)}, f32[4,256,384]{2,1,0:T(8,128)}, f32[4,256,128]{2,1,0:T(8,128)}, bf...) custom-call(s32[51]{0:T(128)S(1)} %get-tuple-element.57.table_ref, ...), custom_call_target="tpu_custom_call", output_to_operand_aliasing={{0}: (8, {}), {1}: (9, {}), {2}: (10, {}), {3}: (11, {}), {... | custom-call | flops 1000000000 | bytes 1024 | tf_op jit(solution)/shard_map/forward_block_1/pallas_call | solution.py:485
  30.9 0.9 forward_block_2.1
  31.8 2.8 %tile_rows.1 = (bf16[256,512]{1,0:T(8,128)(2,1)}, f32[4,1,1152]{2,1,0:T(1,128)}) custom-call(s32[51]{0:T(128)} %copy-done.12, f32[4,8,768]{2,1,0:T(8,128)} %get-tuple-element.84.embed_ref, f32[1,1152]{1,0:T(1,128)} %copy-done.15, bf16[33,16,384]{2,1,0:T(8,128)(2,1)} %copy-done.9, bf16[17,16,384]{2,1,0:T(8,128)(2,1)} %copy-done.10, ...), custom_call_target="tpu_custom_call" | custom-call | flops 1000000000 | bytes 1024 | tf_op jit(solution)/shard_map/tile_rows/pallas_call | solution.py:587
  34.5 11.8 %all-to-all-start = ((bf16[32,8,512]{2,1,0:T(8,128)(2,1)}), bf16[32,8,512]{2,1,0:T(8,128)(2,1)S(1)}, u32[]{:S(2)}, u32[]{:S(2)}) async-start(bf16[32,8,512]{2,1,0:T(8,128)(2,1)} %bitcast.56), calls=%async_computation | async-start | bytes 524288 | tf_op jit(solution)/shard_map/all_to_all | solution.py:1111
  46.3 0.0 copy-start.13
  46.3 0.0 copy-start.16
  46.4 1.3 %turned_normed.1.normed_ref = bf16[384,1024]{1,0:T(8,128)(2,1)S(1)} custom-call(f32[4,256,384]{2,1,0:T(8,128)S(1)} %copy-done.4, f32[8,1536]{1,0:T(8,128)S(1)} %get-tuple-element.63.refs_3_.vectors_ref), custom_call_target="tpu_custom_call" | custom-call | flops 3000000000 | bytes 1024 | tf_op jit(solution)/shard_map/turned_normed/pallas_call | solution.py:816
  47.7 9.1 %all-to-all-done = bf16[32,8,512]{2,1,0:T(8,128)(2,1)S(1)} async-done(((bf16[32,8,512]{2,1,0:T(8,128)(2,1)}), bf16[32,8,512]{2,1,0:T(8,128)(2,1)S(1)}, u32[]{:S(2)}, u32[]{:S(2)}) %all-to-all-start) | async-done | bytes 262176 | tf_op jit(solution)/shard_map/all_to_all | solution.py:1111
  56.8 0.0 copy-start.6
  56.8 3.3 %slide_grads.1 = (f32[1,768]{1,0:T(1,128)}, f32[4,1,768]{2,1,0:T(1,128)S(1)}) custom-call(s32[51]{0:T(128)S(1)} %copy-done.13, bf16[256,512]{1,0:T(8,128)(2,1)S(1)} %bitcast.54, f32[7,768]{1,0:T(8,128)} %taps_hbm.1, bf16[768,768]{1,0:T(8,128)(2,1)} %matrix_hbm.1, f32[8,1536]{1,0:T(8,128)S(1)} %get-tuple-element.63.refs_3_.vectors_ref, ...), custom_call_target="tpu_custom_call" | custom-call | flops 3000000000 | bytes 1024 | tf_op jit(solution)/shard_map/slide_grads/pallas_call | solution.py:730
  60.2 0.1 copy-done.2
  60.3 0.5 copy-done.5
  60.8 0.1 copy-done.6
  60.9 10.4 %weight_grads.1 = (bf16[4,256,1536]{2,1,0:T(8,128)(2,1)}, bf16[2,2,2,4,48,384]{5,4,3,2,1,0:T(8,128)(2,1)S(1)}, bf16[2,2,2,4,48,384]{5,4,3,2,1,0:T(8,128)(2,1)S(1)}) custom-call(f32[4,1,768]{2,1,0:T(1,128)S(1)} %get-tuple-element.91.grad_ref, bf16[1024,1536]{1,0:T(8,128)(2,1)S(1)} %bitcast.53, bf16[4,256,768]{2,1,0:T(8,128)(2,1)S(1)} %copy-done.5, ...), custom_call_target="tpu_custom_call" | custom-call | flops 12000000000 | bytes 1024 | tf_op jit(solution)/shard_map/weight_grads/pallas_call | solution.py:1033
  71.2 0.1 collective-permute-start.5
  71.4 4.8 %tap_grads_0.1.before_ref = f32[3,49,8,128]{3,2,1,0:T(8,128)S(1)} custom-call(s32[51]{0:T(128)S(1)} %copy-done.13, bf16[4,16,16,384]{3,2,1,0:T(8,128)(2,1)S(1)} %copy-done.7, bf16[4,256,1536]{2,1,0:T(8,128)(2,1)} %get-tuple-element.99.grad_pre_ref, f32[4,256,384]{2,1,0:T(8,128)S(1)} %copy-done.4, f32[4,256,128]{2,1,0:T(8,128)S(1)} %copy-done.8, ...), custom_call_target="tpu_custom_call" | custom-call | flops 4000000000 | bytes 1024 | tf_op jit(solution)/shard_map/tap_grads_0/pallas_call | solution.py:1063
  76.2 0.3 add_convert_fusion
  76.6 1.2 %collective-permute-start.6 = (bf16[2,4,48,384]{3,2,1,0:T(8,128)(2,1)S(1)}, bf16[2,4,48,384]{3,2,1,0:T(8,128)(2,1)S(1)}, u32[]{:S(2)}, u32[]{:S(2)}) collective-permute-start(bf16[2,4,48,384]{3,2,1,0:T(8,128)(2,1)S(1)} %get-tuple-element.103), channel_id=1, source_target_pairs={{0,1},{1,0},{2,3},{3,2},{4,5},{5,4},{6,7},{7,6},{8,9},{9,8},{10,11... | collective-permute-start | bytes 884744 | tf_op jit(solution)/shard_map/ppermute | solution.py:1100
  77.8 0.6 collective-permute-start.7
  78.3 4.9 %tap_grads_2.1 = f32[32,8,384]{2,1,0:T(8,128)S(1)} custom-call(s32[51]{0:T(128)S(1)} %copy-done.13, bf16[4,16,16,384]{3,2,1,0:T(8,128)(2,1)S(1)} %copy-done.7, bf16[4,256,1536]{2,1,0:T(8,128)(2,1)} %get-tuple-element.99.grad_pre_ref, f32[4,256,384]{2,1,0:T(8,128)S(1)} %copy-done.4, f32[4,256,128]{2,1,0:T(8,128)S(1)} %copy-done.8, ...), custom_call_target="tpu_custom_call" | custom-call | flops 4000000000 | bytes 1024 | tf_op jit(solution)/shard_map/tap_grads_2/pallas_call | solution.py:1063
  83.3 0.7 slice.165
  83.9 2.1 %collective-permute-done.6 = bf16[2,4,48,384]{3,2,1,0:T(8,128)(2,1)S(1)} collective-permute-done((bf16[2,4,48,384]{3,2,1,0:T(8,128)(2,1)S(1)}, bf16[2,4,48,384]{3,2,1,0:T(8,128)(2,1)S(1)}, u32[]{:S(2)}, u32[]{:S(2)}) %collective-permute-start.6) | collective-permute-done | bytes 294944 | tf_op jit(solution)/shard_map/ppermute | solution.py:1100
  86.1 0.7 collective-permute-done.7
  86.8 0.6 collective-permute-start.8
  87.4 1.0 collective-permute-start.9
  88.4 3.2 %all-to-all-start.1 = ((bf16[32,4,384]{2,1,0:T(4,128)(2,1)}), bf16[32,4,384]{2,1,0:T(4,128)(2,1)S(1)}, u32[]{:S(2)}, u32[]{:S(2)}) async-start(bf16[32,4,384]{2,1,0:T(4,128)(2,1)} %slice.165), calls=%async_computation.1 | async-start | bytes 196608 | tf_op jit(solution)/shard_map/all_to_all | solution.py:1111
  91.6 0.4 collective-permute-done.8
  92.0 0.1 fusion.6
  92.1 0.5 collective-permute-done.9
  92.6 0.1 fusion.2
  92.7 2.8 %collective-permute-start.12 = (bf16[96,384]{1,0:T(8,128)(2,1)S(1)}, bf16[96,384]{1,0:T(8,128)(2,1)S(1)}, u32[]{:S(2)}, u32[]{:S(2)}) collective-permute-start(bf16[96,384]{1,0:T(8,128)(2,1)S(1)} %get-tuple-element.114), channel_id=1, source_target_pairs={{0,6},{2,0},{4,2},{6,4},{1,7},{3,1},{5,3},{7,5},{8,14},{10,8},{12,... | collective-permute-start | bytes 221192 | tf_op jit(solution)/shard_map/ppermute | solution.py:1100
  95.5 1.1 %collective-permute-start.10 = (bf16[96,384]{1,0:T(8,128)(2,1)S(1)}, bf16[96,384]{1,0:T(8,128)(2,1)S(1)}, u32[]{:S(2)}, u32[]{:S(2)}) collective-permute-start(bf16[96,384]{1,0:T(8,128)(2,1)S(1)} %get-tuple-element.113), channel_id=1, source_target_pairs={{0,2},{2,4},{4,6},{6,0},{1,3},{3,5},{5,7},{7,1},{8,10},{10,12},{12... | collective-permute-start | bytes 221192 | tf_op jit(solution)/shard_map/ppermute | solution.py:1100
  96.5 2.6 %all-to-all-done.1 = bf16[32,4,384]{2,1,0:T(4,128)(2,1)S(1)} async-done(((bf16[32,4,384]{2,1,0:T(4,128)(2,1)}), bf16[32,4,384]{2,1,0:T(4,128)(2,1)S(1)}, u32[]{:S(2)}, u32[]{:S(2)}) %all-to-all-start.1) | async-done | bytes 98336 | tf_op jit(solution)/shard_map/all_to_all | solution.py:1111
  99.2 0.1 convert_reduce_fusion
  99.3 0.7 dynamic_slice.3
  99.9 3.9 %collective-permute-done.11 = bf16[96,384]{1,0:T(8,128)(2,1)S(1)} collective-permute-done((bf16[96,384]{1,0:T(8,128)(2,1)S(1)}, bf16[96,384]{1,0:T(8,128)(2,1)S(1)}, u32[]{:S(2)}, u32[]{:S(2)}) %collective-permute-start.11) | collective-permute-done | bytes 73760 | tf_op jit(solution)/shard_map/ppermute | solution.py:1100
  103.9 0.7 reshape.79
  104.6 0.6 reshape.80
  (43 shorter events, 0.3 us)
Async XLA Ops:
  1.3 0.7 copy-start.14
  4.8 19.3 %copy-start.15 = (f32[1,1152]{1,0:T(1,128)}, f32[1,1152]{1,0:T(1,128)S(1)}, u32[]{:S(2)}) copy-start(f32[1,1152]{1,0:T(1,128)S(1)} %get-tuple-element.85.small_ref) | copy-start | bytes 13828
  4.8 26.1 %copy-start.12 = (s32[51]{0:T(128)}, s32[51]{0:T(128)S(1)}, u32[]{:S(2)}) copy-start(s32[51]{0:T(128)S(1)} %get-tuple-element.57.table_ref) | copy-start | bytes 616
  4.8 3.1 %collective-permute-start = (bf16[33,16,384]{2,1,0:T(8,128)(2,1)S(1)}, bf16[33,16,384]{2,1,0:T(8,128)(2,1)S(1)}, u32[]{:S(2)}, u32[]{:S(2)}) collective-permute-start(bf16[33,16,384]{2,1,0:T(8,128)(2,1)S(1)} %get-tuple-element.60), channel_id=1, source_target_pairs={{0,8},{8,0},{16,24},{24,16},{1,9},{9,1},{17,25},{25,17},{2,10},{10... | collective-permute-start | bytes 1216520 | tf_op jit(solution)/shard_map/ppermute | solution.py:1170
  5.3 18.9 %collective-permute-start.3 = (bf16[17,16,384]{2,1,0:T(8,128)(2,1)S(1)}, bf16[17,16,384]{2,1,0:T(8,128)(2,1)S(1)}, u32[]{:S(2)}, u32[]{:S(2)}) collective-permute-start(bf16[17,16,384]{2,1,0:T(8,128)(2,1)S(1)} %get-tuple-element.64), channel_id=1, source_target_pairs={{0,16},{8,24},{16,0},{24,8},{1,17},{9,25},{17,1},{25,9},{2,18},{10... | collective-permute-start | bytes 626696 | tf_op jit(solution)/shard_map/ppermute | solution.py:1170
  7.9 16.3 %collective-permute-start.4 = (bf16[17,16,384]{2,1,0:T(8,128)(2,1)S(1)}, bf16[17,16,384]{2,1,0:T(8,128)(2,1)S(1)}, u32[]{:S(2)}, u32[]{:S(2)}) collective-permute-start(bf16[17,16,384]{2,1,0:T(8,128)(2,1)S(1)} %get-tuple-element.65), channel_id=1, source_target_pairs={{0,24},{8,16},{16,8},{24,0},{1,25},{9,17},{17,9},{25,1},{2,26},{10... | collective-permute-start | bytes 626696 | tf_op jit(solution)/shard_map/ppermute | solution.py:1170
  7.9 16.2 %copy-start.9 = (bf16[33,16,384]{2,1,0:T(8,128)(2,1)}, bf16[33,16,384]{2,1,0:T(8,128)(2,1)S(1)}, u32[]{:S(2)}) copy-start(bf16[33,16,384]{2,1,0:T(8,128)(2,1)S(1)} %collective-permute-done.refs_1_.refs_0_) | copy-start | bytes 1216516
  8.0 22.9 %collective-permute-start.1 = (bf16[16,16,384]{2,1,0:T(8,128)(2,1)S(1)}, bf16[16,16,384]{2,1,0:T(8,128)(2,1)S(1)}, u32[]{:S(2)}, u32[]{:S(2)}) collective-permute-start(bf16[16,16,384]{2,1,0:T(8,128)(2,1)S(1)} %get-tuple-element.61), channel_id=1, source_target_pairs={{0,16},{8,24},{16,0},{24,8},{1,17},{9,25},{17,1},{25,9},{2,18},{10... | collective-permute-start | bytes 589832 | tf_op jit(solution)/shard_map/ppermute | solution.py:1170
  9.7 21.2 %collective-permute-start.2 = (bf16[16,16,384]{2,1,0:T(8,128)(2,1)S(1)}, bf16[16,16,384]{2,1,0:T(8,128)(2,1)S(1)}, u32[]{:S(2)}, u32[]{:S(2)}) collective-permute-start(bf16[16,16,384]{2,1,0:T(8,128)(2,1)S(1)} %get-tuple-element.62), channel_id=1, source_target_pairs={{0,24},{8,16},{16,8},{24,0},{1,25},{9,17},{17,9},{25,1},{2,26},{10... | collective-permute-start | bytes 589832 | tf_op jit(solution)/shard_map/ppermute | solution.py:1170
  24.2 6.7 %copy-start.10 = (bf16[17,16,384]{2,1,0:T(8,128)(2,1)}, bf16[17,16,384]{2,1,0:T(8,128)(2,1)S(1)}, u32[]{:S(2)}) copy-start(bf16[17,16,384]{2,1,0:T(8,128)(2,1)S(1)} %collective-permute-done.3.refs_0_.refs_1_) | copy-start | bytes 626692
  24.2 6.7 %copy-start.11 = (bf16[17,16,384]{2,1,0:T(8,128)(2,1)}, bf16[17,16,384]{2,1,0:T(8,128)(2,1)S(1)}, u32[]{:S(2)}) copy-start(bf16[17,16,384]{2,1,0:T(8,128)(2,1)S(1)} %collective-permute-done.4.refs_1_.refs_2_) | copy-start | bytes 626692
  31.8 14.6 %copy-start.4 = (f32[4,256,384]{2,1,0:T(8,128)S(1)}, f32[4,256,384]{2,1,0:T(8,128)}, u32[]{:S(2)}) copy-start(f32[4,256,384]{2,1,0:T(8,128)} %get-tuple-element.87.unit_ref) | copy-start | bytes 4718596
  34.5 22.3 %all-to-all-start = ((bf16[32,8,512]{2,1,0:T(8,128)(2,1)}), bf16[32,8,512]{2,1,0:T(8,128)(2,1)S(1)}, u32[]{:S(2)}, u32[]{:S(2)}) async-start(bf16[32,8,512]{2,1,0:T(8,128)(2,1)} %bitcast.56), calls=%async_computation | async-start | bytes 524288 | tf_op jit(solution)/shard_map/all_to_all | solution.py:1111
  46.3 10.5 %copy-start.13 = (s32[51]{0:T(128)S(1)}, s32[51]{0:T(128)}, u32[]{:S(2)}) copy-start(s32[51]{0:T(128)} %copy-done.12) | copy-start | bytes 616
  46.3 10.4 %copy-start.16 = (f32[4,1,1152]{2,1,0:T(1,128)S(1)}, f32[4,1,1152]{2,1,0:T(1,128)}, u32[]{:S(2)}) copy-start(f32[4,1,1152]{2,1,0:T(1,128)} %get-tuple-element.89.smalls_ref) | copy-start | bytes 55300
  56.8 3.3 %copy-start = (bf16[4,256,1536]{2,1,0:T(8,128)(2,1)S(1)}, bf16[4,256,1536]{2,1,0:T(8,128)(2,1)}, u32[]{:S(2)}) copy-start(bf16[4,256,1536]{2,1,0:T(8,128)(2,1)} %get-tuple-element.92) | copy-start | bytes 9437188
  56.8 3.4 %copy-start.1 = (bf16[4,256,1536]{2,1,0:T(8,128)(2,1)S(1)}, bf16[4,256,1536]{2,1,0:T(8,128)(2,1)}, u32[]{:S(2)}) copy-start(bf16[4,256,1536]{2,1,0:T(8,128)(2,1)} %get-tuple-element.94.slope_ref) | copy-start | bytes 9437188
  56.8 3.5 %copy-start.2 = (bf16[1536,384]{1,0:T(8,128)(2,1)S(1)}, bf16[1536,384]{1,0:T(8,128)(2,1)}, u32[]{:S(2)}) copy-start(bf16[1536,384]{1,0:T(8,128)(2,1)} %reduce_ref.1) | copy-start | bytes 3538948
  56.8 4.0 %copy-start.5 = (bf16[4,256,768]{2,1,0:T(8,128)(2,1)S(1)}, bf16[4,256,768]{2,1,0:T(8,128)(2,1)}, u32[]{:S(2)}) copy-start(bf16[4,256,768]{2,1,0:T(8,128)(2,1)} %get-tuple-element.93.head_slope_ref) | copy-start | bytes 4718596
  56.8 4.0 %copy-start.6 = (bf16[384,768]{1,0:T(8,128)(2,1)S(1)}, bf16[384,768]{1,0:T(8,128)(2,1)}, u32[]{:S(2)}) copy-start(bf16[384,768]{1,0:T(8,128)(2,1)} %head_ref.1) | copy-start | bytes 1769476
  60.9 10.5 %copy-start.3 = (bf16[384,1536]{1,0:T(8,128)(2,1)S(1)}, bf16[384,1536]{1,0:T(8,128)(2,1)}, u32[]{:S(2)}) copy-start(bf16[384,1536]{1,0:T(8,128)(2,1)} %expand_ref.3) | copy-start | bytes 3538948
  60.9 10.5 %copy-start.7 = (bf16[4,16,16,384]{3,2,1,0:T(8,128)(2,1)S(1)}, bf16[4,16,16,384]{3,2,1,0:T(8,128)(2,1)}, u32[]{:S(2)}) copy-start(bf16[4,16,16,384]{3,2,1,0:T(8,128)(2,1)} %get-tuple-element.98.source_ref) | copy-start | bytes 2359300
  60.9 10.5 %copy-start.8 = (f32[4,256,128]{2,1,0:T(8,128)S(1)}, f32[4,256,128]{2,1,0:T(8,128)}, u32[]{:S(2)}) copy-start(f32[4,256,128]{2,1,0:T(8,128)} %get-tuple-element.100.inv_ref) | copy-start | bytes 1572868
  71.2 5.0 %collective-permute-start.5 = (bf16[2,2,2,4,48,384]{5,4,3,2,1,0:T(8,128)(2,1)S(1)}, bf16[2,2,2,4,48,384]{5,4,3,2,1,0:T(8,128)(2,1)S(1)}, u32[]{:S(2)}, u32[]{:S(2)}) collective-permute-start(bf16[2,2,2,4,48,384]{5,4,3,2,1,0:T(8,128)(2,1)S(1)} %get-tuple-element.97), channel_id=1, source_target_pairs={{0,8},{8,0},{1,9},{9,1},{2,10},{10,2},{3,11},{11,3},{4,12},{12,4},... | collective-permute-start | bytes 3538952 | tf_op jit(solution)/shard_map/ppermute | solution.py:1100
  76.6 9.5 %collective-permute-start.6 = (bf16[2,4,48,384]{3,2,1,0:T(8,128)(2,1)S(1)}, bf16[2,4,48,384]{3,2,1,0:T(8,128)(2,1)S(1)}, u32[]{:S(2)}, u32[]{:S(2)}) collective-permute-start(bf16[2,4,48,384]{3,2,1,0:T(8,128)(2,1)S(1)} %get-tuple-element.103), channel_id=1, source_target_pairs={{0,1},{1,0},{2,3},{3,2},{4,5},{5,4},{6,7},{7,6},{8,9},{9,8},{10,11... | collective-permute-start | bytes 884744 | tf_op jit(solution)/shard_map/ppermute | solution.py:1100
  77.8 9.0 %collective-permute-start.7 = (bf16[2,4,48,384]{3,2,1,0:T(8,128)(2,1)S(1)}, bf16[2,4,48,384]{3,2,1,0:T(8,128)(2,1)S(1)}, u32[]{:S(2)}, u32[]{:S(2)}) collective-permute-start(bf16[2,4,48,384]{3,2,1,0:T(8,128)(2,1)S(1)} %get-tuple-element.104), channel_id=1, source_target_pairs={{0,16},{16,0},{1,17},{17,1},{2,18},{18,2},{3,19},{19,3},{4,20},{20... | collective-permute-start | bytes 884744 | tf_op jit(solution)/shard_map/ppermute | solution.py:1100
  86.8 5.2 %collective-permute-start.8 = (bf16[4,48,384]{2,1,0:T(8,128)(2,1)S(1)}, bf16[4,48,384]{2,1,0:T(8,128)(2,1)S(1)}, u32[]{:S(2)}, u32[]{:S(2)}) collective-permute-start(bf16[4,48,384]{2,1,0:T(8,128)(2,1)S(1)} %fusion.9), channel_id=1, source_target_pairs={{0,16},{16,0},{1,17},{17,1},{2,18},{18,2},{3,19},{19,3},{4,20},{20... | collective-permute-start | bytes 442376 | tf_op jit(solution)/shard_map/ppermute | solution.py:1100
  87.4 5.1 %collective-permute-start.9 = (bf16[4,48,384]{2,1,0:T(8,128)(2,1)S(1)}, bf16[4,48,384]{2,1,0:T(8,128)(2,1)S(1)}, u32[]{:S(2)}, u32[]{:S(2)}) collective-permute-start(bf16[4,48,384]{2,1,0:T(8,128)(2,1)S(1)} %fusion.10), channel_id=1, source_target_pairs={{0,1},{1,0},{2,3},{3,2},{4,5},{5,4},{6,7},{7,6},{8,9},{9,8},{10,11... | collective-permute-start | bytes 442376 | tf_op jit(solution)/shard_map/ppermute | solution.py:1100
  88.4 10.8 %all-to-all-start.1 = ((bf16[32,4,384]{2,1,0:T(4,128)(2,1)}), bf16[32,4,384]{2,1,0:T(4,128)(2,1)S(1)}, u32[]{:S(2)}, u32[]{:S(2)}) async-start(bf16[32,4,384]{2,1,0:T(4,128)(2,1)} %slice.165), calls=%async_computation.1 | async-start | bytes 196608 | tf_op jit(solution)/shard_map/all_to_all | solution.py:1111
  92.7 7.3 %collective-permute-start.12 = (bf16[96,384]{1,0:T(8,128)(2,1)S(1)}, bf16[96,384]{1,0:T(8,128)(2,1)S(1)}, u32[]{:S(2)}, u32[]{:S(2)}) collective-permute-start(bf16[96,384]{1,0:T(8,128)(2,1)S(1)} %get-tuple-element.114), channel_id=1, source_target_pairs={{0,6},{2,0},{4,2},{6,4},{1,7},{3,1},{5,3},{7,5},{8,14},{10,8},{12,... | collective-permute-start | bytes 221192 | tf_op jit(solution)/shard_map/ppermute | solution.py:1100
  95.5 8.3 %collective-permute-start.11 = (bf16[96,384]{1,0:T(8,128)(2,1)S(1)}, bf16[96,384]{1,0:T(8,128)(2,1)S(1)}, u32[]{:S(2)}, u32[]{:S(2)}) collective-permute-start(bf16[96,384]{1,0:T(8,128)(2,1)S(1)} %get-tuple-element.115), channel_id=1, source_target_pairs={{0,4},{2,6},{4,0},{6,2},{1,5},{3,7},{5,1},{7,3},{8,12},{10,14},{12... | collective-permute-start | bytes 221192 | tf_op jit(solution)/shard_map/ppermute | solution.py:1100
  95.5 8.3 %collective-permute-start.10 = (bf16[96,384]{1,0:T(8,128)(2,1)S(1)}, bf16[96,384]{1,0:T(8,128)(2,1)S(1)}, u32[]{:S(2)}, u32[]{:S(2)}) collective-permute-start(bf16[96,384]{1,0:T(8,128)(2,1)S(1)} %get-tuple-element.113), channel_id=1, source_target_pairs={{0,2},{2,4},{4,6},{6,0},{1,3},{3,5},{5,7},{7,1},{8,10},{10,12},{12... | collective-permute-start | bytes 221192 | tf_op jit(solution)/shard_map/ppermute | solution.py:1100

commit v10 on v9

--- a/solution.py
+++ b/solution.py
@@ -571,23 +571,29 @@
         there = there | ((row_id == proc) & (table_ref[FILLED + proc] != 0))
     total = jnp.where(there, embed + code, 0.0)
     rows_ref[0 : 2 * PROC, 0:E] = total
-    lines_ref[...] = jnp.zeros(lines_ref.shape, jnp.float32)
-    for copied in range(0, ROW_UNIT, 2 * PROC):
-        lines_ref[copied : copied + PROC, :] = rows_ref[0:PROC, 0:HALF]
-        lines_ref[copied + PROC : copied + 2 * PROC, 0 : E + LANES - HALF] = rows_ref[0:PROC, HALF:]
-    sent = lines_ref[...].astype(jnp.bfloat16)
-    for start in range(0, out_ref.shape[0], ROW_UNIT):
-        out_ref[start : start + ROW_UNIT, :] = sent
-
-
-def tile_rows(table, embeds, small, buffers, devices):
+    halves = jnp.concatenate(
+        [
+            rows_ref[0:PROC, 0:HALF],
+            jnp.concatenate(
+                [rows_ref[0:PROC, HALF:], jnp.zeros((PROC, 2 * HALF - E - LANES), jnp.float32)], axis=1
+            ),
+        ],
+        axis=0,
+    )
+    core = lax.axis_index("core")
+    for half in range(2):
+        lines_ref[half * 2 * PROC : (half + 1) * 2 * PROC, :] = jnp.where(core == half, halves, 0.0)
+    out_ref[...] = lines_ref[...].astype(jnp.bfloat16)
+
+
+def tile_rows(table, embeds, small, buffers):
     smem = pl.BlockSpec(memory_space=pltpu.SMEM)
     vmem = pl.BlockSpec(memory_space=pltpu.VMEM)
     slides = 1 + len(buffers)
     return pl.pallas_call(
         functools.partial(rows_kernel, slides),
         out_shape=(
-            jax.ShapeDtypeStruct((devices * 2 * PROC, HALF), jnp.bfloat16),
+            jax.ShapeDtypeStruct((ROW_UNIT, HALF), jnp.bfloat16),
             jax.ShapeDtypeStruct((slides, 1, SMALL), jnp.float32),
         ),
         in_specs=[smem, vmem, vmem] + [HBM] * len(buffers),
@@ -607,14 +613,26 @@
     length,
     members,
     slides,
+    pieces,
     table_ref,
-    came_ref,
+    *refs,
+):
+    slide_parts(length, members, slides, table_ref, refs[:pieces], *refs[pieces:])
+
+
+def slide_parts(
+    length,
+    members,
+    slides,
+    table_ref,
+    piece_refs,
     taps_hbm,
     matrix_hbm,
     vectors_ref,
     smalls_ref,
     feature_ref,
     grad_ref,
+    came_ref,
     picks,
     own_rows,
     tile_rows,
@@ -630,6 +648,9 @@
     ]
     for load in loads:
         load.start()
+    for index, ref in enumerate(piece_refs):
+        size = ref.shape[0]
+        came_ref[index * size : (index + 1) * size, :] = ref[...]
     my_slide, my_member = lax.axis_index(DP), lax.axis_index(GROUP)
     border = ROW_UNIT
     reach = KERNEL_TAPS // 2
@@ -725,18 +746,20 @@
 
 def slide_grads(length, members, table, came, taps, matrix, vectors, smalls):
     slides = smalls.shape[0]
+    lines = sum(piece.shape[0] for piece in came)
     smem = pl.BlockSpec(memory_space=pltpu.SMEM)
     vmem = pl.BlockSpec(memory_space=pltpu.VMEM)
     return pl.pallas_call(
-        functools.partial(slide_kernel, length, members, slides),
+        functools.partial(slide_kernel, length, members, slides, len(came)),
         out_shape=(
             jax.ShapeDtypeStruct((1, E), jnp.float32),
             jax.ShapeDtypeStruct((PROC, 1, E), jnp.float32),
         ),
-        in_specs=[smem, vmem, IN_HBM, IN_HBM, vmem, vmem],
+        in_specs=[smem] + [vmem] * len(came) + [IN_HBM, IN_HBM, vmem, vmem],
         out_specs=(vmem, vmem),
         scratch_shapes=[
-            pltpu.VMEM((length + PROC * ROW_UNIT, came.shape[0]), jnp.float32),
+            pltpu.VMEM((lines, HALF), jnp.bfloat16),
+            pltpu.VMEM((length + PROC * ROW_UNIT, lines), jnp.float32),
             pltpu.VMEM((length + 2 * ROW_UNIT, E), jnp.float32),
             pltpu.VMEM((PROC * ROW_UNIT, E), jnp.float32),
             pltpu.VMEM((length + PROC * 8, E), jnp.bfloat16),
@@ -748,7 +771,7 @@
         compiler_params=pltpu.CompilerParams(vmem_limit_bytes=16 * MIB),
         cost_estimate=cost(3.0),
         name="slide_grads",
-    )(table, came, pinned(taps), pinned(matrix), vectors, smalls)
+    )(table, *came, pinned(taps), pinned(matrix), vectors, smalls)
 
 
 class Plan:
@@ -1111,6 +1134,16 @@
     return lax.all_to_all(values, names, split_axis=0, concat_axis=0, tiled=True)
 
 
+def gather_all(plan, lines):
+    pair = lines + other_core(lines)
+    sizes = (plan.ys, plan.g2)
+    column = [pair] + [
+        shifted(pair, ("y", "g2"), sizes, (y, x)) for y in range(plan.ys) for x in range(plan.g2) if y + x
+    ]
+    column = jnp.concatenate(column, axis=0)
+    return [column] + [shifted(column, ("g1",), (plan.g1,), (step,)) for step in range(1, plan.g1)]
+
+
 def add_all(parts, kind=jnp.bfloat16):
     total = parts[0].astype(jnp.float32)
     for part in parts[1:]:
@@ -1182,8 +1215,8 @@
     for rank in range(places):
         saved = forward_block(1 + rank, rank + 1 == places, table, arrived[rank], *consts, saved)
     tile_out, tile_embed, unit, inv, hidden, slope, head_slope, source = saved
-    came, smalls = tile_rows(table, tile_embed, small, [from_core] + arrived[0], devices)
-    came = exchange(came, ALL)
+    lines, smalls = tile_rows(table, tile_embed, small, [from_core] + arrived[0])
+    came = gather_all(plan, lines)
     normed = turned_normed(unit, vectors)
     came, normed = lax.optimization_barrier((came, normed))
 

time: 104 us -> 106 us (1.019); the launches traced: 105 us -> 105 us
  waiting for transfers between devices: 19.3 us -> 17.3 us
  starting transfers between devices: 27.2 us -> 28.3 us
    ppermute x8 -> x15, starting transfers between devices: 7.32 us -> 20.5 us  [shifted(): return lax.ppermute(values, names, pairs)]
    all_to_all x2 -> x1, starting transfers between devices: 15 us -> 2.8 us  [exchange(): lax.all_to_all(values, names, split_axis=0, concat_axis=0, tiled=True)]
    all_to_all x2 -> x1, waiting for transfers between devices: 11.7 us -> 2.63 us  [exchange(): lax.all_to_all(values, names, split_axis=0, concat_axis=0, tiled=True)]
    ppermute x8 -> x15, waiting for transfers between devices: 7.58 us -> 14.6 us  [shifted(): return lax.ppermute(values, names, pairs)]
  transfers between devices with their start and end apart: 15 -> 21, of which waited for: 7 -> 11; matrix products, arithmetic and copies ran while one was open for 2% -> 2% of each run, Pallas kernels for 31% -> 31%
where the time goes in v10:
time: 106 us; the launch traced here: 105 us
  Pallas kernels  52.3 us (49%)
  starting transfers between devices  28.3 us (27%)
  waiting for transfers between devices  17.3 us (16%)
  local copies, waits for them, and re-layouts  4.16 us (4%)
  between operations  1.67 us (2%)
  other arithmetic  1.38 us (1%)
    pallas_call x3, Pallas kernels, forward_block(): pl.pallas_call(functools.partial(forward_kernel, kind, last, len(tiles),...  22.1 us
    ppermute x15, starting transfers between devices, shifted(): return lax.ppermute(values, names, pairs)  20.5 us
    ppermute x15, waiting for transfers between devices, shifted(): return lax.ppermute(values, names, pairs)  14.6 us
    pallas_call x1, Pallas kernels, weight_grads(): pl.pallas_call(functools.partial(weights_kernel, plan), out_shape=(pltpu....  10.4 us
    pallas_call x2, Pallas kernels, tap_grads(): pl.pallas_call(functools.partial(taps_kernel, plan, first, last), out_sha...  9.78 us
    ppermute x5, starting transfers between devices, from_other(): lax.ppermute(buffer, DP, [(index, index ^ other) for index in range(slide...  4.94 us
    pallas_call x1, Pallas kernels, slide_grads(): pl.pallas_call(functools.partial(slide_kernel, length, members, slides, l...  3.32 us
    all_to_all x1, starting transfers between devices, exchange(): lax.all_to_all(values, names, split_axis=0, concat_axis=0, tiled=True)  2.8 us
  transfers between devices with their start and end apart: 21, of which 11 were waited for; matrix products, arithmetic and copies ran while one was open for 2% of the time, Pallas kernels for 31%

profile of v10, /device:TPU:0, one launch (start us, length us, event | category | flops | bytes accessed | tf_op | source)
XLA Modules:
  0.0 105.1 jit_solution(18362570825583065970)
XLA Ops:
  1.3 0.7 copy-done.14
  2.0 2.8 %pack_tiles.1 = (bf16[33,16,384]{2,1,0:T(8,128)(2,1)S(1)}, bf16[17,16,384]{2,1,0:T(8,128)(2,1)S(1)}, bf16[17,16,384]{2,1,0:T(8,128)(2,1)S(1)}, bf16[16,16,384]{2...) custom-call(s32[1]{0:T(128)S(6)} %copy.56.counts_ref, ...), custom_call_target="tpu_custom_call" | custom-call | tf_op jit(solution)/shard_map/pack_tiles/pallas_call | solution.py:225
  4.8 0.6 collective-permute-start
  5.3 2.5 %collective-permute-start.3 = (bf16[17,16,384]{2,1,0:T(8,128)(2,1)S(1)}, bf16[17,16,384]{2,1,0:T(8,128)(2,1)S(1)}, u32[]{:S(2)}, u32[]{:S(2)}) collective-permute-start(bf16[17,16,384]{2,1,0:T(8,128)(2,1)S(1)} %get-tuple-element.67), channel_id=1, source_target_pairs={{0,16},{8,24},{16,0},{24,8},{1,17},{9,25},{17,1},{25,9},{2,18},{10... | collective-permute-start | bytes 626696 | tf_op jit(solution)/shard_map/ppermute | solution.py:1203
  7.9 1.7 %collective-permute-start.1 = (bf16[16,16,384]{2,1,0:T(8,128)(2,1)S(1)}, bf16[16,16,384]{2,1,0:T(8,128)(2,1)S(1)}, u32[]{:S(2)}, u32[]{:S(2)}) collective-permute-start(bf16[16,16,384]{2,1,0:T(8,128)(2,1)S(1)} %get-tuple-element.64), channel_id=1, source_target_pairs={{0,16},{8,24},{16,0},{24,8},{1,17},{9,25},{17,1},{25,9},{2,18},{10... | collective-permute-start | bytes 589832 | tf_op jit(solution)/shard_map/ppermute | solution.py:1203
  9.7 14.6 %forward_block_0.1 = (bf16[4,16,16,384]{3,2,1,0:T(8,128)(2,1)}, f32[4,8,768]{2,1,0:T(8,128)}, f32[4,256,384]{2,1,0:T(8,128)}, f32[4,256,128]{2,1,0:T(8,128)}, bf...) custom-call(s32[51]{0:T(128)S(1)} %get-tuple-element.60.table_ref, ...), custom_call_target="tpu_custom_call" | custom-call | flops 1000000000 | bytes 1024 | tf_op jit(solution)/shard_map/forward_block_0/pallas_call | solution.py:485
  24.4 6.6 %forward_block_1.1 = (bf16[4,16,16,384]{3,2,1,0:T(8,128)(2,1)}, f32[4,8,768]{2,1,0:T(8,128)}, f32[4,256,384]{2,1,0:T(8,128)}, f32[4,256,128]{2,1,0:T(8,128)}, bf...) custom-call(s32[51]{0:T(128)S(1)} %get-tuple-element.60.table_ref, ...), custom_call_target="tpu_custom_call", output_to_operand_aliasing={{0}: (8, {}), {1}: (9, {}), {2}: (10, {}), {3}: (11, {}), {... | custom-call | flops 1000000000 | bytes 1024 | tf_op jit(solution)/shard_map/forward_block_1/pallas_call | solution.py:485
  31.1 0.9 forward_block_2.1
  32.0 2.6 %tile_rows.1 = (bf16[16,512]{1,0:T(8,128)(2,1)}, f32[4,1,1152]{2,1,0:T(1,128)}) custom-call(s32[51]{0:T(128)} %copy-done.12, f32[4,8,768]{2,1,0:T(8,128)} %get-tuple-element.87.embed_ref, f32[1,1152]{1,0:T(1,128)} %copy-done.15, bf16[33,16,384]{2,1,0:T(8,128)(2,1)} %copy-done.9, bf16[17,16,384]{2,1,0:T(8,128)(2,1)} %copy-done.10, bf16[17,16,384]{2,1,0:T(8,128)(2,1)} %copy-done.11), custom_call_target="tpu_custom_call" | custom-call | flops 1000000000 | bytes 1024 | tf_op jit(solution)/shard_map/tile_rows/pallas_call | solution.py:593
  34.6 0.2 collective-permute-start.5
  34.8 1.3 %collective-permute-done.5 = bf16[16,512]{1,0:T(8,128)(2,1)S(1)} collective-permute-done((bf16[16,512]{1,0:T(8,128)(2,1)}, bf16[16,512]{1,0:T(8,128)(2,1)S(1)}, u32[]{:S(2)}, u32[]{:S(2)}) %collective-permute-start.5) | collective-permute-done | bytes 16416 | tf_op jit(solution)/shard_map/ppermute | solution.py:1123
  36.1 0.7 add.66
  36.8 6.2 %collective-permute-start.8 = (bf16[16,512]{1,0:T(8,128)(2,1)S(1)}, bf16[16,512]{1,0:T(8,128)(2,1)S(1)}, u32[]{:S(2)}, u32[]{:S(2)}) collective-permute-start(bf16[16,512]{1,0:T(8,128)(2,1)S(1)} %add.66), channel_id=1, source_target_pairs={{0,17},{1,16},{16,1},{17,0},{2,19},{3,18},{18,3},{19,2},{4,21},{5,... | collective-permute-start | bytes 49160 | tf_op jit(solution)/shard_map/ppermute | solution.py:1123
  43.0 0.6 collective-permute-start.6
  43.6 1.1 %collective-permute-done.8 = bf16[16,512]{1,0:T(8,128)(2,1)S(1)} collective-permute-done((bf16[16,512]{1,0:T(8,128)(2,1)S(1)}, bf16[16,512]{1,0:T(8,128)(2,1)S(1)}, u32[]{:S(2)}, u32[]{:S(2)}) %collective-permute-start.8) | collective-permute-done | bytes 16416 | tf_op jit(solution)/shard_map/ppermute | solution.py:1123
  44.7 2.0 %collective-permute-done.7 = bf16[16,512]{1,0:T(8,128)(2,1)S(1)} collective-permute-done((bf16[16,512]{1,0:T(8,128)(2,1)S(1)}, bf16[16,512]{1,0:T(8,128)(2,1)S(1)}, u32[]{:S(2)}, u32[]{:S(2)}) %collective-permute-start.7) | collective-permute-done | bytes 16416 | tf_op jit(solution)/shard_map/ppermute | solution.py:1123
  46.7 1.6 %collective-permute-start.9 = (bf16[64,512]{1,0:T(8,128)(2,1)S(1)}, bf16[64,512]{1,0:T(8,128)(2,1)S(1)}, u32[]{:S(2)}, u32[]{:S(2)}) collective-permute-start(bf16[64,512]{1,0:T(8,128)(2,1)S(1)} %pad_maximum_fusion.1.refs_0_), channel_id=1, source_target_pairs={{0,2},{2,4},{4,6},{6,0},{1,3},{3,5},{5,7},{7,1},{8,10},{10,12},{12... | collective-permute-start | bytes 196616 | tf_op jit(solution)/shard_map/ppermute | solution.py:1123
  48.4 2.6 %collective-permute-start.10 = (bf16[64,512]{1,0:T(8,128)(2,1)S(1)}, bf16[64,512]{1,0:T(8,128)(2,1)S(1)}, u32[]{:S(2)}, u32[]{:S(2)}) collective-permute-start(bf16[64,512]{1,0:T(8,128)(2,1)S(1)} %pad_maximum_fusion.1.refs_0_), channel_id=1, source_target_pairs={{0,4},{2,6},{4,0},{6,2},{1,5},{3,7},{5,1},{7,3},{8,12},{10,14},{12... | collective-permute-start | bytes 196616 | tf_op jit(solution)/shard_map/ppermute | solution.py:1123
  51.0 0.3 collective-permute-start.11
  51.3 1.3 %turned_normed.1.normed_ref = bf16[384,1024]{1,0:T(8,128)(2,1)S(1)} custom-call(f32[4,256,384]{2,1,0:T(8,128)S(1)} %copy-done.4, f32[8,1536]{1,0:T(8,128)S(1)} %get-tuple-element.66.refs_3_.vectors_ref.refs_6_), custom_call_target="tpu_custom_call" | custom-call | flops 3000000000 | bytes 1024 | tf_op jit(solution)/shard_map/turned_normed/pallas_call | solution.py:839
  52.6 0.5 collective-permute-done.9.refs_1_
  53.1 2.1 %collective-permute-done.10.refs_2_ = bf16[64,512]{1,0:T(8,128)(2,1)S(1)} collective-permute-done((bf16[64,512]{1,0:T(8,128)(2,1)S(1)}, bf16[64,512]{1,0:T(8,128)(2,1)S(1)}, u32[]{:S(2)}, u32[]{:S(2)}) %collective-permute-start.10) | collective-permute-done | bytes 65568 | tf_op jit(solution)/shard_map/ppermute | solution.py:1123
  55.2 0.4 collective-permute-done.11.refs_3_
  55.7 3.3 %slide_grads.1 = (f32[1,768]{1,0:T(1,128)}, f32[4,1,768]{2,1,0:T(1,128)S(1)}) custom-call(s32[51]{0:T(128)S(1)} %copy-done.13, bf16[64,512]{1,0:T(8,128)(2,1)S(1)} %pad_maximum_fusion.1.refs_0_, bf16[64,512]{1,0:T(8,128)(2,1)S(1)} %collective-permute-done.9.refs_1_, bf16[64,512]{1,0:T(8,128)(2,1)S(1)} %collective-permute-done.10.refs_2_, ...), custom_call_target="tpu_custom_call" | custom-call | flops 3000000000 | bytes 1024 | tf_op jit(solution)/shard_map/slide_grads/pallas_call | solution.py:752
  59.0 0.1 copy-done.2
  59.1 0.5 copy-done.5
  59.6 0.1 copy-done.6
  59.7 10.4 %weight_grads.1 = (bf16[4,256,1536]{2,1,0:T(8,128)(2,1)}, bf16[2,2,2,4,48,384]{5,4,3,2,1,0:T(8,128)(2,1)S(1)}, bf16[2,2,2,4,48,384]{5,4,3,2,1,0:T(8,128)(2,1)S(1)}) custom-call(f32[4,1,768]{2,1,0:T(1,128)S(1)} %get-tuple-element.97.grad_ref, bf16[1024,1536]{1,0:T(8,128)(2,1)S(1)} %bitcast.51, bf16[4,256,768]{2,1,0:T(8,128)(2,1)S(1)} %copy-done.5, ...), custom_call_target="tpu_custom_call" | custom-call | flops 12000000000 | bytes 1024 | tf_op jit(solution)/shard_map/weight_grads/pallas_call | solution.py:1056
  70.1 0.1 collective-permute-start.12
  70.3 4.8 %tap_grads_0.1.before_ref = f32[3,49,8,128]{3,2,1,0:T(8,128)S(1)} custom-call(s32[51]{0:T(128)S(1)} %copy-done.13, bf16[4,16,16,384]{3,2,1,0:T(8,128)(2,1)S(1)} %copy-done.7, bf16[4,256,1536]{2,1,0:T(8,128)(2,1)} %get-tuple-element.105.grad_pre_ref, f32[4,256,384]{2,1,0:T(8,128)S(1)} %copy-done.4, f32[4,256,128]{2,1,0:T(8,128)S(1)} %copy-done.8, ...), custom_call_target="tpu_custom_call" | custom-call | flops 4000000000 | bytes 1024 | tf_op jit(solution)/shard_map/tap_grads_0/pallas_call | solution.py:1086
  75.1 0.3 add_convert_fusion
  75.4 0.6 collective-permute-start.13
  76.1 1.4 %collective-permute-start.14 = (bf16[2,4,48,384]{3,2,1,0:T(8,128)(2,1)S(1)}, bf16[2,4,48,384]{3,2,1,0:T(8,128)(2,1)S(1)}, u32[]{:S(2)}, u32[]{:S(2)}) collective-permute-start(bf16[2,4,48,384]{3,2,1,0:T(8,128)(2,1)S(1)} %get-tuple-element.110), channel_id=1, source_target_pairs={{0,16},{16,0},{1,17},{17,1},{2,18},{18,2},{3,19},{19,3},{4,20},{20... | collective-permute-start | bytes 884744 | tf_op jit(solution)/shard_map/ppermute | solution.py:1123
  77.5 4.9 %tap_grads_2.1 = f32[32,8,384]{2,1,0:T(8,128)S(1)} custom-call(s32[51]{0:T(128)S(1)} %copy-done.13, bf16[4,16,16,384]{3,2,1,0:T(8,128)(2,1)S(1)} %copy-done.7, bf16[4,256,1536]{2,1,0:T(8,128)(2,1)} %get-tuple-element.105.grad_pre_ref, f32[4,256,384]{2,1,0:T(8,128)S(1)} %copy-done.4, f32[4,256,128]{2,1,0:T(8,128)S(1)} %copy-done.8, ...), custom_call_target="tpu_custom_call" | custom-call | flops 4000000000 | bytes 1024 | tf_op jit(solution)/shard_map/tap_grads_2/pallas_call | solution.py:1086
  82.4 0.7 slice.165
  83.1 1.8 %collective-permute-done.13 = bf16[2,4,48,384]{3,2,1,0:T(8,128)(2,1)S(1)} collective-permute-done((bf16[2,4,48,384]{3,2,1,0:T(8,128)(2,1)S(1)}, bf16[2,4,48,384]{3,2,1,0:T(8,128)(2,1)S(1)}, u32[]{:S(2)}, u32[]{:S(2)}) %collective-permute-start.13) | collective-permute-done | bytes 294944 | tf_op jit(solution)/shard_map/ppermute | solution.py:1123
  85.0 0.4 collective-permute-done.14
  85.5 1.8 %collective-permute-start.15 = (bf16[4,48,384]{2,1,0:T(8,128)(2,1)S(1)}, bf16[4,48,384]{2,1,0:T(8,128)(2,1)S(1)}, u32[]{:S(2)}, u32[]{:S(2)}) collective-permute-start(bf16[4,48,384]{2,1,0:T(8,128)(2,1)S(1)} %fusion.9), channel_id=1, source_target_pairs={{0,16},{16,0},{1,17},{17,1},{2,18},{18,2},{3,19},{19,3},{4,20},{20... | collective-permute-start | bytes 442376 | tf_op jit(solution)/shard_map/ppermute | solution.py:1123
  87.3 1.4 %collective-permute-start.16 = (bf16[4,48,384]{2,1,0:T(8,128)(2,1)S(1)}, bf16[4,48,384]{2,1,0:T(8,128)(2,1)S(1)}, u32[]{:S(2)}, u32[]{:S(2)}) collective-permute-start(bf16[4,48,384]{2,1,0:T(8,128)(2,1)S(1)} %fusion.10), channel_id=1, source_target_pairs={{0,1},{1,0},{2,3},{3,2},{4,5},{5,4},{6,7},{7,6},{8,9},{9,8},{10,11... | collective-permute-start | bytes 442376 | tf_op jit(solution)/shard_map/ppermute | solution.py:1123
  88.7 2.8 %all-to-all-start = ((bf16[32,4,384]{2,1,0:T(4,128)(2,1)}), bf16[32,4,384]{2,1,0:T(4,128)(2,1)S(1)}, u32[]{:S(2)}, u32[]{:S(2)}) async-start(bf16[32,4,384]{2,1,0:T(4,128)(2,1)} %slice.165), calls=%async_computation | async-start | bytes 196608 | tf_op jit(solution)/shard_map/all_to_all | solution.py:1134
  91.5 1.1 %collective-permute-done.16 = bf16[4,48,384]{2,1,0:T(8,128)(2,1)S(1)} collective-permute-done((bf16[4,48,384]{2,1,0:T(8,128)(2,1)S(1)}, bf16[4,48,384]{2,1,0:T(8,128)(2,1)S(1)}, u32[]{:S(2)}, u32[]{:S(2)}) %collective-permute-start.16) | collective-permute-done | bytes 147488 | tf_op jit(solution)/shard_map/ppermute | solution.py:1123
  92.7 2.6 %collective-permute-start.19 = (bf16[96,384]{1,0:T(8,128)(2,1)S(1)}, bf16[96,384]{1,0:T(8,128)(2,1)S(1)}, u32[]{:S(2)}, u32[]{:S(2)}) collective-permute-start(bf16[96,384]{1,0:T(8,128)(2,1)S(1)} %get-tuple-element.120), channel_id=1, source_target_pairs={{0,6},{2,0},{4,2},{6,4},{1,7},{3,1},{5,3},{7,5},{8,14},{10,8},{12,... | collective-permute-start | bytes 221192 | tf_op jit(solution)/shard_map/ppermute | solution.py:1123
  95.3 1.1 %collective-permute-start.17 = (bf16[96,384]{1,0:T(8,128)(2,1)S(1)}, bf16[96,384]{1,0:T(8,128)(2,1)S(1)}, u32[]{:S(2)}, u32[]{:S(2)}) collective-permute-start(bf16[96,384]{1,0:T(8,128)(2,1)S(1)} %get-tuple-element.119), channel_id=1, source_target_pairs={{0,2},{2,4},{4,6},{6,0},{1,3},{3,5},{5,7},{7,1},{8,10},{10,12},{12... | collective-permute-start | bytes 221192 | tf_op jit(solution)/shard_map/ppermute | solution.py:1123
  96.4 2.6 %all-to-all-done = bf16[32,4,384]{2,1,0:T(4,128)(2,1)S(1)} async-done(((bf16[32,4,384]{2,1,0:T(4,128)(2,1)}), bf16[32,4,384]{2,1,0:T(4,128)(2,1)S(1)}, u32[]{:S(2)}, u32[]{:S(2)}) %all-to-all-start) | async-done | bytes 98336 | tf_op jit(solution)/shard_map/all_to_all | solution.py:1134
  99.1 0.7 dynamic_slice.3
  99.8 3.9 %collective-permute-done.18 = bf16[96,384]{1,0:T(8,128)(2,1)S(1)} collective-permute-done((bf16[96,384]{1,0:T(8,128)(2,1)S(1)}, bf16[96,384]{1,0:T(8,128)(2,1)S(1)}, u32[]{:S(2)}, u32[]{:S(2)}) %collective-permute-start.18) | collective-permute-done | bytes 73760 | tf_op jit(solution)/shard_map/ppermute | solution.py:1123
  103.8 0.7 reshape.77
  104.4 0.6 reshape.78
  (57 shorter events, 0.6 us)
Async XLA Ops:
  1.3 0.7 copy-start.14
  4.7 19.6 %copy-start.15 = (f32[1,1152]{1,0:T(1,128)}, f32[1,1152]{1,0:T(1,128)S(1)}, u32[]{:S(2)}) copy-start(f32[1,1152]{1,0:T(1,128)S(1)} %get-tuple-element.88.small_ref) | copy-start | bytes 13828
  4.7 26.3 %copy-start.12 = (s32[51]{0:T(128)}, s32[51]{0:T(128)S(1)}, u32[]{:S(2)}) copy-start(s32[51]{0:T(128)S(1)} %get-tuple-element.60.table_ref) | copy-start | bytes 616
  4.8 3.2 %collective-permute-start = (bf16[33,16,384]{2,1,0:T(8,128)(2,1)S(1)}, bf16[33,16,384]{2,1,0:T(8,128)(2,1)S(1)}, u32[]{:S(2)}, u32[]{:S(2)}) collective-permute-start(bf16[33,16,384]{2,1,0:T(8,128)(2,1)S(1)} %get-tuple-element.63), channel_id=1, source_target_pairs={{0,8},{8,0},{16,24},{24,16},{1,9},{9,1},{17,25},{25,17},{2,10},{10... | collective-permute-start | bytes 1216520 | tf_op jit(solution)/shard_map/ppermute | solution.py:1203
  5.3 19.0 %collective-permute-start.3 = (bf16[17,16,384]{2,1,0:T(8,128)(2,1)S(1)}, bf16[17,16,384]{2,1,0:T(8,128)(2,1)S(1)}, u32[]{:S(2)}, u32[]{:S(2)}) collective-permute-start(bf16[17,16,384]{2,1,0:T(8,128)(2,1)S(1)} %get-tuple-element.67), channel_id=1, source_target_pairs={{0,16},{8,24},{16,0},{24,8},{1,17},{9,25},{17,1},{25,9},{2,18},{10... | collective-permute-start | bytes 626696 | tf_op jit(solution)/shard_map/ppermute | solution.py:1203
  7.9 16.5 %collective-permute-start.4 = (bf16[17,16,384]{2,1,0:T(8,128)(2,1)S(1)}, bf16[17,16,384]{2,1,0:T(8,128)(2,1)S(1)}, u32[]{:S(2)}, u32[]{:S(2)}) collective-permute-start(bf16[17,16,384]{2,1,0:T(8,128)(2,1)S(1)} %get-tuple-element.68), channel_id=1, source_target_pairs={{0,24},{8,16},{16,8},{24,0},{1,25},{9,17},{17,9},{25,1},{2,26},{10... | collective-permute-start | bytes 626696 | tf_op jit(solution)/shard_map/ppermute | solution.py:1203
  7.9 16.4 %copy-start.9 = (bf16[33,16,384]{2,1,0:T(8,128)(2,1)}, bf16[33,16,384]{2,1,0:T(8,128)(2,1)S(1)}, u32[]{:S(2)}) copy-start(bf16[33,16,384]{2,1,0:T(8,128)(2,1)S(1)} %collective-permute-done.refs_1_.refs_0_) | copy-start | bytes 1216516
  7.9 23.1 %collective-permute-start.1 = (bf16[16,16,384]{2,1,0:T(8,128)(2,1)S(1)}, bf16[16,16,384]{2,1,0:T(8,128)(2,1)S(1)}, u32[]{:S(2)}, u32[]{:S(2)}) collective-permute-start(bf16[16,16,384]{2,1,0:T(8,128)(2,1)S(1)} %get-tuple-element.64), channel_id=1, source_target_pairs={{0,16},{8,24},{16,0},{24,8},{1,17},{9,25},{17,1},{25,9},{2,18},{10... | collective-permute-start | bytes 589832 | tf_op jit(solution)/shard_map/ppermute | solution.py:1203
  9.7 21.4 %collective-permute-start.2 = (bf16[16,16,384]{2,1,0:T(8,128)(2,1)S(1)}, bf16[16,16,384]{2,1,0:T(8,128)(2,1)S(1)}, u32[]{:S(2)}, u32[]{:S(2)}) collective-permute-start(bf16[16,16,384]{2,1,0:T(8,128)(2,1)S(1)} %get-tuple-element.65), channel_id=1, source_target_pairs={{0,24},{8,16},{16,8},{24,0},{1,25},{9,17},{17,9},{25,1},{2,26},{10... | collective-permute-start | bytes 589832 | tf_op jit(solution)/shard_map/ppermute | solution.py:1203
  24.4 6.7 %copy-start.10 = (bf16[17,16,384]{2,1,0:T(8,128)(2,1)}, bf16[17,16,384]{2,1,0:T(8,128)(2,1)S(1)}, u32[]{:S(2)}) copy-start(bf16[17,16,384]{2,1,0:T(8,128)(2,1)S(1)} %collective-permute-done.3.refs_0_.refs_1_) | copy-start | bytes 626692
  24.4 6.7 %copy-start.11 = (bf16[17,16,384]{2,1,0:T(8,128)(2,1)}, bf16[17,16,384]{2,1,0:T(8,128)(2,1)S(1)}, u32[]{:S(2)}) copy-start(bf16[17,16,384]{2,1,0:T(8,128)(2,1)S(1)} %collective-permute-done.4.refs_1_.refs_2_) | copy-start | bytes 626692
  32.0 19.3 %copy-start.4 = (f32[4,256,384]{2,1,0:T(8,128)S(1)}, f32[4,256,384]{2,1,0:T(8,128)}, u32[]{:S(2)}) copy-start(f32[4,256,384]{2,1,0:T(8,128)} %get-tuple-element.90.unit_ref) | copy-start | bytes 4718596
  34.6 1.5 %collective-permute-start.5 = (bf16[16,512]{1,0:T(8,128)(2,1)}, bf16[16,512]{1,0:T(8,128)(2,1)S(1)}, u32[]{:S(2)}, u32[]{:S(2)}) collective-permute-start(bf16[16,512]{1,0:T(8,128)(2,1)} %get-tuple-element.89), channel_id=1, source_target_pairs={{0,8},{8,0},{1,9},{9,1},{2,10},{10,2},{3,11},{11,3},{4,12},{12,4},... | collective-permute-start | bytes 49160 | tf_op jit(solution)/shard_map/ppermute | solution.py:1123
  36.8 7.9 %collective-permute-start.8 = (bf16[16,512]{1,0:T(8,128)(2,1)S(1)}, bf16[16,512]{1,0:T(8,128)(2,1)S(1)}, u32[]{:S(2)}, u32[]{:S(2)}) collective-permute-start(bf16[16,512]{1,0:T(8,128)(2,1)S(1)} %add.66), channel_id=1, source_target_pairs={{0,17},{1,16},{16,1},{17,0},{2,19},{3,18},{18,3},{19,2},{4,21},{5,... | collective-permute-start | bytes 49160 | tf_op jit(solution)/shard_map/ppermute | solution.py:1123
  43.0 3.7 %collective-permute-start.7 = (bf16[16,512]{1,0:T(8,128)(2,1)S(1)}, bf16[16,512]{1,0:T(8,128)(2,1)S(1)}, u32[]{:S(2)}, u32[]{:S(2)}) collective-permute-start(bf16[16,512]{1,0:T(8,128)(2,1)S(1)} %add.66), channel_id=1, source_target_pairs={{0,16},{1,17},{16,0},{17,1},{2,18},{3,19},{18,2},{19,3},{4,20},{5,... | collective-permute-start | bytes 49160 | tf_op jit(solution)/shard_map/ppermute | solution.py:1123
  43.0 3.7 %collective-permute-start.6 = (bf16[16,512]{1,0:T(8,128)(2,1)S(1)}, bf16[16,512]{1,0:T(8,128)(2,1)S(1)}, u32[]{:S(2)}, u32[]{:S(2)}) collective-permute-start(bf16[16,512]{1,0:T(8,128)(2,1)S(1)} %add.66), channel_id=1, source_target_pairs={{0,1},{1,0},{16,17},{17,16},{2,3},{3,2},{18,19},{19,18},{4,5},{5,4... | collective-permute-start | bytes 49160 | tf_op jit(solution)/shard_map/ppermute | solution.py:1123
  46.7 6.4 %collective-permute-start.9 = (bf16[64,512]{1,0:T(8,128)(2,1)S(1)}, bf16[64,512]{1,0:T(8,128)(2,1)S(1)}, u32[]{:S(2)}, u32[]{:S(2)}) collective-permute-start(bf16[64,512]{1,0:T(8,128)(2,1)S(1)} %pad_maximum_fusion.1.refs_0_), channel_id=1, source_target_pairs={{0,2},{2,4},{4,6},{6,0},{1,3},{3,5},{5,7},{7,1},{8,10},{10,12},{12... | collective-permute-start | bytes 196616 | tf_op jit(solution)/shard_map/ppermute | solution.py:1123
  48.4 6.9 %collective-permute-start.10 = (bf16[64,512]{1,0:T(8,128)(2,1)S(1)}, bf16[64,512]{1,0:T(8,128)(2,1)S(1)}, u32[]{:S(2)}, u32[]{:S(2)}) collective-permute-start(bf16[64,512]{1,0:T(8,128)(2,1)S(1)} %pad_maximum_fusion.1.refs_0_), channel_id=1, source_target_pairs={{0,4},{2,6},{4,0},{6,2},{1,5},{3,7},{5,1},{7,3},{8,12},{10,14},{12... | collective-permute-start | bytes 196616 | tf_op jit(solution)/shard_map/ppermute | solution.py:1123
  51.0 4.6 %collective-permute-start.11 = (bf16[64,512]{1,0:T(8,128)(2,1)S(1)}, bf16[64,512]{1,0:T(8,128)(2,1)S(1)}, u32[]{:S(2)}, u32[]{:S(2)}) collective-permute-start(bf16[64,512]{1,0:T(8,128)(2,1)S(1)} %pad_maximum_fusion.1.refs_0_), channel_id=1, source_target_pairs={{0,6},{2,0},{4,2},{6,4},{1,7},{3,1},{5,3},{7,5},{8,14},{10,8},{12,... | collective-permute-start | bytes 196616 | tf_op jit(solution)/shard_map/ppermute | solution.py:1123
  51.3 4.3 %copy-start.13 = (s32[51]{0:T(128)S(1)}, s32[51]{0:T(128)}, u32[]{:S(2)}) copy-start(s32[51]{0:T(128)} %copy-done.12) | copy-start | bytes 616
  51.3 4.3 %copy-start.16 = (f32[4,1,1152]{2,1,0:T(1,128)S(1)}, f32[4,1,1152]{2,1,0:T(1,128)}, u32[]{:S(2)}) copy-start(f32[4,1,1152]{2,1,0:T(1,128)} %get-tuple-element.95.refs_7_) | copy-start | bytes 55300
  55.6 3.4 %copy-start = (bf16[4,256,1536]{2,1,0:T(8,128)(2,1)S(1)}, bf16[4,256,1536]{2,1,0:T(8,128)(2,1)}, u32[]{:S(2)}) copy-start(bf16[4,256,1536]{2,1,0:T(8,128)(2,1)} %get-tuple-element.98) | copy-start | bytes 9437188
  55.6 3.4 %copy-start.1 = (bf16[4,256,1536]{2,1,0:T(8,128)(2,1)S(1)}, bf16[4,256,1536]{2,1,0:T(8,128)(2,1)}, u32[]{:S(2)}) copy-start(bf16[4,256,1536]{2,1,0:T(8,128)(2,1)} %get-tuple-element.100.slope_ref) | copy-start | bytes 9437188
  55.6 3.5 %copy-start.2 = (bf16[1536,384]{1,0:T(8,128)(2,1)S(1)}, bf16[1536,384]{1,0:T(8,128)(2,1)}, u32[]{:S(2)}) copy-start(bf16[1536,384]{1,0:T(8,128)(2,1)} %reduce_ref.1) | copy-start | bytes 3538948
  55.6 4.0 %copy-start.5 = (bf16[4,256,768]{2,1,0:T(8,128)(2,1)S(1)}, bf16[4,256,768]{2,1,0:T(8,128)(2,1)}, u32[]{:S(2)}) copy-start(bf16[4,256,768]{2,1,0:T(8,128)(2,1)} %get-tuple-element.99.head_slope_ref) | copy-start | bytes 4718596
  55.7 4.0 %copy-start.6 = (bf16[384,768]{1,0:T(8,128)(2,1)S(1)}, bf16[384,768]{1,0:T(8,128)(2,1)}, u32[]{:S(2)}) copy-start(bf16[384,768]{1,0:T(8,128)(2,1)} %head_ref.1) | copy-start | bytes 1769476
  59.7 10.5 %copy-start.3 = (bf16[384,1536]{1,0:T(8,128)(2,1)S(1)}, bf16[384,1536]{1,0:T(8,128)(2,1)}, u32[]{:S(2)}) copy-start(bf16[384,1536]{1,0:T(8,128)(2,1)} %expand_ref.3) | copy-start | bytes 3538948
  59.7 10.5 %copy-start.7 = (bf16[4,16,16,384]{3,2,1,0:T(8,128)(2,1)S(1)}, bf16[4,16,16,384]{3,2,1,0:T(8,128)(2,1)}, u32[]{:S(2)}) copy-start(bf16[4,16,16,384]{3,2,1,0:T(8,128)(2,1)} %get-tuple-element.104.source_ref) | copy-start | bytes 2359300
  59.7 10.5 %copy-start.8 = (f32[4,256,128]{2,1,0:T(8,128)S(1)}, f32[4,256,128]{2,1,0:T(8,128)}, u32[]{:S(2)}) copy-start(f32[4,256,128]{2,1,0:T(8,128)} %get-tuple-element.106.inv_ref) | copy-start | bytes 1572868
  70.1 5.0 %collective-permute-start.12 = (bf16[2,2,2,4,48,384]{5,4,3,2,1,0:T(8,128)(2,1)S(1)}, bf16[2,2,2,4,48,384]{5,4,3,2,1,0:T(8,128)(2,1)S(1)}, u32[]{:S(2)}, u32[]{:S(2)}) collective-permute-start(bf16[2,2,2,4,48,384]{5,4,3,2,1,0:T(8,128)(2,1)S(1)} %get-tuple-element.103), channel_id=1, source_target_pairs={{0,8},{8,0},{1,9},{9,1},{2,10},{10,2},{3,11},{11,3},{4,12},{12,4},... | collective-permute-start | bytes 3538952 | tf_op jit(solution)/shard_map/ppermute | solution.py:1123
  75.4 9.5 %collective-permute-start.13 = (bf16[2,4,48,384]{3,2,1,0:T(8,128)(2,1)S(1)}, bf16[2,4,48,384]{3,2,1,0:T(8,128)(2,1)S(1)}, u32[]{:S(2)}, u32[]{:S(2)}) collective-permute-start(bf16[2,4,48,384]{3,2,1,0:T(8,128)(2,1)S(1)} %get-tuple-element.109), channel_id=1, source_target_pairs={{0,1},{1,0},{2,3},{3,2},{4,5},{5,4},{6,7},{7,6},{8,9},{9,8},{10,11... | collective-permute-start | bytes 884744 | tf_op jit(solution)/shard_map/ppermute | solution.py:1123
  76.1 9.3 %collective-permute-start.14 = (bf16[2,4,48,384]{3,2,1,0:T(8,128)(2,1)S(1)}, bf16[2,4,48,384]{3,2,1,0:T(8,128)(2,1)S(1)}, u32[]{:S(2)}, u32[]{:S(2)}) collective-permute-start(bf16[2,4,48,384]{3,2,1,0:T(8,128)(2,1)S(1)} %get-tuple-element.110), channel_id=1, source_target_pairs={{0,16},{16,0},{1,17},{17,1},{2,18},{18,2},{3,19},{19,3},{4,20},{20... | collective-permute-start | bytes 884744 | tf_op jit(solution)/shard_map/ppermute | solution.py:1123
  85.5 6.0 %collective-permute-start.15 = (bf16[4,48,384]{2,1,0:T(8,128)(2,1)S(1)}, bf16[4,48,384]{2,1,0:T(8,128)(2,1)S(1)}, u32[]{:S(2)}, u32[]{:S(2)}) collective-permute-start(bf16[4,48,384]{2,1,0:T(8,128)(2,1)S(1)} %fusion.9), channel_id=1, source_target_pairs={{0,16},{16,0},{1,17},{17,1},{2,18},{18,2},{3,19},{19,3},{4,20},{20... | collective-permute-start | bytes 442376 | tf_op jit(solution)/shard_map/ppermute | solution.py:1123
  87.3 5.4 %collective-permute-start.16 = (bf16[4,48,384]{2,1,0:T(8,128)(2,1)S(1)}, bf16[4,48,384]{2,1,0:T(8,128)(2,1)S(1)}, u32[]{:S(2)}, u32[]{:S(2)}) collective-permute-start(bf16[4,48,384]{2,1,0:T(8,128)(2,1)S(1)} %fusion.10), channel_id=1, source_target_pairs={{0,1},{1,0},{2,3},{3,2},{4,5},{5,4},{6,7},{7,6},{8,9},{9,8},{10,11... | collective-permute-start | bytes 442376 | tf_op jit(solution)/shard_map/ppermute | solution.py:1123
  88.7 10.4 %all-to-all-start = ((bf16[32,4,384]{2,1,0:T(4,128)(2,1)}), bf16[32,4,384]{2,1,0:T(4,128)(2,1)S(1)}, u32[]{:S(2)}, u32[]{:S(2)}) async-start(bf16[32,4,384]{2,1,0:T(4,128)(2,1)} %slice.165), calls=%async_computation | async-start | bytes 196608 | tf_op jit(solution)/shard_map/all_to_all | solution.py:1134
  92.7 7.0 %collective-permute-start.19 = (bf16[96,384]{1,0:T(8,128)(2,1)S(1)}, bf16[96,384]{1,0:T(8,128)(2,1)S(1)}, u32[]{:S(2)}, u32[]{:S(2)}) collective-permute-start(bf16[96,384]{1,0:T(8,128)(2,1)S(1)} %get-tuple-element.120), channel_id=1, source_target_pairs={{0,6},{2,0},{4,2},{6,4},{1,7},{3,1},{5,3},{7,5},{8,14},{10,8},{12,... | collective-permute-start | bytes 221192 | tf_op jit(solution)/shard_map/ppermute | solution.py:1123
  95.3 8.3 %collective-permute-start.18 = (bf16[96,384]{1,0:T(8,128)(2,1)S(1)}, bf16[96,384]{1,0:T(8,128)(2,1)S(1)}, u32[]{:S(2)}, u32[]{:S(2)}) collective-permute-start(bf16[96,384]{1,0:T(8,128)(2,1)S(1)} %get-tuple-element.121), channel_id=1, source_target_pairs={{0,4},{2,6},{4,0},{6,2},{1,5},{3,7},{5,1},{7,3},{8,12},{10,14},{12... | collective-permute-start | bytes 221192 | tf_op jit(solution)/shard_map/ppermute | solution.py:1123
  95.3 8.3 %collective-permute-start.17 = (bf16[96,384]{1,0:T(8,128)(2,1)S(1)}, bf16[96,384]{1,0:T(8,128)(2,1)S(1)}, u32[]{:S(2)}, u32[]{:S(2)}) collective-permute-start(bf16[96,384]{1,0:T(8,128)(2,1)S(1)} %get-tuple-element.119), channel_id=1, source_target_pairs={{0,2},{2,4},{4,6},{6,0},{1,3},{3,5},{5,7},{7,1},{8,10},{10,12},{12... | collective-permute-start | bytes 221192 | tf_op jit(solution)/shard_map/ppermute | solution.py:1123

commit v11 on v9

--- a/solution.py
+++ b/solution.py
@@ -335,7 +335,7 @@
                 ].astype(jnp.float32)
 
         def convolve(band, carry):
-            lanes = pl.ds(pl.multiple_of(band * LANES, LANES), LANES)
+            lanes = slice(band * LANES, (band + 1) * LANES)
             bias = jnp.broadcast_to(vectors_ref[DEPTH_BIAS : DEPTH_BIAS + 1, lanes], (side, LANES))
             totals = [bias for _ in range(side)]
             for col in range(KS):
@@ -360,7 +360,8 @@
                 depth_out[band, place * side : (place + 1) * side, :] = totals[place]
             return carry
 
-        lax.fori_loop(0, bands, convolve, 0)
+        for band in range(bands):
+            convolve(band, 0)
         for start in range(0, cells, PART):
             rows = slice(start, start + PART)
             pieces = [depth_out[band, rows, :] for band in range(bands)]
@@ -1001,7 +1002,8 @@
                     tap_sums[band, row * KS + col] = tap_sums[band, row * KS + col] + folded[row]
             return carry
 
-        lax.fori_loop(0, bands, taps_of, 0)
+        for band in range(bands):
+            taps_of(band, 0)
 
     @pl.when(step == pl.num_programs(0) - 1)
     def _finish():

time: 104 us -> 103 us (level); the launches traced: 105 us -> 103 us
  starting transfers between devices: 27.2 us -> 20.7 us
  Pallas kernels: 52.2 us -> 54.5 us
  waiting for transfers between devices: 19.3 us -> 20.9 us
    all_to_all x2, starting transfers between devices: 15 us -> 8.4 us  [exchange(): lax.all_to_all(values, names, split_axis=0, concat_axis=0, tiled=True)]
    ppermute x5, waiting for transfers between devices: 0.01 us -> 1.79 us  [from_other(): lax.ppermute(buffer, DP, [(index, index ^ other) for index in range(slide...]
    pallas_call x3, Pallas kernels: 21.9 us -> 23.6 us  [forward_block(): pl.pallas_call(functools.partial(forward_kernel, kind, last, len(tiles),...]
  transfers between devices with their start and end apart: 15 -> 15, of which waited for: 7 -> 8; matrix products, arithmetic and copies ran while one was open for 2% -> 2% of each run, Pallas kernels for 31% -> 28%
where the time goes in v11:
time: 103 us
  Pallas kernels  54.5 us (53%)
  waiting for transfers between devices  20.9 us (20%)
  starting transfers between devices  20.7 us (20%)
  local copies, waits for them, and re-layouts  4.18 us (4%)
  between operations  1.67 us (2%)
    pallas_call x3, Pallas kernels, forward_block(): pl.pallas_call(functools.partial(forward_kernel, kind, last, len(tiles),...  23.6 us
    all_to_all x2, waiting for transfers between devices, exchange(): lax.all_to_all(values, names, split_axis=0, concat_axis=0, tiled=True)  11.9 us
    pallas_call x2, Pallas kernels, tap_grads(): pl.pallas_call(functools.partial(taps_kernel, plan, first, last), out_sha...  10.4 us
    pallas_call x1, Pallas kernels, weight_grads(): pl.pallas_call(functools.partial(weights_kernel, plan), out_shape=(pltpu....  10.4 us
    all_to_all x2, starting transfers between devices, exchange(): lax.all_to_all(values, names, split_axis=0, concat_axis=0, tiled=True)  8.4 us
    ppermute x8, starting transfers between devices, shifted(): return lax.ppermute(values, names, pairs)  7.32 us
    ppermute x8, waiting for transfers between devices, shifted(): return lax.ppermute(values, names, pairs)  7.23 us
    ppermute x5, starting transfers between devices, from_other(): lax.ppermute(buffer, DP, [(index, index ^ other) for index in range(slide...  5 us
  transfers between devices with their start and end apart: 15, of which 8 were waited for; matrix products, arithmetic and copies ran while one was open for 2% of the time, Pallas kernels for 28%

profile of v11, /device:TPU:0, one launch (start us, length us, event | category | flops | bytes accessed | tf_op | source)
XLA Modules:
  0.0 102.6 jit_solution(7570567486823660189)
XLA Ops:
  1.3 0.7 copy-done.14
  2.0 2.8 %pack_tiles.1 = (bf16[33,16,384]{2,1,0:T(8,128)(2,1)S(1)}, bf16[17,16,384]{2,1,0:T(8,128)(2,1)S(1)}, bf16[17,16,384]{2,1,0:T(8,128)(2,1)S(1)}, bf16[16,16,384]{2...) custom-call(s32[1]{0:T(128)S(6)} %copy.56.counts_ref, ...), custom_call_target="tpu_custom_call" | custom-call | tf_op jit(solution)/shard_map/pack_tiles/pallas_call | solution.py:225
  4.7 0.0 copy-start.15
  4.8 0.0 copy-start.12
  4.8 0.5 collective-permute-start
  5.3 2.7 %collective-permute-start.3 = (bf16[17,16,384]{2,1,0:T(8,128)(2,1)S(1)}, bf16[17,16,384]{2,1,0:T(8,128)(2,1)S(1)}, u32[]{:S(2)}, u32[]{:S(2)}) collective-permute-start(bf16[17,16,384]{2,1,0:T(8,128)(2,1)S(1)} %get-tuple-element.64), channel_id=1, source_target_pairs={{0,16},{8,24},{16,0},{24,8},{1,17},{9,25},{17,1},{25,9},{2,18},{10... | collective-permute-start | bytes 626696 | tf_op jit(solution)/shard_map/ppermute | solution.py:1172
  7.9 0.1 collective-permute-start.4
  8.0 1.7 %collective-permute-start.1 = (bf16[16,16,384]{2,1,0:T(8,128)(2,1)S(1)}, bf16[16,16,384]{2,1,0:T(8,128)(2,1)S(1)}, u32[]{:S(2)}, u32[]{:S(2)}) collective-permute-start(bf16[16,16,384]{2,1,0:T(8,128)(2,1)S(1)} %get-tuple-element.61), channel_id=1, source_target_pairs={{0,16},{8,24},{16,0},{24,8},{1,17},{9,25},{17,1},{25,9},{2,18},{10... | collective-permute-start | bytes 589832 | tf_op jit(solution)/shard_map/ppermute | solution.py:1172
  9.7 0.0 collective-permute-start.2
  9.8 6.3 %forward_block_0.1 = (bf16[4,16,16,384]{3,2,1,0:T(8,128)(2,1)}, f32[4,8,768]{2,1,0:T(8,128)}, f32[4,256,384]{2,1,0:T(8,128)}, f32[4,256,128]{2,1,0:T(8,128)}, bf...) custom-call(s32[51]{0:T(128)S(1)} %get-tuple-element.57.table_ref, ...), custom_call_target="tpu_custom_call" | custom-call | flops 1000000000 | bytes 1024 | tf_op jit(solution)/shard_map/forward_block_0/pallas_call | solution.py:486
  16.1 1.8 %collective-permute-done.4.refs_1_.refs_2_ = bf16[17,16,384]{2,1,0:T(8,128)(2,1)S(1)} collective-permute-done((bf16[17,16,384]{2,1,0:T(8,128)(2,1)S(1)}, bf16[17,16,384]{2,1,0:T(8,128)(2,1)S(1)}, u32[]{:S(2)}, u32[]{:S(2)}) %collective-permute-start.4) | collective-permute-done | bytes 208928 | tf_op jit(solution)/shard_map/ppermute | solution.py:1172
  17.9 10.7 %forward_block_1.1 = (bf16[4,16,16,384]{3,2,1,0:T(8,128)(2,1)}, f32[4,8,768]{2,1,0:T(8,128)}, f32[4,256,384]{2,1,0:T(8,128)}, f32[4,256,128]{2,1,0:T(8,128)}, bf...) custom-call(s32[51]{0:T(128)S(1)} %get-tuple-element.57.table_ref, ...), custom_call_target="tpu_custom_call", output_to_operand_aliasing={{0}: (8, {}), {1}: (9, {}), {2}: (10, {}), {3}: (11, {}), {... | custom-call | flops 1000000000 | bytes 1024 | tf_op jit(solution)/shard_map/forward_block_1/pallas_call | solution.py:486
  28.7 6.5 %forward_block_2.1 = (bf16[4,16,16,384]{3,2,1,0:T(8,128)(2,1)}, f32[4,8,768]{2,1,0:T(8,128)}, f32[4,256,384]{2,1,0:T(8,128)}, f32[4,256,128]{2,1,0:T(8,128)}, bf...) custom-call(s32[51]{0:T(128)S(1)} %get-tuple-element.57.table_ref, ...), custom_call_target="tpu_custom_call", output_to_operand_aliasing={{0}: (8, {}), {1}: (9, {}), {2}: (10, {}), {3}: (11, {}), {... | custom-call | flops 1000000000 | bytes 1024 | tf_op jit(solution)/shard_map/forward_block_2/pallas_call | solution.py:486
  35.2 2.8 %tile_rows.1 = (bf16[256,512]{1,0:T(8,128)(2,1)}, f32[4,1,1152]{2,1,0:T(1,128)}) custom-call(s32[51]{0:T(128)} %copy-done.12, f32[4,8,768]{2,1,0:T(8,128)} %get-tuple-element.84.embed_ref, f32[1,1152]{1,0:T(1,128)} %copy-done.15, bf16[33,16,384]{2,1,0:T(8,128)(2,1)} %copy-done.9, bf16[17,16,384]{2,1,0:T(8,128)(2,1)} %copy-done.10, ...), custom_call_target="tpu_custom_call" | custom-call | flops 1000000000 | bytes 1024 | tf_op jit(solution)/shard_map/tile_rows/pallas_call | solution.py:588
  38.0 5.2 %all-to-all-start = ((bf16[32,8,512]{2,1,0:T(8,128)(2,1)}), bf16[32,8,512]{2,1,0:T(8,128)(2,1)S(1)}, u32[]{:S(2)}, u32[]{:S(2)}) async-start(bf16[32,8,512]{2,1,0:T(8,128)(2,1)} %bitcast.56), calls=%async_computation | async-start | bytes 524288 | tf_op jit(solution)/shard_map/all_to_all | solution.py:1113
  43.2 0.0 copy-start.13
  43.2 1.3 %turned_normed.1.normed_ref = bf16[384,1024]{1,0:T(8,128)(2,1)S(1)} custom-call(f32[4,256,384]{2,1,0:T(8,128)S(1)} %copy-done.4, f32[8,1536]{1,0:T(8,128)S(1)} %get-tuple-element.63.refs_3_.vectors_ref), custom_call_target="tpu_custom_call" | custom-call | flops 3000000000 | bytes 1024 | tf_op jit(solution)/shard_map/turned_normed/pallas_call | solution.py:817
  44.6 9.3 %all-to-all-done = bf16[32,8,512]{2,1,0:T(8,128)(2,1)S(1)} async-done(((bf16[32,8,512]{2,1,0:T(8,128)(2,1)}), bf16[32,8,512]{2,1,0:T(8,128)(2,1)S(1)}, u32[]{:S(2)}, u32[]{:S(2)}) %all-to-all-start) | async-done | bytes 262176 | tf_op jit(solution)/shard_map/all_to_all | solution.py:1113
  53.9 0.0 copy-start.6
  53.9 3.3 %slide_grads.1 = (f32[1,768]{1,0:T(1,128)}, f32[4,1,768]{2,1,0:T(1,128)S(1)}) custom-call(s32[51]{0:T(128)S(1)} %copy-done.13, bf16[256,512]{1,0:T(8,128)(2,1)S(1)} %bitcast.54, f32[7,768]{1,0:T(8,128)} %taps_hbm.1, bf16[768,768]{1,0:T(8,128)(2,1)} %matrix_hbm.1, f32[8,1536]{1,0:T(8,128)S(1)} %get-tuple-element.63.refs_3_.vectors_ref, ...), custom_call_target="tpu_custom_call" | custom-call | flops 3000000000 | bytes 1024 | tf_op jit(solution)/shard_map/slide_grads/pallas_call | solution.py:731
  57.2 0.1 copy-done.2
  57.4 0.5 copy-done.5
  57.8 0.1 copy-done.6
  57.9 10.4 %weight_grads.1 = (bf16[4,256,1536]{2,1,0:T(8,128)(2,1)}, bf16[2,2,2,4,48,384]{5,4,3,2,1,0:T(8,128)(2,1)S(1)}, bf16[2,2,2,4,48,384]{5,4,3,2,1,0:T(8,128)(2,1)S(1)}) custom-call(f32[4,1,768]{2,1,0:T(1,128)S(1)} %get-tuple-element.91.grad_ref, bf16[1024,1536]{1,0:T(8,128)(2,1)S(1)} %bitcast.53, bf16[4,256,768]{2,1,0:T(8,128)(2,1)S(1)} %copy-done.5, ...), custom_call_target="tpu_custom_call" | custom-call | flops 12000000000 | bytes 1024 | tf_op jit(solution)/shard_map/weight_grads/pallas_call | solution.py:1035
  68.3 0.1 collective-permute-start.5
  68.5 5.1 %tap_grads_0.1.before_ref = f32[3,49,8,128]{3,2,1,0:T(8,128)S(1)} custom-call(s32[51]{0:T(128)S(1)} %copy-done.13, bf16[4,16,16,384]{3,2,1,0:T(8,128)(2,1)S(1)} %copy-done.7, bf16[4,256,1536]{2,1,0:T(8,128)(2,1)} %get-tuple-element.99.grad_pre_ref, f32[4,256,384]{2,1,0:T(8,128)S(1)} %copy-done.4, f32[4,256,128]{2,1,0:T(8,128)S(1)} %copy-done.8, ...), custom_call_target="tpu_custom_call" | custom-call | flops 4000000000 | bytes 1024 | tf_op jit(solution)/shard_map/tap_grads_0/pallas_call | solution.py:1065
  73.6 0.3 add_convert_fusion
  73.9 1.2 %collective-permute-start.6 = (bf16[2,4,48,384]{3,2,1,0:T(8,128)(2,1)S(1)}, bf16[2,4,48,384]{3,2,1,0:T(8,128)(2,1)S(1)}, u32[]{:S(2)}, u32[]{:S(2)}) collective-permute-start(bf16[2,4,48,384]{3,2,1,0:T(8,128)(2,1)S(1)} %get-tuple-element.103), channel_id=1, source_target_pairs={{0,1},{1,0},{2,3},{3,2},{4,5},{5,4},{6,7},{7,6},{8,9},{9,8},{10,11... | collective-permute-start | bytes 884744 | tf_op jit(solution)/shard_map/ppermute | solution.py:1102
  75.2 0.6 collective-permute-start.7
  75.7 5.3 %tap_grads_2.1 = f32[32,8,384]{2,1,0:T(8,128)S(1)} custom-call(s32[51]{0:T(128)S(1)} %copy-done.13, bf16[4,16,16,384]{3,2,1,0:T(8,128)(2,1)S(1)} %copy-done.7, bf16[4,256,1536]{2,1,0:T(8,128)(2,1)} %get-tuple-element.99.grad_pre_ref, f32[4,256,384]{2,1,0:T(8,128)S(1)} %copy-done.4, f32[4,256,128]{2,1,0:T(8,128)S(1)} %copy-done.8, ...), custom_call_target="tpu_custom_call" | custom-call | flops 4000000000 | bytes 1024 | tf_op jit(solution)/shard_map/tap_grads_2/pallas_call | solution.py:1065
  81.0 0.7 slice.165
  81.7 1.7 %collective-permute-done.6 = bf16[2,4,48,384]{3,2,1,0:T(8,128)(2,1)S(1)} collective-permute-done((bf16[2,4,48,384]{3,2,1,0:T(8,128)(2,1)S(1)}, bf16[2,4,48,384]{3,2,1,0:T(8,128)(2,1)S(1)}, u32[]{:S(2)}, u32[]{:S(2)}) %collective-permute-start.6) | collective-permute-done | bytes 294944 | tf_op jit(solution)/shard_map/ppermute | solution.py:1102
  83.4 0.7 collective-permute-done.7
  84.2 0.6 collective-permute-start.8
  84.8 1.0 collective-permute-start.9
  85.8 3.2 %all-to-all-start.1 = ((bf16[32,4,384]{2,1,0:T(4,128)(2,1)}), bf16[32,4,384]{2,1,0:T(4,128)(2,1)S(1)}, u32[]{:S(2)}, u32[]{:S(2)}) async-start(bf16[32,4,384]{2,1,0:T(4,128)(2,1)} %slice.165), calls=%async_computation.1 | async-start | bytes 196608 | tf_op jit(solution)/shard_map/all_to_all | solution.py:1113
  89.0 0.4 collective-permute-done.8
  89.4 0.1 fusion.6
  89.5 0.5 collective-permute-done.9
  90.0 0.1 fusion.2
  90.0 2.8 %collective-permute-start.12 = (bf16[96,384]{1,0:T(8,128)(2,1)S(1)}, bf16[96,384]{1,0:T(8,128)(2,1)S(1)}, u32[]{:S(2)}, u32[]{:S(2)}) collective-permute-start(bf16[96,384]{1,0:T(8,128)(2,1)S(1)} %get-tuple-element.114), channel_id=1, source_target_pairs={{0,6},{2,0},{4,2},{6,4},{1,7},{3,1},{5,3},{7,5},{8,14},{10,8},{12,... | collective-permute-start | bytes 221192 | tf_op jit(solution)/shard_map/ppermute | solution.py:1102
  92.9 1.1 %collective-permute-start.10 = (bf16[96,384]{1,0:T(8,128)(2,1)S(1)}, bf16[96,384]{1,0:T(8,128)(2,1)S(1)}, u32[]{:S(2)}, u32[]{:S(2)}) collective-permute-start(bf16[96,384]{1,0:T(8,128)(2,1)S(1)} %get-tuple-element.113), channel_id=1, source_target_pairs={{0,2},{2,4},{4,6},{6,0},{1,3},{3,5},{5,7},{7,1},{8,10},{10,12},{12... | collective-permute-start | bytes 221192 | tf_op jit(solution)/shard_map/ppermute | solution.py:1102
  93.9 2.6 %all-to-all-done.1 = bf16[32,4,384]{2,1,0:T(4,128)(2,1)S(1)} async-done(((bf16[32,4,384]{2,1,0:T(4,128)(2,1)}), bf16[32,4,384]{2,1,0:T(4,128)(2,1)S(1)}, u32[]{:S(2)}, u32[]{:S(2)}) %all-to-all-start.1) | async-done | bytes 98336 | tf_op jit(solution)/shard_map/all_to_all | solution.py:1113
  96.6 0.1 convert_reduce_fusion
  96.6 0.7 dynamic_slice.3
  97.3 3.9 %collective-permute-done.11 = bf16[96,384]{1,0:T(8,128)(2,1)S(1)} collective-permute-done((bf16[96,384]{1,0:T(8,128)(2,1)S(1)}, bf16[96,384]{1,0:T(8,128)(2,1)S(1)}, u32[]{:S(2)}, u32[]{:S(2)}) %collective-permute-start.11) | collective-permute-done | bytes 73760 | tf_op jit(solution)/shard_map/ppermute | solution.py:1102
  101.3 0.7 reshape.79
  102.0 0.6 reshape.80
  (43 shorter events, 0.3 us)
Async XLA Ops:
  1.3 0.7 copy-start.14
  4.7 11.3 %copy-start.15 = (f32[1,1152]{1,0:T(1,128)}, f32[1,1152]{1,0:T(1,128)S(1)}, u32[]{:S(2)}) copy-start(f32[1,1152]{1,0:T(1,128)S(1)} %get-tuple-element.85.small_ref) | copy-start | bytes 13828
  4.8 23.9 %copy-start.12 = (s32[51]{0:T(128)}, s32[51]{0:T(128)S(1)}, u32[]{:S(2)}) copy-start(s32[51]{0:T(128)S(1)} %get-tuple-element.57.table_ref) | copy-start | bytes 616
  4.8 3.2 %collective-permute-start = (bf16[33,16,384]{2,1,0:T(8,128)(2,1)S(1)}, bf16[33,16,384]{2,1,0:T(8,128)(2,1)S(1)}, u32[]{:S(2)}, u32[]{:S(2)}) collective-permute-start(bf16[33,16,384]{2,1,0:T(8,128)(2,1)S(1)} %get-tuple-element.60), channel_id=1, source_target_pairs={{0,8},{8,0},{16,24},{24,16},{1,9},{9,1},{17,25},{25,17},{2,10},{10... | collective-permute-start | bytes 1216520 | tf_op jit(solution)/shard_map/ppermute | solution.py:1172
  5.3 10.8 %collective-permute-start.3 = (bf16[17,16,384]{2,1,0:T(8,128)(2,1)S(1)}, bf16[17,16,384]{2,1,0:T(8,128)(2,1)S(1)}, u32[]{:S(2)}, u32[]{:S(2)}) collective-permute-start(bf16[17,16,384]{2,1,0:T(8,128)(2,1)S(1)} %get-tuple-element.64), channel_id=1, source_target_pairs={{0,16},{8,24},{16,0},{24,8},{1,17},{9,25},{17,1},{25,9},{2,18},{10... | collective-permute-start | bytes 626696 | tf_op jit(solution)/shard_map/ppermute | solution.py:1172
  7.9 10.0 %collective-permute-start.4 = (bf16[17,16,384]{2,1,0:T(8,128)(2,1)S(1)}, bf16[17,16,384]{2,1,0:T(8,128)(2,1)S(1)}, u32[]{:S(2)}, u32[]{:S(2)}) collective-permute-start(bf16[17,16,384]{2,1,0:T(8,128)(2,1)S(1)} %get-tuple-element.65), channel_id=1, source_target_pairs={{0,24},{8,16},{16,8},{24,0},{1,25},{9,17},{17,9},{25,1},{2,26},{10... | collective-permute-start | bytes 626696 | tf_op jit(solution)/shard_map/ppermute | solution.py:1172
  8.0 8.1 %copy-start.9 = (bf16[33,16,384]{2,1,0:T(8,128)(2,1)}, bf16[33,16,384]{2,1,0:T(8,128)(2,1)S(1)}, u32[]{:S(2)}) copy-start(bf16[33,16,384]{2,1,0:T(8,128)(2,1)S(1)} %collective-permute-done.refs_1_.refs_0_) | copy-start | bytes 1216516
  8.0 20.6 %collective-permute-start.1 = (bf16[16,16,384]{2,1,0:T(8,128)(2,1)S(1)}, bf16[16,16,384]{2,1,0:T(8,128)(2,1)S(1)}, u32[]{:S(2)}, u32[]{:S(2)}) collective-permute-start(bf16[16,16,384]{2,1,0:T(8,128)(2,1)S(1)} %get-tuple-element.61), channel_id=1, source_target_pairs={{0,16},{8,24},{16,0},{24,8},{1,17},{9,25},{17,1},{25,9},{2,18},{10... | collective-permute-start | bytes 589832 | tf_op jit(solution)/shard_map/ppermute | solution.py:1172
  9.7 18.9 %collective-permute-start.2 = (bf16[16,16,384]{2,1,0:T(8,128)(2,1)S(1)}, bf16[16,16,384]{2,1,0:T(8,128)(2,1)S(1)}, u32[]{:S(2)}, u32[]{:S(2)}) collective-permute-start(bf16[16,16,384]{2,1,0:T(8,128)(2,1)S(1)} %get-tuple-element.62), channel_id=1, source_target_pairs={{0,24},{8,16},{16,8},{24,0},{1,25},{9,17},{17,9},{25,1},{2,26},{10... | collective-permute-start | bytes 589832 | tf_op jit(solution)/shard_map/ppermute | solution.py:1172
  16.1 12.5 %copy-start.10 = (bf16[17,16,384]{2,1,0:T(8,128)(2,1)}, bf16[17,16,384]{2,1,0:T(8,128)(2,1)S(1)}, u32[]{:S(2)}) copy-start(bf16[17,16,384]{2,1,0:T(8,128)(2,1)S(1)} %collective-permute-done.3.refs_0_.refs_1_) | copy-start | bytes 626692
  17.9 10.7 %copy-start.11 = (bf16[17,16,384]{2,1,0:T(8,128)(2,1)}, bf16[17,16,384]{2,1,0:T(8,128)(2,1)S(1)}, u32[]{:S(2)}) copy-start(bf16[17,16,384]{2,1,0:T(8,128)(2,1)S(1)} %collective-permute-done.4.refs_1_.refs_2_) | copy-start | bytes 626692
  35.2 8.0 %copy-start.4 = (f32[4,256,384]{2,1,0:T(8,128)S(1)}, f32[4,256,384]{2,1,0:T(8,128)}, u32[]{:S(2)}) copy-start(f32[4,256,384]{2,1,0:T(8,128)} %get-tuple-element.87.unit_ref) | copy-start | bytes 4718596
  38.0 15.9 %all-to-all-start = ((bf16[32,8,512]{2,1,0:T(8,128)(2,1)}), bf16[32,8,512]{2,1,0:T(8,128)(2,1)S(1)}, u32[]{:S(2)}, u32[]{:S(2)}) async-start(bf16[32,8,512]{2,1,0:T(8,128)(2,1)} %bitcast.56), calls=%async_computation | async-start | bytes 524288 | tf_op jit(solution)/shard_map/all_to_all | solution.py:1113
  43.2 10.6 %copy-start.13 = (s32[51]{0:T(128)S(1)}, s32[51]{0:T(128)}, u32[]{:S(2)}) copy-start(s32[51]{0:T(128)} %copy-done.12) | copy-start | bytes 616
  43.2 10.6 %copy-start.16 = (f32[4,1,1152]{2,1,0:T(1,128)S(1)}, f32[4,1,1152]{2,1,0:T(1,128)}, u32[]{:S(2)}) copy-start(f32[4,1,1152]{2,1,0:T(1,128)} %get-tuple-element.89.smalls_ref) | copy-start | bytes 55300
  53.9 3.3 %copy-start = (bf16[4,256,1536]{2,1,0:T(8,128)(2,1)S(1)}, bf16[4,256,1536]{2,1,0:T(8,128)(2,1)}, u32[]{:S(2)}) copy-start(bf16[4,256,1536]{2,1,0:T(8,128)(2,1)} %get-tuple-element.92) | copy-start | bytes 9437188
  53.9 3.4 %copy-start.1 = (bf16[4,256,1536]{2,1,0:T(8,128)(2,1)S(1)}, bf16[4,256,1536]{2,1,0:T(8,128)(2,1)}, u32[]{:S(2)}) copy-start(bf16[4,256,1536]{2,1,0:T(8,128)(2,1)} %get-tuple-element.94.slope_ref) | copy-start | bytes 9437188
  53.9 3.5 %copy-start.2 = (bf16[1536,384]{1,0:T(8,128)(2,1)S(1)}, bf16[1536,384]{1,0:T(8,128)(2,1)}, u32[]{:S(2)}) copy-start(bf16[1536,384]{1,0:T(8,128)(2,1)} %reduce_ref.1) | copy-start | bytes 3538948
  53.9 4.0 %copy-start.5 = (bf16[4,256,768]{2,1,0:T(8,128)(2,1)S(1)}, bf16[4,256,768]{2,1,0:T(8,128)(2,1)}, u32[]{:S(2)}) copy-start(bf16[4,256,768]{2,1,0:T(8,128)(2,1)} %get-tuple-element.93.head_slope_ref) | copy-start | bytes 4718596
  53.9 4.0 %copy-start.6 = (bf16[384,768]{1,0:T(8,128)(2,1)S(1)}, bf16[384,768]{1,0:T(8,128)(2,1)}, u32[]{:S(2)}) copy-start(bf16[384,768]{1,0:T(8,128)(2,1)} %head_ref.1) | copy-start | bytes 1769476
  57.9 10.5 %copy-start.3 = (bf16[384,1536]{1,0:T(8,128)(2,1)S(1)}, bf16[384,1536]{1,0:T(8,128)(2,1)}, u32[]{:S(2)}) copy-start(bf16[384,1536]{1,0:T(8,128)(2,1)} %expand_ref.3) | copy-start | bytes 3538948
  57.9 10.5 %copy-start.7 = (bf16[4,16,16,384]{3,2,1,0:T(8,128)(2,1)S(1)}, bf16[4,16,16,384]{3,2,1,0:T(8,128)(2,1)}, u32[]{:S(2)}) copy-start(bf16[4,16,16,384]{3,2,1,0:T(8,128)(2,1)} %get-tuple-element.98.source_ref) | copy-start | bytes 2359300
  57.9 10.5 %copy-start.8 = (f32[4,256,128]{2,1,0:T(8,128)S(1)}, f32[4,256,128]{2,1,0:T(8,128)}, u32[]{:S(2)}) copy-start(f32[4,256,128]{2,1,0:T(8,128)} %get-tuple-element.100.inv_ref) | copy-start | bytes 1572868
  68.3 5.3 %collective-permute-start.5 = (bf16[2,2,2,4,48,384]{5,4,3,2,1,0:T(8,128)(2,1)S(1)}, bf16[2,2,2,4,48,384]{5,4,3,2,1,0:T(8,128)(2,1)S(1)}, u32[]{:S(2)}, u32[]{:S(2)}) collective-permute-start(bf16[2,2,2,4,48,384]{5,4,3,2,1,0:T(8,128)(2,1)S(1)} %get-tuple-element.97), channel_id=1, source_target_pairs={{0,8},{8,0},{1,9},{9,1},{2,10},{10,2},{3,11},{11,3},{4,12},{12,4},... | collective-permute-start | bytes 3538952 | tf_op jit(solution)/shard_map/ppermute | solution.py:1102
  73.9 9.5 %collective-permute-start.6 = (bf16[2,4,48,384]{3,2,1,0:T(8,128)(2,1)S(1)}, bf16[2,4,48,384]{3,2,1,0:T(8,128)(2,1)S(1)}, u32[]{:S(2)}, u32[]{:S(2)}) collective-permute-start(bf16[2,4,48,384]{3,2,1,0:T(8,128)(2,1)S(1)} %get-tuple-element.103), channel_id=1, source_target_pairs={{0,1},{1,0},{2,3},{3,2},{4,5},{5,4},{6,7},{7,6},{8,9},{9,8},{10,11... | collective-permute-start | bytes 884744 | tf_op jit(solution)/shard_map/ppermute | solution.py:1102
  75.2 9.0 %collective-permute-start.7 = (bf16[2,4,48,384]{3,2,1,0:T(8,128)(2,1)S(1)}, bf16[2,4,48,384]{3,2,1,0:T(8,128)(2,1)S(1)}, u32[]{:S(2)}, u32[]{:S(2)}) collective-permute-start(bf16[2,4,48,384]{3,2,1,0:T(8,128)(2,1)S(1)} %get-tuple-element.104), channel_id=1, source_target_pairs={{0,16},{16,0},{1,17},{17,1},{2,18},{18,2},{3,19},{19,3},{4,20},{20... | collective-permute-start | bytes 884744 | tf_op jit(solution)/shard_map/ppermute | solution.py:1102
  84.2 5.2 %collective-permute-start.8 = (bf16[4,48,384]{2,1,0:T(8,128)(2,1)S(1)}, bf16[4,48,384]{2,1,0:T(8,128)(2,1)S(1)}, u32[]{:S(2)}, u32[]{:S(2)}) collective-permute-start(bf16[4,48,384]{2,1,0:T(8,128)(2,1)S(1)} %fusion.9), channel_id=1, source_target_pairs={{0,16},{16,0},{1,17},{17,1},{2,18},{18,2},{3,19},{19,3},{4,20},{20... | collective-permute-start | bytes 442376 | tf_op jit(solution)/shard_map/ppermute | solution.py:1102
  84.8 5.1 %collective-permute-start.9 = (bf16[4,48,384]{2,1,0:T(8,128)(2,1)S(1)}, bf16[4,48,384]{2,1,0:T(8,128)(2,1)S(1)}, u32[]{:S(2)}, u32[]{:S(2)}) collective-permute-start(bf16[4,48,384]{2,1,0:T(8,128)(2,1)S(1)} %fusion.10), channel_id=1, source_target_pairs={{0,1},{1,0},{2,3},{3,2},{4,5},{5,4},{6,7},{7,6},{8,9},{9,8},{10,11... | collective-permute-start | bytes 442376 | tf_op jit(solution)/shard_map/ppermute | solution.py:1102
  85.8 10.8 %all-to-all-start.1 = ((bf16[32,4,384]{2,1,0:T(4,128)(2,1)}), bf16[32,4,384]{2,1,0:T(4,128)(2,1)S(1)}, u32[]{:S(2)}, u32[]{:S(2)}) async-start(bf16[32,4,384]{2,1,0:T(4,128)(2,1)} %slice.165), calls=%async_computation.1 | async-start | bytes 196608 | tf_op jit(solution)/shard_map/all_to_all | solution.py:1113
  90.0 7.3 %collective-permute-start.12 = (bf16[96,384]{1,0:T(8,128)(2,1)S(1)}, bf16[96,384]{1,0:T(8,128)(2,1)S(1)}, u32[]{:S(2)}, u32[]{:S(2)}) collective-permute-start(bf16[96,384]{1,0:T(8,128)(2,1)S(1)} %get-tuple-element.114), channel_id=1, source_target_pairs={{0,6},{2,0},{4,2},{6,4},{1,7},{3,1},{5,3},{7,5},{8,14},{10,8},{12,... | collective-permute-start | bytes 221192 | tf_op jit(solution)/shard_map/ppermute | solution.py:1102
  92.9 8.3 %collective-permute-start.11 = (bf16[96,384]{1,0:T(8,128)(2,1)S(1)}, bf16[96,384]{1,0:T(8,128)(2,1)S(1)}, u32[]{:S(2)}, u32[]{:S(2)}) collective-permute-start(bf16[96,384]{1,0:T(8,128)(2,1)S(1)} %get-tuple-element.115), channel_id=1, source_target_pairs={{0,4},{2,6},{4,0},{6,2},{1,5},{3,7},{5,1},{7,3},{8,12},{10,14},{12... | collective-permute-start | bytes 221192 | tf_op jit(solution)/shard_map/ppermute | solution.py:1102
  92.9 8.3 %collective-permute-start.10 = (bf16[96,384]{1,0:T(8,128)(2,1)S(1)}, bf16[96,384]{1,0:T(8,128)(2,1)S(1)}, u32[]{:S(2)}, u32[]{:S(2)}) collective-permute-start(bf16[96,384]{1,0:T(8,128)(2,1)S(1)} %get-tuple-element.113), channel_id=1, source_target_pairs={{0,2},{2,4},{4,6},{6,0},{1,3},{3,5},{5,7},{7,1},{8,10},{10,12},{12... | collective-permute-start | bytes 221192 | tf_op jit(solution)/shard_map/ppermute | solution.py:1102
